TPU v7x, 32 devices: a whole 2x2x4 slice. The times are simulated.
32 devices in a mesh: feat: 4 (over y, core), node: 8 (over z, x).
Axes of the slice: x: 2, y: 2, z: 4, core: 2. Of those that a mesh axis runs over, the one named last changes fastest.
Arguments:
- node_feats: float32 [256, 32768], P('feat', 'node'), may hold values from -6 to 6
- tiles: float32 [64, 16, 128, 128], P('node'), may hold values from -0.5 to 0.5
- send_col: int32 [64, 16], P('node'), may hold values from 0 to 31
- recv_row: int32 [64, 16], P('node'), may hold values from -1 to 31, as said below
- degree: int32 [32768], P('node'), may hold values from 1 to 8
- w_self: float32 [256, 256], replicated, may hold values from -0.375 to 0.375
- w_neigh: float32 [256, 256], replicated, may hold values from -0.375 to 0.375
- bias: float32 [256], replicated, may hold values from -3 to 3
- cotangent: float32 [32768, 256], P(('node', 'feat')), may hold values from -6 to 6
Outputs:
- activated: float32 [32768, 256], P(('node', 'feat'))
- grad_feats: float32 [256, 32768], P('feat', 'node')
- grad_self: float32 [256, 256], replicated
- grad_neigh: float32 [256, 256], replicated
- grad_bias: float32 [256], replicated
Inputs may be any that keep to these rules, and one draw needn't show every extreme that they name: `recv_row`: at most 16 live slots from one sender to one owner; every sender fills all 16 slots to itself, and one owner receives 16 live slots from every sender; -1 marks an empty slot.
All inputs are finite; a program needn't handle non-finite values.
Results may differ from a plain program's by a relative error of at most 0.0003.
Values sent between devices are 32-bit elements; how exact they have to be, the bound alone decides.
No kernel may reach another device: no remote copies, remote signals or barrier semaphores. Data moves between devices by JAX's collectives and lax.ppermute only.
A program may use at most 64 MiB of HBM per device.

v0:
```python
import jax
import jax.numpy as jnp
from jax import lax
from jax.sharding import PartitionSpec as P

TB = 128


def shards(node_feats, tiles, send_col, recv_row, degree, w_self, w_neigh, bias, cotangent):
    slices, owned = node_feats.shape
    blocks = owned // TB
    block_ids = jnp.arange(blocks, dtype=jnp.int32)
    scale = degree.astype(jnp.float32)[None, :]
    col_onehot = (send_col[..., None] == block_ids).astype(jnp.float32)
    row_onehot = (recv_row[..., None] == block_ids).astype(jnp.float32)
    feat_blocks = node_feats.reshape(slices, blocks, TB)
    picked = jnp.einsum("dcb,fbj->dcfj", col_onehot, feat_blocks, precision=lax.Precision.HIGHEST)
    partial_value = jnp.einsum("dcfj,dcij->dcfi", picked, tiles, precision=lax.Precision.HIGHEST)
    arrived = lax.all_to_all(partial_value, "node", split_axis=0, concat_axis=0, tiled=True)
    summed = jnp.einsum("scfi,scb->fbi", arrived, row_onehot, precision=lax.Precision.HIGHEST)
    neighbour = summed.reshape(slices, owned) / scale
    offset = lax.axis_index("feat") * slices
    self_rows = lax.dynamic_slice_in_dim(w_self, offset, slices, 0)
    neigh_rows = lax.dynamic_slice_in_dim(w_neigh, offset, slices, 0)
    first = lax.dot_general(
        node_feats, self_rows, (((0,), (0,)), ((), ())), precision=lax.Precision.HIGHEST
    )
    second = lax.dot_general(
        neighbour, neigh_rows, (((0,), (0,)), ((), ())), precision=lax.Precision.HIGHEST
    )
    pre = lax.psum_scatter(first + second, "feat", scatter_dimension=0, tiled=True) + bias
    sigma = jax.nn.sigmoid(pre)
    activated = pre * sigma
    gpre = cotangent * sigma * (1.0 + pre * (1.0 - sigma))
    piece = lax.all_gather(gpre, "feat", axis=0, tiled=True)
    self_back = lax.dot_general(
        self_rows, piece, (((1,), (1,)), ((), ())), precision=lax.Precision.HIGHEST
    )
    neigh_back = lax.dot_general(
        neigh_rows, piece, (((1,), (1,)), ((), ())), precision=lax.Precision.HIGHEST
    )
    gathered = piece.T
    slice_self = lax.dot_general(
        node_feats, gathered, (((1,), (1,)), ((), ())), precision=lax.Precision.HIGHEST
    )
    slice_neigh = lax.dot_general(
        neighbour, gathered, (((1,), (1,)), ((), ())), precision=lax.Precision.HIGHEST
    )
    grad_bias_part = jnp.sum(gathered, axis=1)
    slice_self, slice_neigh, grad_bias = lax.psum((slice_self, slice_neigh, grad_bias_part), "node")
    grad_self, grad_neigh = (
        lax.all_gather(slice_self, "feat", axis=0, tiled=True),
        lax.all_gather(slice_neigh, "feat", axis=0, tiled=True),
    )
    gneigh = (neigh_back / scale).reshape(slices, blocks, TB)
    outgoing = jnp.einsum("scb,fbi->scfi", row_onehot, gneigh, precision=lax.Precision.HIGHEST)
    returned = lax.all_to_all(outgoing, "node", split_axis=0, concat_axis=0, tiled=True)
    spread = jnp.einsum("dcfi,dcij->dcfj", returned, tiles, precision=lax.Precision.HIGHEST)
    placed = jnp.einsum("dcfj,dcb->fbj", spread, col_onehot, precision=lax.Precision.HIGHEST)
    grad_feats = self_back + placed.reshape(slices, owned)
    return (activated, grad_feats, grad_self, grad_neigh, grad_bias)


def solution(mesh):
    return jax.shard_map(
        shards,
        mesh=mesh,
        in_specs=(
            P("feat", "node"),
            P("node", None, None, None),
            P("node", None),
            P("node", None),
            P("node"),
            P(),
            P(),
            P(),
            P(("node", "feat"), None),
        ),
        out_specs=(P(("node", "feat"), None), P("feat", "node"), P(), P(), P()),
        check_vma=False,
    )
```

profile of v0, /device:TPU:0, one launch (start us, length us, event | category | flops | bytes accessed | tf_op | source)
XLA Modules:
  0.0 404.1 jit_solution(2562620880896973926)
XLA Ops:
  7.2 0.0 copy-start
  7.2 1.5 copy.30
  8.6 2.5 fusion.17
  11.2 18.7 %fusion.3 = f32[8,16,64,128]{3,2,1,0:T(8,128)S(1)} fusion(f32[8,16,128,128]{3,2,1,0:T(8,128)} %param.10, f32[8,16,64,128]{3,1,2,0:T(8,128)S(1)} %fusion.17), kind=kOutput, calls=%fused_computation.6 | convolution fusion | flops 1610612736 | bytes 16777216 | tf_op jit(solution)/shard_map/dcfj,dcij->dcfi/dot_general | solution.py:18
  29.9 4.3 %copy.23 = f32[8,16,64,128]{3,1,2,0:T(8,128)} copy(f32[8,16,64,128]{3,2,1,0:T(8,128)S(1)} %fusion.3) | data formatting | bytes 8388608 | tf_op jit(solution)/shard_map/dcfj,dcij->dcfi/dot_general | solution.py:18
  34.2 7.4 %all-to-all-start = ((f32[8,16,64,128]{3,1,2,0:T(8,128)}), f32[8,16,64,128]{3,1,2,0:T(8,128)}, u32[]{:S(2)}, u32[]{:S(2)}) async-start(f32[8,16,64,128]{3,1,2,0:T(8,128)} %copy.23), calls=%async_computation | async-start | bytes 8388608 | tf_op jit(solution)/shard_map/all_to_all | solution.py:19
  41.6 0.6 reduce-scatter.2.cloned.1.call-start
  42.2 0.0 copy-done.6
  42.2 0.0 copy-start.4
  42.2 92.7 %all-to-all-done = f32[8,16,64,128]{3,1,2,0:T(8,128)} async-done(((f32[8,16,64,128]{3,1,2,0:T(8,128)}), f32[8,16,64,128]{3,1,2,0:T(8,128)}, u32[]{:S(2)}, u32[]{:S(2)}) %all-to-all-start) | async-done | bytes 4194336 | tf_op jit(solution)/shard_map/all_to_all | solution.py:19
  134.9 0.0 copy-done.7
  134.9 3.8 fusion.14
  138.7 0.0 copy-done
  138.8 4.0 fusion.8
  142.7 0.0 copy-done.4
  142.7 6.0 %fusion = f32[4096,256]{0,1:T(8,128)} fusion(f32[4096,256]{0,1:T(8,128)S(1)} %fusion.8, f32[64,4096]{1,0:T(8,128)S(1)} %copy-done.4, f32[256,256]{1,0:T(8,128)} %param.14, s32[]{:T(128)S(6)} %select_n.4), kind=kOutput, calls=%fused_computation.1 | convolution fusion | flops 806354944 | bytes 9502724 | tf_op jit(solution)/shard_map/dot_general | solution.py:25
  148.8 0.0 reduce-scatter.2.cloned.1.call-update
  148.8 0.2 all-gather.2.cloned.1.call-start
  149.0 1.0 copy-done.5
  150.0 1.3 copy.19
  151.3 41.2 %reduce-scatter.2.cloned.1.call-done = f32[1024,256]{0,1:T(8,128)} async-done(((f32[4096,256]{0,1:T(8,128)}), f32[1024,256]{0,1:T(8,128)}) %reduce-scatter.2.cloned.1.call-update) | async-done | bytes 1048592 | tf_op jit(solution)/shard_map/reduce_scatter | solution.py:31
  192.5 0.0 copy-done.9
  192.5 3.0 add_multiply_fusion
  195.6 0.0 all-gather.2.cloned.1.call-update
  195.6 34.6 %all-gather.2.cloned.1.call-done = f32[4096,256]{0,1:T(8,128)} async-done(((f32[1024,256]{0,1:T(8,128)}), f32[4096,256]{0,1:T(8,128)}) %all-gather.2.cloned.1.call-update) | async-done | bytes 4194320 | tf_op jit(solution)/shard_map/all_gather | solution.py:35
  230.2 4.8 %fusion.5 = f32[8,8,32,128]{3,1,2,0:T(8,128)S(1)} fusion(f32[4096,256]{0,1:T(8,128)} %all-gather.2.cloned.1.call-done, f32[4096]{0:T(1024)S(1)} %convert_element_type.2, f32[256,256]{1,0:T(8,128)S(1)} %copy-done, s32[]{:T(128)S(6)} %select_n.4), kind=kOutput, calls=%fused_computation.8 | convolution fusion | flops 805568512 | bytes 5324804 | tf_op jit(solution)/shard_map/dot_general | solution.py:39
  235.0 0.2 copy.32
  235.2 1.8 fusion.12
  237.1 3.2 copy.27
  240.3 5.5 %all-to-all-start.1 = ((f32[8,16,64,128]{3,2,1,0:T(8,128)}), f32[8,16,64,128]{3,2,1,0:T(8,128)}, u32[]{:S(2)}, u32[]{:S(2)}) async-start(f32[8,16,64,128]{3,2,1,0:T(8,128)} %copy.27), calls=%async_computation.2 | async-start | bytes 8388608 | tf_op jit(solution)/shard_map/all_to_all | solution.py:57
  245.8 0.2 all-reduce.3.cloned.1.call-start
  246.1 6.9 %convolution_bitcast_fusion.1 = f32[64,256]{1,0:T(8,128)} fusion(f32[4096,256]{0,1:T(8,128)} %all-gather.2.cloned.1.call-done, f32[64,4096]{1,0:T(8,128)S(1)} %copy-done.4), kind=kOutput, calls=%fused_computation.9 | convolution fusion | flops 805306368 | bytes 5308416 | tf_op jit(solution)/shard_map/dot_general | solution.py:43
  253.0 4.7 %fusion.7 = f32[64,256]{1,0:T(8,128)} fusion(f32[4096,256]{0,1:T(8,128)S(1)} %copy-done.2, f32[8,8,32,128]{3,2,1,0:T(8,128)S(1)} %bitcast.62, f32[4096]{0:T(1024)S(1)} %convert_element_type.2), kind=kOutput, calls=%fused_computation.14 | convolution fusion | flops 805568512 | bytes 5324800 | tf_op jit(solution)/shard_map/dot_general | solution.py:46
  257.7 0.0 all-reduce.3.cloned.1.call-update
  257.7 1.3 copy.20
  259.0 2.5 reduce_sum.9
  261.5 70.9 %psum.23 = f32[256]{0:T(256)} all-reduce(f32[256]{0:T(256)S(1)} %reduce_sum.9), channel_id=1, replica_groups=mesh['feat'=4,'node'=8] {'node'}, use_global_device_ids=true, to_apply=%region_4.0 | all-reduce | flops 256 | bytes 2048 | tf_op jit(solution)/shard_map/psum | solution.py:50
  332.4 31.7 %all-reduce.3.cloned.1.call-done = (f32[64,256]{1,0:T(8,128)}, f32[64,256]{1,0:T(8,128)}) async-done(((f32[64,256]{1,0:T(8,128)}, f32[64,256]{1,0:T(8,128)}), (f32[64,256]{1,0:T(8,128)}, f32[64,256]{1,0:T(8,128)})) %all-reduce.3.cloned.1.call-update) | async-done | bytes 131088 | tf_op jit(solution)/shard_map/psum | solution.py:50
  364.0 6.0 %all_gather.10 = f32[256,256]{1,0:T(8,128)S(1)} all-gather(f32[64,256]{1,0:T(8,128)} %get-tuple-element.15), channel_id=1, replica_groups=mesh['feat'=4,'node'=8] {'feat'}, dimensions={0}, use_global_device_ids=true | all-gather | bytes 327680 | tf_op jit(solution)/shard_map/all_gather | solution.py:52
  370.0 6.3 %all_gather.11 = f32[256,256]{1,0:T(8,128)S(1)} all-gather(f32[64,256]{1,0:T(8,128)} %get-tuple-element.16), channel_id=1, replica_groups=mesh['feat'=4,'node'=8] {'feat'}, dimensions={0}, use_global_device_ids=true | all-gather | bytes 327680 | tf_op jit(solution)/shard_map/all_gather | solution.py:53
  376.4 0.0 all-to-all-done.1
  376.4 10.6 %fusion.31 = f32[8,16,64,128]{3,2,1,0:T(8,128)S(1)} fusion(f32[8,16,64,128]{3,2,1,0:T(8,128)} %all-to-all-done.1, f32[8,16,128,128]{3,2,1,0:T(8,128)} %param.10), kind=kOutput, calls=%fused_computation.36 | convolution fusion | flops 1610612736 | bytes 16777216 | tf_op jit(solution)/shard_map/dcfi,dcij->dcfj/dot_general | solution.py:58
  386.9 0.0 copy-start.1
  386.9 4.0 %fusion.1 = f32[32,64,128,1]{2,0,3,1:T(8,128)S(1)} fusion(f32[8,16,64,128]{3,2,1,0:T(8,128)S(1)} %fusion.31, s32[8,16]{1,0:T(8,128)S(1)} %copy-done.8), kind=kOutput, calls=%fused_computation.4 | convolution fusion | flops 402657280 | bytes 5243392 | tf_op jit(solution)/shard_map/dcfj,dcb->fbj/dot_general | solution.py:59
  391.0 0.0 copy-done.3
  391.0 4.9 %convolution_add_fusion = f32[64,4096]{1,0:T(8,128)} fusion(f32[4096,256]{0,1:T(8,128)S(1)} %copy-done.3, f32[8,8,32,128]{3,2,1,0:T(8,128)S(1)} %bitcast.63, f32[256,256]{1,0:T(8,128)} %param.14, s32[]{:T(128)S(6)} %select_n.4), kind=kOutput, calls=%fused_computation.3 | convolution fusion | flops 805568512 | bytes 6356996 | tf_op jit(solution)/shard_map/dot_general | solution.py:36
  395.9 0.7 copy.46
  396.6 0.7 copy.47
  (11 shorter events, 0.0 us)
Async XLA Ops:
  7.2 131.6 %copy-start = (f32[256,256]{1,0:T(8,128)S(1)}, f32[256,256]{1,0:T(8,128)}, u32[]{:S(2)}) copy-start(f32[256,256]{1,0:T(8,128)} %param.15) | copy-start | bytes 786436
  34.2 8.0 %copy-start.6 = (s32[4096]{0:T(1024)S(1)}, s32[4096]{0:T(1024)}, u32[]{:S(2)}) copy-start(s32[4096]{0:T(1024)} %param.13) | copy-start | bytes 49156
  34.2 100.7 %copy-start.7 = (s32[8,16]{1,0:T(8,128)S(1)}, s32[8,16]{1,0:T(8,128)}, u32[]{:S(2)}) copy-start(s32[8,16]{1,0:T(8,128)} %param.12) | copy-start | bytes 1540
  34.2 100.7 %all-to-all-start = ((f32[8,16,64,128]{3,1,2,0:T(8,128)}), f32[8,16,64,128]{3,1,2,0:T(8,128)}, u32[]{:S(2)}, u32[]{:S(2)}) async-start(f32[8,16,64,128]{3,1,2,0:T(8,128)} %copy.23), calls=%async_computation | async-start | bytes 8388608 | tf_op jit(solution)/shard_map/all_to_all | solution.py:19
  41.6 150.9 %reduce-scatter.2.cloned.1.call-start = ((), (), s32[]{:S(2)}) async-start(), calls=%async_computation.3 | async-start | bytes 5242880 | tf_op jit(solution)/shard_map/reduce_scatter | solution.py:31
  42.2 100.5 %copy-start.4 = (f32[64,4096]{1,0:T(8,128)S(1)}, f32[64,4096]{1,0:T(8,128)}, u32[]{:S(2)}) copy-start(f32[64,4096]{1,0:T(8,128)} %param.9) | copy-start | bytes 3145732
  148.8 1.2 copy-start.5
  148.8 43.8 %copy-start.9 = (f32[256]{0:T(256)S(1)}, f32[256]{0:T(256)}, u32[]{:S(2)}) copy-start(f32[256]{0:T(256)} %param.16) | copy-start | bytes 3076
  148.8 81.4 %all-gather.2.cloned.1.call-start = ((), (), s32[]{:S(2)}) async-start(), calls=%async_computation.4 | async-start | bytes 5242880 | tf_op jit(solution)/shard_map/all_gather | solution.py:35
  240.3 136.1 %all-to-all-start.1 = ((f32[8,16,64,128]{3,2,1,0:T(8,128)}), f32[8,16,64,128]{3,2,1,0:T(8,128)}, u32[]{:S(2)}, u32[]{:S(2)}) async-start(f32[8,16,64,128]{3,2,1,0:T(8,128)} %copy.27), calls=%async_computation.2 | async-start | bytes 8388608 | tf_op jit(solution)/shard_map/all_to_all | solution.py:57
  245.8 118.2 %all-reduce.3.cloned.1.call-start = ((), (), s32[]{:S(2)}) async-start(), calls=%async_computation.5 | async-start | bytes 262144 | tf_op jit(solution)/shard_map/psum | solution.py:50
  246.1 6.9 %copy-start.2 = (f32[4096,256]{0,1:T(8,128)S(1)}, f32[4096,256]{0,1:T(8,128)}, u32[]{:S(2)}) copy-start(f32[4096,256]{0,1:T(8,128)} %all-gather.2.cloned.1.call-done) | copy-start | bytes 12582916
  376.3 10.6 %copy-start.8 = (s32[8,16]{1,0:T(8,128)S(1)}, s32[8,16]{1,0:T(8,128)}, u32[]{:S(2)}) copy-start(s32[8,16]{1,0:T(8,128)} %param.11) | copy-start | bytes 1540
  386.9 4.1 %copy-start.3 = (f32[4096,256]{0,1:T(8,128)S(1)}, f32[4096,256]{0,1:T(8,128)}, u32[]{:S(2)}) copy-start(f32[4096,256]{0,1:T(8,128)} %all-gather.2.cloned.1.call-done) | copy-start | bytes 12582916
  386.9 10.4 %copy-start.1 = (f32[256,256]{1,0:T(8,128)S(1)}, f32[256,256]{1,0:T(8,128)}, u32[]{:S(2)}) copy-start(f32[256,256]{1,0:T(8,128)} %param.15) | copy-start | bytes 786436
Sparse Core Ops, SparseCore 0:
  148.9 43.5 reduce-scatter.1
  195.7 34.4 all-gather.1
  257.9 106.1 all-reduce.2
where the time goes:
time: 412 us; the launch traced here: 404 us
  waiting for transfers between devices  200 us (49%)
  blocking collectives  83.2 us (20%)
  matrix products  72.8 us (18%)
  local copies, waits for them, and re-layouts  14.2 us (3%)
  between operations  14.2 us (3%)
  starting transfers between devices  13.9 us (3%)
  other arithmetic  5.5 us (1%)
    all_to_all x1, waiting for transfers between devices, shards(): lax.all_to_all(partial_value, 'node', split_axis=0, concat_axis=0, tiled=...  92.7 us
    psum x1, blocking collectives, shards(): lax.psum((slice_self, slice_neigh, grad_bias_part), 'node')  70.9 us
    reduce_scatter x1, waiting for transfers between devices, shards(): lax.psum_scatter(first + second, 'feat', scatter_dimension=0, tiled=True)  41.2 us
    all_gather x1, waiting for transfers between devices, shards(): piece = lax.all_gather(gpre, 'feat', axis=0, tiled=True)  34.6 us
    psum x1, waiting for transfers between devices, shards(): lax.psum((slice_self, slice_neigh, grad_bias_part), 'node')  31.7 us
    dot_general x1, matrix products, shards(): jnp.einsum('dcfj,dcij->dcfi', picked, tiles, precision=lax.Precision.HIGH...  18.7 us
    dot_general x1, matrix products, shards(): jnp.einsum('dcfi,dcij->dcfj', returned, tiles, precision=lax.Precision.HI...  10.6 us
  transfers between devices with their start and end apart: 5, of which 4 were waited for; matrix products, arithmetic and copies ran while one was open for 4% of the time, Pallas kernels for 0%

commit v1 on v0

v1 whole, which is shorter than its diff:
```python
import functools

import jax
import jax.numpy as jnp
from jax import lax
from jax.experimental import pallas as pl
from jax.experimental.pallas import tpu as pltpu
from jax.sharding import PartitionSpec as P

TB = 128
F32 = jnp.float32
BF16 = jnp.bfloat16
HIGH = lax.Precision.HIGH
CHUNKS = 2
VMEM_BYTES = 28 * 2**20

FAR_OUTER, FAR_INNER, NEAR, SELF = range(4)


def owner(role, z):
    if role == FAR_OUTER:
        return jnp.where(z < 2, 3, 0)
    if role == FAR_INNER:
        return jnp.where(z < 2, 2, 1)
    if role == NEAR:
        return z + 1 - 2 * (z % 2)
    return z


def owner_dynamic(role, z):
    return jnp.where(
        role == FAR_OUTER,
        owner(FAR_OUTER, z),
        jnp.where(role == FAR_INNER, owner(FAR_INNER, z), jnp.where(role == NEAR, owner(NEAR, z), z)),
    )


def split(value):
    high = value.astype(BF16)
    return high, (value - high.astype(F32)).astype(BF16)


def dot_nn(a, b):
    return lax.dot_general(a, b, (((1,), (0,)), ((), ())), preferred_element_type=F32)


def dot_nt(a, b):
    return lax.dot_general(a, b, (((1,), (1,)), ((), ())), preferred_element_type=F32)


def stacked(value):
    high, low = split(value)
    return jnp.concatenate(
        [jnp.concatenate([high, high], 1), jnp.concatenate([low, jnp.zeros_like(low)], 1)], 0
    )


def times_tile_t(value, tile):
    rows = value.shape[0]
    out = dot_nt(stacked(value), jnp.concatenate(split(tile), 1))
    return out[:rows] + out[rows:]


def times_tile(value, tile):
    rows = value.shape[0]
    out = dot_nn(stacked(value), jnp.concatenate(split(tile), 0))
    return out[:rows] + out[rows:]


def lanes(block):
    return pl.ds(pl.multiple_of(block * TB, TB), TB)


class Layer:
    def __init__(self, slices, owned, cap, parts, width):
        self.slices, self.owned, self.cap, self.parts, self.width = slices, owned, cap, parts, width
        self.blocks = owned // TB
        self.per_part = self.blocks // parts
        self.per_piece = self.per_part // CHUNKS
        self.per_chunk = self.blocks // CHUNKS
        self.piece_rows = self.per_piece * TB

    def spot(self, row):
        row = jnp.maximum(row, 0)
        part, inside = row // self.per_part, row % self.per_part
        return inside // self.per_piece, part * self.per_piece + inside % self.per_piece

    def block(self, chunk, part, inside):
        return part * self.per_part + chunk * self.per_piece + inside

    def full(self, *shape):
        return pl.BlockSpec(shape, lambda i, *_: (0,) * len(shape))

    def tile_spec(self, role, other):
        def where(i, place, *_):
            x = 1 - place[1] if other else place[1]
            return (owner(role, place[0]) * 2 + x, 0, 0, 0)

        return pl.BlockSpec((1, self.cap, TB, TB), where)

    def call(self, body, scalars, grid, in_specs, args, out_specs, out_shape, scratch=(), aliases=None, work=1):
        return pl.pallas_call(
            body,
            grid_spec=pltpu.PrefetchScalarGridSpec(
                num_scalar_prefetch=len(scalars),
                grid=grid,
                in_specs=in_specs,
                out_specs=out_specs,
                scratch_shapes=scratch,
            ),
            out_shape=out_shape,
            input_output_aliases=aliases or {},
            compiler_params=pltpu.CompilerParams(vmem_limit_bytes=VMEM_BYTES),
            cost_estimate=pl.CostEstimate(flops=work * 10**8, bytes_accessed=4 * 2**20, transcendentals=0),
        )(*scalars, *args)

    def slots(self):
        return jax.ShapeDtypeStruct((self.cap, self.slices, TB), F32)

    def dense(self):
        return jax.ShapeDtypeStruct((self.per_chunk, self.slices, TB), F32)

    def partial(self, role, place, cols, feats, tiles):
        def body(place, cols, feats, tile, out):
            owned_by = owner(role, place[0]) * 2 + 1 - place[1]
            for c in range(self.cap):
                out[c] = times_tile_t(feats[:, lanes(cols[owned_by * self.cap + c])], tile[0, c])

        return self.call(
            body, (place, cols), (1,),
            [self.full(self.slices, self.owned), self.tile_spec(role, True)], (feats, tiles),
            self.full(self.cap, self.slices, TB), self.slots(),
        )

    def local(self, place, cols, rows, feats, tiles):
        def where(i, place, *_):
            return (owner_dynamic(i, place[0]) * 2 + place[1], 0, 0, 0)

        def body(place, cols, rows, feats, tile, out):
            owned_by = owner_dynamic(pl.program_id(0), place[0]) * 2 + place[1]
            out[...] = jnp.zeros_like(out)
            for c in range(self.cap):
                row = rows[owned_by * self.cap + c]
                chunk, spot = self.spot(row)
                value = times_tile_t(feats[:, lanes(cols[owned_by * self.cap + c])], tile[0, c])
                out[0, chunk * self.per_chunk + spot] += jnp.where(row >= 0, value, 0.0)

        return self.call(
            body, (place, cols, rows), (4,),
            [self.full(self.slices, self.owned), pl.BlockSpec((1, self.cap, TB, TB), where)], (feats, tiles),
            pl.BlockSpec((1, self.blocks, self.slices, TB), lambda i, *_: (i, 0, 0, 0)),
            jax.ShapeDtypeStruct((4, self.blocks, self.slices, TB), F32), work=4,
        )

    def joined(self, role, place, rows, sums, slots):
        def body(place, rows, sums, slots, *outs):
            z, x = place[0], place[1]
            for k, out in enumerate(outs):
                out[...] = sums[0, k * self.per_chunk : (k + 1) * self.per_chunk]
            for c in range(self.cap):
                row = rows[(owner(role, z) * 2 + 1 - x) * self.cap + c]
                chunk, spot = self.spot(row)
                for k, out in enumerate(outs):
                    out[spot] += jnp.where((row >= 0) & (chunk == k), slots[c], 0.0)

        shape = (self.per_chunk, self.slices, TB)
        return self.call(
            body, (place, rows), (1,),
            [pl.BlockSpec((1, self.blocks, self.slices, TB), lambda i, *_: (role, 0, 0, 0)),
             self.full(self.cap, self.slices, TB)], (sums, slots),
            [self.full(*shape)] * CHUNKS, [self.dense()] * CHUNKS,
        )

    def project(self, k, place, pieces, feats, w_self, w_neigh, inverse):
        def body(place, own, near, inner, outer, feats, w_self, w_neigh, inverse, neighbour, send, keep):
            core = place[3]
            high, low = split(jnp.concatenate([w_self[...], w_neigh[...]], 0))
            twice = jnp.concatenate([high, high], 0)
            for y in range(2):
                for out, side in ((send, 1 - core), (keep, core)):
                    for j in range(self.per_piece):
                        part = 2 * y + side
                        spot, block = part * self.per_piece + j, self.block(k, part, j)
                        mean = (own[spot] + near[spot] + inner[spot] + outer[spot]) * inverse[pl.ds(block, 1), :]
                        neighbour[spot] = mean
                        both = jnp.concatenate([feats[:, lanes(block)], mean], 0).T
                        both_high, both_low = split(both)
                        out[y, j * TB : (j + 1) * TB, :] = dot_nn(
                            jnp.concatenate([both_high, both_low], 1), twice
                        ) + dot_nn(both_high, low)

        dense = self.full(self.per_chunk, self.slices, TB)
        share = jax.ShapeDtypeStruct((2, self.piece_rows, self.width), F32)
        return self.call(
            body, (place,), (1,),
            [dense] * 4 + [self.full(self.slices, self.owned)] + [self.weight_spec()] * 2 + [self.full(self.blocks, TB)],
            (*pieces, feats, w_self, w_neigh, inverse),
            [dense] + [self.full(2, self.piece_rows, self.width)] * 2, [self.dense(), share, share],
        )

    def weight_spec(self):
        return pl.BlockSpec((self.slices, self.width), lambda i, place, *_: (2 * place[2] + place[3], 0))

    def half_spec(self, other):
        return pl.BlockSpec(
            (1, self.piece_rows, self.width),
            lambda i, place, *_: (1 - place[2] if other else place[2], 0, 0),
        )

    def for_other_y(self, place, keep, got):
        def body(place, keep, got, out):
            out[...] = keep[0] + got[0]

        shape = (self.piece_rows, self.width)
        return self.call(
            body, (place,), (1,), [self.half_spec(True)] * 2, (keep, got),
            self.full(*shape), jax.ShapeDtypeStruct(shape, F32),
        )

    def activate(self, k, place, keep, got, far, bias, cotangent, activated):
        def body(place, keep, got, far, bias, cotangent, *rest):
            out, grad = rest[-2:]
            pre = keep[0] + got[0] + far[...] + bias[...]
            sigma = jax.nn.sigmoid(pre)
            out[...] = pre * sigma
            grad[...] = cotangent[...] * (sigma * (1.0 + pre * (1.0 - sigma)))

        shape = (self.piece_rows, self.width)
        rows = pl.BlockSpec(shape, lambda i, *_: (k, 0))
        in_specs = [self.half_spec(False)] * 2 + [self.full(*shape), self.full(1, self.width), rows]
        args = [keep, got, far, bias, cotangent]
        aliases = {}
        if activated is not None:
            aliases = {1 + len(args): 0}
            in_specs.append(pl.BlockSpec(memory_space=pl.ANY))
            args.append(activated)
        return self.call(
            body, (place,), (1,), in_specs, args, [rows, self.full(*shape)],
            [jax.ShapeDtypeStruct(cotangent.shape, F32), jax.ShapeDtypeStruct(shape, F32)], aliases=aliases,
        )

    def back(self, weight, grad):
        rows = weight.shape[0]
        high, low = split(weight)
        grad_high, grad_low = split(grad)
        out = dot_nt(jnp.concatenate([high, low], 0), grad_high)
        return out[:rows] + out[rows:] + dot_nt(high, grad_low)

    def parts_of(self, place, grads):
        y, core = place[2], place[3]
        return (
            (2 * y + core, grads[0]),
            (2 * (1 - y) + core, grads[1]),
            (2 * y + 1 - core, grads[2]),
            (2 * (1 - y) + 1 - core, grads[3]),
        )

    def neighbour_grad(self, k, place, w_neigh, inverse, grads):
        def body(place, w_neigh, inverse, *rest):
            out = rest[-1]
            for part, grad in self.parts_of(place, rest[:-1]):
                value = self.back(w_neigh[...], grad[...])
                for j in range(self.per_piece):
                    block = self.block(k, part, j)
                    out[part * self.per_piece + j] = value[:, j * TB : (j + 1) * TB] * inverse[pl.ds(block, 1), :]

        return self.call(
            body, (place,), (1,),
            [self.weight_spec(), self.full(self.blocks, TB)] + [self.full(self.piece_rows, self.width)] * 4,
            (w_neigh, inverse, *grads),
            self.full(self.per_chunk, self.slices, TB), self.dense(),
        )

    def weight_grad(self, k, place, w_self, feats, neighbour, grads):
        def body(place, w_self, feats, neighbour, *rest):
            self_out, weights_out = rest[-2:]
            total = jnp.zeros((2 * self.slices, self.width), F32)
            bias = jnp.zeros((1, self.width), F32)
            for part, grad in self.parts_of(place, rest[:-2]):
                value = self.back(w_self[...], grad[...])
                first = part * self.per_piece
                for j in range(self.per_piece):
                    self_out[first + j] = value[:, j * TB : (j + 1) * TB]
                start = pl.multiple_of(self.block(k, part, 0) * TB, TB)
                rows = jnp.concatenate(
                    [
                        feats[:, pl.ds(start, self.piece_rows)],
                        jnp.concatenate([neighbour[first + j] for j in range(self.per_piece)], 1),
                    ],
                    0,
                )
                high, low = split(rows)
                grad_high, grad_low = split(grad[...])
                total += (dot_nn(high, grad_high) + dot_nn(low, grad_high)) + dot_nn(high, grad_low)
                bias += jnp.sum(grad[...], axis=0, keepdims=True)
            weights_out[: 2 * self.slices, :] = total
            weights_out[2 * self.slices :, :] = jnp.broadcast_to(bias, (8, self.width))

        dense = self.full(self.per_chunk, self.slices, TB)
        shape = (2 * self.slices + 8, self.width)
        return self.call(
            body, (place,), (1,),
            [self.weight_spec(), self.full(self.slices, self.owned), dense]
            + [self.full(self.piece_rows, self.width)] * 4,
            (w_self, feats, neighbour, *grads),
            [dense, self.full(*shape)], [self.dense(), jax.ShapeDtypeStruct(shape, F32)], work=2,
        )

    def gather(self, place, sources, held):
        z = place[0]
        for k in range(CHUNKS):
            spots = slice(k * self.per_chunk, (k + 1) * self.per_chunk)
            if len(sources) == CHUNKS:
                held[spots] = sources[k][...]
            else:
                outer = (z == 0) | (z == 3)

                @pl.when(outer)
                def _():
                    held[spots] = sources[CHUNKS + k][...]

                @pl.when(jnp.logical_not(outer))
                def _():
                    held[spots] = sources[k][...]

    def held(self):
        return pltpu.VMEM((self.blocks, self.slices, TB), F32)

    def picked(self, role, place, rows, sources):
        def body(place, rows, *rest):
            out, held = rest[-2:]
            self.gather(place, rest[:-2], held)
            first = (owner(role, place[0]) * 2 + 1 - place[1]) * self.cap
            for c in range(self.cap):
                row = rows[first + c]
                chunk, spot = self.spot(row)
                out[c] = jnp.where(row >= 0, held[chunk * self.per_chunk + spot], 0.0)

        return self.call(
            body, (place, rows), (1,), [self.full(self.per_chunk, self.slices, TB)] * len(sources), sources,
            self.full(self.cap, self.slices, TB), self.slots(), scratch=[self.held()],
        )

    def spread_local(self, role, place, cols, rows, tiles, sources, total, through_self=None):
        first_call = through_self is not None

        def body(place, cols, rows, tile, *rest):
            out, held = rest[-2:]
            if first_call:
                self.gather(place, rest[:CHUNKS], held)
                for k, back in enumerate(rest[CHUNKS : 2 * CHUNKS]):
                    for part in range(self.parts):
                        for j in range(self.per_piece):
                            block = self.block(k, part, j)
                            out[:, block * TB : (block + 1) * TB] = back[part * self.per_piece + j]
            else:
                self.gather(place, rest[:-3], held)
                out[...] = rest[-3][...]
            owned_by = owner(role, place[0]) * 2 + place[1]
            for c in range(self.cap):
                row = rows[owned_by * self.cap + c]
                chunk, spot = self.spot(row)
                value = jnp.where(row >= 0, held[chunk * self.per_chunk + spot], 0.0)
                out[:, lanes(cols[owned_by * self.cap + c])] += times_tile(value, tile[0, c])

        whole = self.full(self.slices, self.owned)
        args = [tiles, *sources] + (list(through_self) if first_call else [total])
        dense = self.full(self.per_chunk, self.slices, TB)
        in_specs = [self.tile_spec(role, False)] + [dense] * len(sources)
        in_specs += [dense] * CHUNKS if first_call else [whole]
        return self.call(
            body, (place, cols, rows), (1,), in_specs, args, whole,
            jax.ShapeDtypeStruct((self.slices, self.owned), F32), scratch=[self.held()],
            aliases={} if first_call else {3 + len(args) - 1: 0},
        )

    def spread_slots(self, role, place, cols, tiles, slots, total):
        def body(place, cols, tile, slots, total, out):
            out[...] = total[...]
            owned_by = owner(role, place[0]) * 2 + 1 - place[1]
            for c in range(self.cap):
                out[:, lanes(cols[owned_by * self.cap + c])] += times_tile(slots[c], tile[0, c])

        whole = self.full(self.slices, self.owned)
        return self.call(
            body, (place, cols), (1,),
            [self.tile_spec(role, True), self.full(self.cap, self.slices, TB), whole], (tiles, slots, total),
            whole, jax.ShapeDtypeStruct((self.slices, self.owned), F32), aliases={4: 0},
        )


def pairs_z(steps):
    return [(2 * a + x, 2 * b + x) for a, b in steps for x in range(2)]


INWARD = pairs_z([(0, 1), (3, 2)])
ACROSS = pairs_z([(1, 2), (2, 1)])
OUTWARD = pairs_z([(1, 0), (2, 3)])
NEARBY = pairs_z([(0, 1), (1, 0), (2, 3), (3, 2)])
OTHER_X = [(n, n ^ 1) for n in range(8)]
OTHER_CORE = [(f, f ^ 1) for f in range(4)]
OTHER_Y = [(f, f ^ 2) for f in range(4)]


def chain_shards(node_feats, tiles, send_col, recv_row, degree, w_self, w_neigh, bias, cotangent):
    slices, owned = node_feats.shape
    cap = tiles.shape[1]
    width = w_self.shape[1]
    layer = Layer(slices, owned, cap, 4, width)
    node, feat = lax.axis_index("node"), lax.axis_index("feat")
    z, x = node // 2, node % 2
    place = jnp.stack([z, x, feat // 2, feat % 2]).astype(jnp.int32)
    cols = send_col.reshape(-1)
    every_row = lax.all_gather(recv_row, "node", axis=0, tiled=True)
    rows = every_row.reshape(4, 2, 4, 2, cap)
    rows = lax.dynamic_slice(rows, (0, x, z, 0, 0), (4, 1, 1, 2, cap)).reshape(-1)
    inverse = (1.0 / degree.astype(F32)).reshape(-1, TB)
    bias_row = bias.reshape(1, width)

    slots = []
    for role in range(4):
        part = layer.partial(role, place, cols, node_feats, tiles)
        slots.append(lax.ppermute(part, "node", OTHER_X))
    sums = layer.local(place, cols, rows, node_feats, tiles)
    joined = [layer.joined(role, place, rows, sums, slots[role]) for role in range(4)]

    activated = None
    weights = None
    self_back, own, near = [], [], []
    inner_got, inner_far, outer_got, outer_far = [], [], [], []
    for k in range(CHUNKS):
        far_outer, far_inner, nearby, mine = (joined[role][k] for role in range(4))
        first = lax.ppermute(far_outer, "node", INWARD)
        second = lax.ppermute(far_inner, "node", INWARD)
        third = lax.ppermute(nearby, "node", INWARD)
        for_outer = lax.ppermute(far_outer + first, "node", ACROSS)
        for_inner = lax.ppermute(far_inner + second, "node", ACROSS)
        last = lax.ppermute(nearby + for_outer, "node", OUTWARD)
        neighbour, send, keep = layer.project(
            k, place, (mine, third, for_inner, last), node_feats, w_self, w_neigh, inverse
        )
        got = lax.ppermute(send, "feat", OTHER_CORE)
        far = lax.ppermute(layer.for_other_y(place, keep, got), "feat", OTHER_Y)
        activated, grad = layer.activate(k, place, keep, got, far, bias_row, cotangent, activated)
        grad_y = lax.ppermute(grad, "feat", OTHER_Y)
        grad_core = lax.ppermute(grad, "feat", OTHER_CORE)
        grad_both = lax.ppermute(grad_y, "feat", OTHER_CORE)
        grads = (grad, grad_y, grad_core, grad_both)
        mine_back = layer.neighbour_grad(k, place, w_neigh, inverse, grads)
        own.append(mine_back)
        near.append(lax.ppermute(mine_back, "node", NEARBY))
        inner_got.append(lax.ppermute(mine_back, "node", ACROSS))
        inner_far.append(lax.ppermute(near[k], "node", ACROSS))
        outer_got.append(lax.ppermute(inner_got[k], "node", OUTWARD))
        outer_far.append(lax.ppermute(inner_far[k], "node", OUTWARD))
        back, chunk_weights = layer.weight_grad(k, place, w_self, node_feats, neighbour, grads)
        self_back.append(back)
        weights = chunk_weights if weights is None else weights + chunk_weights

    weights = lax.psum(weights, "node")
    weights = lax.all_gather(weights, "feat", axis=0)
    grad_self = weights[:, :slices].reshape(-1, width)
    grad_neigh = weights[:, slices : 2 * slices].reshape(-1, width)
    grad_bias = weights[0, 2 * slices]

    sources = {
        SELF: own, NEAR: near, FAR_INNER: inner_got + outer_got, FAR_OUTER: inner_far + outer_far,
    }
    order = (SELF, NEAR, FAR_INNER, FAR_OUTER)
    returned = {}
    for role in order:
        returned[role] = lax.ppermute(layer.picked(role, place, rows, sources[role]), "node", OTHER_X)
    total = layer.spread_local(SELF, place, cols, rows, tiles, own, None, self_back)
    total = layer.spread_local(NEAR, place, cols, rows, tiles, near, total)
    total = layer.spread_slots(SELF, place, cols, tiles, returned[SELF], total)
    total = layer.spread_local(FAR_INNER, place, cols, rows, tiles, sources[FAR_INNER], total)
    total = layer.spread_slots(NEAR, place, cols, tiles, returned[NEAR], total)
    total = layer.spread_local(FAR_OUTER, place, cols, rows, tiles, sources[FAR_OUTER], total)
    total = layer.spread_slots(FAR_INNER, place, cols, tiles, returned[FAR_INNER], total)
    total = layer.spread_slots(FAR_OUTER, place, cols, tiles, returned[FAR_OUTER], total)
    return (activated, total, grad_self, grad_neigh, grad_bias)


def slot_shards(node_feats, tiles, send_col, recv_row, degree, w_self, w_neigh, bias, cotangent):
    slices, owned = node_feats.shape
    blocks = owned // TB
    block_ids = jnp.arange(blocks, dtype=jnp.int32)
    scale = degree.astype(F32)[None, :]
    col_onehot = (send_col[..., None] == block_ids).astype(F32)
    row_onehot = (recv_row[..., None] == block_ids).astype(F32)
    feat_blocks = node_feats.reshape(slices, blocks, TB)
    picked = jnp.einsum("dcb,fbj->dcfj", col_onehot, feat_blocks, precision=HIGH)
    partial_value = jnp.einsum("dcfj,dcij->dcfi", picked, tiles, precision=HIGH)
    arrived = lax.all_to_all(partial_value, "node", split_axis=0, concat_axis=0, tiled=True)
    summed = jnp.einsum("scfi,scb->fbi", arrived, row_onehot, precision=HIGH)
    neighbour = summed.reshape(slices, owned) / scale
    offset = lax.axis_index("feat") * slices
    self_rows = lax.dynamic_slice_in_dim(w_self, offset, slices, 0)
    neigh_rows = lax.dynamic_slice_in_dim(w_neigh, offset, slices, 0)
    dims = (((0,), (0,)), ((), ()))
    first = lax.dot_general(node_feats, self_rows, dims, precision=HIGH)
    second = lax.dot_general(neighbour, neigh_rows, dims, precision=HIGH)
    pre = lax.psum_scatter(first + second, "feat", scatter_dimension=0, tiled=True) + bias
    sigma = jax.nn.sigmoid(pre)
    activated = pre * sigma
    gpre = cotangent * sigma * (1.0 + pre * (1.0 - sigma))
    piece = lax.all_gather(gpre, "feat", axis=0, tiled=True)
    dims = (((1,), (1,)), ((), ()))
    self_back = lax.dot_general(self_rows, piece, dims, precision=HIGH)
    neigh_back = lax.dot_general(neigh_rows, piece, dims, precision=HIGH)
    slice_self = jnp.dot(node_feats, piece, precision=HIGH)
    slice_neigh = jnp.dot(neighbour, piece, precision=HIGH)
    sums = lax.psum((slice_self, slice_neigh, jnp.sum(piece, axis=0)), "node")
    grad_self, grad_neigh = (lax.all_gather(part, "feat", axis=0, tiled=True) for part in sums[:2])
    gneigh = (neigh_back / scale).reshape(slices, blocks, TB)
    outgoing = jnp.einsum("scb,fbi->scfi", row_onehot, gneigh, precision=HIGH)
    returned = lax.all_to_all(outgoing, "node", split_axis=0, concat_axis=0, tiled=True)
    spread = jnp.einsum("dcfi,dcij->dcfj", returned, tiles, precision=HIGH)
    placed = jnp.einsum("dcfj,dcb->fbj", spread, col_onehot, precision=HIGH)
    grad_feats = self_back + placed.reshape(slices, owned)
    return (activated, grad_feats, grad_self, grad_neigh, sums[2])


def solution(mesh):
    chain = mesh.shape["node"] == 8 and mesh.shape["feat"] == 4
    return jax.shard_map(
        chain_shards if chain else slot_shards,
        mesh=mesh,
        in_specs=(
            P("feat", "node"),
            P("node", None, None, None),
            P("node", None),
            P("node", None),
            P("node"),
            P(),
            P(),
            P(),
            P(("node", "feat"), None),
        ),
        out_specs=(P(("node", "feat"), None), P("feat", "node"), P(), P(), P()),
        check_vma=False,
    )
```

time: 412 us -> 377 us (0.915); the launches traced: 404 us -> 376 us
  matrix products: 72.8 us -> 0 us
  Pallas kernels: 0 us -> 58.9 us
  waiting for transfers between devices: 200 us -> 156 us
  starting transfers between devices: 13.9 us -> 56.5 us
  blocking collectives: 83.2 us -> 53.8 us
  local copies, waits for them, and re-layouts: 14.2 us -> 35 us
  other arithmetic: 5.5 us -> 1.18 us
    ppermute x0 -> x40, waiting for transfers between devices: none -> 115 us  [the longest x2 22.2 us: chain_shards(): grad_y = lax.ppermute(grad, 'feat', OTHER_Y)]
    all_to_all x2 -> x0, waiting for transfers between devices: 92.7 us -> none  [the longest x1 92.7 us: shards(): lax.all_to_all(partial_value, 'node', split_axis=0, concat_axis=0, tiled=...]
    dot_general x12 -> x0, matrix products: 72.8 us -> none  [the longest x1 18.7 us: shards(): jnp.einsum('dcfj,dcij->dcfi', picked, tiles, precision=lax.Precision.HIGH...]
    psum x1 -> x0, blocking collectives: 70.9 us -> none  [shards(): lax.psum((slice_self, slice_neigh, grad_bias_part), 'node')]
    pallas_call x0 -> x31, Pallas kernels: none -> 58.9 us  [call(): pl.pallas_call(body, grid_spec=pltpu.PrefetchScalarGridSpec(num_scalar_pr...]
    ppermute x0 -> x40, starting transfers between devices: none -> 56.4 us  [the longest x2 9.01 us: chain_shards(): third = lax.ppermute(nearby, 'node', INWARD)]
    all_gather x2, blocking collectives: 12.3 us -> 53.8 us  [the longest x1 46.3 us: chain_shards(): every_row = lax.all_gather(recv_row, 'node', axis=0, tiled=True)]
    reduce_scatter x1 -> x0, waiting for transfers between devices: 41.2 us -> none  [shards(): lax.psum_scatter(first + second, 'feat', scatter_dimension=0, tiled=True)]
  transfers between devices with their start and end apart: 5 -> 41, of which waited for: 4 -> 20; matrix products, arithmetic and copies ran while one was open for 4% -> 1% of each run, Pallas kernels for 0% -> 14%
where the time goes in v1:
time: 377 us; the launch traced here: 376 us
  waiting for transfers between devices  156 us (41%)
  Pallas kernels  58.9 us (16%)
  starting transfers between devices  56.5 us (15%)
  blocking collectives  53.8 us (14%)
  local copies, waits for them, and re-layouts  35 us (9%)
  between operations  14.6 us (4%)
    pallas_call x31, Pallas kernels, call(): pl.pallas_call(body, grid_spec=pltpu.PrefetchScalarGridSpec(num_scalar_pr...  58.9 us
    all_gather x1, blocking collectives, chain_shards(): every_row = lax.all_gather(recv_row, 'node', axis=0, tiled=True)  46.3 us
    psum x1, waiting for transfers between devices, chain_shards(): weights = lax.psum(weights, 'node')  41.1 us
    unnamed x57, local copies, waits for them, and re-layouts  32.8 us
    ppermute x2, waiting for transfers between devices, chain_shards(): grad_y = lax.ppermute(grad, 'feat', OTHER_Y)  22.2 us
    ppermute x2, waiting for transfers between devices, chain_shards(): far = lax.ppermute(layer.for_other_y(place, keep, got), 'feat', OTHER_Y)  19.9 us
    ppermute x2, waiting for transfers between devices, chain_shards(): near.append(lax.ppermute(mine_back, 'node', NEARBY))  18.5 us
    ppermute x2, waiting for transfers between devices, chain_shards(): outer_far.append(lax.ppermute(inner_far[k], 'node', OUTWARD))  18 us
  transfers between devices with their start and end apart: 41, of which 20 were waited for; matrix products, arithmetic and copies ran while one was open for 1% of the time, Pallas kernels for 14%

profile of v1, /device:TPU:0, one launch (start us, length us, event | category | flops | bytes accessed | tf_op | source)
XLA Modules:
  0.0 375.8 jit_solution(10860649168532354493)
XLA Ops:
  8.1 3.4 copy-done
  13.7 3.0 collective-permute-start.6
  17.8 46.3 %all_gather.9 = s32[64,16]{1,0:T(8,128)S(1)} all-gather(s32[8,16]{1,0:T(8,128)S(1)} %copy-done.25), channel_id=1, replica_groups=mesh['feat'=4,'node'=8] {'node'}, dimensions={0}, use_global_device_ids=true | all-gather | bytes 4608 | tf_op jit(solution)/shard_map/all_gather | solution.py:414
  64.2 3.4 copy-done.1
  67.6 2.8 shard_map.128.sums
  73.8 3.4 copy-done.2
  81.8 3.0 collective-permute-done.15
  85.6 3.4 copy-done.3
  90.0 5.8 %collective-permute-start.4 = (f32[16,64,128]{2,1,0:T(8,128)S(1)}, f32[16,64,128]{2,1,0:T(8,128)S(1)}, u32[]{:S(2)}, u32[]{:S(2)}) collective-permute-start(f32[16,64,128]{2,1,0:T(8,128)S(1)} %get-tuple-element.29), channel_id=1, source_target_pairs={{0,2},{1,3},{6,4},{7,5},{8,10},{9,11},{14,12},{15,13},{16,18},{17,... | collective-permute-start | bytes 1572872 | tf_op jit(solution)/shard_map/ppermute | solution.py:434
  96.0 3.6 collective-permute-start
  101.2 6.1 %collective-permute-done.13 = f32[16,64,128]{2,1,0:T(8,128)S(1)} collective-permute-done((f32[16,64,128]{2,1,0:T(8,128)S(1)}, f32[16,64,128]{2,1,0:T(8,128)S(1)}, u32[]{:S(2)}, u32[]{:S(2)}) %collective-permute-start.13) | collective-permute-done | bytes 524320 | tf_op jit(solution)/shard_map/ppermute | solution.py:434
  107.3 4.4 %collective-permute-start.12 = (f32[16,64,128]{2,1,0:T(8,128)S(1)}, f32[16,64,128]{2,1,0:T(8,128)S(1)}, u32[]{:S(2)}, u32[]{:S(2)}) collective-permute-start(f32[16,64,128]{2,1,0:T(8,128)S(1)} %get-tuple-element.34), channel_id=1, source_target_pairs={{0,2},{1,3},{6,4},{7,5},{8,10},{9,11},{14,12},{15,13},{16,18},{17,... | collective-permute-start | bytes 1572872 | tf_op jit(solution)/shard_map/ppermute | solution.py:435
  112.5 6.0 %collective-permute-done.4 = f32[16,64,128]{2,1,0:T(8,128)S(1)} collective-permute-done((f32[16,64,128]{2,1,0:T(8,128)S(1)}, f32[16,64,128]{2,1,0:T(8,128)S(1)}, u32[]{:S(2)}, u32[]{:S(2)}) %collective-permute-start.4) | collective-permute-done | bytes 524320 | tf_op jit(solution)/shard_map/ppermute | solution.py:434
  119.9 4.6 %collective-permute-start.2 = (f32[16,64,128]{2,1,0:T(8,128)S(1)}, f32[16,64,128]{2,1,0:T(8,128)S(1)}, u32[]{:S(2)}, u32[]{:S(2)}) collective-permute-start(f32[16,64,128]{2,1,0:T(8,128)S(1)} %get-tuple-element.28), channel_id=1, source_target_pairs={{0,2},{1,3},{6,4},{7,5},{8,10},{9,11},{14,12},{15,13},{16,18},{17,... | collective-permute-start | bytes 1572872 | tf_op jit(solution)/shard_map/ppermute | solution.py:435
  125.3 3.0 collective-permute-done.12.near
  133.9 5.4 %collective-permute-done.9.outer = f32[16,64,128]{2,1,0:T(8,128)S(1)} collective-permute-done((f32[16,64,128]{2,1,0:T(8,128)S(1)}, f32[16,64,128]{2,1,0:T(8,128)S(1)}, u32[]{:S(2)}, u32[]{:S(2)}) %collective-permute-start.9) | collective-permute-done | bytes 524320 | tf_op jit(solution)/shard_map/ppermute | solution.py:438
  141.4 1.6 collective-permute-start.19
  144.0 1.6 collective-permute-start.11
  145.6 10.6 %collective-permute-done.19.far = f32[512,256]{1,0:T(8,128)S(1)} collective-permute-done((f32[512,256]{1,0:T(8,128)S(1)}, f32[512,256]{1,0:T(8,128)S(1)}, u32[]{:S(2)}, u32[]{:S(2)}) %collective-permute-start.19) | collective-permute-done | bytes 524320 | tf_op jit(solution)/shard_map/ppermute | solution.py:443
  157.6 9.4 %collective-permute-done.11.far = f32[512,256]{1,0:T(8,128)S(1)} collective-permute-done((f32[512,256]{1,0:T(8,128)S(1)}, f32[512,256]{1,0:T(8,128)S(1)}, u32[]{:S(2)}, u32[]{:S(2)}) %collective-permute-start.11) | collective-permute-done | bytes 524320 | tf_op jit(solution)/shard_map/ppermute | solution.py:443
  170.5 12.8 %collective-permute-done.25.rest_1_ = f32[512,256]{1,0:T(8,128)S(1)} collective-permute-done((f32[512,256]{1,0:T(8,128)S(1)}, f32[512,256]{1,0:T(8,128)S(1)}, u32[]{:S(2)}, u32[]{:S(2)}) %collective-permute-start.25) | collective-permute-done | bytes 524320 | tf_op jit(solution)/shard_map/ppermute | solution.py:445
  183.8 9.4 %collective-permute-done.20.rest_1_ = f32[512,256]{1,0:T(8,128)S(1)} collective-permute-done((f32[512,256]{1,0:T(8,128)S(1)}, f32[512,256]{1,0:T(8,128)S(1)}, u32[]{:S(2)}, u32[]{:S(2)}) %collective-permute-start.20) | collective-permute-done | bytes 524320 | tf_op jit(solution)/shard_map/ppermute | solution.py:445
  196.5 1.6 collective-permute-start.23
  200.2 9.1 %collective-permute-done.28.rest_1_ = f32[16,64,128]{2,1,0:T(8,128)S(1)} collective-permute-done((f32[16,64,128]{2,1,0:T(8,128)S(1)}, f32[16,64,128]{2,1,0:T(8,128)S(1)}, u32[]{:S(2)}, u32[]{:S(2)}) %collective-permute-start.28) | collective-permute-done | bytes 524320 | tf_op jit(solution)/shard_map/ppermute | solution.py:451
  210.9 9.4 %collective-permute-done.23.rest_0_ = f32[16,64,128]{2,1,0:T(8,128)S(1)} collective-permute-done((f32[16,64,128]{2,1,0:T(8,128)S(1)}, f32[16,64,128]{2,1,0:T(8,128)S(1)}, u32[]{:S(2)}, u32[]{:S(2)}) %collective-permute-start.23) | collective-permute-done | bytes 524320 | tf_op jit(solution)/shard_map/ppermute | solution.py:451
  227.9 1.9 shard_map.150
  229.8 1.9 shard_map.149
  241.2 9.4 %collective-permute-done.35.rest_2_ = f32[16,64,128]{2,1,0:T(8,128)} collective-permute-done((f32[16,64,128]{2,1,0:T(8,128)}, f32[16,64,128]{2,1,0:T(8,128)}, u32[]{:S(2)}, u32[]{:S(2)}) %collective-permute-start.35) | collective-permute-done | bytes 524320 | tf_op jit(solution)/shard_map/ppermute | solution.py:454
  250.5 2.9 shard_map.146
  253.5 1.9 collective-permute-start.37
  255.3 6.4 %collective-permute-done.31.rest_3_ = f32[16,64,128]{2,1,0:T(8,128)} collective-permute-done((f32[16,64,128]{2,1,0:T(8,128)S(1)}, f32[16,64,128]{2,1,0:T(8,128)}, u32[]{:S(2)}, u32[]{:S(2)}) %collective-permute-start.31) | collective-permute-done | bytes 524320 | tf_op jit(solution)/shard_map/ppermute | solution.py:455
  261.8 11.5 %collective-permute-done.30.rest_2_ = f32[16,64,128]{2,1,0:T(8,128)} collective-permute-done((f32[16,64,128]{2,1,0:T(8,128)}, f32[16,64,128]{2,1,0:T(8,128)}, u32[]{:S(2)}, u32[]{:S(2)}) %collective-permute-start.30) | collective-permute-done | bytes 524320 | tf_op jit(solution)/shard_map/ppermute | solution.py:455
  273.3 2.9 shard_map.145
  276.2 2.2 collective-permute-start.32
  278.5 3.4 copy-done.4
  281.9 2.0 shard_map.151.rest_2_
  283.9 41.1 %all-reduce.2.cloned.1.call-done = f32[1,136,256]{2,1,0:T(8,128)} async-done(((f32[1,136,256]{2,1,0:T(8,128)}), f32[1,136,256]{2,1,0:T(8,128)}) %all-reduce.2.cloned.1.call-update) | async-done | bytes 139280 | tf_op jit(solution)/shard_map/psum | solution.py:460
  325.0 7.5 %all_gather.11 = f32[4,136,256]{2,1,0:T(8,128)S(1)} all-gather(f32[1,136,256]{2,1,0:T(8,128)} %all-reduce.2.cloned.1.call-done), channel_id=1, replica_groups=mesh['feat'=4,'node'=8] {'feat'}, dimensions={0}, use_global_device_ids=true | all-gather | bytes 696320 | tf_op jit(solution)/shard_map/all_gather | solution.py:461
  334.0 3.4 copy-done.5
  337.3 3.3 shard_map.152.total
  340.6 3.4 copy-done.6
  344.0 3.6 shard_map.153.rest_4_
  347.6 3.4 copy-done.7
  351.0 4.0 %shard_map.154.total = f32[64,4096]{1,0:T(8,128)} custom-call(s32[4]{0:T(128)S(1)} %pad_add_fusion.place, s32[128]{0:T(128)S(1)} %reshape.33.cols, s32[128]{0:T(128)S(1)} %reshape.32.rows, f32[8,16,128,128]{3,2,1,0:T(8,128)S(1)} %copy-done.7, f32[16,64,128]{2,1,0:T(8,128)} %collective-permute-done.33.rest_0_, ...), custom_call_target="tpu_custom_call", output_to_operand_aliasing={{}: (8, {})} | custom-call | flops 100000000 | bytes 4194304 | tf_op jit(solution)/shard_map/pallas_call | solution.py:102
  355.1 3.4 shard_map.155.rest_4_
  358.5 3.8 %shard_map.156.total = f32[64,4096]{1,0:T(8,128)} custom-call(s32[4]{0:T(128)S(1)} %pad_add_fusion.place, s32[128]{0:T(128)S(1)} %reshape.33.cols, s32[128]{0:T(128)S(1)} %reshape.32.rows, f32[8,16,128,128]{3,2,1,0:T(8,128)S(1)} %bitcast.18, f32[16,64,128]{2,1,0:T(8,128)} %collective-permute-done.24.rest_0_, ...), custom_call_target="tpu_custom_call", output_to_operand_aliasing={{}: (8, {})} | custom-call | flops 100000000 | bytes 4194304 | tf_op jit(solution)/shard_map/pallas_call | solution.py:102
  362.2 3.4 shard_map.157.total
  365.6 3.4 shard_map.158
  (139 shorter events, 58.3 us)
Async XLA Ops:
  7.2 317.9 %all-reduce.2.cloned.1.call-start = ((), (), s32[]{:S(2)}) async-start(), calls=%async_computation | async-start | bytes 278528 | tf_op jit(solution)/shard_map/psum | solution.py:460
  12.7 51.5 %copy-start.9 = (f32[64,4096]{1,0:T(8,128)S(1)}, f32[64,4096]{1,0:T(8,128)}, u32[]{:S(2)}) copy-start(f32[64,4096]{1,0:T(8,128)} %feats.17) | copy-start | bytes 3145732
  13.7 56.7 %collective-permute-start.6 = (f32[16,64,128]{2,1,0:T(8,128)S(1)}, f32[16,64,128]{2,1,0:T(8,128)S(1)}, u32[]{:S(2)}, u32[]{:S(2)}) collective-permute-start(f32[16,64,128]{2,1,0:T(8,128)S(1)} %shard_map.135), channel_id=1, source_target_pairs={{0,1},{1,0},{2,3},{3,2},{4,5},{5,4},{6,7},{7,6},{8,9},{9,8},{10,11... | collective-permute-start | bytes 1572872 | tf_op jit(solution)/shard_map/ppermute | solution.py:423
  17.7 62.0 %collective-permute-start.3 = (f32[16,64,128]{2,1,0:T(8,128)S(1)}, f32[16,64,128]{2,1,0:T(8,128)S(1)}, u32[]{:S(2)}, u32[]{:S(2)}) collective-permute-start(f32[16,64,128]{2,1,0:T(8,128)S(1)} %shard_map.133), channel_id=1, source_target_pairs={{0,1},{1,0},{2,3},{3,2},{4,5},{5,4},{6,7},{7,6},{8,9},{9,8},{10,11... | collective-permute-start | bytes 1572872 | tf_op jit(solution)/shard_map/ppermute | solution.py:423
  71.1 13.7 %collective-permute-start.15 = (f32[16,64,128]{2,1,0:T(8,128)S(1)}, f32[16,64,128]{2,1,0:T(8,128)S(1)}, u32[]{:S(2)}, u32[]{:S(2)}) collective-permute-start(f32[16,64,128]{2,1,0:T(8,128)S(1)} %get-tuple-element.36), channel_id=1, source_target_pairs={{0,2},{1,3},{6,4},{7,5},{8,10},{9,11},{14,12},{15,13},{16,18},{17,... | collective-permute-start | bytes 1572872 | tf_op jit(solution)/shard_map/ppermute | solution.py:433
  72.5 23.6 %collective-permute-start.7 = (f32[16,64,128]{2,1,0:T(8,128)S(1)}, f32[16,64,128]{2,1,0:T(8,128)S(1)}, u32[]{:S(2)}, u32[]{:S(2)}) collective-permute-start(f32[16,64,128]{2,1,0:T(8,128)S(1)} %get-tuple-element.30), channel_id=1, source_target_pairs={{0,2},{1,3},{6,4},{7,5},{8,10},{9,11},{14,12},{15,13},{16,18},{17,... | collective-permute-start | bytes 1572872 | tf_op jit(solution)/shard_map/ppermute | solution.py:433
  78.2 21.5 %collective-permute-start.1 = (f32[16,64,128]{2,1,0:T(8,128)S(1)}, f32[16,64,128]{2,1,0:T(8,128)S(1)}, u32[]{:S(2)}, u32[]{:S(2)}) collective-permute-start(f32[16,64,128]{2,1,0:T(8,128)S(1)} %shard_map.131), channel_id=1, source_target_pairs={{0,1},{1,0},{2,3},{3,2},{4,5},{5,4},{6,7},{7,6},{8,9},{9,8},{10,11... | collective-permute-start | bytes 1572872 | tf_op jit(solution)/shard_map/ppermute | solution.py:423
  80.5 26.8 %collective-permute-start.13 = (f32[16,64,128]{2,1,0:T(8,128)S(1)}, f32[16,64,128]{2,1,0:T(8,128)S(1)}, u32[]{:S(2)}, u32[]{:S(2)}) collective-permute-start(f32[16,64,128]{2,1,0:T(8,128)S(1)} %get-tuple-element.35), channel_id=1, source_target_pairs={{0,2},{1,3},{6,4},{7,5},{8,10},{9,11},{14,12},{15,13},{16,18},{17,... | collective-permute-start | bytes 1572872 | tf_op jit(solution)/shard_map/ppermute | solution.py:434
  84.9 26.9 %collective-permute-start.16 = (f32[16,64,128]{2,1,0:T(8,128)S(1)}, f32[16,64,128]{2,1,0:T(8,128)S(1)}, u32[]{:S(2)}, u32[]{:S(2)}) collective-permute-start(f32[16,64,128]{2,1,0:T(8,128)S(1)} %add.46), channel_id=1, source_target_pairs={{2,4},{3,5},{4,2},{5,3},{10,12},{11,13},{12,10},{13,11},{18,20},{1... | collective-permute-start | bytes 1572872 | tf_op jit(solution)/shard_map/ppermute | solution.py:436
  90.0 41.6 %copy-start.11 = (f32[256,256]{1,0:T(8,128)S(1)}, f32[256,256]{1,0:T(8,128)}, u32[]{:S(2)}) copy-start(f32[256,256]{1,0:T(8,128)} %w_neigh.7) | copy-start | bytes 786436
  90.0 41.5 %copy-start.12 = (f32[256,256]{1,0:T(8,128)S(1)}, f32[256,256]{1,0:T(8,128)}, u32[]{:S(2)}) copy-start(f32[256,256]{1,0:T(8,128)} %w_self.7) | copy-start | bytes 786436
  90.0 28.5 %collective-permute-start.4 = (f32[16,64,128]{2,1,0:T(8,128)S(1)}, f32[16,64,128]{2,1,0:T(8,128)S(1)}, u32[]{:S(2)}, u32[]{:S(2)}) collective-permute-start(f32[16,64,128]{2,1,0:T(8,128)S(1)} %get-tuple-element.29), channel_id=1, source_target_pairs={{0,2},{1,3},{6,4},{7,5},{8,10},{9,11},{14,12},{15,13},{16,18},{17,... | collective-permute-start | bytes 1572872 | tf_op jit(solution)/shard_map/ppermute | solution.py:434
  96.0 28.5 %collective-permute-start = (f32[16,64,128]{2,1,0:T(8,128)S(1)}, f32[16,64,128]{2,1,0:T(8,128)S(1)}, u32[]{:S(2)}, u32[]{:S(2)}) collective-permute-start(f32[16,64,128]{2,1,0:T(8,128)S(1)} %shard_map.129), channel_id=1, source_target_pairs={{0,1},{1,0},{2,3},{3,2},{4,5},{5,4},{6,7},{7,6},{8,9},{9,8},{10,11... | collective-permute-start | bytes 1572872 | tf_op jit(solution)/shard_map/ppermute | solution.py:423
  99.7 20.1 %collective-permute-start.8 = (f32[16,64,128]{2,1,0:T(8,128)S(1)}, f32[16,64,128]{2,1,0:T(8,128)S(1)}, u32[]{:S(2)}, u32[]{:S(2)}) collective-permute-start(f32[16,64,128]{2,1,0:T(8,128)S(1)} %add.43), channel_id=1, source_target_pairs={{2,4},{3,5},{4,2},{5,3},{10,12},{11,13},{12,10},{13,11},{18,20},{1... | collective-permute-start | bytes 1572872 | tf_op jit(solution)/shard_map/ppermute | solution.py:436
  107.3 21.0 %collective-permute-start.12 = (f32[16,64,128]{2,1,0:T(8,128)S(1)}, f32[16,64,128]{2,1,0:T(8,128)S(1)}, u32[]{:S(2)}, u32[]{:S(2)}) collective-permute-start(f32[16,64,128]{2,1,0:T(8,128)S(1)} %get-tuple-element.34), channel_id=1, source_target_pairs={{0,2},{1,3},{6,4},{7,5},{8,10},{9,11},{14,12},{15,13},{16,18},{17,... | collective-permute-start | bytes 1572872 | tf_op jit(solution)/shard_map/ppermute | solution.py:435
  111.8 18.6 %collective-permute-start.14 = (f32[16,64,128]{2,1,0:T(8,128)S(1)}, f32[16,64,128]{2,1,0:T(8,128)S(1)}, u32[]{:S(2)}, u32[]{:S(2)}) collective-permute-start(f32[16,64,128]{2,1,0:T(8,128)S(1)} %add.45), channel_id=1, source_target_pairs={{2,4},{3,5},{4,2},{5,3},{10,12},{11,13},{12,10},{13,11},{18,20},{1... | collective-permute-start | bytes 1572872 | tf_op jit(solution)/shard_map/ppermute | solution.py:437
  118.5 13.0 %collective-permute-start.17 = (f32[16,64,128]{2,1,0:T(8,128)S(1)}, f32[16,64,128]{2,1,0:T(8,128)S(1)}, u32[]{:S(2)}, u32[]{:S(2)}) collective-permute-start(f32[16,64,128]{2,1,0:T(8,128)S(1)} %add.47), channel_id=1, source_target_pairs={{2,0},{3,1},{4,6},{5,7},{10,8},{11,9},{12,14},{13,15},{18,16},{19,... | collective-permute-start | bytes 1572872 | tf_op jit(solution)/shard_map/ppermute | solution.py:438
  119.9 14.0 %collective-permute-start.2 = (f32[16,64,128]{2,1,0:T(8,128)S(1)}, f32[16,64,128]{2,1,0:T(8,128)S(1)}, u32[]{:S(2)}, u32[]{:S(2)}) collective-permute-start(f32[16,64,128]{2,1,0:T(8,128)S(1)} %get-tuple-element.28), channel_id=1, source_target_pairs={{0,2},{1,3},{6,4},{7,5},{8,10},{9,11},{14,12},{15,13},{16,18},{17,... | collective-permute-start | bytes 1572872 | tf_op jit(solution)/shard_map/ppermute | solution.py:435
  124.6 9.3 %collective-permute-start.5 = (f32[16,64,128]{2,1,0:T(8,128)S(1)}, f32[16,64,128]{2,1,0:T(8,128)S(1)}, u32[]{:S(2)}, u32[]{:S(2)}) collective-permute-start(f32[16,64,128]{2,1,0:T(8,128)S(1)} %add.42), channel_id=1, source_target_pairs={{2,4},{3,5},{4,2},{5,3},{10,12},{11,13},{12,10},{13,11},{18,20},{1... | collective-permute-start | bytes 1572872 | tf_op jit(solution)/shard_map/ppermute | solution.py:437
  128.3 11.1 %collective-permute-start.9 = (f32[16,64,128]{2,1,0:T(8,128)S(1)}, f32[16,64,128]{2,1,0:T(8,128)S(1)}, u32[]{:S(2)}, u32[]{:S(2)}) collective-permute-start(f32[16,64,128]{2,1,0:T(8,128)S(1)} %add.44), channel_id=1, source_target_pairs={{2,0},{3,1},{4,6},{5,7},{10,8},{11,9},{12,14},{13,15},{18,16},{19,... | collective-permute-start | bytes 1572872 | tf_op jit(solution)/shard_map/ppermute | solution.py:438
  132.9 7.9 %collective-permute-start.18 = (f32[2,512,256]{2,1,0:T(8,128)S(1)}, f32[2,512,256]{2,1,0:T(8,128)S(1)}, u32[]{:S(2)}, u32[]{:S(2)}) collective-permute-start(f32[2,512,256]{2,1,0:T(8,128)S(1)} %get-tuple-element.38), channel_id=1, source_target_pairs={{0,8},{8,0},{16,24},{24,16},{1,9},{9,1},{17,25},{25,17},{2,10},{10... | collective-permute-start | bytes 3145736 | tf_op jit(solution)/shard_map/ppermute | solution.py:442
  140.7 2.7 collective-permute-start.10
  141.4 14.8 %collective-permute-start.19 = (f32[512,256]{1,0:T(8,128)S(1)}, f32[512,256]{1,0:T(8,128)S(1)}, u32[]{:S(2)}, u32[]{:S(2)}) collective-permute-start(f32[512,256]{1,0:T(8,128)S(1)} %shard_map.140), channel_id=1, source_target_pairs={{0,16},{8,24},{16,0},{24,8},{1,17},{9,25},{17,1},{25,9},{2,18},{10... | collective-permute-start | bytes 1572872 | tf_op jit(solution)/shard_map/ppermute | solution.py:443
  144.0 23.0 %collective-permute-start.11 = (f32[512,256]{1,0:T(8,128)S(1)}, f32[512,256]{1,0:T(8,128)S(1)}, u32[]{:S(2)}, u32[]{:S(2)}) collective-permute-start(f32[512,256]{1,0:T(8,128)S(1)} %shard_map.138), channel_id=1, source_target_pairs={{0,16},{8,24},{16,0},{24,8},{1,17},{9,25},{17,1},{25,9},{2,18},{10... | collective-permute-start | bytes 1572872 | tf_op jit(solution)/shard_map/ppermute | solution.py:443
  168.5 14.8 %collective-permute-start.25 = (f32[512,256]{1,0:T(8,128)S(1)}, f32[512,256]{1,0:T(8,128)S(1)}, u32[]{:S(2)}, u32[]{:S(2)}) collective-permute-start(f32[512,256]{1,0:T(8,128)S(1)} %get-tuple-element.42.rest_0_), channel_id=1, source_target_pairs={{0,16},{8,24},{16,0},{24,8},{1,17},{9,25},{17,1},{25,9},{2,18},{10... | collective-permute-start | bytes 1572872 | tf_op jit(solution)/shard_map/ppermute | solution.py:445
  170.0 23.2 %collective-permute-start.20 = (f32[512,256]{1,0:T(8,128)S(1)}, f32[512,256]{1,0:T(8,128)S(1)}, u32[]{:S(2)}, u32[]{:S(2)}) collective-permute-start(f32[512,256]{1,0:T(8,128)S(1)} %get-tuple-element.41.rest_0_), channel_id=1, source_target_pairs={{0,16},{8,24},{16,0},{24,8},{1,17},{9,25},{17,1},{25,9},{2,18},{10... | collective-permute-start | bytes 1572872 | tf_op jit(solution)/shard_map/ppermute | solution.py:445
  170.5 22.8 %collective-permute-start.26 = (f32[512,256]{1,0:T(8,128)S(1)}, f32[512,256]{1,0:T(8,128)S(1)}, u32[]{:S(2)}, u32[]{:S(2)}) collective-permute-start(f32[512,256]{1,0:T(8,128)S(1)} %get-tuple-element.42.rest_0_), channel_id=1, source_target_pairs={{0,8},{8,0},{16,24},{24,16},{1,9},{9,1},{17,25},{25,17},{2,10},{10... | collective-permute-start | bytes 1572872 | tf_op jit(solution)/shard_map/ppermute | solution.py:446
  183.3 10.0 %collective-permute-start.27 = (f32[512,256]{1,0:T(8,128)S(1)}, f32[512,256]{1,0:T(8,128)S(1)}, u32[]{:S(2)}, u32[]{:S(2)}) collective-permute-start(f32[512,256]{1,0:T(8,128)S(1)} %collective-permute-done.25.rest_1_), channel_id=1, source_target_pairs={{0,8},{8,0},{16,24},{24,16},{1,9},{9,1},{17,25},{25,17},{2,10},{10... | collective-permute-start | bytes 1572872 | tf_op jit(solution)/shard_map/ppermute | solution.py:447
  183.3 11.4 %collective-permute-start.21 = (f32[512,256]{1,0:T(8,128)S(1)}, f32[512,256]{1,0:T(8,128)S(1)}, u32[]{:S(2)}, u32[]{:S(2)}) collective-permute-start(f32[512,256]{1,0:T(8,128)S(1)} %get-tuple-element.41.rest_0_), channel_id=1, source_target_pairs={{0,8},{8,0},{16,24},{24,16},{1,9},{9,1},{17,25},{25,17},{2,10},{10... | collective-permute-start | bytes 1572872 | tf_op jit(solution)/shard_map/ppermute | solution.py:446
  193.2 1.9 collective-permute-start.22
  194.6 14.8 %collective-permute-start.28 = (f32[16,64,128]{2,1,0:T(8,128)S(1)}, f32[16,64,128]{2,1,0:T(8,128)S(1)}, u32[]{:S(2)}, u32[]{:S(2)}) collective-permute-start(f32[16,64,128]{2,1,0:T(8,128)S(1)} %shard_map.144.rest_1_), channel_id=1, source_target_pairs={{0,2},{1,3},{2,0},{3,1},{4,6},{5,7},{6,4},{7,5},{8,10},{9,11},{10,... | collective-permute-start | bytes 1572872 | tf_op jit(solution)/shard_map/ppermute | solution.py:451
  196.5 23.7 %collective-permute-start.23 = (f32[16,64,128]{2,1,0:T(8,128)S(1)}, f32[16,64,128]{2,1,0:T(8,128)S(1)}, u32[]{:S(2)}, u32[]{:S(2)}) collective-permute-start(f32[16,64,128]{2,1,0:T(8,128)S(1)} %shard_map.143.rest_0_), channel_id=1, source_target_pairs={{0,2},{1,3},{2,0},{3,1},{4,6},{5,7},{6,4},{7,5},{8,10},{9,11},{10,... | collective-permute-start | bytes 1572872 | tf_op jit(solution)/shard_map/ppermute | solution.py:451
  198.1 24.4 %collective-permute-start.34 = (f32[16,64,128]{2,1,0:T(8,128)S(1)}, f32[16,64,128]{2,1,0:T(8,128)S(1)}, u32[]{:S(2)}, u32[]{:S(2)}) collective-permute-start(f32[16,64,128]{2,1,0:T(8,128)S(1)} %shard_map.144.rest_1_), channel_id=1, source_target_pairs={{2,4},{3,5},{4,2},{5,3},{10,12},{11,13},{12,10},{13,11},{18,20},{1... | collective-permute-start | bytes 1572872 | tf_op jit(solution)/shard_map/ppermute | solution.py:452
  198.8 25.0 %collective-permute-start.33 = (f32[16,64,128]{2,1,0:T(8,128)S(1)}, f32[16,64,128]{2,1,0:T(8,128)}, u32[]{:S(2)}, u32[]{:S(2)}) collective-permute-start(f32[16,64,128]{2,1,0:T(8,128)S(1)} %shard_map.143.rest_0_), channel_id=1, source_target_pairs={{2,4},{3,5},{4,2},{5,3},{10,12},{11,13},{12,10},{13,11},{18,20},{1... | collective-permute-start | bytes 1572872 | tf_op jit(solution)/shard_map/ppermute | solution.py:452
  209.4 15.7 %collective-permute-start.29 = (f32[16,64,128]{2,1,0:T(8,128)S(1)}, f32[16,64,128]{2,1,0:T(8,128)S(1)}, u32[]{:S(2)}, u32[]{:S(2)}) collective-permute-start(f32[16,64,128]{2,1,0:T(8,128)S(1)} %collective-permute-done.28.rest_1_), channel_id=1, source_target_pairs={{2,4},{3,5},{4,2},{5,3},{10,12},{11,13},{12,10},{13,11},{18,20},{1... | collective-permute-start | bytes 1572872 | tf_op jit(solution)/shard_map/ppermute | solution.py:453
  220.2 6.2 %collective-permute-start.24 = (f32[16,64,128]{2,1,0:T(8,128)S(1)}, f32[16,64,128]{2,1,0:T(8,128)}, u32[]{:S(2)}, u32[]{:S(2)}) collective-permute-start(f32[16,64,128]{2,1,0:T(8,128)S(1)} %collective-permute-done.23.rest_0_), channel_id=1, source_target_pairs={{2,4},{3,5},{4,2},{5,3},{10,12},{11,13},{12,10},{13,11},{18,20},{1... | collective-permute-start | bytes 1572872 | tf_op jit(solution)/shard_map/ppermute | solution.py:453
  222.5 17.3 %collective-permute-start.36 = (f32[16,64,128]{2,1,0:T(8,128)S(1)}, f32[16,64,128]{2,1,0:T(8,128)}, u32[]{:S(2)}, u32[]{:S(2)}) collective-permute-start(f32[16,64,128]{2,1,0:T(8,128)S(1)} %collective-permute-done.34.rest_1_), channel_id=1, source_target_pairs={{2,0},{3,1},{4,6},{5,7},{10,8},{11,9},{12,14},{13,15},{18,16},{19,... | collective-permute-start | bytes 1572872 | tf_op jit(solution)/shard_map/ppermute | solution.py:454
  223.8 26.8 %collective-permute-start.35 = (f32[16,64,128]{2,1,0:T(8,128)}, f32[16,64,128]{2,1,0:T(8,128)}, u32[]{:S(2)}, u32[]{:S(2)}) collective-permute-start(f32[16,64,128]{2,1,0:T(8,128)} %collective-permute-done.33.rest_0_), channel_id=1, source_target_pairs={{2,0},{3,1},{4,6},{5,7},{10,8},{11,9},{12,14},{13,15},{18,16},{19,... | collective-permute-start | bytes 1572872 | tf_op jit(solution)/shard_map/ppermute | solution.py:454
  225.1 36.7 %collective-permute-start.31 = (f32[16,64,128]{2,1,0:T(8,128)S(1)}, f32[16,64,128]{2,1,0:T(8,128)}, u32[]{:S(2)}, u32[]{:S(2)}) collective-permute-start(f32[16,64,128]{2,1,0:T(8,128)S(1)} %collective-permute-done.29.rest_1_), channel_id=1, source_target_pairs={{2,0},{3,1},{4,6},{5,7},{10,8},{11,9},{12,14},{13,15},{18,16},{19,... | collective-permute-start | bytes 1572872 | tf_op jit(solution)/shard_map/ppermute | solution.py:455
  226.4 46.9 %collective-permute-start.30 = (f32[16,64,128]{2,1,0:T(8,128)}, f32[16,64,128]{2,1,0:T(8,128)}, u32[]{:S(2)}, u32[]{:S(2)}) collective-permute-start(f32[16,64,128]{2,1,0:T(8,128)} %collective-permute-done.24.rest_0_), channel_id=1, source_target_pairs={{2,0},{3,1},{4,6},{5,7},{10,8},{11,9},{12,14},{13,15},{18,16},{19,... | collective-permute-start | bytes 1572872 | tf_op jit(solution)/shard_map/ppermute | solution.py:455
  233.2 45.3 %copy-start.20 = (f32[16,64,128]{2,1,0:T(8,128)S(1)}, f32[16,64,128]{2,1,0:T(8,128)}, u32[]{:S(2)}) copy-start(f32[16,64,128]{2,1,0:T(8,128)} %copy-done.19) | copy-start | bytes 1572868
  233.2 45.3 %copy-start.22 = (f32[16,64,128]{2,1,0:T(8,128)S(1)}, f32[16,64,128]{2,1,0:T(8,128)}, u32[]{:S(2)}) copy-start(f32[16,64,128]{2,1,0:T(8,128)} %copy-done.21) | copy-start | bytes 1572868
  234.8 105.9 %collective-permute-start.39 = (f32[16,64,128]{2,1,0:T(8,128)}, f32[16,64,128]{2,1,0:T(8,128)}, u32[]{:S(2)}, u32[]{:S(2)}) collective-permute-start(f32[16,64,128]{2,1,0:T(8,128)} %shard_map.148), channel_id=1, source_target_pairs={{0,1},{1,0},{2,3},{3,2},{4,5},{5,4},{6,7},{7,6},{8,9},{9,8},{10,11... | collective-permute-start | bytes 1572872 | tf_op jit(solution)/shard_map/ppermute | solution.py:472
  239.8 115.2 %collective-permute-start.38 = (f32[16,64,128]{2,1,0:T(8,128)}, f32[16,64,128]{2,1,0:T(8,128)}, u32[]{:S(2)}, u32[]{:S(2)}) collective-permute-start(f32[16,64,128]{2,1,0:T(8,128)} %shard_map.147), channel_id=1, source_target_pairs={{0,1},{1,0},{2,3},{3,2},{4,5},{5,4},{6,7},{7,6},{8,9},{9,8},{10,11... | collective-permute-start | bytes 1572872 | tf_op jit(solution)/shard_map/ppermute | solution.py:472
  253.5 80.5 %copy-start.15 = (f32[16,64,128]{2,1,0:T(8,128)S(1)}, f32[16,64,128]{2,1,0:T(8,128)}, u32[]{:S(2)}) copy-start(f32[16,64,128]{2,1,0:T(8,128)} %copy-done.13) | copy-start | bytes 1572868
  253.5 80.5 %copy-start.18 = (f32[16,64,128]{2,1,0:T(8,128)S(1)}, f32[16,64,128]{2,1,0:T(8,128)}, u32[]{:S(2)}) copy-start(f32[16,64,128]{2,1,0:T(8,128)} %copy-done.16) | copy-start | bytes 1572868
  253.5 108.7 %collective-permute-start.37 = (f32[16,64,128]{2,1,0:T(8,128)}, f32[16,64,128]{2,1,0:T(8,128)}, u32[]{:S(2)}, u32[]{:S(2)}) collective-permute-start(f32[16,64,128]{2,1,0:T(8,128)} %shard_map.146), channel_id=1, source_target_pairs={{0,1},{1,0},{2,3},{3,2},{4,5},{5,4},{6,7},{7,6},{8,9},{9,8},{10,11... | collective-permute-start | bytes 1572872 | tf_op jit(solution)/shard_map/ppermute | solution.py:472
  276.2 89.4 %collective-permute-start.32 = (f32[16,64,128]{2,1,0:T(8,128)}, f32[16,64,128]{2,1,0:T(8,128)}, u32[]{:S(2)}, u32[]{:S(2)}) collective-permute-start(f32[16,64,128]{2,1,0:T(8,128)} %shard_map.145), channel_id=1, source_target_pairs={{0,1},{1,0},{2,3},{3,2},{4,5},{5,4},{6,7},{7,6},{8,9},{9,8},{10,11... | collective-permute-start | bytes 1572872 | tf_op jit(solution)/shard_map/ppermute | solution.py:472
  (21 other events, 147.6 us)
Sparse Core Ops, SparseCore 0:
  233.3 91.6 all-reduce.1

commit v2 on v0

v2 whole, which is shorter than its diff:
```python
import jax
import jax.numpy as jnp
from jax import lax
from jax.experimental import pallas as pl
from jax.experimental.pallas import tpu as pltpu
from jax.sharding import PartitionSpec as P

TB = 128
F32 = jnp.float32
BF16 = jnp.bfloat16
HIGH = lax.Precision.HIGH
CHUNKS = 2
VMEM_BYTES = 28 * 2**20

FAR_OUTER, FAR_INNER, NEAR, SELF = range(4)


def owner(role, z):
    if role == FAR_OUTER:
        return jnp.where(z < 2, 3, 0)
    if role == FAR_INNER:
        return jnp.where(z < 2, 2, 1)
    if role == NEAR:
        return z + 1 - 2 * (z % 2)
    return z


def split(value):
    high = value.astype(BF16)
    return high, (value - high.astype(F32)).astype(BF16)


def dot_nn(a, b):
    return lax.dot_general(a, b, (((1,), (0,)), ((), ())), preferred_element_type=F32)


def dot_nt(a, b):
    return lax.dot_general(a, b, (((1,), (1,)), ((), ())), preferred_element_type=F32)


def stacked(value):
    high, low = split(value)
    return jnp.concatenate(
        [jnp.concatenate([high, high], 1), jnp.concatenate([low, jnp.zeros_like(low)], 1)], 0
    )


def times_tile_t(value, tile):
    rows = value.shape[0]
    out = dot_nt(stacked(value), jnp.concatenate(split(tile), 1))
    return out[:rows] + out[rows:]


def times_tile(value, tile):
    rows = value.shape[0]
    out = dot_nn(stacked(value), jnp.concatenate(split(tile), 0))
    return out[:rows] + out[rows:]


def lanes(block):
    return pl.ds(pl.multiple_of(block * TB, TB), TB)


class Layer:
    def __init__(self, slices, owned, cap, parts, width):
        self.slices, self.owned, self.cap, self.parts, self.width = slices, owned, cap, parts, width
        self.blocks = owned // TB
        self.per_part = self.blocks // parts
        self.per_piece = self.per_part // CHUNKS
        self.per_chunk = self.blocks // CHUNKS
        self.piece = self.per_piece * TB
        self.span = self.per_chunk * TB

    def spot(self, row):
        row = jnp.maximum(row, 0)
        part, inside = row // self.per_part, row % self.per_part
        return inside // self.per_piece, part * self.per_piece + inside % self.per_piece

    def block(self, chunk, part, inside):
        return part * self.per_part + chunk * self.per_piece + inside

    def full(self, *shape):
        return pl.BlockSpec(shape, lambda *_: (0,) * len(shape))

    def dense_spec(self):
        return self.full(self.per_chunk, self.slices, TB)

    def slots_spec(self):
        return self.full(self.cap, self.slices, TB)

    def slots(self):
        return jax.ShapeDtypeStruct((self.cap, self.slices, TB), F32)

    def dense(self):
        return jax.ShapeDtypeStruct((self.per_chunk, self.slices, TB), F32)

    def call(self, body, scalars, grid, in_specs, args, out_specs, out_shape, scratch=(), aliases=None, after=()):
        given = len(scalars) + len(args)

        def ordered(*refs):
            body(*refs[:given], *refs[given + len(after) :])

        return pl.pallas_call(
            ordered,
            grid_spec=pltpu.PrefetchScalarGridSpec(
                num_scalar_prefetch=len(scalars),
                grid=grid,
                in_specs=list(in_specs) + [pl.BlockSpec(memory_space=pl.ANY)] * len(after),
                out_specs=out_specs,
                scratch_shapes=scratch,
            ),
            out_shape=out_shape,
            input_output_aliases=aliases or {},
            compiler_params=pltpu.CompilerParams(vmem_limit_bytes=VMEM_BYTES),
            cost_estimate=pl.CostEstimate(flops=10**8, bytes_accessed=4 * 2**20, transcendentals=0),
        )(*scalars, *args, *after)

    def fetched(self, count):
        return [pltpu.VMEM((count, self.cap, TB, TB), F32), pltpu.SemaphoreType.DMA((count,))]

    def fetch(self, tiles, buffer, sems, index, slot):
        return pltpu.make_async_copy(tiles.at[index], buffer.at[slot], sems.at[slot])

    def tiles_spec(self):
        return pl.BlockSpec(memory_space=pltpu.HBM)

    def partial(self, role, place, cols, feats, tiles, after=()):
        def body(place, cols, feats, tiles, out, buffer, sems):
            owned_by = owner(role, place[0]) * 2 + 1 - place[1]
            copy = self.fetch(tiles, buffer, sems, owned_by, 0)
            copy.start()
            copy.wait()
            for c in range(self.cap):
                out[c] = times_tile_t(feats[:, lanes(cols[owned_by * self.cap + c])], buffer[0, c])

        return self.call(
            body, (place, cols), (1,),
            [self.full(self.slices, self.owned), self.tiles_spec()], (feats, tiles),
            self.slots_spec(), self.slots(), scratch=self.fetched(1), after=after,
        )

    def local(self, place, cols, rows, feats, tiles, after=()):
        def body(place, cols, rows, feats, tiles, out, buffer, sems):
            z, x = place[0], place[1]
            copies = [self.fetch(tiles, buffer, sems, owner(role, z) * 2 + x, role) for role in range(4)]
            for copy in copies:
                copy.start()
            for role in range(4):
                out[role] = jnp.zeros(out.shape[1:], F32)
                copies[role].wait()
                first = (owner(role, z) * 2 + x) * self.cap
                for c in range(self.cap):
                    row = rows[self.row_index(role, z, x) + c]
                    chunk, spot = self.spot(row)
                    value = times_tile_t(feats[:, lanes(cols[first + c])], buffer[role, c])
                    out[role, chunk * self.per_chunk + spot] += jnp.where(row >= 0, value, 0.0)

        shape = (4, self.blocks, self.slices, TB)
        return self.call(
            body, (place, cols, rows), (1,),
            [self.full(self.slices, self.owned), self.tiles_spec()], (feats, tiles),
            self.full(*shape), jax.ShapeDtypeStruct(shape, F32), scratch=self.fetched(4), after=after,
        )

    def row_index(self, role, z, sender_x):
        return ((owner(role, z) ^ z) * 2 + sender_x) * self.cap

    def joined(self, role, k, place, rows, sums, slots, after=()):
        def body(place, rows, sums, slots, out):
            out[...] = sums[0]
            first = self.row_index(role, place[0], 1 - place[1])
            for c in range(self.cap):
                row = rows[first + c]
                chunk, spot = self.spot(row)
                out[spot] += jnp.where((row >= 0) & (chunk == k), slots[c], 0.0)

        return self.call(
            body, (place, rows), (1,),
            [pl.BlockSpec((1, self.per_chunk, self.slices, TB), lambda *_: (role, k, 0, 0)), self.slots_spec()],
            (sums, slots), self.dense_spec(), self.dense(), after=after,
        )

    def means(self, k, pieces, inverse):
        def body(own, near, inner, outer, inverse, out):
            for part in range(self.parts):
                for j in range(self.per_piece):
                    spot, block = part * self.per_piece + j, self.block(k, part, j)
                    total = own[spot] + near[spot] + inner[spot] + outer[spot]
                    out[spot] = total * inverse[block : block + 1, :]

        return self.call(
            body, (), (1,), [self.dense_spec()] * 4 + [self.full(self.blocks, TB)], (*pieces, inverse),
            self.dense_spec(), self.dense(),
        )

    def transposed(self, value, after=()):
        def body(value, out):
            out[...] = value[...].T

        rows, cols = value.shape
        return self.call(
            body, (), (1,), [self.full(rows, cols)], (value,), self.full(cols, rows),
            jax.ShapeDtypeStruct((cols, rows), F32), after=after,
        )

    def feats_of(self, place):
        y, core = place[2], place[3]
        return (2 * y + core, 2 * (1 - y) + core, 2 * y + 1 - core, 2 * (1 - y) + 1 - core)

    def times_weight(self, weight_t, high, low):
        rows = weight_t.shape[0]
        weight_high, weight_low = split(weight_t)
        out = dot_nn(jnp.concatenate([weight_high, weight_low], 0), high)
        return out[:rows] + out[rows:] + dot_nn(weight_high, low)

    def self_part(self, place, slices, w_self, bias, after=()):
        def body(place, own, far, core, both, w_self, bias, out, held):
            for index, piece in zip(self.feats_of(place), (own, far, core, both)):
                held[pl.ds(pl.multiple_of(index * self.slices, self.slices), self.slices), :] = piece[...]
            column = jnp.broadcast_to(bias[...], (TB, self.width)).T
            value = self.times_weight(w_self[...].T, *split(held[...]))
            out[0] = value + jnp.concatenate([column] * self.per_piece, 1)

        columns = pl.BlockSpec((self.slices, self.piece), lambda k, part, *_: (0, part * CHUNKS + k))
        return self.call(
            body, (place,), (CHUNKS, self.parts),
            [columns] * 4 + [self.full(self.width, self.width), self.full(1, self.width)], (*slices, w_self, bias),
            pl.BlockSpec((1, self.width, self.piece), lambda k, part, *_: (k, 0, part)),
            jax.ShapeDtypeStruct((CHUNKS, self.width, self.span), F32),
            scratch=[pltpu.VMEM((self.width, self.piece), F32)], after=after,
        )

    def activate(self, k, place, means, w_neigh, self_part, cotangents, inverse, activated):
        rows = pl.BlockSpec((self.piece, self.width), lambda *_: (k, 0))

        def body(place, m0, m1, m2, m3, weight, self_part, c0, c1, c2, c3, inverse, *rest):
            out, grad, back, high, low = rest[-5:]
            feats = self.feats_of(place)
            for index, piece in zip(feats, (m0, m1, m2, m3)):
                at = pl.ds(pl.multiple_of(index * self.slices, self.slices), self.slices)
                for spot in range(self.per_chunk):
                    columns = slice(spot * TB, (spot + 1) * TB)
                    high[at, columns], low[at, columns] = split(piece[spot])
            weight_t = weight[...].T
            own_rows = weight[pl.ds(pl.multiple_of(feats[0] * self.slices, self.slices), self.slices), :]
            for part, cotangent in zip(feats, (c0, c1, c2, c3)):
                at = pl.ds(pl.multiple_of(part * self.piece, self.piece), self.piece)
                pre = self.times_weight(weight_t, high[:, at], low[:, at]) + self_part[0, :, at]
                sigma = jax.nn.sigmoid(pre)
                if cotangent is c0:
                    out[...] = (pre * sigma).T
                slope = cotangent[...] * (sigma * (1.0 + pre * (1.0 - sigma)))
                grad[:, at] = slope
                value = self.times_weight(own_rows, *split(slope))
                for j in range(self.per_piece):
                    scale = inverse[pl.ds(self.block(k, part, j), 1), :]
                    back[part * self.per_piece + j] = value[:, j * TB : (j + 1) * TB] * scale

        in_specs = (
            [self.dense_spec()] * 4
            + [self.full(self.width, self.width)]
            + [pl.BlockSpec((1, self.width, self.span), lambda *_: (k, 0, 0))]
            + [pl.BlockSpec((self.width, self.piece), lambda *_: (0, k))] * 4
            + [self.full(self.blocks, TB)]
        )
        args = [*means, w_neigh, self_part, *cotangents, inverse]
        aliases = {}
        if activated is not None:
            aliases = {1 + len(args): 0}
            in_specs.append(pl.BlockSpec(memory_space=pl.ANY))
            args.append(activated)
        return self.call(
            body, (place,), (1,), in_specs, args,
            [rows, self.full(self.width, self.span), self.dense_spec()],
            [jax.ShapeDtypeStruct((self.per_part * TB, self.width), F32),
             jax.ShapeDtypeStruct((self.width, self.span), F32), self.dense()],
            scratch=[pltpu.VMEM((self.width, self.span), BF16)] * 2, aliases=aliases,
        )

    def weight_grad(self, k, place, w_self, feats, means, grad, before):
        shape = (2 * self.slices + 16, self.width)

        def body(place, w_self, feats, means, grad, *rest):
            self_out, weights_out = rest[-2:]
            total = rest[0][...] if before is not None else jnp.zeros(shape, F32)
            for part in range(self.parts):
                first = part * self.per_piece
                at = slice(part * self.piece, (part + 1) * self.piece)
                high, low = split(grad[:, at])
                value = self.times_weight(w_self[...], high, low)
                for j in range(self.per_piece):
                    self_out[first + j] = value[:, j * TB : (j + 1) * TB]
                start = self.block(k, part, 0) * TB
                rows = jnp.concatenate(
                    [
                        feats[:, start : start + self.piece],
                        jnp.concatenate([means[first + j] for j in range(self.per_piece)], 1),
                        jnp.ones((16, self.piece), F32),
                    ],
                    0,
                )
                rows_high, rows_low = split(rows)
                total += (dot_nt(rows_high, high) + dot_nt(rows_low, high)) + dot_nt(rows_high, low)
            weights_out[...] = total

        own_rows = pl.BlockSpec((self.slices, self.width), lambda i, place, *_: (2 * place[2] + place[3], 0))
        args = [w_self, feats, means, grad] + ([] if before is None else [before])
        return self.call(
            body, (place,), (1,),
            [own_rows, self.full(self.slices, self.owned), self.dense_spec(), self.full(self.width, self.span)]
            + [self.full(*shape)] * (before is not None),
            args, [self.dense_spec(), self.full(*shape)], [self.dense(), jax.ShapeDtypeStruct(shape, F32)],
        )

    def gather(self, place, sources, held):
        outer = (place[0] == 0) | (place[0] == 3)
        for k in range(CHUNKS):
            spots = slice(k * self.per_chunk, (k + 1) * self.per_chunk)
            if len(sources) == CHUNKS:
                held[spots] = sources[k][...]
            else:

                @pl.when(outer)
                def _():
                    held[spots] = sources[CHUNKS + k][...]

                @pl.when(jnp.logical_not(outer))
                def _():
                    held[spots] = sources[k][...]

    def held(self):
        return pltpu.VMEM((self.blocks, self.slices, TB), F32)

    def pick(self, row, held):
        chunk, spot = self.spot(row)
        return jnp.where(row >= 0, held[chunk * self.per_chunk + spot], 0.0)

    def picked(self, role, place, rows, sources):
        def body(place, rows, *rest):
            out, held = rest[-2:]
            self.gather(place, rest[:-2], held)
            first = self.row_index(role, place[0], 1 - place[1])
            for c in range(self.cap):
                out[c] = self.pick(rows[first + c], held)

        return self.call(
            body, (place, rows), (1,), [self.dense_spec()] * len(sources), sources,
            self.slots_spec(), self.slots(), scratch=[self.held()],
        )

    def spread(self, place, cols, rows, tiles, jobs, total=None, self_back=None):
        counts = [len(sources) for _, sources in jobs]
        extra = [total] if self_back is None else list(self_back)

        def body(place, cols, rows, tiles, *rest):
            arrays, more = rest[: sum(counts)], rest[sum(counts) : sum(counts) + len(extra)]
            out, held, buffer, sems = rest[sum(counts) + len(extra) :]
            z, x = place[0], place[1]
            owners = [owner(role, z) * 2 + (1 - x if n == 1 else x) for (role, _), n in zip(jobs, counts)]
            copies = [self.fetch(tiles, buffer, sems, owned_by, i) for i, owned_by in enumerate(owners)]
            for copy in copies:
                copy.start()
            if self_back is None:
                out[...] = more[0][...]
            else:
                for k, back in enumerate(more):
                    for part in range(self.parts):
                        for j in range(self.per_piece):
                            block = self.block(k, part, j)
                            out[:, block * TB : (block + 1) * TB] = back[part * self.per_piece + j]
            for i, (role, _) in enumerate(jobs):
                sources = arrays[sum(counts[:i]) : sum(counts[: i + 1])]
                if counts[i] > 1:
                    self.gather(place, sources, held)
                copies[i].wait()
                for c in range(self.cap):
                    if counts[i] > 1:
                        value = self.pick(rows[self.row_index(role, z, x) + c], held)
                    else:
                        value = sources[0][c]
                    out[:, lanes(cols[owners[i] * self.cap + c])] += times_tile(value, buffer[i, c])

        whole = self.full(self.slices, self.owned)
        in_specs, args = [self.tiles_spec()], [tiles]
        for _, sources in jobs:
            in_specs += [self.slots_spec() if len(sources) == 1 else self.dense_spec()] * len(sources)
            args += sources
        in_specs += [whole] if self_back is None else [self.dense_spec()] * CHUNKS
        args += extra
        return self.call(
            body, (place, cols, rows), (1,), in_specs, args, whole,
            jax.ShapeDtypeStruct((self.slices, self.owned), F32),
            scratch=[self.held(), *self.fetched(len(jobs))],
            aliases={3 + len(args) - 1: 0} if self_back is None else {},
        )


def pairs_z(steps):
    return [(2 * a + x, 2 * b + x) for a, b in steps for x in range(2)]


INWARD = pairs_z([(0, 1), (3, 2)])
ACROSS = pairs_z([(1, 2), (2, 1)])
OUTWARD = pairs_z([(1, 0), (2, 3)])
OTHER_X = [(n, n ^ 1) for n in range(8)]
OTHER_CORE = [(f, f ^ 1) for f in range(4)]
OTHER_Y = [(f, f ^ 2) for f in range(4)]


def along_z(distance):
    return pairs_z([(z, z ^ distance) for z in range(4)])


def node_swap(value, pairs):
    return lax.ppermute(value, "node", pairs)


def over_feat(value):
    far = lax.ppermute(value, "feat", OTHER_Y)
    core = lax.ppermute(value, "feat", OTHER_CORE)
    return value, far, core, lax.ppermute(far, "feat", OTHER_CORE)


def pair(mine, other, place):
    return jnp.where(place == 0, jnp.stack([mine, other]), jnp.stack([other, mine]))


def spread_weights(weights, x, y, core):
    halves = weights.reshape(2, -1, weights.shape[1])
    keep = lax.dynamic_index_in_dim(halves, x, 0, keepdims=False)
    send = lax.dynamic_index_in_dim(halves, 1 - x, 0, keepdims=False)
    total = keep + node_swap(send, OTHER_X)
    total = total + node_swap(total, along_z(1))
    total = total + node_swap(total, along_z(3))
    whole = pair(total, node_swap(total, OTHER_X), x).reshape(weights.shape)
    cores = pair(whole, lax.ppermute(whole, "feat", OTHER_CORE), core)
    return pair(cores, lax.ppermute(cores, "feat", OTHER_Y), y).reshape(4, *weights.shape)


def chain_shards(node_feats, tiles, send_col, recv_row, degree, w_self, w_neigh, bias, cotangent):
    slices, owned = node_feats.shape
    cap = tiles.shape[1]
    width = w_self.shape[1]
    layer = Layer(slices, owned, cap, 4, width)
    node, feat = lax.axis_index("node"), lax.axis_index("feat")
    z, x, y, core = node // 2, node % 2, feat // 2, feat % 2
    place = jnp.stack([z, x, y, core]).astype(jnp.int32)
    cols = send_col.reshape(-1)

    slots = []
    for role in range(4):
        part = layer.partial(role, place, cols, node_feats, tiles, after=slots[-1:])
        slots.append(node_swap(part, OTHER_X))
    every_row = jnp.stack([recv_row] + [node_swap(recv_row, along_z(d)) for d in (1, 2, 3)])
    rows = lax.dynamic_slice(every_row, (0, 2 * z, 0), (4, 2, cap)).reshape(-1)
    inverse = (1.0 / degree.astype(F32)).reshape(-1, TB)
    feat_slices = over_feat(node_feats)
    cotangents = over_feat(layer.transposed(cotangent))
    self_part = layer.self_part(place, feat_slices, w_self, bias.reshape(1, width))
    sums = layer.local(place, cols, rows, node_feats, tiles)

    activated = None
    weights = None
    order = []
    self_back, own, near = [], [], []
    inner_got, inner_far, outer_got, outer_far = [], [], [], []
    for k in range(CHUNKS):
        parts = []
        for role in range(3):
            part = layer.joined(role, k, place, rows, sums, slots[role], after=order[-2:-1])
            parts.append(part)
            order.append(node_swap(part, INWARD))
        mine = layer.joined(SELF, k, place, rows, sums, slots[SELF])
        first, second, third = order[-3:]
        for_outer = node_swap(parts[FAR_OUTER] + first, ACROSS)
        for_inner = node_swap(parts[FAR_INNER] + second, ACROSS)
        last = node_swap(parts[NEAR] + for_outer, OUTWARD)
        means = layer.means(k, (mine, third, for_inner, last), inverse)
        activated, grad, mine_back = layer.activate(
            k, place, over_feat(means), w_neigh, self_part, cotangents, inverse, activated
        )
        own.append(mine_back)
        near.append(node_swap(mine_back, along_z(1)))
        inner_got.append(node_swap(mine_back, ACROSS))
        inner_far.append(node_swap(near[k], ACROSS))
        outer_got.append(node_swap(inner_got[k], OUTWARD))
        outer_far.append(node_swap(inner_far[k], OUTWARD))
        back, weights = layer.weight_grad(k, place, w_self, node_feats, means, grad, weights)
        self_back.append(back)

    weights = spread_weights(weights, x, y, core)
    grad_self = weights[:, :slices].reshape(-1, width)
    grad_neigh = weights[:, slices : 2 * slices].reshape(-1, width)
    grad_bias = weights[0, 2 * slices]

    sources = {
        SELF: own, NEAR: near, FAR_INNER: inner_got + outer_got, FAR_OUTER: inner_far + outer_far,
    }
    returned = {}
    for role in (SELF, NEAR, FAR_INNER, FAR_OUTER):
        returned[role] = [node_swap(layer.picked(role, place, rows, sources[role]), OTHER_X)]
    local = {role: (role, sources[role]) for role in sources}
    other = {role: (role, returned[role]) for role in sources}
    total = layer.spread(place, cols, rows, tiles, [local[SELF]], self_back=self_back)
    total = layer.spread(place, cols, rows, tiles, [local[NEAR], other[SELF]], total)
    total = layer.spread(place, cols, rows, tiles, [local[FAR_INNER], other[NEAR]], total)
    total = layer.spread(place, cols, rows, tiles, [local[FAR_OUTER], other[FAR_INNER]], total)
    total = layer.spread(place, cols, rows, tiles, [other[FAR_OUTER]], total)
    return (activated, total, grad_self, grad_neigh, grad_bias)


def slot_shards(node_feats, tiles, send_col, recv_row, degree, w_self, w_neigh, bias, cotangent):
    slices, owned = node_feats.shape
    blocks = owned // TB
    block_ids = jnp.arange(blocks, dtype=jnp.int32)
    scale = degree.astype(F32)[None, :]
    col_onehot = (send_col[..., None] == block_ids).astype(F32)
    row_onehot = (recv_row[..., None] == block_ids).astype(F32)
    feat_blocks = node_feats.reshape(slices, blocks, TB)
    picked = jnp.einsum("dcb,fbj->dcfj", col_onehot, feat_blocks, precision=HIGH)
    partial_value = jnp.einsum("dcfj,dcij->dcfi", picked, tiles, precision=HIGH)
    arrived = lax.all_to_all(partial_value, "node", split_axis=0, concat_axis=0, tiled=True)
    summed = jnp.einsum("scfi,scb->fbi", arrived, row_onehot, precision=HIGH)
    neighbour = summed.reshape(slices, owned) / scale
    offset = lax.axis_index("feat") * slices
    self_rows = lax.dynamic_slice_in_dim(w_self, offset, slices, 0)
    neigh_rows = lax.dynamic_slice_in_dim(w_neigh, offset, slices, 0)
    dims = (((0,), (0,)), ((), ()))
    first = lax.dot_general(node_feats, self_rows, dims, precision=HIGH)
    second = lax.dot_general(neighbour, neigh_rows, dims, precision=HIGH)
    pre = lax.psum_scatter(first + second, "feat", scatter_dimension=0, tiled=True) + bias
    sigma = jax.nn.sigmoid(pre)
    activated = pre * sigma
    gpre = cotangent * sigma * (1.0 + pre * (1.0 - sigma))
    piece = lax.all_gather(gpre, "feat", axis=0, tiled=True)
    dims = (((1,), (1,)), ((), ()))
    self_back = lax.dot_general(self_rows, piece, dims, precision=HIGH)
    neigh_back = lax.dot_general(neigh_rows, piece, dims, precision=HIGH)
    slice_self = jnp.dot(node_feats, piece, precision=HIGH)
    slice_neigh = jnp.dot(neighbour, piece, precision=HIGH)
    sums = lax.psum((slice_self, slice_neigh, jnp.sum(piece, axis=0)), "node")
    grad_self, grad_neigh = (lax.all_gather(part, "feat", axis=0, tiled=True) for part in sums[:2])
    gneigh = (neigh_back / scale).reshape(slices, blocks, TB)
    outgoing = jnp.einsum("scb,fbi->scfi", row_onehot, gneigh, precision=HIGH)
    returned = lax.all_to_all(outgoing, "node", split_axis=0, concat_axis=0, tiled=True)
    spread = jnp.einsum("dcfi,dcij->dcfj", returned, tiles, precision=HIGH)
    placed = jnp.einsum("dcfj,dcb->fbj", spread, col_onehot, precision=HIGH)
    grad_feats = self_back + placed.reshape(slices, owned)
    return (activated, grad_feats, grad_self, grad_neigh, sums[2])


def solution(mesh):
    chain = mesh.shape["node"] == 8 and mesh.shape["feat"] == 4
    return jax.shard_map(
        chain_shards if chain else slot_shards,
        mesh=mesh,
        in_specs=(
            P("feat", "node"),
            P("node", None, None, None),
            P("node", None),
            P("node", None),
            P("node"),
            P(),
            P(),
            P(),
            P(("node", "feat"), None),
        ),
        out_specs=(P(("node", "feat"), None), P("feat", "node"), P(), P(), P()),
        check_vma=False,
    )
```

time: 412 us -> 294 us (0.71); the launches traced: 404 us -> 293 us
  blocking collectives: 83.2 us -> 0 us
  matrix products: 72.8 us -> 0 us
  waiting for transfers between devices: 200 us -> 138 us
  Pallas kernels: 0 us -> 58.9 us
  starting transfers between devices: 13.9 us -> 70.1 us
  between operations: 14.2 us -> 1.59 us
  local copies, waits for them, and re-layouts: 14.2 us -> 21.5 us
    ppermute x0 -> x51, waiting for transfers between devices: none -> 138 us  [the longest x37 113 us: node_swap(): return lax.ppermute(value, 'node', pairs)]
    all_to_all x2 -> x0, waiting for transfers between devices: 92.7 us -> none  [the longest x1 92.7 us: shards(): lax.all_to_all(partial_value, 'node', split_axis=0, concat_axis=0, tiled=...]
    dot_general x12 -> x0, matrix products: 72.8 us -> none  [the longest x1 18.7 us: shards(): jnp.einsum('dcfj,dcij->dcfi', picked, tiles, precision=lax.Precision.HIGH...]
    psum x1 -> x0, blocking collectives: 70.9 us -> none  [shards(): lax.psum((slice_self, slice_neigh, grad_bias_part), 'node')]
    ppermute x0 -> x51, starting transfers between devices: none -> 70.1 us  [the longest x37 63.7 us: node_swap(): return lax.ppermute(value, 'node', pairs)]
    pallas_call x0 -> x30, Pallas kernels: none -> 58.9 us  [call(): pl.pallas_call(ordered, grid_spec=pltpu.PrefetchScalarGridSpec(num_scalar...]
    reduce_scatter x1 -> x0, waiting for transfers between devices: 41.2 us -> none  [shards(): lax.psum_scatter(first + second, 'feat', scatter_dimension=0, tiled=True)]
    all_gather x1 -> x0, waiting for transfers between devices: 34.6 us -> none  [shards(): piece = lax.all_gather(gpre, 'feat', axis=0, tiled=True)]
  transfers between devices with their start and end apart: 5 -> 51, of which waited for: 4 -> 22; matrix products, arithmetic and copies ran while one was open for 4% -> 2% of each run, Pallas kernels for 0% -> 18%
where the time goes in v2:
time: 294 us; the launch traced here: 293 us
  waiting for transfers between devices  138 us (47%)
  starting transfers between devices  70.1 us (24%)
  Pallas kernels  58.9 us (20%)
  local copies, waits for them, and re-layouts  21.5 us (7%)
  other arithmetic  3.27 us (1%)
    ppermute x37, waiting for transfers between devices, node_swap(): return lax.ppermute(value, 'node', pairs)  113 us
    ppermute x37, starting transfers between devices, node_swap(): return lax.ppermute(value, 'node', pairs)  63.7 us
    pallas_call x30, Pallas kernels, call(): pl.pallas_call(ordered, grid_spec=pltpu.PrefetchScalarGridSpec(num_scalar...  58.9 us
    ppermute x4, waiting for transfers between devices, over_feat(): far = lax.ppermute(value, 'feat', OTHER_Y)  24.9 us
    unnamed x46, local copies, waits for them, and re-layouts  19.2 us
  transfers between devices with their start and end apart: 51, of which 22 were waited for; matrix products, arithmetic and copies ran while one was open for 2% of the time, Pallas kernels for 18%

profile of v2, /device:TPU:0, one launch (start us, length us, event | category | flops | bytes accessed | tf_op | source)
XLA Modules:
  0.0 293.3 jit_solution(17013918987866554262)
XLA Ops:
  1.5 3.4 %copy-done = f32[8,16,128,128]{3,2,1,0:T(8,128)S(1)} copy-done((f32[8,16,128,128]{3,2,1,0:T(8,128)S(1)}, f32[8,16,128,128]{3,2,1,0:T(8,128)}, u32[]{:S(2)}) %copy-start) | copy-done | bytes 8388632
  7.2 3.0 %collective-permute-start.3 = (f32[16,64,128]{2,1,0:T(8,128)S(1)}, f32[16,64,128]{2,1,0:T(8,128)S(1)}, u32[]{:S(2)}, u32[]{:S(2)}) collective-permute-start(f32[16,64,128]{2,1,0:T(8,128)S(1)} %shard_map.129), channel_id=1, source_target_pairs={{0,1},{1,0},{2,3},{3,2},{4,5},{5,4},{6,7},{7,6},{8,9},{9,8},{10,11... | collective-permute-start | bytes 1572872 | tf_op jit(solution)/shard_map/ppermute | solution.py:415
  10.2 11.9 %collective-permute-done.3.refs_4_.refs_3_ = f32[16,64,128]{2,1,0:T(8,128)S(1)} collective-permute-done((f32[16,64,128]{2,1,0:T(8,128)S(1)}, f32[16,64,128]{2,1,0:T(8,128)S(1)}, u32[]{:S(2)}, u32[]{:S(2)}) %collective-permute-start.3) | collective-permute-done | bytes 524320 | tf_op jit(solution)/shard_map/ppermute | solution.py:415
  26.6 2.5 collective-permute-start.2
  29.2 2.8 collective-permute-done.2
  33.7 3.4 %copy-done.1 = f32[8,16,128,128]{3,2,1,0:T(8,128)S(1)} copy-done((f32[8,16,128,128]{3,2,1,0:T(8,128)S(1)}, f32[8,16,128,128]{3,2,1,0:T(8,128)}, u32[]{:S(2)}) %copy-start.1) | copy-done | bytes 8388632
  37.1 3.0 %shard_map.128.refs_2_ = f32[4,32,64,128]{3,2,1,0:T(8,128)S(1)} custom-call(s32[4]{0:T(128)S(1)} %pad_add_fusion.refs_0_, s32[128]{0:T(128)S(1)} %reshape.125.refs_1_, s32[128]{0:T(128)S(1)} %reshape.124.refs_2_.refs_1_, f32[64,4096]{1,0:T(8,128)S(1)} %copy-done.5, f32[8,16,128,128]{3,2,1,0:T(8,128)S(1)} %copy-done.1), custom_call_target="tpu_custom_call" | custom-call | flops 100000000 | bytes 4194304 | tf_op jit(solution)/shard_map/pallas_call | solution.py:103
  40.9 2.6 collective-permute-start.7
  45.6 3.4 %copy-done.2 = f32[8,16,128,128]{3,2,1,0:T(8,128)S(1)} copy-done((f32[8,16,128,128]{3,2,1,0:T(8,128)S(1)}, f32[8,16,128,128]{3,2,1,0:T(8,128)}, u32[]{:S(2)}) %copy-start.2) | copy-done | bytes 8388632
  53.0 2.8 collective-permute-done.7.refs_4_
  56.5 4.4 %collective-permute-start.8 = (f32[16,64,128]{2,1,0:T(8,128)S(1)}, f32[16,64,128]{2,1,0:T(8,128)S(1)}, u32[]{:S(2)}, u32[]{:S(2)}) collective-permute-start(f32[16,64,128]{2,1,0:T(8,128)S(1)} %shard_map.135), channel_id=1, source_target_pairs={{0,2},{1,3},{6,4},{7,5},{8,10},{9,11},{14,12},{15,13},{16,18},{17,... | collective-permute-start | bytes 1572872 | tf_op jit(solution)/shard_map/ppermute | solution.py:415
  61.0 6.1 %collective-permute-done.10.refs_4_ = f32[16,64,128]{2,1,0:T(8,128)S(1)} collective-permute-done((f32[16,64,128]{2,1,0:T(8,128)S(1)}, f32[16,64,128]{2,1,0:T(8,128)S(1)}, u32[]{:S(2)}, u32[]{:S(2)}) %collective-permute-start.10) | collective-permute-done | bytes 524320 | tf_op jit(solution)/shard_map/ppermute | solution.py:415
  67.8 4.5 %collective-permute-start.11 = (f32[16,64,128]{2,1,0:T(8,128)S(1)}, f32[16,64,128]{2,1,0:T(8,128)S(1)}, u32[]{:S(2)}, u32[]{:S(2)}) collective-permute-start(f32[16,64,128]{2,1,0:T(8,128)S(1)} %shard_map.138), channel_id=1, source_target_pairs={{0,2},{1,3},{6,4},{7,5},{8,10},{9,11},{14,12},{15,13},{16,18},{17,... | collective-permute-start | bytes 1572872 | tf_op jit(solution)/shard_map/ppermute | solution.py:415
  73.3 5.0 %collective-permute-done.8.refs_4_ = f32[16,64,128]{2,1,0:T(8,128)S(1)} collective-permute-done((f32[16,64,128]{2,1,0:T(8,128)S(1)}, f32[16,64,128]{2,1,0:T(8,128)S(1)}, u32[]{:S(2)}, u32[]{:S(2)}) %collective-permute-start.8) | collective-permute-done | bytes 524320 | tf_op jit(solution)/shard_map/ppermute | solution.py:415
  79.0 6.4 %collective-permute-done.11.refs_4_.refs_1_ = f32[16,64,128]{2,1,0:T(8,128)S(1)} collective-permute-done((f32[16,64,128]{2,1,0:T(8,128)S(1)}, f32[16,64,128]{2,1,0:T(8,128)S(1)}, u32[]{:S(2)}, u32[]{:S(2)}) %collective-permute-start.11) | collective-permute-done | bytes 524320 | tf_op jit(solution)/shard_map/ppermute | solution.py:415
  86.2 4.4 %collective-permute-start.12 = (f32[16,64,128]{2,1,0:T(8,128)S(1)}, f32[16,64,128]{2,1,0:T(8,128)S(1)}, u32[]{:S(2)}, u32[]{:S(2)}) collective-permute-start(f32[16,64,128]{2,1,0:T(8,128)S(1)} %shard_map.139), channel_id=1, source_target_pairs={{0,2},{1,3},{6,4},{7,5},{8,10},{9,11},{14,12},{15,13},{16,18},{17,... | collective-permute-start | bytes 1572872 | tf_op jit(solution)/shard_map/ppermute | solution.py:415
  91.8 2.8 collective-permute-done.22.refs_8_
  98.9 4.6 %collective-permute-start.9 = (f32[16,64,128]{2,1,0:T(8,128)S(1)}, f32[16,64,128]{2,1,0:T(8,128)S(1)}, u32[]{:S(2)}, u32[]{:S(2)}) collective-permute-start(f32[16,64,128]{2,1,0:T(8,128)S(1)} %shard_map.136), channel_id=1, source_target_pairs={{0,2},{1,3},{6,4},{7,5},{8,10},{9,11},{14,12},{15,13},{16,18},{17,... | collective-permute-start | bytes 1572872 | tf_op jit(solution)/shard_map/ppermute | solution.py:415
  107.9 2.2 collective-permute-done.9.refs_1_
  111.1 8.9 %collective-permute-done.15.refs_3_ = f32[16,64,128]{2,1,0:T(8,128)S(1)} collective-permute-done((f32[16,64,128]{2,1,0:T(8,128)S(1)}, f32[16,64,128]{2,1,0:T(8,128)S(1)}, u32[]{:S(2)}, u32[]{:S(2)}) %collective-permute-start.15) | collective-permute-done | bytes 524320 | tf_op jit(solution)/shard_map/ppermute | solution.py:415
  122.9 11.8 %collective-permute-done.28.refs_2_ = f32[16,64,128]{2,1,0:T(8,128)S(1)} collective-permute-done((f32[16,64,128]{2,1,0:T(8,128)S(1)}, f32[16,64,128]{2,1,0:T(8,128)S(1)}, u32[]{:S(2)}, u32[]{:S(2)}) %collective-permute-start.28) | collective-permute-done | bytes 524320 | tf_op jit(solution)/shard_map/ppermute | solution.py:419
  135.2 10.3 %collective-permute-done.16.refs_2_ = f32[16,64,128]{2,1,0:T(8,128)S(1)} collective-permute-done((f32[16,64,128]{2,1,0:T(8,128)S(1)}, f32[16,64,128]{2,1,0:T(8,128)S(1)}, u32[]{:S(2)}, u32[]{:S(2)}) %collective-permute-start.16) | collective-permute-done | bytes 524320 | tf_op jit(solution)/shard_map/ppermute | solution.py:419
  145.6 4.9 %shard_map.141.refs_6_ = f32[2,256,2048]{2,1,0:T(8,128)S(1)} custom-call(s32[4]{0:T(128)S(1)} %pad_add_fusion.refs_0_, f32[64,4096]{1,0:T(8,128)S(1)} %copy-done.5, f32[64,4096]{1,0:T(8,128)S(1)} %collective-permute-done.19.refs_2_, f32[64,4096]{1,0:T(8,128)S(1)} %collective-permute-done.20.refs_3_, f32[64,4096]{1,0:T(8,128)S(1)} %collective-permute-done.21.refs_4_, ...), custom_call_target="tpu_custom_call" | custom-call | flops 100000000 | bytes 4194304 | tf_op jit(solution)/shard_map/pallas_call | solution.py:103
  150.5 4.1 %shard_map.145 = (f32[1024,256]{1,0:T(8,128)}, f32[256,2048]{1,0:T(8,128)S(1)}, f32[16,64,128]{2,1,0:T(8,128)S(1)}) custom-call(s32[4]{0:T(128)S(1)} %pad_add_fusion.refs_0_, f32[16,64,128]{2,1,0:T(8,128)S(1)} %shard_map.144.refs_1_.refs_3_, f32[16,64,128]{2,1,0:T(8,128)S(1)} %collective-permute-done.28.refs_2_, ...), custom_call_target="tpu_custom_call" | custom-call | flops 100000000 | bytes 4194304 | tf_op jit(solution)/shard_map/pallas_call | solution.py:103
  154.6 2.4 collective-permute-start.31
  157.0 4.2 %shard_map.146 = (f32[1024,256]{1,0:T(8,128)}, f32[256,2048]{1,0:T(8,128)S(1)}, f32[16,64,128]{2,1,0:T(8,128)}) custom-call(s32[4]{0:T(128)S(1)} %pad_add_fusion.refs_0_, f32[16,64,128]{2,1,0:T(8,128)S(1)} %shard_map.140.refs_1_.refs_3_, f32[16,64,128]{2,1,0:T(8,128)S(1)} %collective-permute-done.16.refs_2_, ...), custom_call_target="tpu_custom_call", output_to_operand_aliasing={{0}: (12, {})} | custom-call | flops 100000000 | bytes 4194304 | tf_op jit(solution)/shard_map/pallas_call | solution.py:103
  165.7 2.0 shard_map.151
  168.5 2.1 shard_map.152
  172.8 8.1 %collective-permute-done.33.refs_3_.refs_5_ = f32[16,64,128]{2,1,0:T(8,128)} collective-permute-done((f32[16,64,128]{2,1,0:T(8,128)}, f32[16,64,128]{2,1,0:T(8,128)}, u32[]{:S(2)}, u32[]{:S(2)}) %collective-permute-start.33) | collective-permute-done | bytes 524320 | tf_op jit(solution)/shard_map/ppermute | solution.py:415
  182.5 3.0 %collective-permute-start.46 = (f32[72,256]{1,0:T(8,128)S(1)}, f32[72,256]{1,0:T(8,128)S(1)}, u32[]{:S(2)}, u32[]{:S(2)}) collective-permute-start(f32[72,256]{1,0:T(8,128)S(1)} %bitcast_add_fusion), channel_id=1, source_target_pairs={{0,2},{1,3},{2,0},{3,1},{4,6},{5,7},{6,4},{7,5},{8,10},{9,11},{10,... | collective-permute-start | bytes 221192 | tf_op jit(solution)/shard_map/ppermute | solution.py:415
  185.6 2.3 collective-permute-done.46
  187.9 3.0 %collective-permute-start.47 = (f32[72,256]{1,0:T(8,128)S(1)}, f32[72,256]{1,0:T(8,128)S(1)}, u32[]{:S(2)}, u32[]{:S(2)}) collective-permute-start(f32[72,256]{1,0:T(8,128)S(1)} %add.59), channel_id=1, source_target_pairs={{0,6},{1,7},{2,4},{3,5},{4,2},{5,3},{6,0},{7,1},{8,14},{9,15},{10,... | collective-permute-start | bytes 221192 | tf_op jit(solution)/shard_map/ppermute | solution.py:415
  190.9 3.3 %collective-permute-done.47 = f32[72,256]{1,0:T(8,128)S(1)} collective-permute-done((f32[72,256]{1,0:T(8,128)S(1)}, f32[72,256]{1,0:T(8,128)S(1)}, u32[]{:S(2)}, u32[]{:S(2)}) %collective-permute-start.47) | collective-permute-done | bytes 73760 | tf_op jit(solution)/shard_map/ppermute | solution.py:415
  201.4 2.6 shard_map.150
  205.7 25.9 %collective-permute-done.40.refs_4_.refs_6_ = f32[16,64,128]{2,1,0:T(8,128)S(1)} collective-permute-done((f32[16,64,128]{2,1,0:T(8,128)}, f32[16,64,128]{2,1,0:T(8,128)S(1)}, u32[]{:S(2)}, u32[]{:S(2)}) %collective-permute-start.40) | collective-permute-done | bytes 524320 | tf_op jit(solution)/shard_map/ppermute | solution.py:415
  234.9 8.0 %collective-permute-done.41.refs_5_.refs_7_ = f32[16,64,128]{2,1,0:T(8,128)} collective-permute-done((f32[16,64,128]{2,1,0:T(8,128)S(1)}, f32[16,64,128]{2,1,0:T(8,128)}, u32[]{:S(2)}, u32[]{:S(2)}) %collective-permute-start.41) | collective-permute-done | bytes 524320 | tf_op jit(solution)/shard_map/ppermute | solution.py:415
  242.9 2.0 collective-permute-start.43
  244.9 2.0 shard_map.148
  246.9 7.3 %collective-permute-done.35.refs_4_.refs_6_ = f32[16,64,128]{2,1,0:T(8,128)} collective-permute-done((f32[16,64,128]{2,1,0:T(8,128)S(1)}, f32[16,64,128]{2,1,0:T(8,128)}, u32[]{:S(2)}, u32[]{:S(2)}) %collective-permute-start.35) | collective-permute-done | bytes 524320 | tf_op jit(solution)/shard_map/ppermute | solution.py:415
  254.2 2.0 collective-permute-start.42
  256.2 7.6 %collective-permute-done.36.refs_5_.refs_7_ = f32[16,64,128]{2,1,0:T(8,128)} collective-permute-done((f32[16,64,128]{2,1,0:T(8,128)S(1)}, f32[16,64,128]{2,1,0:T(8,128)}, u32[]{:S(2)}, u32[]{:S(2)}) %collective-permute-start.36) | collective-permute-done | bytes 524320 | tf_op jit(solution)/shard_map/ppermute | solution.py:415
  263.7 2.2 shard_map.147
  267.7 3.4 %copy-done.3 = f32[8,16,128,128]{3,2,1,0:T(8,128)S(1)} copy-done((f32[8,16,128,128]{3,2,1,0:T(8,128)S(1)}, f32[8,16,128,128]{3,2,1,0:T(8,128)}, u32[]{:S(2)}) %copy-start.3) | copy-done | bytes 8388632
  271.1 3.2 %shard_map.153.refs_7_ = f32[64,4096]{1,0:T(8,128)} custom-call(s32[4]{0:T(128)S(1)} %pad_add_fusion.refs_0_, s32[128]{0:T(128)S(1)} %reshape.125.refs_1_, s32[128]{0:T(128)S(1)} %reshape.124.refs_2_.refs_1_, f32[8,16,128,128]{3,2,1,0:T(8,128)S(1)} %copy-done.3, f32[16,64,128]{2,1,0:T(8,128)S(1)} %get-tuple-element.17.refs_2_.refs_4_, ...), custom_call_target="tpu_custom_call" | custom-call | flops 100000000 | bytes 4194304 | tf_op jit(solution)/shard_map/pallas_call | solution.py:103
  274.4 4.3 %shard_map.154.refs_9_ = f32[64,4096]{1,0:T(8,128)} custom-call(s32[4]{0:T(128)S(1)} %pad_add_fusion.refs_0_, s32[128]{0:T(128)S(1)} %reshape.125.refs_1_, s32[128]{0:T(128)S(1)} %reshape.124.refs_2_.refs_1_, f32[8,16,128,128]{3,2,1,0:T(8,128)S(1)} %copy-done.3, ...), custom_call_target="tpu_custom_call", output_to_operand_aliasing={{}: (7, {})} | custom-call | flops 100000000 | bytes 4194304 | tf_op jit(solution)/shard_map/pallas_call | solution.py:103
  281.2 4.3 %shard_map.155.refs_9_ = f32[64,4096]{1,0:T(8,128)} custom-call(s32[4]{0:T(128)S(1)} %pad_add_fusion.refs_0_, s32[128]{0:T(128)S(1)} %reshape.125.refs_1_, s32[128]{0:T(128)S(1)} %reshape.124.refs_2_.refs_1_, f32[8,16,128,128]{3,2,1,0:T(8,128)S(1)} %copy-done.3, ...), custom_call_target="tpu_custom_call", output_to_operand_aliasing={{}: (9, {})} | custom-call | flops 100000000 | bytes 4194304 | tf_op jit(solution)/shard_map/pallas_call | solution.py:103
  285.5 4.3 %shard_map.156.refs_5_ = f32[64,4096]{1,0:T(8,128)} custom-call(s32[4]{0:T(128)S(1)} %pad_add_fusion.refs_0_, s32[128]{0:T(128)S(1)} %reshape.125.refs_1_, s32[128]{0:T(128)S(1)} %reshape.124.refs_2_.refs_1_, f32[8,16,128,128]{3,2,1,0:T(8,128)S(1)} %copy-done.3, ...), custom_call_target="tpu_custom_call", output_to_operand_aliasing={{}: (9, {})} | custom-call | flops 100000000 | bytes 4194304 | tf_op jit(solution)/shard_map/pallas_call | solution.py:103
  289.8 3.3 %shard_map.157 = f32[64,4096]{1,0:T(8,128)} custom-call(s32[4]{0:T(128)S(1)} %pad_add_fusion.refs_0_, s32[128]{0:T(128)S(1)} %reshape.125.refs_1_, s32[128]{0:T(128)S(1)} %reshape.124.refs_2_.refs_1_, f32[8,16,128,128]{3,2,1,0:T(8,128)S(1)} %copy-done.3, f32[16,64,128]{2,1,0:T(8,128)S(1)} %collective-permute-done.37.refs_4_, ...), custom_call_target="tpu_custom_call", output_to_operand_aliasing={{}: (5, {})} | custom-call | flops 100000000 | bytes 4194304 | tf_op jit(solution)/shard_map/pallas_call | solution.py:103
  (152 shorter events, 59.8 us)
Async XLA Ops:
  7.2 14.9 %collective-permute-start.3 = (f32[16,64,128]{2,1,0:T(8,128)S(1)}, f32[16,64,128]{2,1,0:T(8,128)S(1)}, u32[]{:S(2)}, u32[]{:S(2)}) collective-permute-start(f32[16,64,128]{2,1,0:T(8,128)S(1)} %shard_map.129), channel_id=1, source_target_pairs={{0,1},{1,0},{2,3},{3,2},{4,5},{5,4},{6,7},{7,6},{8,9},{9,8},{10,11... | collective-permute-start | bytes 1572872 | tf_op jit(solution)/shard_map/ppermute | solution.py:415
  23.3 16.9 %collective-permute-start.4 = (f32[16,64,128]{2,1,0:T(8,128)S(1)}, f32[16,64,128]{2,1,0:T(8,128)S(1)}, u32[]{:S(2)}, u32[]{:S(2)}) collective-permute-start(f32[16,64,128]{2,1,0:T(8,128)S(1)} %shard_map.130), channel_id=1, source_target_pairs={{0,1},{1,0},{2,3},{3,2},{4,5},{5,4},{6,7},{7,6},{8,9},{9,8},{10,11... | collective-permute-start | bytes 1572872 | tf_op jit(solution)/shard_map/ppermute | solution.py:415
  26.6 5.4 %collective-permute-start.2 = (s32[8,16]{1,0:T(8,128)S(1)}, s32[8,16]{1,0:T(8,128)S(1)}, u32[]{:S(2)}, u32[]{:S(2)}) collective-permute-start(s32[8,16]{1,0:T(8,128)S(1)} %copy-done.20), channel_id=1, source_target_pairs={{0,6},{1,7},{2,4},{3,5},{4,2},{5,3},{6,0},{7,1},{8,14},{9,15},{10,... | collective-permute-start | bytes 1544 | tf_op jit(solution)/shard_map/ppermute | solution.py:415
  40.9 15.0 %collective-permute-start.7 = (f32[16,64,128]{2,1,0:T(8,128)S(1)}, f32[16,64,128]{2,1,0:T(8,128)S(1)}, u32[]{:S(2)}, u32[]{:S(2)}) collective-permute-start(f32[16,64,128]{2,1,0:T(8,128)S(1)} %shard_map.134), channel_id=1, source_target_pairs={{0,2},{1,3},{6,4},{7,5},{8,10},{9,11},{14,12},{15,13},{16,18},{17,... | collective-permute-start | bytes 1572872 | tf_op jit(solution)/shard_map/ppermute | solution.py:415
  44.2 22.8 %collective-permute-start.10 = (f32[16,64,128]{2,1,0:T(8,128)S(1)}, f32[16,64,128]{2,1,0:T(8,128)S(1)}, u32[]{:S(2)}, u32[]{:S(2)}) collective-permute-start(f32[16,64,128]{2,1,0:T(8,128)S(1)} %shard_map.137), channel_id=1, source_target_pairs={{0,2},{1,3},{6,4},{7,5},{8,10},{9,11},{14,12},{15,13},{16,18},{17,... | collective-permute-start | bytes 1572872 | tf_op jit(solution)/shard_map/ppermute | solution.py:415
  50.0 17.0 %collective-permute-start.5 = (f32[16,64,128]{2,1,0:T(8,128)S(1)}, f32[16,64,128]{2,1,0:T(8,128)S(1)}, u32[]{:S(2)}, u32[]{:S(2)}) collective-permute-start(f32[16,64,128]{2,1,0:T(8,128)S(1)} %shard_map.131), channel_id=1, source_target_pairs={{0,1},{1,0},{2,3},{3,2},{4,5},{5,4},{6,7},{7,6},{8,9},{9,8},{10,11... | collective-permute-start | bytes 1572872 | tf_op jit(solution)/shard_map/ppermute | solution.py:415
  50.6 46.2 %collective-permute-start.19 = (f32[64,4096]{1,0:T(8,128)S(1)}, f32[64,4096]{1,0:T(8,128)S(1)}, u32[]{:S(2)}, u32[]{:S(2)}) collective-permute-start(f32[64,4096]{1,0:T(8,128)S(1)} %copy-done.5), channel_id=1, source_target_pairs={{0,16},{8,24},{16,0},{24,8},{1,17},{9,25},{17,1},{25,9},{2,18},{10... | collective-permute-start | bytes 3145736 | tf_op jit(solution)/shard_map/ppermute | solution.py:419
  52.5 42.1 %collective-permute-start.22 = (f32[256,1024]{1,0:T(8,128)S(1)}, f32[256,1024]{1,0:T(8,128)S(1)}, u32[]{:S(2)}, u32[]{:S(2)}) collective-permute-start(f32[256,1024]{1,0:T(8,128)S(1)} %shard_map.142.refs_7_), channel_id=1, source_target_pairs={{0,16},{8,24},{16,0},{24,8},{1,17},{9,25},{17,1},{25,9},{2,18},{10... | collective-permute-start | bytes 3145736 | tf_op jit(solution)/shard_map/ppermute | solution.py:419
  56.5 21.7 %collective-permute-start.8 = (f32[16,64,128]{2,1,0:T(8,128)S(1)}, f32[16,64,128]{2,1,0:T(8,128)S(1)}, u32[]{:S(2)}, u32[]{:S(2)}) collective-permute-start(f32[16,64,128]{2,1,0:T(8,128)S(1)} %shard_map.135), channel_id=1, source_target_pairs={{0,2},{1,3},{6,4},{7,5},{8,10},{9,11},{14,12},{15,13},{16,18},{17,... | collective-permute-start | bytes 1572872 | tf_op jit(solution)/shard_map/ppermute | solution.py:415
  67.8 17.7 %collective-permute-start.11 = (f32[16,64,128]{2,1,0:T(8,128)S(1)}, f32[16,64,128]{2,1,0:T(8,128)S(1)}, u32[]{:S(2)}, u32[]{:S(2)}) collective-permute-start(f32[16,64,128]{2,1,0:T(8,128)S(1)} %shard_map.138), channel_id=1, source_target_pairs={{0,2},{1,3},{6,4},{7,5},{8,10},{9,11},{14,12},{15,13},{16,18},{17,... | collective-permute-start | bytes 1572872 | tf_op jit(solution)/shard_map/ppermute | solution.py:415
  72.4 23.6 %collective-permute-start.26 = (f32[16,64,128]{2,1,0:T(8,128)S(1)}, f32[16,64,128]{2,1,0:T(8,128)S(1)}, u32[]{:S(2)}, u32[]{:S(2)}) collective-permute-start(f32[16,64,128]{2,1,0:T(8,128)S(1)} %add.54), channel_id=1, source_target_pairs={{2,4},{3,5},{4,2},{5,3},{10,12},{11,13},{12,10},{13,11},{18,20},{1... | collective-permute-start | bytes 1572872 | tf_op jit(solution)/shard_map/ppermute | solution.py:415
  78.3 20.6 %collective-permute-start.14 = (f32[16,64,128]{2,1,0:T(8,128)S(1)}, f32[16,64,128]{2,1,0:T(8,128)S(1)}, u32[]{:S(2)}, u32[]{:S(2)}) collective-permute-start(f32[16,64,128]{2,1,0:T(8,128)S(1)} %add.51), channel_id=1, source_target_pairs={{2,4},{3,5},{4,2},{5,3},{10,12},{11,13},{12,10},{13,11},{18,20},{1... | collective-permute-start | bytes 1572872 | tf_op jit(solution)/shard_map/ppermute | solution.py:415
  86.2 17.3 %collective-permute-start.12 = (f32[16,64,128]{2,1,0:T(8,128)S(1)}, f32[16,64,128]{2,1,0:T(8,128)S(1)}, u32[]{:S(2)}, u32[]{:S(2)}) collective-permute-start(f32[16,64,128]{2,1,0:T(8,128)S(1)} %shard_map.139), channel_id=1, source_target_pairs={{0,2},{1,3},{6,4},{7,5},{8,10},{9,11},{14,12},{15,13},{16,18},{17,... | collective-permute-start | bytes 1572872 | tf_op jit(solution)/shard_map/ppermute | solution.py:415
  94.6 9.3 %collective-permute-start.6 = (f32[16,64,128]{2,1,0:T(8,128)S(1)}, f32[16,64,128]{2,1,0:T(8,128)S(1)}, u32[]{:S(2)}, u32[]{:S(2)}) collective-permute-start(f32[16,64,128]{2,1,0:T(8,128)S(1)} %shard_map.132), channel_id=1, source_target_pairs={{0,1},{1,0},{2,3},{3,2},{4,5},{5,4},{6,7},{7,6},{8,9},{9,8},{10,11... | collective-permute-start | bytes 1572872 | tf_op jit(solution)/shard_map/ppermute | solution.py:415
  96.1 9.1 %collective-permute-start.25 = (f32[16,64,128]{2,1,0:T(8,128)S(1)}, f32[16,64,128]{2,1,0:T(8,128)S(1)}, u32[]{:S(2)}, u32[]{:S(2)}) collective-permute-start(f32[16,64,128]{2,1,0:T(8,128)S(1)} %add.53), channel_id=1, source_target_pairs={{2,4},{3,5},{4,2},{5,3},{10,12},{11,13},{12,10},{13,11},{18,20},{1... | collective-permute-start | bytes 1572872 | tf_op jit(solution)/shard_map/ppermute | solution.py:415
  96.9 11.1 %collective-permute-start.27 = (f32[16,64,128]{2,1,0:T(8,128)S(1)}, f32[16,64,128]{2,1,0:T(8,128)S(1)}, u32[]{:S(2)}, u32[]{:S(2)}) collective-permute-start(f32[16,64,128]{2,1,0:T(8,128)S(1)} %add.55), channel_id=1, source_target_pairs={{2,0},{3,1},{4,6},{5,7},{10,8},{11,9},{12,14},{13,15},{18,16},{19,... | collective-permute-start | bytes 1572872 | tf_op jit(solution)/shard_map/ppermute | solution.py:415
  98.9 11.3 %collective-permute-start.9 = (f32[16,64,128]{2,1,0:T(8,128)S(1)}, f32[16,64,128]{2,1,0:T(8,128)S(1)}, u32[]{:S(2)}, u32[]{:S(2)}) collective-permute-start(f32[16,64,128]{2,1,0:T(8,128)S(1)} %shard_map.136), channel_id=1, source_target_pairs={{0,2},{1,3},{6,4},{7,5},{8,10},{9,11},{14,12},{15,13},{16,18},{17,... | collective-permute-start | bytes 1572872 | tf_op jit(solution)/shard_map/ppermute | solution.py:415
  103.5 18.8 %collective-permute-start.23 = (f32[256,1024]{1,0:T(8,128)S(1)}, f32[256,1024]{1,0:T(8,128)S(1)}, u32[]{:S(2)}, u32[]{:S(2)}) collective-permute-start(f32[256,1024]{1,0:T(8,128)S(1)} %shard_map.142.refs_7_), channel_id=1, source_target_pairs={{0,8},{8,0},{16,24},{24,16},{1,9},{9,1},{17,25},{25,17},{2,10},{10... | collective-permute-start | bytes 3145736 | tf_op jit(solution)/shard_map/ppermute | solution.py:420
  103.9 16.1 %collective-permute-start.15 = (f32[16,64,128]{2,1,0:T(8,128)S(1)}, f32[16,64,128]{2,1,0:T(8,128)S(1)}, u32[]{:S(2)}, u32[]{:S(2)}) collective-permute-start(f32[16,64,128]{2,1,0:T(8,128)S(1)} %add.52), channel_id=1, source_target_pairs={{2,0},{3,1},{4,6},{5,7},{10,8},{11,9},{12,14},{13,15},{18,16},{19,... | collective-permute-start | bytes 1572872 | tf_op jit(solution)/shard_map/ppermute | solution.py:415
  105.2 14.8 %collective-permute-start.13 = (f32[16,64,128]{2,1,0:T(8,128)S(1)}, f32[16,64,128]{2,1,0:T(8,128)S(1)}, u32[]{:S(2)}, u32[]{:S(2)}) collective-permute-start(f32[16,64,128]{2,1,0:T(8,128)S(1)} %add.50), channel_id=1, source_target_pairs={{2,4},{3,5},{4,2},{5,3},{10,12},{11,13},{12,10},{13,11},{18,20},{1... | collective-permute-start | bytes 1572872 | tf_op jit(solution)/shard_map/ppermute | solution.py:415
  107.9 15.0 %collective-permute-start.20 = (f32[64,4096]{1,0:T(8,128)S(1)}, f32[64,4096]{1,0:T(8,128)S(1)}, u32[]{:S(2)}, u32[]{:S(2)}) collective-permute-start(f32[64,4096]{1,0:T(8,128)S(1)} %copy-done.5), channel_id=1, source_target_pairs={{0,8},{8,0},{16,24},{24,16},{1,9},{9,1},{17,25},{25,17},{2,10},{10... | collective-permute-start | bytes 3145736 | tf_op jit(solution)/shard_map/ppermute | solution.py:420
  110.2 24.5 %collective-permute-start.21 = (f32[64,4096]{1,0:T(8,128)S(1)}, f32[64,4096]{1,0:T(8,128)S(1)}, u32[]{:S(2)}, u32[]{:S(2)}) collective-permute-start(f32[64,4096]{1,0:T(8,128)S(1)} %collective-permute-done.19.refs_2_), channel_id=1, source_target_pairs={{0,8},{8,0},{16,24},{24,16},{1,9},{9,1},{17,25},{25,17},{2,10},{10... | collective-permute-start | bytes 3145736 | tf_op jit(solution)/shard_map/ppermute | solution.py:421
  120.0 30.5 %collective-permute-start.24 = (f32[256,1024]{1,0:T(8,128)S(1)}, f32[256,1024]{1,0:T(8,128)S(1)}, u32[]{:S(2)}, u32[]{:S(2)}) collective-permute-start(f32[256,1024]{1,0:T(8,128)S(1)} %collective-permute-done.22.refs_8_), channel_id=1, source_target_pairs={{0,8},{8,0},{16,24},{24,16},{1,9},{9,1},{17,25},{25,17},{2,10},{10... | collective-permute-start | bytes 3145736 | tf_op jit(solution)/shard_map/ppermute | solution.py:421
  120.0 14.7 %collective-permute-start.28 = (f32[16,64,128]{2,1,0:T(8,128)S(1)}, f32[16,64,128]{2,1,0:T(8,128)S(1)}, u32[]{:S(2)}, u32[]{:S(2)}) collective-permute-start(f32[16,64,128]{2,1,0:T(8,128)S(1)} %shard_map.144.refs_1_.refs_3_), channel_id=1, source_target_pairs={{0,16},{8,24},{16,0},{24,8},{1,17},{9,25},{17,1},{25,9},{2,18},{10... | collective-permute-start | bytes 1572872 | tf_op jit(solution)/shard_map/ppermute | solution.py:419
  122.4 23.2 %collective-permute-start.16 = (f32[16,64,128]{2,1,0:T(8,128)S(1)}, f32[16,64,128]{2,1,0:T(8,128)S(1)}, u32[]{:S(2)}, u32[]{:S(2)}) collective-permute-start(f32[16,64,128]{2,1,0:T(8,128)S(1)} %shard_map.140.refs_1_.refs_3_), channel_id=1, source_target_pairs={{0,16},{8,24},{16,0},{24,8},{1,17},{9,25},{17,1},{25,9},{2,18},{10... | collective-permute-start | bytes 1572872 | tf_op jit(solution)/shard_map/ppermute | solution.py:419
  122.9 27.6 %collective-permute-start.29 = (f32[16,64,128]{2,1,0:T(8,128)S(1)}, f32[16,64,128]{2,1,0:T(8,128)S(1)}, u32[]{:S(2)}, u32[]{:S(2)}) collective-permute-start(f32[16,64,128]{2,1,0:T(8,128)S(1)} %shard_map.144.refs_1_.refs_3_), channel_id=1, source_target_pairs={{0,8},{8,0},{16,24},{24,16},{1,9},{9,1},{17,25},{25,17},{2,10},{10... | collective-permute-start | bytes 1572872 | tf_op jit(solution)/shard_map/ppermute | solution.py:420
  134.7 15.8 %collective-permute-start.30 = (f32[16,64,128]{2,1,0:T(8,128)S(1)}, f32[16,64,128]{2,1,0:T(8,128)S(1)}, u32[]{:S(2)}, u32[]{:S(2)}) collective-permute-start(f32[16,64,128]{2,1,0:T(8,128)S(1)} %collective-permute-done.28.refs_2_), channel_id=1, source_target_pairs={{0,8},{8,0},{16,24},{24,16},{1,9},{9,1},{17,25},{25,17},{2,10},{10... | collective-permute-start | bytes 1572872 | tf_op jit(solution)/shard_map/ppermute | solution.py:421
  134.7 22.3 %collective-permute-start.17 = (f32[16,64,128]{2,1,0:T(8,128)S(1)}, f32[16,64,128]{2,1,0:T(8,128)S(1)}, u32[]{:S(2)}, u32[]{:S(2)}) collective-permute-start(f32[16,64,128]{2,1,0:T(8,128)S(1)} %shard_map.140.refs_1_.refs_3_), channel_id=1, source_target_pairs={{0,8},{8,0},{16,24},{24,16},{1,9},{9,1},{17,25},{25,17},{2,10},{10... | collective-permute-start | bytes 1572872 | tf_op jit(solution)/shard_map/ppermute | solution.py:420
  145.5 11.5 %collective-permute-start.18 = (f32[16,64,128]{2,1,0:T(8,128)S(1)}, f32[16,64,128]{2,1,0:T(8,128)S(1)}, u32[]{:S(2)}, u32[]{:S(2)}) collective-permute-start(f32[16,64,128]{2,1,0:T(8,128)S(1)} %collective-permute-done.16.refs_2_), channel_id=1, source_target_pairs={{0,8},{8,0},{16,24},{24,16},{1,9},{9,1},{17,25},{25,17},{2,10},{10... | collective-permute-start | bytes 1572872 | tf_op jit(solution)/shard_map/ppermute | solution.py:421
  154.6 17.6 %collective-permute-start.31 = (f32[16,64,128]{2,1,0:T(8,128)S(1)}, f32[16,64,128]{2,1,0:T(8,128)S(1)}, u32[]{:S(2)}, u32[]{:S(2)}) collective-permute-start(f32[16,64,128]{2,1,0:T(8,128)S(1)} %get-tuple-element.17.refs_2_.refs_4_), channel_id=1, source_target_pairs={{0,2},{1,3},{2,0},{3,1},{4,6},{5,7},{6,4},{7,5},{8,10},{9,11},{10,... | collective-permute-start | bytes 1572872 | tf_op jit(solution)/shard_map/ppermute | solution.py:415
  162.6 18.3 %collective-permute-start.33 = (f32[16,64,128]{2,1,0:T(8,128)}, f32[16,64,128]{2,1,0:T(8,128)}, u32[]{:S(2)}, u32[]{:S(2)}) collective-permute-start(f32[16,64,128]{2,1,0:T(8,128)} %get-tuple-element.18.refs_3_.refs_5_), channel_id=1, source_target_pairs={{0,2},{1,3},{2,0},{3,1},{4,6},{5,7},{6,4},{7,5},{8,10},{9,11},{10,... | collective-permute-start | bytes 1572872 | tf_op jit(solution)/shard_map/ppermute | solution.py:415
  162.6 32.7 %collective-permute-start.38 = (f32[16,64,128]{2,1,0:T(8,128)S(1)}, f32[16,64,128]{2,1,0:T(8,128)}, u32[]{:S(2)}, u32[]{:S(2)}) collective-permute-start(f32[16,64,128]{2,1,0:T(8,128)S(1)} %get-tuple-element.17.refs_2_.refs_4_), channel_id=1, source_target_pairs={{2,4},{3,5},{4,2},{5,3},{10,12},{11,13},{12,10},{13,11},{18,20},{1... | collective-permute-start | bytes 1572872 | tf_op jit(solution)/shard_map/ppermute | solution.py:415
  167.8 28.8 %collective-permute-start.39 = (f32[16,64,128]{2,1,0:T(8,128)}, f32[16,64,128]{2,1,0:T(8,128)S(1)}, u32[]{:S(2)}, u32[]{:S(2)}) collective-permute-start(f32[16,64,128]{2,1,0:T(8,128)} %get-tuple-element.18.refs_3_.refs_5_), channel_id=1, source_target_pairs={{2,4},{3,5},{4,2},{5,3},{10,12},{11,13},{12,10},{13,11},{18,20},{1... | collective-permute-start | bytes 1572872 | tf_op jit(solution)/shard_map/ppermute | solution.py:415
  172.0 9.6 %collective-permute-start.45 = (f32[72,256]{1,0:T(8,128)S(1)}, f32[72,256]{1,0:T(8,128)S(1)}, u32[]{:S(2)}, u32[]{:S(2)}) collective-permute-start(f32[72,256]{1,0:T(8,128)S(1)} %dynamic-slice_bitcast_fusion), channel_id=1, source_target_pairs={{0,1},{1,0},{2,3},{3,2},{4,5},{5,4},{6,7},{7,6},{8,9},{9,8},{10,11... | collective-permute-start | bytes 221192 | tf_op jit(solution)/shard_map/ppermute | solution.py:415
  172.2 26.6 %collective-permute-start.32 = (f32[16,64,128]{2,1,0:T(8,128)S(1)}, f32[16,64,128]{2,1,0:T(8,128)S(1)}, u32[]{:S(2)}, u32[]{:S(2)}) collective-permute-start(f32[16,64,128]{2,1,0:T(8,128)S(1)} %collective-permute-done.31.refs_2_.refs_4_), channel_id=1, source_target_pairs={{2,4},{3,5},{4,2},{5,3},{10,12},{11,13},{12,10},{13,11},{18,20},{1... | collective-permute-start | bytes 1572872 | tf_op jit(solution)/shard_map/ppermute | solution.py:415
  180.9 19.1 %collective-permute-start.34 = (f32[16,64,128]{2,1,0:T(8,128)}, f32[16,64,128]{2,1,0:T(8,128)S(1)}, u32[]{:S(2)}, u32[]{:S(2)}) collective-permute-start(f32[16,64,128]{2,1,0:T(8,128)} %collective-permute-done.33.refs_3_.refs_5_), channel_id=1, source_target_pairs={{2,4},{3,5},{4,2},{5,3},{10,12},{11,13},{12,10},{13,11},{18,20},{1... | collective-permute-start | bytes 1572872 | tf_op jit(solution)/shard_map/ppermute | solution.py:415
  182.5 5.4 %collective-permute-start.46 = (f32[72,256]{1,0:T(8,128)S(1)}, f32[72,256]{1,0:T(8,128)S(1)}, u32[]{:S(2)}, u32[]{:S(2)}) collective-permute-start(f32[72,256]{1,0:T(8,128)S(1)} %bitcast_add_fusion), channel_id=1, source_target_pairs={{0,2},{1,3},{2,0},{3,1},{4,6},{5,7},{6,4},{7,5},{8,10},{9,11},{10,... | collective-permute-start | bytes 221192 | tf_op jit(solution)/shard_map/ppermute | solution.py:415
  187.9 6.3 %collective-permute-start.47 = (f32[72,256]{1,0:T(8,128)S(1)}, f32[72,256]{1,0:T(8,128)S(1)}, u32[]{:S(2)}, u32[]{:S(2)}) collective-permute-start(f32[72,256]{1,0:T(8,128)S(1)} %add.59), channel_id=1, source_target_pairs={{0,6},{1,7},{2,4},{3,5},{4,2},{5,3},{6,0},{7,1},{8,14},{9,15},{10,... | collective-permute-start | bytes 221192 | tf_op jit(solution)/shard_map/ppermute | solution.py:415
  195.3 36.3 %collective-permute-start.40 = (f32[16,64,128]{2,1,0:T(8,128)}, f32[16,64,128]{2,1,0:T(8,128)S(1)}, u32[]{:S(2)}, u32[]{:S(2)}) collective-permute-start(f32[16,64,128]{2,1,0:T(8,128)} %collective-permute-done.38.refs_2_.refs_4_), channel_id=1, source_target_pairs={{2,0},{3,1},{4,6},{5,7},{10,8},{11,9},{12,14},{13,15},{18,16},{19,... | collective-permute-start | bytes 1572872 | tf_op jit(solution)/shard_map/ppermute | solution.py:415
  196.6 46.3 %collective-permute-start.41 = (f32[16,64,128]{2,1,0:T(8,128)S(1)}, f32[16,64,128]{2,1,0:T(8,128)}, u32[]{:S(2)}, u32[]{:S(2)}) collective-permute-start(f32[16,64,128]{2,1,0:T(8,128)S(1)} %collective-permute-done.39.refs_3_.refs_5_), channel_id=1, source_target_pairs={{2,0},{3,1},{4,6},{5,7},{10,8},{11,9},{12,14},{13,15},{18,16},{19,... | collective-permute-start | bytes 1572872 | tf_op jit(solution)/shard_map/ppermute | solution.py:415
  198.7 5.3 %collective-permute-start.49 = (f32[144,256]{1,0:T(8,128)S(1)}, f32[144,256]{1,0:T(8,128)S(1)}, u32[]{:S(2)}, u32[]{:S(2)}) collective-permute-start(f32[144,256]{1,0:T(8,128)S(1)} %bitcast.35), channel_id=1, source_target_pairs={{0,8},{8,0},{16,24},{24,16},{1,9},{9,1},{17,25},{25,17},{2,10},{10... | collective-permute-start | bytes 442376 | tf_op jit(solution)/shard_map/ppermute | solution.py:436
  198.8 55.4 %collective-permute-start.35 = (f32[16,64,128]{2,1,0:T(8,128)S(1)}, f32[16,64,128]{2,1,0:T(8,128)}, u32[]{:S(2)}, u32[]{:S(2)}) collective-permute-start(f32[16,64,128]{2,1,0:T(8,128)S(1)} %collective-permute-done.32.refs_2_.refs_4_), channel_id=1, source_target_pairs={{2,0},{3,1},{4,6},{5,7},{10,8},{11,9},{12,14},{13,15},{18,16},{19,... | collective-permute-start | bytes 1572872 | tf_op jit(solution)/shard_map/ppermute | solution.py:415
  200.1 63.7 %collective-permute-start.36 = (f32[16,64,128]{2,1,0:T(8,128)S(1)}, f32[16,64,128]{2,1,0:T(8,128)}, u32[]{:S(2)}, u32[]{:S(2)}) collective-permute-start(f32[16,64,128]{2,1,0:T(8,128)S(1)} %collective-permute-done.34.refs_3_.refs_5_), channel_id=1, source_target_pairs={{2,0},{3,1},{4,6},{5,7},{10,8},{11,9},{12,14},{13,15},{18,16},{19,... | collective-permute-start | bytes 1572872 | tf_op jit(solution)/shard_map/ppermute | solution.py:415
  204.0 70.4 %collective-permute-start.44 = (f32[16,64,128]{2,1,0:T(8,128)}, f32[16,64,128]{2,1,0:T(8,128)}, u32[]{:S(2)}, u32[]{:S(2)}) collective-permute-start(f32[16,64,128]{2,1,0:T(8,128)} %shard_map.150), channel_id=1, source_target_pairs={{0,1},{1,0},{2,3},{3,2},{4,5},{5,4},{6,7},{7,6},{8,9},{9,8},{10,11... | collective-permute-start | bytes 1572872 | tf_op jit(solution)/shard_map/ppermute | solution.py:415
  231.6 47.1 %collective-permute-start.50 = (f32[2,144,256]{2,1,0:T(8,128)}, f32[2,144,256]{2,1,0:T(8,128)}, u32[]{:S(2)}, u32[]{:S(2)}) collective-permute-start(f32[2,144,256]{2,1,0:T(8,128)} %maximum_select_fusion.2), channel_id=1, source_target_pairs={{0,16},{8,24},{16,0},{24,8},{1,17},{9,25},{17,1},{25,9},{2,18},{10... | collective-permute-start | bytes 884744 | tf_op jit(solution)/shard_map/ppermute | solution.py:437
  242.9 38.3 %collective-permute-start.43 = (f32[16,64,128]{2,1,0:T(8,128)S(1)}, f32[16,64,128]{2,1,0:T(8,128)S(1)}, u32[]{:S(2)}, u32[]{:S(2)}) collective-permute-start(f32[16,64,128]{2,1,0:T(8,128)S(1)} %shard_map.149), channel_id=1, source_target_pairs={{0,1},{1,0},{2,3},{3,2},{4,5},{5,4},{6,7},{7,6},{8,9},{9,8},{10,11... | collective-permute-start | bytes 1572872 | tf_op jit(solution)/shard_map/ppermute | solution.py:415
  254.2 31.3 %collective-permute-start.42 = (f32[16,64,128]{2,1,0:T(8,128)S(1)}, f32[16,64,128]{2,1,0:T(8,128)S(1)}, u32[]{:S(2)}, u32[]{:S(2)}) collective-permute-start(f32[16,64,128]{2,1,0:T(8,128)S(1)} %shard_map.148), channel_id=1, source_target_pairs={{0,1},{1,0},{2,3},{3,2},{4,5},{5,4},{6,7},{7,6},{8,9},{9,8},{10,11... | collective-permute-start | bytes 1572872 | tf_op jit(solution)/shard_map/ppermute | solution.py:415
  265.9 23.8 %collective-permute-start.37 = (f32[16,64,128]{2,1,0:T(8,128)S(1)}, f32[16,64,128]{2,1,0:T(8,128)S(1)}, u32[]{:S(2)}, u32[]{:S(2)}) collective-permute-start(f32[16,64,128]{2,1,0:T(8,128)S(1)} %shard_map.147), channel_id=1, source_target_pairs={{0,1},{1,0},{2,3},{3,2},{4,5},{5,4},{6,7},{7,6},{8,9},{9,8},{10,11... | collective-permute-start | bytes 1572872 | tf_op jit(solution)/shard_map/ppermute | solution.py:415
  (26 other events, 290.5 us)

commit v3 on v2

--- a/solution.py
+++ b/solution.py
@@ -11,6 +11,7 @@
 HIGH = lax.Precision.HIGH
 CHUNKS = 2
 VMEM_BYTES = 28 * 2**20
+TILE_VMEM_BYTES = 57 * 2**20
 
 FAR_OUTER, FAR_INNER, NEAR, SELF = range(4)
 
@@ -70,6 +71,7 @@
         self.per_chunk = self.blocks // CHUNKS
         self.piece = self.per_piece * TB
         self.span = self.per_chunk * TB
+        self.token = None
 
     def spot(self, row):
         row = jnp.maximum(row, 0)
@@ -94,26 +96,46 @@
     def dense(self):
         return jax.ShapeDtypeStruct((self.per_chunk, self.slices, TB), F32)
 
-    def call(self, body, scalars, grid, in_specs, args, out_specs, out_shape, scratch=(), aliases=None, after=()):
+    def call(self, body, scalars, grid, in_specs, args, out_specs, out_shape, scratch=(), aliases=None, after=(), vmem=VMEM_BYTES):
         given = len(scalars) + len(args)
+        waits = list(after) + ([] if self.token is None else [self.token])
 
         def ordered(*refs):
-            body(*refs[:given], *refs[given + len(after) :])
-
-        return pl.pallas_call(
+            body(*refs[:given], *refs[given + len(waits) :])
+
+        out = pl.pallas_call(
             ordered,
             grid_spec=pltpu.PrefetchScalarGridSpec(
                 num_scalar_prefetch=len(scalars),
                 grid=grid,
-                in_specs=list(in_specs) + [pl.BlockSpec(memory_space=pl.ANY)] * len(after),
+                in_specs=list(in_specs) + [pl.BlockSpec(memory_space=pl.ANY)] * len(waits),
                 out_specs=out_specs,
                 scratch_shapes=scratch,
             ),
             out_shape=out_shape,
             input_output_aliases=aliases or {},
-            compiler_params=pltpu.CompilerParams(vmem_limit_bytes=VMEM_BYTES),
-            cost_estimate=pl.CostEstimate(flops=10**8, bytes_accessed=4 * 2**20, transcendentals=0),
-        )(*scalars, *args, *after)
+            compiler_params=pltpu.CompilerParams(vmem_limit_bytes=vmem),
+            cost_estimate=pl.CostEstimate(flops=1, bytes_accessed=1, transcendentals=0),
+        )(*scalars, *args, *waits)
+        self.token = jax.tree.leaves(out)[-1]
+        return out
+
+    def relay(self, value):
+        def body(value, out):
+            pass
+
+        anywhere = pl.BlockSpec(memory_space=pl.ANY)
+        return self.call(
+            body, (), (1,), [anywhere], (value,), anywhere, jax.ShapeDtypeStruct(value.shape, value.dtype),
+            aliases={0: 0},
+        )
+
+    def added(self, a, b):
+        def body(a, b, out):
+            out[...] = a[...] + b[...]
+
+        spec = self.full(*a.shape)
+        return self.call(body, (), (1,), [spec] * 2, (a, b), spec, jax.ShapeDtypeStruct(a.shape, F32))
 
     def fetched(self, count):
         return [pltpu.VMEM((count, self.cap, TB, TB), F32), pltpu.SemaphoreType.DMA((count,))]
@@ -131,15 +153,15 @@
             copy.start()
             copy.wait()
             for c in range(self.cap):
-                out[c] = times_tile_t(feats[:, lanes(cols[owned_by * self.cap + c])], buffer[0, c])
+                out[c] = times_tile_t(feats[:, lanes(cols[owned_by, c])], buffer[0, c])
 
         return self.call(
             body, (place, cols), (1,),
             [self.full(self.slices, self.owned), self.tiles_spec()], (feats, tiles),
-            self.slots_spec(), self.slots(), scratch=self.fetched(1), after=after,
-        )
-
-    def local(self, place, cols, rows, feats, tiles, after=()):
+            self.slots_spec(), self.slots(), scratch=self.fetched(1), after=after, vmem=TILE_VMEM_BYTES,
+        )
+
+    def local(self, place, cols, rows, feats, tiles):
         def body(place, cols, rows, feats, tiles, out, buffer, sems):
             z, x = place[0], place[1]
             copies = [self.fetch(tiles, buffer, sems, owner(role, z) * 2 + x, role) for role in range(4)]
@@ -148,29 +170,39 @@
             for role in range(4):
                 out[role] = jnp.zeros(out.shape[1:], F32)
                 copies[role].wait()
-                first = (owner(role, z) * 2 + x) * self.cap
+                owned_by, row_of = owner(role, z) * 2 + x, self.row_index(role, z, x)
                 for c in range(self.cap):
-                    row = rows[self.row_index(role, z, x) + c]
+                    row = rows[row_of, c]
                     chunk, spot = self.spot(row)
-                    value = times_tile_t(feats[:, lanes(cols[first + c])], buffer[role, c])
+                    value = times_tile_t(feats[:, lanes(cols[owned_by, c])], buffer[role, c])
                     out[role, chunk * self.per_chunk + spot] += jnp.where(row >= 0, value, 0.0)
 
         shape = (4, self.blocks, self.slices, TB)
         return self.call(
             body, (place, cols, rows), (1,),
             [self.full(self.slices, self.owned), self.tiles_spec()], (feats, tiles),
-            self.full(*shape), jax.ShapeDtypeStruct(shape, F32), scratch=self.fetched(4), after=after,
+            self.full(*shape), jax.ShapeDtypeStruct(shape, F32), scratch=self.fetched(4), vmem=TILE_VMEM_BYTES,
+        )
+
+    def own_rows(self, place, tables):
+        def body(place, *refs):
+            for distance, table in enumerate(refs[:4]):
+                refs[4][2 * distance : 2 * distance + 2, :] = table[pl.ds(2 * place[0], 2), :]
+
+        spec = self.full(*tables[0].shape)
+        return self.call(
+            body, (place,), (1,), [spec] * 4, tables, spec, jax.ShapeDtypeStruct(tables[0].shape, jnp.int32)
         )
 
     def row_index(self, role, z, sender_x):
-        return ((owner(role, z) ^ z) * 2 + sender_x) * self.cap
+        return (owner(role, z) ^ z) * 2 + sender_x
 
     def joined(self, role, k, place, rows, sums, slots, after=()):
         def body(place, rows, sums, slots, out):
             out[...] = sums[0]
-            first = self.row_index(role, place[0], 1 - place[1])
+            row_of = self.row_index(role, place[0], 1 - place[1])
             for c in range(self.cap):
-                row = rows[first + c]
+                row = rows[row_of, c]
                 chunk, spot = self.spot(row)
                 out[spot] += jnp.where((row >= 0) & (chunk == k), slots[c], 0.0)
 
@@ -193,15 +225,24 @@
             self.dense_spec(), self.dense(),
         )
 
-    def transposed(self, value, after=()):
-        def body(value, out):
-            out[...] = value[...].T
-
-        rows, cols = value.shape
-        return self.call(
-            body, (), (1,), [self.full(rows, cols)], (value,), self.full(cols, rows),
-            jax.ShapeDtypeStruct((cols, rows), F32), after=after,
-        )
+    def turned(self, feats, cotangent):
+        def body(feats, cotangent, feats_out, cotangent_out):
+            feats_out[...] = feats[...]
+            cotangent_out[...] = cotangent[...].T
+
+        rows, cols = cotangent.shape
+        whole, turned = self.full(*feats.shape), self.full(cols, rows)
+        return self.call(
+            body, (), (1,), [whole, self.full(rows, cols)], (feats, cotangent), [whole, turned],
+            [jax.ShapeDtypeStruct(feats.shape, F32), jax.ShapeDtypeStruct((cols, rows), F32)],
+        )
+
+    def copied(self, table):
+        def body(table, out):
+            out[...] = table[...]
+
+        spec = self.full(*table.shape)
+        return self.call(body, (), (1,), [spec], (table,), spec, jax.ShapeDtypeStruct(table.shape, table.dtype))
 
     def feats_of(self, place):
         y, core = place[2], place[3]
@@ -213,7 +254,7 @@
         out = dot_nn(jnp.concatenate([weight_high, weight_low], 0), high)
         return out[:rows] + out[rows:] + dot_nn(weight_high, low)
 
-    def self_part(self, place, slices, w_self, bias, after=()):
+    def self_part(self, place, slices, w_self, bias):
         def body(place, own, far, core, both, w_self, bias, out, held):
             for index, piece in zip(self.feats_of(place), (own, far, core, both)):
                 held[pl.ds(pl.multiple_of(index * self.slices, self.slices), self.slices), :] = piece[...]
@@ -227,7 +268,7 @@
             [columns] * 4 + [self.full(self.width, self.width), self.full(1, self.width)], (*slices, w_self, bias),
             pl.BlockSpec((1, self.width, self.piece), lambda k, part, *_: (k, 0, part)),
             jax.ShapeDtypeStruct((CHUNKS, self.width, self.span), F32),
-            scratch=[pltpu.VMEM((self.width, self.piece), F32)], after=after,
+            scratch=[pltpu.VMEM((self.width, self.piece), F32)],
         )
 
     def activate(self, k, place, means, w_neigh, self_part, cotangents, inverse, activated):
@@ -278,11 +319,13 @@
         )
 
     def weight_grad(self, k, place, w_self, feats, means, grad, before):
-        shape = (2 * self.slices + 16, self.width)
+        last = k == CHUNKS - 1
+        rows_all = 2 * self.slices + 16
+        shapes = [(rows_all // 2, self.width)] * 2 if last else [(rows_all, self.width)]
 
         def body(place, w_self, feats, means, grad, *rest):
-            self_out, weights_out = rest[-2:]
-            total = rest[0][...] if before is not None else jnp.zeros(shape, F32)
+            total = rest[0][...] if before is not None else jnp.zeros((rows_all, self.width), F32)
+            self_out, outs = rest[before is not None], rest[1 + (before is not None) :]
             for part in range(self.parts):
                 first = part * self.per_piece
                 at = slice(part * self.piece, (part + 1) * self.piece)
@@ -301,15 +344,62 @@
                 )
                 rows_high, rows_low = split(rows)
                 total += (dot_nt(rows_high, high) + dot_nt(rows_low, high)) + dot_nt(rows_high, low)
-            weights_out[...] = total
-
-        own_rows = pl.BlockSpec((self.slices, self.width), lambda i, place, *_: (2 * place[2] + place[3], 0))
+            if last:
+                x0 = place[1] == 0
+                lower, upper = total[: rows_all // 2], total[rows_all // 2 :]
+                outs[0][...] = jnp.where(x0, upper, lower)
+                outs[1][...] = jnp.where(x0, lower, upper)
+            else:
+                outs[0][...] = total
+
+        weight_rows = pl.BlockSpec((self.slices, self.width), lambda i, place, *_: (2 * place[2] + place[3], 0))
         args = [w_self, feats, means, grad] + ([] if before is None else [before])
         return self.call(
             body, (place,), (1,),
-            [own_rows, self.full(self.slices, self.owned), self.dense_spec(), self.full(self.width, self.span)]
-            + [self.full(*shape)] * (before is not None),
-            args, [self.dense_spec(), self.full(*shape)], [self.dense(), jax.ShapeDtypeStruct(shape, F32)],
+            [weight_rows, self.full(self.slices, self.owned), self.dense_spec(), self.full(self.width, self.span)]
+            + [self.full(rows_all, self.width)] * (before is not None),
+            args, [self.dense_spec()] + [self.full(*shape) for shape in shapes],
+            [self.dense()] + [jax.ShapeDtypeStruct(shape, F32) for shape in shapes],
+        )
+
+    def both_halves(self, place, mine, other):
+        half = mine.shape[0]
+
+        def body(place, mine, other, out):
+            out[pl.ds(pl.multiple_of(place[1] * half, 8), half), :] = mine[...]
+            out[pl.ds(pl.multiple_of((1 - place[1]) * half, 8), half), :] = other[...]
+
+        shape = (2 * half, self.width)
+        return self.call(
+            body, (place,), (1,), [self.full(*mine.shape)] * 2, (mine, other), self.full(*shape),
+            jax.ShapeDtypeStruct(shape, F32),
+        )
+
+    def both_cores(self, place, mine, other):
+        def body(place, mine, other, out):
+            out[place[3]] = mine[...]
+            out[1 - place[3]] = other[...]
+
+        shape = (2, *mine.shape)
+        return self.call(
+            body, (place,), (1,), [self.full(*mine.shape)] * 2, (mine, other), self.full(*shape),
+            jax.ShapeDtypeStruct(shape, F32),
+        )
+
+    def whole_weights(self, place, mine, other):
+        def body(place, mine, other, w_self, w_neigh, bias):
+            for y, block in ((place[2], mine), (1 - place[2], other)):
+                for core in range(2):
+                    at = pl.ds(pl.multiple_of((2 * y + core) * self.slices, self.slices), self.slices)
+                    w_self[at, :] = block[core, : self.slices, :]
+                    w_neigh[at, :] = block[core, self.slices : 2 * self.slices, :]
+            bias[...] = mine[0, 2 * self.slices : 2 * self.slices + 1, :]
+
+        square, row = (self.width, self.width), (1, self.width)
+        return self.call(
+            body, (place,), (1,), [self.full(*mine.shape)] * 2, (mine, other),
+            [self.full(*square), self.full(*square), self.full(*row)],
+            [jax.ShapeDtypeStruct(shape, F32) for shape in (square, square, row)],
         )
 
     def gather(self, place, sources, held):
@@ -339,9 +429,9 @@
         def body(place, rows, *rest):
             out, held = rest[-2:]
             self.gather(place, rest[:-2], held)
-            first = self.row_index(role, place[0], 1 - place[1])
+            row_of = self.row_index(role, place[0], 1 - place[1])
             for c in range(self.cap):
-                out[c] = self.pick(rows[first + c], held)
+                out[c] = self.pick(rows[row_of, c], held)
 
         return self.call(
             body, (place, rows), (1,), [self.dense_spec()] * len(sources), sources,
@@ -375,10 +465,10 @@
                 copies[i].wait()
                 for c in range(self.cap):
                     if counts[i] > 1:
-                        value = self.pick(rows[self.row_index(role, z, x) + c], held)
+                        value = self.pick(rows[self.row_index(role, z, x), c], held)
                     else:
                         value = sources[0][c]
-                    out[:, lanes(cols[owners[i] * self.cap + c])] += times_tile(value, buffer[i, c])
+                    out[:, lanes(cols[owners[i], c])] += times_tile(value, buffer[i, c])
 
         whole = self.full(self.slices, self.owned)
         in_specs, args = [self.tiles_spec()], [tiles]
@@ -391,7 +481,7 @@
             body, (place, cols, rows), (1,), in_specs, args, whole,
             jax.ShapeDtypeStruct((self.slices, self.owned), F32),
             scratch=[self.held(), *self.fetched(len(jobs))],
-            aliases={3 + len(args) - 1: 0} if self_back is None else {},
+            aliases={3 + len(args) - 1: 0} if self_back is None else {}, vmem=TILE_VMEM_BYTES,
         )
 
 
@@ -415,98 +505,222 @@
     return lax.ppermute(value, "node", pairs)
 
 
-def over_feat(value):
-    far = lax.ppermute(value, "feat", OTHER_Y)
-    core = lax.ppermute(value, "feat", OTHER_CORE)
-    return value, far, core, lax.ppermute(far, "feat", OTHER_CORE)
-
-
-def pair(mine, other, place):
-    return jnp.where(place == 0, jnp.stack([mine, other]), jnp.stack([other, mine]))
-
-
-def spread_weights(weights, x, y, core):
-    halves = weights.reshape(2, -1, weights.shape[1])
-    keep = lax.dynamic_index_in_dim(halves, x, 0, keepdims=False)
-    send = lax.dynamic_index_in_dim(halves, 1 - x, 0, keepdims=False)
-    total = keep + node_swap(send, OTHER_X)
-    total = total + node_swap(total, along_z(1))
-    total = total + node_swap(total, along_z(3))
-    whole = pair(total, node_swap(total, OTHER_X), x).reshape(weights.shape)
-    cores = pair(whole, lax.ppermute(whole, "feat", OTHER_CORE), core)
-    return pair(cores, lax.ppermute(cores, "feat", OTHER_Y), y).reshape(4, *weights.shape)
+def feat_swap(value, pairs):
+    return lax.ppermute(value, "feat", pairs)
+
+
+ORDER = [
+    ("slots", FAR_OUTER),
+    ("table_out",),
+    ("turn",),
+    ("rows_in",),
+    ("local",),
+    ("slots", FAR_INNER),
+    ("join", FAR_OUTER, 0),
+    ("join", FAR_INNER, 0),
+    ("slots", NEAR),
+    ("pass_on", FAR_OUTER, 0),
+    ("feats_on",),
+    ("join", FAR_OUTER, 1),
+    ("join", NEAR, 0),
+    ("pass_on", FAR_INNER, 0),
+    ("slots", SELF),
+    ("pass_on", NEAR, 0),
+    ("self_part",),
+    ("pass_on", FAR_OUTER, 1),
+    ("join", SELF, 0),
+    ("join", FAR_INNER, 1),
+    ("mean", 0),
+    ("cotangents_on",),
+    ("join", SELF, 1),
+    ("join", NEAR, 1),
+    ("pass_on", NEAR, 1),
+    ("pass_on", FAR_INNER, 1),
+    ("means_on", 0),
+    ("activate", 0),
+    ("mean", 1),
+    ("inner_on", 0),
+    ("means_on", 1),
+    ("near_on", 0),
+    ("weight", 0),
+    ("activate", 1),
+    ("weight", 1),
+    ("weight_x",),
+    ("outer_on", 0),
+    ("pick", SELF),
+    ("inner_on", 1),
+    ("weight_near",),
+    ("near_on", 1),
+    ("weight_far",),
+    ("pick", NEAR),
+    ("spread", SELF, None),
+    ("spread", NEAR, SELF),
+    ("outer_on", 1),
+    ("pick", FAR_INNER),
+    ("weight_halves",),
+    ("pick", FAR_OUTER),
+    ("weight_cores",),
+    ("spread", FAR_INNER, NEAR),
+    ("spread", FAR_OUTER, FAR_INNER),
+    ("weight_whole",),
+    ("spread", None, FAR_OUTER),
+]
+
+
+class Steps:
+    def __init__(self, layer, place, node_feats, tiles, send_col, recv_row, inverse, w_self, w_neigh, bias, cotangent):
+        self.layer, self.place, self.feats, self.tiles = layer, place, node_feats, tiles
+        self.cols, self.table, self.inverse = send_col, recv_row, inverse
+        self.w_self, self.w_neigh, self.bias, self.cotangent = w_self, w_neigh, bias, cotangent
+        self.slots_in, self.joined, self.inward, self.returned = {}, {}, {}, {}
+        self.sent = []
+        self.across, self.outward, self.means, self.mean_parts = {}, {}, {}, {}
+        self.grads, self.own, self.near, self.inner, self.outer = {}, {}, {}, {}, {}
+        self.self_back, self.activated, self.weights, self.total = {}, None, None, None
+
+    def slots(self, role):
+        after = [self.slots_in[role - 1]] if role else []
+        part = self.layer.partial(role, self.place, self.cols, self.feats, self.tiles, after=after)
+        self.slots_in[role] = node_swap(part, OTHER_X)
+
+    def table_out(self):
+        table = self.layer.copied(self.table)
+        self.tables = [self.table] + [node_swap(table, along_z(distance)) for distance in (1, 2, 3)]
+
+    def rows_in(self):
+        self.rows = self.layer.own_rows(self.place, self.tables)
+
+    def local(self):
+        self.sums = self.layer.local(self.place, self.cols, self.rows, self.feats, self.tiles)
+
+    def turn(self):
+        feats, cotangent = self.layer.turned(self.feats, self.cotangent)
+        self.feat_parts = [self.feats, feat_swap(feats, OTHER_Y), feat_swap(feats, OTHER_CORE)]
+        self.cotangents = [cotangent, feat_swap(cotangent, OTHER_Y), feat_swap(cotangent, OTHER_CORE)]
+
+    def on(self, parts):
+        parts[1] = self.layer.relay(parts[1])
+        parts.append(feat_swap(parts[1], OTHER_CORE))
+
+    def feats_on(self):
+        self.on(self.feat_parts)
+
+    def cotangents_on(self):
+        self.on(self.cotangents)
+
+    def self_part(self):
+        self.self_parts = self.layer.self_part(self.place, self.feat_parts, self.w_self, self.bias)
+
+    def join(self, role, k):
+        after = [] if role == SELF else self.sent[-2:-1]
+        part = self.layer.joined(role, k, self.place, self.rows, self.sums, self.slots_in[role], after=after)
+        self.joined[role, k] = part
+        if role != SELF:
+            self.inward[role, k] = node_swap(part, INWARD)
+            self.sent.append(self.inward[role, k])
+
+    def pass_on(self, role, k):
+        if role == NEAR:
+            part = self.layer.added(self.joined[NEAR, k], self.across[FAR_OUTER, k])
+            self.outward[k] = node_swap(part, OUTWARD)
+        else:
+            part = self.layer.added(self.joined[role, k], self.inward[role, k])
+            self.across[role, k] = node_swap(part, ACROSS)
+
+    def mean(self, k):
+        pieces = (self.joined[SELF, k], self.inward[NEAR, k], self.across[FAR_INNER, k], self.outward[k])
+        means = self.layer.means(k, pieces, self.inverse)
+        self.means[k] = means
+        self.mean_parts[k] = [means, feat_swap(means, OTHER_Y), feat_swap(means, OTHER_CORE)]
+
+    def means_on(self, k):
+        self.on(self.mean_parts[k])
+
+    def activate(self, k):
+        self.activated, self.grads[k], back = self.layer.activate(
+            k, self.place, self.mean_parts[k], self.w_neigh, self.self_parts, self.cotangents, self.inverse, self.activated
+        )
+        self.own[k] = back
+        self.near[k] = node_swap(back, along_z(1))
+        self.inner[k] = [node_swap(back, ACROSS)]
+
+    def near_on(self, k):
+        self.near[k] = self.layer.relay(self.near[k])
+        self.outer[k] = [node_swap(self.near[k], ACROSS)]
+
+    def inner_on(self, k):
+        self.inner[k][0] = self.layer.relay(self.inner[k][0])
+        self.inner[k].append(node_swap(self.inner[k][0], OUTWARD))
+
+    def outer_on(self, k):
+        self.outer[k][0] = self.layer.relay(self.outer[k][0])
+        self.outer[k].append(node_swap(self.outer[k][0], OUTWARD))
+
+    def weight(self, k):
+        back, *weights = self.layer.weight_grad(
+            k, self.place, self.w_self, self.feats, self.means[k], self.grads[k], self.weights
+        )
+        self.self_back[k] = back
+        if k == CHUNKS - 1:
+            send, self.weights = weights
+            self.weights_in = node_swap(send, OTHER_X)
+        else:
+            self.weights = weights[0]
+
+    def weight_x(self):
+        self.weights = self.layer.added(self.weights, self.weights_in)
+        self.weights_in = node_swap(self.weights, along_z(1))
+
+    def weight_near(self):
+        self.weights = self.layer.added(self.weights, self.weights_in)
+        self.weights_in = node_swap(self.weights, along_z(3))
+
+    def weight_far(self):
+        self.weights = self.layer.added(self.weights, self.weights_in)
+        self.weights_in = node_swap(self.weights, OTHER_X)
+
+    def weight_halves(self):
+        self.weights = self.layer.both_halves(self.place, self.weights, self.weights_in)
+        self.weights_in = feat_swap(self.weights, OTHER_CORE)
+
+    def weight_cores(self):
+        self.weights = self.layer.both_cores(self.place, self.weights, self.weights_in)
+        self.weights_in = feat_swap(self.weights, OTHER_Y)
+
+    def weight_whole(self):
+        self.weights = self.layer.whole_weights(self.place, self.weights, self.weights_in)
+
+    def sources(self, role):
+        if role in (SELF, NEAR):
+            return [(self.own if role == SELF else self.near)[k] for k in range(CHUNKS)]
+        held = self.inner if role == FAR_INNER else self.outer
+        return [held[k][0] for k in range(CHUNKS)] + [held[k][1] for k in range(CHUNKS)]
+
+    def pick(self, role):
+        self.returned[role] = node_swap(self.layer.picked(role, self.place, self.rows, self.sources(role)), OTHER_X)
+
+    def spread(self, local, slots):
+        jobs = [] if local is None else [(local, self.sources(local))]
+        jobs += [] if slots is None else [(slots, [self.returned[slots]])]
+        first = self.total is None
+        back = [self.self_back[k] for k in range(CHUNKS)] if first else None
+        self.total = self.layer.spread(self.place, self.cols, self.rows, self.tiles, jobs, self.total, back)
 
 
 def chain_shards(node_feats, tiles, send_col, recv_row, degree, w_self, w_neigh, bias, cotangent):
     slices, owned = node_feats.shape
-    cap = tiles.shape[1]
     width = w_self.shape[1]
-    layer = Layer(slices, owned, cap, 4, width)
+    layer = Layer(slices, owned, tiles.shape[1], 4, width)
     node, feat = lax.axis_index("node"), lax.axis_index("feat")
-    z, x, y, core = node // 2, node % 2, feat // 2, feat % 2
-    place = jnp.stack([z, x, y, core]).astype(jnp.int32)
-    cols = send_col.reshape(-1)
-
-    slots = []
-    for role in range(4):
-        part = layer.partial(role, place, cols, node_feats, tiles, after=slots[-1:])
-        slots.append(node_swap(part, OTHER_X))
-    every_row = jnp.stack([recv_row] + [node_swap(recv_row, along_z(d)) for d in (1, 2, 3)])
-    rows = lax.dynamic_slice(every_row, (0, 2 * z, 0), (4, 2, cap)).reshape(-1)
+    place = jnp.stack([node // 2, node % 2, feat // 2, feat % 2]).astype(jnp.int32)
     inverse = (1.0 / degree.astype(F32)).reshape(-1, TB)
-    feat_slices = over_feat(node_feats)
-    cotangents = over_feat(layer.transposed(cotangent))
-    self_part = layer.self_part(place, feat_slices, w_self, bias.reshape(1, width))
-    sums = layer.local(place, cols, rows, node_feats, tiles)
-
-    activated = None
-    weights = None
-    order = []
-    self_back, own, near = [], [], []
-    inner_got, inner_far, outer_got, outer_far = [], [], [], []
-    for k in range(CHUNKS):
-        parts = []
-        for role in range(3):
-            part = layer.joined(role, k, place, rows, sums, slots[role], after=order[-2:-1])
-            parts.append(part)
-            order.append(node_swap(part, INWARD))
-        mine = layer.joined(SELF, k, place, rows, sums, slots[SELF])
-        first, second, third = order[-3:]
-        for_outer = node_swap(parts[FAR_OUTER] + first, ACROSS)
-        for_inner = node_swap(parts[FAR_INNER] + second, ACROSS)
-        last = node_swap(parts[NEAR] + for_outer, OUTWARD)
-        means = layer.means(k, (mine, third, for_inner, last), inverse)
-        activated, grad, mine_back = layer.activate(
-            k, place, over_feat(means), w_neigh, self_part, cotangents, inverse, activated
-        )
-        own.append(mine_back)
-        near.append(node_swap(mine_back, along_z(1)))
-        inner_got.append(node_swap(mine_back, ACROSS))
-        inner_far.append(node_swap(near[k], ACROSS))
-        outer_got.append(node_swap(inner_got[k], OUTWARD))
-        outer_far.append(node_swap(inner_far[k], OUTWARD))
-        back, weights = layer.weight_grad(k, place, w_self, node_feats, means, grad, weights)
-        self_back.append(back)
-
-    weights = spread_weights(weights, x, y, core)
-    grad_self = weights[:, :slices].reshape(-1, width)
-    grad_neigh = weights[:, slices : 2 * slices].reshape(-1, width)
-    grad_bias = weights[0, 2 * slices]
-
-    sources = {
-        SELF: own, NEAR: near, FAR_INNER: inner_got + outer_got, FAR_OUTER: inner_far + outer_far,
-    }
-    returned = {}
-    for role in (SELF, NEAR, FAR_INNER, FAR_OUTER):
-        returned[role] = [node_swap(layer.picked(role, place, rows, sources[role]), OTHER_X)]
-    local = {role: (role, sources[role]) for role in sources}
-    other = {role: (role, returned[role]) for role in sources}
-    total = layer.spread(place, cols, rows, tiles, [local[SELF]], self_back=self_back)
-    total = layer.spread(place, cols, rows, tiles, [local[NEAR], other[SELF]], total)
-    total = layer.spread(place, cols, rows, tiles, [local[FAR_INNER], other[NEAR]], total)
-    total = layer.spread(place, cols, rows, tiles, [local[FAR_OUTER], other[FAR_INNER]], total)
-    total = layer.spread(place, cols, rows, tiles, [other[FAR_OUTER]], total)
-    return (activated, total, grad_self, grad_neigh, grad_bias)
+    steps = Steps(
+        layer, place, node_feats, tiles, send_col, recv_row, inverse, w_self, w_neigh, bias.reshape(1, width), cotangent
+    )
+    for name, *arguments in ORDER:
+        getattr(steps, name)(*arguments)
+    grad_self, grad_neigh, grad_bias = steps.weights
+    return (steps.activated, steps.total, grad_self, grad_neigh, grad_bias.reshape(width))
 
 
 def slot_shards(node_feats, tiles, send_col, recv_row, degree, w_self, w_neigh, bias, cotangent):

time: 294 us -> 264 us (0.90)
  waiting for transfers between devices: 138 us -> 81.4 us
  Pallas kernels: 58.9 us -> 95.8 us
  starting transfers between devices: 70.1 us -> 60.7 us
    ppermute x37, waiting for transfers between devices: 113 us -> 66 us  [node_swap(): return lax.ppermute(value, 'node', pairs)]
    pallas_call x30 -> x54, Pallas kernels: 58.9 us -> 95.8 us  [call(): pl.pallas_call(ordered, grid_spec=pltpu.PrefetchScalarGridSpec(num_scalar...]
    ppermute x37, starting transfers between devices: 63.7 us -> 52.5 us  [node_swap(): return lax.ppermute(value, 'node', pairs)]
    ppermute x14, waiting for transfers between devices: 24.9 us -> 15.5 us  [feat_swap(): return lax.ppermute(value, 'feat', pairs)]
    unnamed x46 -> x114, local copies, waits for them, and re-layouts: 19.2 us -> 21.3 us
  transfers between devices with their start and end apart: 51 -> 51, of which waited for: 22 -> 17; matrix products, arithmetic and copies ran while one was open for 2% -> 2% of each run, Pallas kernels for 18% -> 33%
where the time goes in v3:
time: 264 us; the launch traced here: 262 us
  Pallas kernels  95.8 us (36%)
  waiting for transfers between devices  81.4 us (31%)
  starting transfers between devices  60.7 us (23%)
  local copies, waits for them, and re-layouts  21.3 us (8%)
    pallas_call x54, Pallas kernels, call(): pl.pallas_call(ordered, grid_spec=pltpu.PrefetchScalarGridSpec(num_scalar...  95.8 us
    ppermute x37, waiting for transfers between devices, node_swap(): return lax.ppermute(value, 'node', pairs)  66 us
    ppermute x37, starting transfers between devices, node_swap(): return lax.ppermute(value, 'node', pairs)  52.5 us
    unnamed x114, local copies, waits for them, and re-layouts  21.3 us
    ppermute x14, waiting for transfers between devices, feat_swap(): return lax.ppermute(value, 'feat', pairs)  15.5 us
    ppermute x14, starting transfers between devices, feat_swap(): return lax.ppermute(value, 'feat', pairs)  8.2 us
  transfers between devices with their start and end apart: 51, of which 17 were waited for; matrix products, arithmetic and copies ran while one was open for 2% of the time, Pallas kernels for 33%

profile of v3, /device:TPU:0, one launch (start us, length us, event | category | flops | bytes accessed | tf_op | source)
XLA Modules:
  0.0 261.7 jit_solution(10253363949574285040)
XLA Ops:
  1.3 4.6 %shard_map.128.refs_1_ = f32[16,64,128]{2,1,0:T(8,128)} custom-call(s32[4]{0:T(128)} %pad_add_fusion.refs_0_, s32[8,16]{1,0:T(8,128)} %refs_1_.29, f32[64,4096]{1,0:T(8,128)} %refs_2_.11, f32[8,16,128,128]{3,2,1,0:T(8,128)} %refs_3_.19), custom_call_target="tpu_custom_call" | custom-call | flops 1 | bytes 1 | tf_op jit(solution)/shard_map/pallas_call | solution.py:106
  5.9 3.0 %collective-permute-start.3 = (f32[16,64,128]{2,1,0:T(8,128)}, f32[16,64,128]{2,1,0:T(8,128)S(1)}, u32[]{:S(2)}, u32[]{:S(2)}) collective-permute-start(f32[16,64,128]{2,1,0:T(8,128)} %shard_map.128.refs_1_), channel_id=1, source_target_pairs={{0,1},{1,0},{2,3},{3,2},{4,5},{5,4},{6,7},{7,6},{8,9},{9,8},{10,11... | collective-permute-start | bytes 1572872 | tf_op jit(solution)/shard_map/ppermute | solution.py:505
  9.9 1.6 shard_map.130
  13.1 1.6 collective-permute-start
  14.7 2.6 collective-permute-start.1
  17.5 1.7 collective-permute-done.1.refs_3_
  19.2 3.5 %collective-permute-done.2.refs_4_ = s32[8,16]{1,0:T(8,128)S(1)} collective-permute-done((s32[8,16]{1,0:T(8,128)S(1)}, s32[8,16]{1,0:T(8,128)S(1)}, u32[]{:S(2)}, u32[]{:S(2)}) %collective-permute-start.2) | collective-permute-done | bytes 544 | tf_op jit(solution)/shard_map/ppermute | solution.py:505
  23.8 7.4 %shard_map.132.refs_5_.refs_2_ = f32[4,32,64,128]{3,2,1,0:T(8,128)} custom-call(s32[4]{0:T(128)} %pad_add_fusion.refs_0_, s32[8,16]{1,0:T(8,128)} %refs_1_.29, s32[8,16]{1,0:T(8,128)} %copy-done.36, f32[64,4096]{1,0:T(8,128)} %refs_2_.11, f32[8,16,128,128]{3,2,1,0:T(8,128)} %refs_3_.19, s32[8,16]{1,0:T(8,128)} %copy-done.36), custom_call_target="tpu_custom_call" | custom-call | flops 1 | bytes 1 | tf_op jit(solution)/shard_map/pallas_call | solution.py:106
  32.0 4.6 %shard_map.133.refs_4_ = f32[16,64,128]{2,1,0:T(8,128)} custom-call(s32[4]{0:T(128)} %pad_add_fusion.refs_0_, s32[8,16]{1,0:T(8,128)} %refs_1_.29, f32[64,4096]{1,0:T(8,128)} %refs_2_.11, f32[8,16,128,128]{3,2,1,0:T(8,128)} %refs_3_.19, f32[16,64,128]{2,1,0:T(8,128)} %copy-done.15, f32[4,32,64,128]{3,2,1,0:T(8,128)} %shard_map.132.refs_5_.refs_2_), custom_call_target="tpu_custom_call" | custom-call | flops 1 | bytes 1 | tf_op jit(solution)/shard_map/pallas_call | solution.py:106
  41.5 6.8 %collective-permute-done.4.refs_3_.refs_4_ = f32[16,64,128]{2,1,0:T(8,128)S(1)} collective-permute-done((f32[16,64,128]{2,1,0:T(8,128)}, f32[16,64,128]{2,1,0:T(8,128)S(1)}, u32[]{:S(2)}, u32[]{:S(2)}) %collective-permute-start.4) | collective-permute-done | bytes 524320 | tf_op jit(solution)/shard_map/ppermute | solution.py:505
  49.9 4.6 %shard_map.136.refs_2_ = f32[16,64,128]{2,1,0:T(8,128)} custom-call(s32[4]{0:T(128)} %pad_add_fusion.refs_0_, s32[8,16]{1,0:T(8,128)} %refs_1_.29, f32[64,4096]{1,0:T(8,128)} %refs_2_.11, f32[8,16,128,128]{3,2,1,0:T(8,128)} %refs_3_.19, f32[16,64,128]{2,1,0:T(8,128)} %copy-done.13, f32[16,64,128]{2,1,0:T(8,128)} %copy-done.18), custom_call_target="tpu_custom_call" | custom-call | flops 1 | bytes 1 | tf_op jit(solution)/shard_map/pallas_call | solution.py:106
  61.7 1.6 shard_map.139.refs_5_.refs_0_
  63.4 1.9 collective-permute-done.5.refs_3_.refs_4_
  65.3 2.2 collective-permute-start.11
  67.5 5.0 %collective-permute-done.6.refs_4_.refs_1_ = f32[16,64,128]{2,1,0:T(8,128)S(1)} collective-permute-done((f32[16,64,128]{2,1,0:T(8,128)S(1)}, f32[16,64,128]{2,1,0:T(8,128)S(1)}, u32[]{:S(2)}, u32[]{:S(2)}) %collective-permute-start.6) | collective-permute-done | bytes 524320 | tf_op jit(solution)/shard_map/ppermute | solution.py:505
  73.0 1.6 shard_map.140.refs_2_.refs_0_
  75.5 4.6 %shard_map.142.refs_2_ = f32[16,64,128]{2,1,0:T(8,128)} custom-call(s32[4]{0:T(128)} %pad_add_fusion.refs_0_, s32[8,16]{1,0:T(8,128)} %refs_1_.29, f32[64,4096]{1,0:T(8,128)} %refs_2_.11, f32[8,16,128,128]{3,2,1,0:T(8,128)} %refs_3_.19, f32[16,64,128]{2,1,0:T(8,128)} %copy-done.11, f32[16,64,128]{2,1,0:T(8,128)} %copy-done.26), custom_call_target="tpu_custom_call" | custom-call | flops 1 | bytes 1 | tf_op jit(solution)/shard_map/pallas_call | solution.py:106
  80.1 1.6 collective-permute-start.9
  86.1 6.3 %collective-permute-start.15 = (f32[16,64,128]{2,1,0:T(8,128)}, f32[16,64,128]{2,1,0:T(8,128)S(1)}, u32[]{:S(2)}, u32[]{:S(2)}) collective-permute-start(f32[16,64,128]{2,1,0:T(8,128)} %shard_map.140.refs_2_.refs_0_), channel_id=1, source_target_pairs={{0,2},{1,3},{6,4},{7,5},{8,10},{9,11},{14,12},{15,13},{16,18},{17,... | collective-permute-start | bytes 1572872 | tf_op jit(solution)/shard_map/ppermute | solution.py:505
  92.4 7.2 %shard_map.144.refs_2_.refs_6_ = f32[2,256,2048]{2,1,0:T(8,128)S(1)} custom-call(s32[4]{0:T(128)S(1)} %copy-done.46, f32[64,4096]{1,0:T(8,128)S(1)} %copy-done.2, f32[64,4096]{1,0:T(8,128)} %shard_map.138.refs_5_.refs_2_, f32[64,4096]{1,0:T(8,128)} %collective-permute-done.12.refs_3_, f32[64,4096]{1,0:T(8,128)} %collective-permute-done.13.refs_4_, ...), custom_call_target="tpu_custom_call" | custom-call | flops 1 | bytes 1 | tf_op jit(solution)/shard_map/pallas_call | solution.py:106
  103.5 4.1 %collective-permute-start.19 = (f32[16,64,128]{2,1,0:T(8,128)S(1)}, f32[16,64,128]{2,1,0:T(8,128)S(1)}, u32[]{:S(2)}, u32[]{:S(2)}) collective-permute-start(f32[16,64,128]{2,1,0:T(8,128)S(1)} %shard_map.147.refs_5_.refs_0_), channel_id=1, source_target_pairs={{0,2},{1,3},{6,4},{7,5},{8,10},{9,11},{14,12},{15,13},{16,18},{17,... | collective-permute-start | bytes 1572872 | tf_op jit(solution)/shard_map/ppermute | solution.py:505
  107.7 1.6 collective-permute-start.23
  111.5 7.4 %collective-permute-done.19.refs_1_ = f32[16,64,128]{2,1,0:T(8,128)S(1)} collective-permute-done((f32[16,64,128]{2,1,0:T(8,128)S(1)}, f32[16,64,128]{2,1,0:T(8,128)S(1)}, u32[]{:S(2)}, u32[]{:S(2)}) %collective-permute-start.19) | collective-permute-done | bytes 524320 | tf_op jit(solution)/shard_map/ppermute | solution.py:505
  119.0 2.4 collective-permute-done.23.refs_0_
  121.4 2.1 collective-permute-start.18
  125.5 5.0 %shard_map.155 = (f32[1024,256]{1,0:T(8,128)}, f32[256,2048]{1,0:T(8,128)S(1)}, f32[16,64,128]{2,1,0:T(8,128)S(1)}) custom-call(s32[4]{0:T(128)S(1)} %copy-done.46, f32[16,64,128]{2,1,0:T(8,128)S(1)} %shard_map.148.refs_1_.refs_3_, f32[16,64,128]{2,1,0:T(8,128)S(1)} %shard_map.154.refs_2_.refs_12_, f32[16,64,128]{2,1,0:T(8,128)S(1)} %collective-permute-done.24.refs_3_, ...), custom_call_target="tpu_custom_call" | custom-call | flops 1 | bytes 1 | tf_op jit(solution)/shard_map/pallas_call | solution.py:106
  131.4 3.8 %collective-permute-done.18.refs_1_ = f32[16,64,128]{2,1,0:T(8,128)S(1)} collective-permute-done((f32[16,64,128]{2,1,0:T(8,128)S(1)}, f32[16,64,128]{2,1,0:T(8,128)S(1)}, u32[]{:S(2)}, u32[]{:S(2)}) %collective-permute-start.18) | collective-permute-done | bytes 524320 | tf_op jit(solution)/shard_map/ppermute | solution.py:505
  135.3 4.9 %collective-permute-done.22.refs_3_ = f32[16,64,128]{2,1,0:T(8,128)S(1)} collective-permute-done((f32[16,64,128]{2,1,0:T(8,128)S(1)}, f32[16,64,128]{2,1,0:T(8,128)S(1)}, u32[]{:S(2)}, u32[]{:S(2)}) %collective-permute-start.22) | collective-permute-done | bytes 524320 | tf_op jit(solution)/shard_map/ppermute | solution.py:505
  140.3 1.6 collective-permute-start.28
  141.9 11.6 %collective-permute-done.28.refs_0_ = f32[16,64,128]{2,1,0:T(8,128)S(1)} collective-permute-done((f32[16,64,128]{2,1,0:T(8,128)S(1)}, f32[16,64,128]{2,1,0:T(8,128)S(1)}, u32[]{:S(2)}, u32[]{:S(2)}) %collective-permute-start.28) | collective-permute-done | bytes 524320 | tf_op jit(solution)/shard_map/ppermute | solution.py:509
  155.5 2.0 shard_map.160
  157.5 5.0 %shard_map.161 = (f32[1024,256]{1,0:T(8,128)}, f32[256,2048]{1,0:T(8,128)S(1)}, f32[16,64,128]{2,1,0:T(8,128)S(1)}) custom-call(s32[4]{0:T(128)S(1)} %copy-done.46, f32[16,64,128]{2,1,0:T(8,128)S(1)} %shard_map.156.refs_1_.refs_3_, f32[16,64,128]{2,1,0:T(8,128)S(1)} %shard_map.158.refs_1_.refs_2_, ...), custom_call_target="tpu_custom_call", output_to_operand_aliasing={{0}: (12, {})} | custom-call | flops 1 | bytes 1 | tf_op jit(solution)/shard_map/pallas_call | solution.py:106
  163.3 4.8 %collective-permute-start.35 = (f32[16,64,128]{2,1,0:T(8,128)S(1)}, f32[16,64,128]{2,1,0:T(8,128)S(1)}, u32[]{:S(2)}, u32[]{:S(2)}) collective-permute-start(f32[16,64,128]{2,1,0:T(8,128)S(1)} %get-tuple-element.29.refs_6_.refs_3_.refs_5_), channel_id=1, source_target_pairs={{0,2},{1,3},{2,0},{3,1},{4,6},{5,7},{6,4},{7,5},{8,10},{9,11},{10,... | collective-permute-start | bytes 1572872 | tf_op jit(solution)/shard_map/ppermute | solution.py:505
  168.0 2.0 shard_map.162
  170.6 3.8 %collective-permute-done.34.refs_1_ = f32[72,256]{1,0:T(8,128)S(1)} collective-permute-done((f32[72,256]{1,0:T(8,128)S(1)}, f32[72,256]{1,0:T(8,128)S(1)}, u32[]{:S(2)}, u32[]{:S(2)}) %collective-permute-start.34) | collective-permute-done | bytes 73760 | tf_op jit(solution)/shard_map/ppermute | solution.py:505
  176.0 3.7 %collective-permute-done.36.refs_1_ = f32[72,256]{1,0:T(8,128)S(1)} collective-permute-done((f32[72,256]{1,0:T(8,128)S(1)}, f32[72,256]{1,0:T(8,128)S(1)}, u32[]{:S(2)}, u32[]{:S(2)}) %collective-permute-start.36) | collective-permute-done | bytes 73760 | tf_op jit(solution)/shard_map/ppermute | solution.py:505
  184.5 2.4 collective-permute-done.40.refs_1_
  189.8 5.0 %shard_map.171.refs_8_ = f32[64,4096]{1,0:T(8,128)} custom-call(s32[4]{0:T(128)} %pad_add_fusion.refs_0_, s32[8,16]{1,0:T(8,128)} %refs_1_.29, s32[8,16]{1,0:T(8,128)} %copy-done.36, f32[8,16,128,128]{3,2,1,0:T(8,128)} %refs_3_.19, f32[16,64,128]{2,1,0:T(8,128)} %copy-done.21, f32[16,64,128]{2,1,0:T(8,128)} %copy-done.20, f32[16,64,128]{2,1,0:T(8,128)} %copy-done.41, ...), custom_call_target="tpu_custom_call" | custom-call | flops 1 | bytes 1 | tf_op jit(solution)/shard_map/pallas_call | solution.py:106
  194.7 2.3 copy.39.refs_7_
  197.9 5.6 %shard_map.172.refs_1_.refs_9_ = f32[64,4096]{1,0:T(8,128)} custom-call(s32[4]{0:T(128)} %pad_add_fusion.refs_0_, s32[8,16]{1,0:T(8,128)} %refs_1_.29, s32[8,16]{1,0:T(8,128)} %copy-done.36, f32[8,16,128,128]{3,2,1,0:T(8,128)} %refs_3_.19, f32[16,64,128]{2,1,0:T(8,128)} %copy-done.5, f32[16,64,128]{2,1,0:T(8,128)} %copy-done.7, ...), custom_call_target="tpu_custom_call", output_to_operand_aliasing={{}: (7, {})} | custom-call | flops 1 | bytes 1 | tf_op jit(solution)/shard_map/pallas_call | solution.py:106
  208.2 13.8 %collective-permute-done.45.refs_5_.refs_7_ = f32[16,64,128]{2,1,0:T(8,128)S(1)} collective-permute-done((f32[16,64,128]{2,1,0:T(8,128)S(1)}, f32[16,64,128]{2,1,0:T(8,128)S(1)}, u32[]{:S(2)}, u32[]{:S(2)}) %collective-permute-start.45) | collective-permute-done | bytes 524320 | tf_op jit(solution)/shard_map/ppermute | solution.py:505
  224.1 5.9 %collective-permute-done.42.refs_5_.refs_7_ = f32[16,64,128]{2,1,0:T(8,128)S(1)} collective-permute-done((f32[16,64,128]{2,1,0:T(8,128)S(1)}, f32[16,64,128]{2,1,0:T(8,128)S(1)}, u32[]{:S(2)}, u32[]{:S(2)}) %collective-permute-start.42) | collective-permute-done | bytes 524320 | tf_op jit(solution)/shard_map/ppermute | solution.py:505
  234.2 2.3 collective-permute-start.50
  237.3 6.0 %shard_map.178.refs_10_ = f32[64,4096]{1,0:T(8,128)} custom-call(s32[4]{0:T(128)} %pad_add_fusion.refs_0_, s32[8,16]{1,0:T(8,128)} %refs_1_.29, s32[8,16]{1,0:T(8,128)} %copy-done.36, f32[8,16,128,128]{3,2,1,0:T(8,128)} %refs_3_.19, f32[16,64,128]{2,1,0:T(8,128)} %copy-done.6, f32[16,64,128]{2,1,0:T(8,128)} %copy-done.8, ...), custom_call_target="tpu_custom_call", output_to_operand_aliasing={{}: (9, {})} | custom-call | flops 1 | bytes 1 | tf_op jit(solution)/shard_map/pallas_call | solution.py:106
  243.3 2.3 copy.42.refs_9_
  246.3 5.9 %shard_map.179.refs_3_.refs_5_ = f32[64,4096]{1,0:T(8,128)} custom-call(s32[4]{0:T(128)} %pad_add_fusion.refs_0_, s32[8,16]{1,0:T(8,128)} %refs_1_.29, s32[8,16]{1,0:T(8,128)} %copy-done.36, f32[8,16,128,128]{3,2,1,0:T(8,128)} %refs_3_.19, f32[16,64,128]{2,1,0:T(8,128)} %copy-done.9, f32[16,64,128]{2,1,0:T(8,128)} %copy-done.10, ...), custom_call_target="tpu_custom_call", output_to_operand_aliasing={{}: (9, {})} | custom-call | flops 1 | bytes 1 | tf_op jit(solution)/shard_map/pallas_call | solution.py:106
  253.5 2.3 shard_map.180
  256.7 4.8 %shard_map.181 = f32[64,4096]{1,0:T(8,128)} custom-call(s32[4]{0:T(128)} %pad_add_fusion.refs_0_, s32[8,16]{1,0:T(8,128)} %refs_1_.29, s32[8,16]{1,0:T(8,128)} %copy-done.36, f32[8,16,128,128]{3,2,1,0:T(8,128)} %refs_3_.19, f32[16,64,128]{2,1,0:T(8,128)} %copy-done.52, f32[64,4096]{1,0:T(8,128)} %shard_map.179.refs_3_.refs_5_, ...), custom_call_target="tpu_custom_call", output_to_operand_aliasing={{}: (5, {})} | custom-call | flops 1 | bytes 1 | tf_op jit(solution)/shard_map/pallas_call | solution.py:106
  (224 shorter events, 61.4 us)
Async XLA Ops:
  5.9 25.4 %collective-permute-start.3 = (f32[16,64,128]{2,1,0:T(8,128)}, f32[16,64,128]{2,1,0:T(8,128)S(1)}, u32[]{:S(2)}, u32[]{:S(2)}) collective-permute-start(f32[16,64,128]{2,1,0:T(8,128)} %shard_map.128.refs_1_), channel_id=1, source_target_pairs={{0,1},{1,0},{2,3},{3,2},{4,5},{5,4},{6,7},{7,6},{8,9},{9,8},{10,11... | collective-permute-start | bytes 1572872 | tf_op jit(solution)/shard_map/ppermute | solution.py:505
  11.6 47.3 %collective-permute-start.8 = (f32[64,4096]{1,0:T(8,128)}, f32[64,4096]{1,0:T(8,128)}, u32[]{:S(2)}, u32[]{:S(2)}) collective-permute-start(f32[64,4096]{1,0:T(8,128)} %get-tuple-element.22), channel_id=1, source_target_pairs={{0,16},{8,24},{16,0},{24,8},{1,17},{9,25},{17,1},{25,9},{2,18},{10... | collective-permute-start | bytes 3145736 | tf_op jit(solution)/shard_map/ppermute | solution.py:509
  13.1 4.4 %collective-permute-start = (s32[8,16]{1,0:T(8,128)S(1)}, s32[8,16]{1,0:T(8,128)S(1)}, u32[]{:S(2)}, u32[]{:S(2)}) collective-permute-start(s32[8,16]{1,0:T(8,128)S(1)} %shard_map.129.refs_2_), channel_id=1, source_target_pairs={{0,2},{1,3},{2,0},{3,1},{4,6},{5,7},{6,4},{7,5},{8,10},{9,11},{10,... | collective-permute-start | bytes 1544 | tf_op jit(solution)/shard_map/ppermute | solution.py:505
  14.7 4.5 %collective-permute-start.1 = (s32[8,16]{1,0:T(8,128)S(1)}, s32[8,16]{1,0:T(8,128)S(1)}, u32[]{:S(2)}, u32[]{:S(2)}) collective-permute-start(s32[8,16]{1,0:T(8,128)S(1)} %shard_map.129.refs_2_), channel_id=1, source_target_pairs={{0,4},{1,5},{2,6},{3,7},{4,0},{5,1},{6,2},{7,3},{8,12},{9,13},{10,... | collective-permute-start | bytes 1544 | tf_op jit(solution)/shard_map/ppermute | solution.py:505
  17.3 5.4 %collective-permute-start.2 = (s32[8,16]{1,0:T(8,128)S(1)}, s32[8,16]{1,0:T(8,128)S(1)}, u32[]{:S(2)}, u32[]{:S(2)}) collective-permute-start(s32[8,16]{1,0:T(8,128)S(1)} %shard_map.129.refs_2_), channel_id=1, source_target_pairs={{0,6},{1,7},{2,4},{3,5},{4,2},{5,3},{6,0},{7,1},{8,14},{9,15},{10,... | collective-permute-start | bytes 1544 | tf_op jit(solution)/shard_map/ppermute | solution.py:505
  36.6 11.7 %collective-permute-start.4 = (f32[16,64,128]{2,1,0:T(8,128)}, f32[16,64,128]{2,1,0:T(8,128)S(1)}, u32[]{:S(2)}, u32[]{:S(2)}) collective-permute-start(f32[16,64,128]{2,1,0:T(8,128)} %shard_map.133.refs_4_), channel_id=1, source_target_pairs={{0,1},{1,0},{2,3},{3,2},{4,5},{5,4},{6,7},{7,6},{8,9},{9,8},{10,11... | collective-permute-start | bytes 1572872 | tf_op jit(solution)/shard_map/ppermute | solution.py:505
  40.1 15.0 %collective-permute-start.7 = (f32[16,64,128]{2,1,0:T(8,128)S(1)}, f32[16,64,128]{2,1,0:T(8,128)S(1)}, u32[]{:S(2)}, u32[]{:S(2)}) collective-permute-start(f32[16,64,128]{2,1,0:T(8,128)S(1)} %shard_map.134.refs_4_.refs_0_), channel_id=1, source_target_pairs={{0,2},{1,3},{6,4},{7,5},{8,10},{9,11},{14,12},{15,13},{16,18},{17,... | collective-permute-start | bytes 1572872 | tf_op jit(solution)/shard_map/ppermute | solution.py:505
  41.4 42.6 %collective-permute-start.12 = (f32[64,4096]{1,0:T(8,128)}, f32[64,4096]{1,0:T(8,128)}, u32[]{:S(2)}, u32[]{:S(2)}) collective-permute-start(f32[64,4096]{1,0:T(8,128)} %get-tuple-element.22), channel_id=1, source_target_pairs={{0,8},{8,0},{16,24},{24,16},{1,9},{9,1},{17,25},{25,17},{2,10},{10... | collective-permute-start | bytes 3145736 | tf_op jit(solution)/shard_map/ppermute | solution.py:509
  54.5 10.7 %collective-permute-start.5 = (f32[16,64,128]{2,1,0:T(8,128)}, f32[16,64,128]{2,1,0:T(8,128)S(1)}, u32[]{:S(2)}, u32[]{:S(2)}) collective-permute-start(f32[16,64,128]{2,1,0:T(8,128)} %shard_map.136.refs_2_), channel_id=1, source_target_pairs={{0,1},{1,0},{2,3},{3,2},{4,5},{5,4},{6,7},{7,6},{8,9},{9,8},{10,11... | collective-permute-start | bytes 1572872 | tf_op jit(solution)/shard_map/ppermute | solution.py:505
  58.9 27.2 %collective-permute-start.13 = (f32[64,4096]{1,0:T(8,128)}, f32[64,4096]{1,0:T(8,128)}, u32[]{:S(2)}, u32[]{:S(2)}) collective-permute-start(f32[64,4096]{1,0:T(8,128)} %shard_map.138.refs_5_.refs_2_), channel_id=1, source_target_pairs={{0,8},{8,0},{16,24},{24,16},{1,9},{9,1},{17,25},{25,17},{2,10},{10... | collective-permute-start | bytes 3145736 | tf_op jit(solution)/shard_map/ppermute | solution.py:509
  58.9 13.6 %collective-permute-start.6 = (f32[16,64,128]{2,1,0:T(8,128)S(1)}, f32[16,64,128]{2,1,0:T(8,128)S(1)}, u32[]{:S(2)}, u32[]{:S(2)}) collective-permute-start(f32[16,64,128]{2,1,0:T(8,128)S(1)} %copy-done.19), channel_id=1, source_target_pairs={{0,2},{1,3},{6,4},{7,5},{8,10},{9,11},{14,12},{15,13},{16,18},{17,... | collective-permute-start | bytes 1572872 | tf_op jit(solution)/shard_map/ppermute | solution.py:505
  60.2 19.9 %collective-permute-start.14 = (f32[16,64,128]{2,1,0:T(8,128)}, f32[16,64,128]{2,1,0:T(8,128)}, u32[]{:S(2)}, u32[]{:S(2)}) collective-permute-start(f32[16,64,128]{2,1,0:T(8,128)} %shard_map.137.refs_1_), channel_id=1, source_target_pairs={{2,4},{3,5},{4,2},{5,3},{10,12},{11,13},{12,10},{13,11},{18,20},{1... | collective-permute-start | bytes 1572872 | tf_op jit(solution)/shard_map/ppermute | solution.py:505
  65.3 20.0 %collective-permute-start.11 = (f32[16,64,128]{2,1,0:T(8,128)}, f32[16,64,128]{2,1,0:T(8,128)}, u32[]{:S(2)}, u32[]{:S(2)}) collective-permute-start(f32[16,64,128]{2,1,0:T(8,128)} %shard_map.139.refs_5_.refs_0_), channel_id=1, source_target_pairs={{0,2},{1,3},{6,4},{7,5},{8,10},{9,11},{14,12},{15,13},{16,18},{17,... | collective-permute-start | bytes 1572872 | tf_op jit(solution)/shard_map/ppermute | solution.py:505
  72.5 36.8 %collective-permute-start.10 = (f32[256,1024]{1,0:T(8,128)}, f32[256,1024]{1,0:T(8,128)S(1)}, u32[]{:S(2)}, u32[]{:S(2)}) collective-permute-start(f32[256,1024]{1,0:T(8,128)} %get-tuple-element.21.refs_5_.refs_7_), channel_id=1, source_target_pairs={{0,16},{8,24},{16,0},{24,8},{1,17},{9,25},{17,1},{25,9},{2,18},{10... | collective-permute-start | bytes 3145736 | tf_op jit(solution)/shard_map/ppermute | solution.py:509
  80.1 20.8 %collective-permute-start.9 = (f32[16,64,128]{2,1,0:T(8,128)}, f32[16,64,128]{2,1,0:T(8,128)S(1)}, u32[]{:S(2)}, u32[]{:S(2)}) collective-permute-start(f32[16,64,128]{2,1,0:T(8,128)} %shard_map.142.refs_2_), channel_id=1, source_target_pairs={{0,1},{1,0},{2,3},{3,2},{4,5},{5,4},{6,7},{7,6},{8,9},{9,8},{10,11... | collective-permute-start | bytes 1572872 | tf_op jit(solution)/shard_map/ppermute | solution.py:505
  84.0 16.9 %collective-permute-start.17 = (f32[16,64,128]{2,1,0:T(8,128)S(1)}, f32[16,64,128]{2,1,0:T(8,128)S(1)}, u32[]{:S(2)}, u32[]{:S(2)}) collective-permute-start(f32[16,64,128]{2,1,0:T(8,128)S(1)} %shard_map.143.refs_7_), channel_id=1, source_target_pairs={{2,0},{3,1},{4,6},{5,7},{10,8},{11,9},{12,14},{13,15},{18,16},{19,... | collective-permute-start | bytes 1572872 | tf_op jit(solution)/shard_map/ppermute | solution.py:505
  85.3 18.1 %collective-permute-start.16 = (f32[16,64,128]{2,1,0:T(8,128)}, f32[16,64,128]{2,1,0:T(8,128)S(1)}, u32[]{:S(2)}, u32[]{:S(2)}) collective-permute-start(f32[16,64,128]{2,1,0:T(8,128)} %copy-done.26), channel_id=1, source_target_pairs={{2,4},{3,5},{4,2},{5,3},{10,12},{11,13},{12,10},{13,11},{18,20},{1... | collective-permute-start | bytes 1572872 | tf_op jit(solution)/shard_map/ppermute | solution.py:505
  86.1 21.5 %collective-permute-start.15 = (f32[16,64,128]{2,1,0:T(8,128)}, f32[16,64,128]{2,1,0:T(8,128)S(1)}, u32[]{:S(2)}, u32[]{:S(2)}) collective-permute-start(f32[16,64,128]{2,1,0:T(8,128)} %shard_map.140.refs_2_.refs_0_), channel_id=1, source_target_pairs={{0,2},{1,3},{6,4},{7,5},{8,10},{9,11},{14,12},{15,13},{16,18},{17,... | collective-permute-start | bytes 1572872 | tf_op jit(solution)/shard_map/ppermute | solution.py:505
  100.9 22.6 %collective-permute-start.26 = (f32[256,1024]{1,0:T(8,128)}, f32[256,1024]{1,0:T(8,128)S(1)}, u32[]{:S(2)}, u32[]{:S(2)}) collective-permute-start(f32[256,1024]{1,0:T(8,128)} %get-tuple-element.21.refs_5_.refs_7_), channel_id=1, source_target_pairs={{0,8},{8,0},{16,24},{24,16},{1,9},{9,1},{17,25},{25,17},{2,10},{10... | collective-permute-start | bytes 3145736 | tf_op jit(solution)/shard_map/ppermute | solution.py:509
  101.0 8.3 %collective-permute-start.20 = (f32[16,64,128]{2,1,0:T(8,128)S(1)}, f32[16,64,128]{2,1,0:T(8,128)S(1)}, u32[]{:S(2)}, u32[]{:S(2)}) collective-permute-start(f32[16,64,128]{2,1,0:T(8,128)S(1)} %shard_map.145.refs_4_), channel_id=1, source_target_pairs={{2,4},{3,5},{4,2},{5,3},{10,12},{11,13},{12,10},{13,11},{18,20},{1... | collective-permute-start | bytes 1572872 | tf_op jit(solution)/shard_map/ppermute | solution.py:505
  103.5 15.4 %collective-permute-start.19 = (f32[16,64,128]{2,1,0:T(8,128)S(1)}, f32[16,64,128]{2,1,0:T(8,128)S(1)}, u32[]{:S(2)}, u32[]{:S(2)}) collective-permute-start(f32[16,64,128]{2,1,0:T(8,128)S(1)} %shard_map.147.refs_5_.refs_0_), channel_id=1, source_target_pairs={{0,2},{1,3},{6,4},{7,5},{8,10},{9,11},{14,12},{15,13},{16,18},{17,... | collective-permute-start | bytes 1572872 | tf_op jit(solution)/shard_map/ppermute | solution.py:505
  107.7 13.7 %collective-permute-start.23 = (f32[16,64,128]{2,1,0:T(8,128)S(1)}, f32[16,64,128]{2,1,0:T(8,128)S(1)}, u32[]{:S(2)}, u32[]{:S(2)}) collective-permute-start(f32[16,64,128]{2,1,0:T(8,128)S(1)} %shard_map.148.refs_1_.refs_3_), channel_id=1, source_target_pairs={{0,16},{8,24},{16,0},{24,8},{1,17},{9,25},{17,1},{25,9},{2,18},{10... | collective-permute-start | bytes 1572872 | tf_op jit(solution)/shard_map/ppermute | solution.py:509
  109.3 16.2 %collective-permute-start.27 = (f32[256,1024]{1,0:T(8,128)S(1)}, f32[256,1024]{1,0:T(8,128)S(1)}, u32[]{:S(2)}, u32[]{:S(2)}) collective-permute-start(f32[256,1024]{1,0:T(8,128)S(1)} %shard_map.149.refs_4_.refs_8_), channel_id=1, source_target_pairs={{0,8},{8,0},{16,24},{24,16},{1,9},{9,1},{17,25},{25,17},{2,10},{10... | collective-permute-start | bytes 3145736 | tf_op jit(solution)/shard_map/ppermute | solution.py:509
  109.3 14.9 %collective-permute-start.24 = (f32[16,64,128]{2,1,0:T(8,128)S(1)}, f32[16,64,128]{2,1,0:T(8,128)S(1)}, u32[]{:S(2)}, u32[]{:S(2)}) collective-permute-start(f32[16,64,128]{2,1,0:T(8,128)S(1)} %shard_map.148.refs_1_.refs_3_), channel_id=1, source_target_pairs={{0,8},{8,0},{16,24},{24,16},{1,9},{9,1},{17,25},{25,17},{2,10},{10... | collective-permute-start | bytes 1572872 | tf_op jit(solution)/shard_map/ppermute | solution.py:509
  121.4 13.9 %collective-permute-start.18 = (f32[16,64,128]{2,1,0:T(8,128)S(1)}, f32[16,64,128]{2,1,0:T(8,128)S(1)}, u32[]{:S(2)}, u32[]{:S(2)}) collective-permute-start(f32[16,64,128]{2,1,0:T(8,128)S(1)} %shard_map.151.refs_0_.refs_2_), channel_id=1, source_target_pairs={{0,2},{1,3},{6,4},{7,5},{8,10},{9,11},{14,12},{15,13},{16,18},{17,... | collective-permute-start | bytes 1572872 | tf_op jit(solution)/shard_map/ppermute | solution.py:505
  123.5 11.8 %collective-permute-start.21 = (f32[16,64,128]{2,1,0:T(8,128)S(1)}, f32[16,64,128]{2,1,0:T(8,128)S(1)}, u32[]{:S(2)}, u32[]{:S(2)}) collective-permute-start(f32[16,64,128]{2,1,0:T(8,128)S(1)} %shard_map.153.refs_1_), channel_id=1, source_target_pairs={{2,4},{3,5},{4,2},{5,3},{10,12},{11,13},{12,10},{13,11},{18,20},{1... | collective-permute-start | bytes 1572872 | tf_op jit(solution)/shard_map/ppermute | solution.py:505
  124.2 15.9 %collective-permute-start.22 = (f32[16,64,128]{2,1,0:T(8,128)S(1)}, f32[16,64,128]{2,1,0:T(8,128)S(1)}, u32[]{:S(2)}, u32[]{:S(2)}) collective-permute-start(f32[16,64,128]{2,1,0:T(8,128)S(1)} %shard_map.152.refs_2_), channel_id=1, source_target_pairs={{2,0},{3,1},{4,6},{5,7},{10,8},{11,9},{12,14},{13,15},{18,16},{19,... | collective-permute-start | bytes 1572872 | tf_op jit(solution)/shard_map/ppermute | solution.py:505
  130.6 11.3 %collective-permute-start.29 = (f32[16,64,128]{2,1,0:T(8,128)S(1)}, f32[16,64,128]{2,1,0:T(8,128)S(1)}, u32[]{:S(2)}, u32[]{:S(2)}) collective-permute-start(f32[16,64,128]{2,1,0:T(8,128)S(1)} %get-tuple-element.23.refs_5_.refs_2_.refs_4_), channel_id=1, source_target_pairs={{2,4},{3,5},{4,2},{5,3},{10,12},{11,13},{12,10},{13,11},{18,20},{1... | collective-permute-start | bytes 1572872 | tf_op jit(solution)/shard_map/ppermute | solution.py:505
  140.3 13.3 %collective-permute-start.28 = (f32[16,64,128]{2,1,0:T(8,128)S(1)}, f32[16,64,128]{2,1,0:T(8,128)S(1)}, u32[]{:S(2)}, u32[]{:S(2)}) collective-permute-start(f32[16,64,128]{2,1,0:T(8,128)S(1)} %shard_map.156.refs_1_.refs_3_), channel_id=1, source_target_pairs={{0,16},{8,24},{16,0},{24,8},{1,17},{9,25},{17,1},{25,9},{2,18},{10... | collective-permute-start | bytes 1572872 | tf_op jit(solution)/shard_map/ppermute | solution.py:509
  141.9 12.9 %collective-permute-start.32 = (f32[16,64,128]{2,1,0:T(8,128)S(1)}, f32[16,64,128]{2,1,0:T(8,128)S(1)}, u32[]{:S(2)}, u32[]{:S(2)}) collective-permute-start(f32[16,64,128]{2,1,0:T(8,128)S(1)} %get-tuple-element.23.refs_5_.refs_2_.refs_4_), channel_id=1, source_target_pairs={{0,2},{1,3},{2,0},{3,1},{4,6},{5,7},{6,4},{7,5},{8,10},{9,11},{10,... | collective-permute-start | bytes 1572872 | tf_op jit(solution)/shard_map/ppermute | solution.py:505
  141.9 15.7 %collective-permute-start.30 = (f32[16,64,128]{2,1,0:T(8,128)S(1)}, f32[16,64,128]{2,1,0:T(8,128)S(1)}, u32[]{:S(2)}, u32[]{:S(2)}) collective-permute-start(f32[16,64,128]{2,1,0:T(8,128)S(1)} %shard_map.156.refs_1_.refs_3_), channel_id=1, source_target_pairs={{0,8},{8,0},{16,24},{24,16},{1,9},{9,1},{17,25},{25,17},{2,10},{10... | collective-permute-start | bytes 1572872 | tf_op jit(solution)/shard_map/ppermute | solution.py:509
  154.8 19.8 %collective-permute-start.33 = (f32[16,64,128]{2,1,0:T(8,128)S(1)}, f32[16,64,128]{2,1,0:T(8,128)S(1)}, u32[]{:S(2)}, u32[]{:S(2)}) collective-permute-start(f32[16,64,128]{2,1,0:T(8,128)S(1)} %shard_map.159.refs_5_.refs_2_.refs_4_), channel_id=1, source_target_pairs={{2,4},{3,5},{4,2},{5,3},{10,12},{11,13},{12,10},{13,11},{18,20},{1... | collective-permute-start | bytes 1572872 | tf_op jit(solution)/shard_map/ppermute | solution.py:505
  162.6 13.4 %collective-permute-start.37 = (f32[16,64,128]{2,1,0:T(8,128)S(1)}, f32[16,64,128]{2,1,0:T(8,128)S(1)}, u32[]{:S(2)}, u32[]{:S(2)}) collective-permute-start(f32[16,64,128]{2,1,0:T(8,128)S(1)} %get-tuple-element.29.refs_6_.refs_3_.refs_5_), channel_id=1, source_target_pairs={{2,4},{3,5},{4,2},{5,3},{10,12},{11,13},{12,10},{13,11},{18,20},{1... | collective-permute-start | bytes 1572872 | tf_op jit(solution)/shard_map/ppermute | solution.py:505
  163.3 16.5 %collective-permute-start.35 = (f32[16,64,128]{2,1,0:T(8,128)S(1)}, f32[16,64,128]{2,1,0:T(8,128)S(1)}, u32[]{:S(2)}, u32[]{:S(2)}) collective-permute-start(f32[16,64,128]{2,1,0:T(8,128)S(1)} %get-tuple-element.29.refs_6_.refs_3_.refs_5_), channel_id=1, source_target_pairs={{0,2},{1,3},{2,0},{3,1},{4,6},{5,7},{6,4},{7,5},{8,10},{9,11},{10,... | collective-permute-start | bytes 1572872 | tf_op jit(solution)/shard_map/ppermute | solution.py:505
  170.1 4.4 %collective-permute-start.34 = (f32[72,256]{1,0:T(8,128)S(1)}, f32[72,256]{1,0:T(8,128)S(1)}, u32[]{:S(2)}, u32[]{:S(2)}) collective-permute-start(f32[72,256]{1,0:T(8,128)S(1)} %get-tuple-element.31), channel_id=1, source_target_pairs={{0,1},{1,0},{2,3},{3,2},{4,5},{5,4},{6,7},{7,6},{8,9},{9,8},{10,11... | collective-permute-start | bytes 221192 | tf_op jit(solution)/shard_map/ppermute | solution.py:505
  174.5 5.2 %collective-permute-start.36 = (f32[72,256]{1,0:T(8,128)S(1)}, f32[72,256]{1,0:T(8,128)S(1)}, u32[]{:S(2)}, u32[]{:S(2)}) collective-permute-start(f32[72,256]{1,0:T(8,128)S(1)} %shard_map.163.refs_1_.refs_0_), channel_id=1, source_target_pairs={{0,2},{1,3},{2,0},{3,1},{4,6},{5,7},{6,4},{7,5},{8,10},{9,11},{10,... | collective-permute-start | bytes 221192 | tf_op jit(solution)/shard_map/ppermute | solution.py:505
  175.4 21.6 %collective-permute-start.39 = (f32[16,64,128]{2,1,0:T(8,128)S(1)}, f32[16,64,128]{2,1,0:T(8,128)S(1)}, u32[]{:S(2)}, u32[]{:S(2)}) collective-permute-start(f32[16,64,128]{2,1,0:T(8,128)S(1)} %shard_map.165.refs_1_), channel_id=1, source_target_pairs={{0,1},{1,0},{2,3},{3,2},{4,5},{5,4},{6,7},{7,6},{8,9},{9,8},{10,11... | collective-permute-start | bytes 1572872 | tf_op jit(solution)/shard_map/ppermute | solution.py:505
  179.7 23.8 %collective-permute-start.38 = (f32[16,64,128]{2,1,0:T(8,128)S(1)}, f32[16,64,128]{2,1,0:T(8,128)S(1)}, u32[]{:S(2)}, u32[]{:S(2)}) collective-permute-start(f32[16,64,128]{2,1,0:T(8,128)S(1)} %shard_map.168.refs_2_.refs_3_.refs_5_), channel_id=1, source_target_pairs={{2,4},{3,5},{4,2},{5,3},{10,12},{11,13},{12,10},{13,11},{18,20},{1... | collective-permute-start | bytes 1572872 | tf_op jit(solution)/shard_map/ppermute | solution.py:505
  180.4 6.4 %collective-permute-start.40 = (f32[72,256]{1,0:T(8,128)S(1)}, f32[72,256]{1,0:T(8,128)S(1)}, u32[]{:S(2)}, u32[]{:S(2)}) collective-permute-start(f32[72,256]{1,0:T(8,128)S(1)} %shard_map.167.refs_1_.refs_0_), channel_id=1, source_target_pairs={{0,6},{1,7},{2,4},{3,5},{4,2},{5,3},{6,0},{7,1},{8,14},{9,15},{10,... | collective-permute-start | bytes 221192 | tf_op jit(solution)/shard_map/ppermute | solution.py:505
  181.9 24.8 %collective-permute-start.44 = (f32[16,64,128]{2,1,0:T(8,128)S(1)}, f32[16,64,128]{2,1,0:T(8,128)S(1)}, u32[]{:S(2)}, u32[]{:S(2)}) collective-permute-start(f32[16,64,128]{2,1,0:T(8,128)S(1)} %shard_map.157.refs_1_.refs_2_.refs_4_), channel_id=1, source_target_pairs={{2,0},{3,1},{4,6},{5,7},{10,8},{11,9},{12,14},{13,15},{18,16},{19,... | collective-permute-start | bytes 1572872 | tf_op jit(solution)/shard_map/ppermute | solution.py:505
  183.2 40.9 %collective-permute-start.41 = (f32[16,64,128]{2,1,0:T(8,128)S(1)}, f32[16,64,128]{2,1,0:T(8,128)S(1)}, u32[]{:S(2)}, u32[]{:S(2)}) collective-permute-start(f32[16,64,128]{2,1,0:T(8,128)S(1)} %shard_map.164.refs_4_.refs_2_), channel_id=1, source_target_pairs={{2,0},{3,1},{4,6},{5,7},{10,8},{11,9},{12,14},{13,15},{18,16},{19,... | collective-permute-start | bytes 1572872 | tf_op jit(solution)/shard_map/ppermute | solution.py:505
  186.8 35.2 %collective-permute-start.45 = (f32[16,64,128]{2,1,0:T(8,128)S(1)}, f32[16,64,128]{2,1,0:T(8,128)S(1)}, u32[]{:S(2)}, u32[]{:S(2)}) collective-permute-start(f32[16,64,128]{2,1,0:T(8,128)S(1)} %shard_map.166.refs_2_.refs_3_.refs_5_), channel_id=1, source_target_pairs={{2,0},{3,1},{4,6},{5,7},{10,8},{11,9},{12,14},{13,15},{18,16},{19,... | collective-permute-start | bytes 1572872 | tf_op jit(solution)/shard_map/ppermute | solution.py:505
  204.8 25.2 %collective-permute-start.42 = (f32[16,64,128]{2,1,0:T(8,128)S(1)}, f32[16,64,128]{2,1,0:T(8,128)S(1)}, u32[]{:S(2)}, u32[]{:S(2)}) collective-permute-start(f32[16,64,128]{2,1,0:T(8,128)S(1)} %shard_map.173.refs_6_.refs_3_.refs_5_), channel_id=1, source_target_pairs={{2,0},{3,1},{4,6},{5,7},{10,8},{11,9},{12,14},{13,15},{18,16},{19,... | collective-permute-start | bytes 1572872 | tf_op jit(solution)/shard_map/ppermute | solution.py:505
  206.1 17.5 %collective-permute-start.43 = (f32[72,256]{1,0:T(8,128)S(1)}, f32[72,256]{1,0:T(8,128)S(1)}, u32[]{:S(2)}, u32[]{:S(2)}) collective-permute-start(f32[72,256]{1,0:T(8,128)S(1)} %shard_map.169.refs_4_.refs_1_), channel_id=1, source_target_pairs={{0,1},{1,0},{2,3},{3,2},{4,5},{5,4},{6,7},{7,6},{8,9},{9,8},{10,11... | collective-permute-start | bytes 221192 | tf_op jit(solution)/shard_map/ppermute | solution.py:505
  206.7 29.8 %collective-permute-start.48 = (f32[16,64,128]{2,1,0:T(8,128)S(1)}, f32[16,64,128]{2,1,0:T(8,128)S(1)}, u32[]{:S(2)}, u32[]{:S(2)}) collective-permute-start(f32[16,64,128]{2,1,0:T(8,128)S(1)} %copy-done.33), channel_id=1, source_target_pairs={{0,1},{1,0},{2,3},{3,2},{4,5},{5,4},{6,7},{7,6},{8,9},{9,8},{10,11... | collective-permute-start | bytes 1572872 | tf_op jit(solution)/shard_map/ppermute | solution.py:505
  222.9 22.6 %collective-permute-start.47 = (f32[16,64,128]{2,1,0:T(8,128)S(1)}, f32[16,64,128]{2,1,0:T(8,128)S(1)}, u32[]{:S(2)}, u32[]{:S(2)}) collective-permute-start(f32[16,64,128]{2,1,0:T(8,128)S(1)} %shard_map.174.refs_3_), channel_id=1, source_target_pairs={{0,1},{1,0},{2,3},{3,2},{4,5},{5,4},{6,7},{7,6},{8,9},{9,8},{10,11... | collective-permute-start | bytes 1572872 | tf_op jit(solution)/shard_map/ppermute | solution.py:505
  230.9 25.0 %collective-permute-start.46 = (f32[16,64,128]{2,1,0:T(8,128)S(1)}, f32[16,64,128]{2,1,0:T(8,128)S(1)}, u32[]{:S(2)}, u32[]{:S(2)}) collective-permute-start(f32[16,64,128]{2,1,0:T(8,128)S(1)} %shard_map.176.refs_3_), channel_id=1, source_target_pairs={{0,1},{1,0},{2,3},{3,2},{4,5},{5,4},{6,7},{7,6},{8,9},{9,8},{10,11... | collective-permute-start | bytes 1572872 | tf_op jit(solution)/shard_map/ppermute | solution.py:505
  234.2 18.1 %collective-permute-start.50 = (f32[2,144,256]{2,1,0:T(8,128)}, f32[2,144,256]{2,1,0:T(8,128)S(1)}, u32[]{:S(2)}, u32[]{:S(2)}) collective-permute-start(f32[2,144,256]{2,1,0:T(8,128)} %shard_map.177.refs_10_.refs_1_), channel_id=1, source_target_pairs={{0,16},{8,24},{16,0},{24,8},{1,17},{9,25},{17,1},{25,9},{2,18},{10... | collective-permute-start | bytes 884744 | tf_op jit(solution)/shard_map/ppermute | solution.py:509
  (59 other events, 704.9 us)

commit v4 on v3

--- a/solution.py
+++ b/solution.py
@@ -11,7 +11,6 @@
 HIGH = lax.Precision.HIGH
 CHUNKS = 2
 VMEM_BYTES = 28 * 2**20
-TILE_VMEM_BYTES = 57 * 2**20
 
 FAR_OUTER, FAR_INNER, NEAR, SELF = range(4)
 
@@ -72,6 +71,7 @@
         self.piece = self.per_piece * TB
         self.span = self.per_chunk * TB
         self.token = None
+        self.pending = []
 
     def spot(self, row):
         row = jnp.maximum(row, 0)
@@ -96,9 +96,10 @@
     def dense(self):
         return jax.ShapeDtypeStruct((self.per_chunk, self.slices, TB), F32)
 
-    def call(self, body, scalars, grid, in_specs, args, out_specs, out_shape, scratch=(), aliases=None, after=(), vmem=VMEM_BYTES):
+    def call(self, body, scalars, grid, in_specs, args, out_specs, out_shape, scratch=(), aliases=None, after=()):
         given = len(scalars) + len(args)
-        waits = list(after) + ([] if self.token is None else [self.token])
+        waits = list(after) + self.pending + ([] if self.token is None else [self.token])
+        self.pending = []
 
         def ordered(*refs):
             body(*refs[:given], *refs[given + len(waits) :])
@@ -114,7 +115,7 @@
             ),
             out_shape=out_shape,
             input_output_aliases=aliases or {},
-            compiler_params=pltpu.CompilerParams(vmem_limit_bytes=vmem),
+            compiler_params=pltpu.CompilerParams(vmem_limit_bytes=VMEM_BYTES),
             cost_estimate=pl.CostEstimate(flops=1, bytes_accessed=1, transcendentals=0),
         )(*scalars, *args, *waits)
         self.token = jax.tree.leaves(out)[-1]
@@ -144,7 +145,7 @@
         return pltpu.make_async_copy(tiles.at[index], buffer.at[slot], sems.at[slot])
 
     def tiles_spec(self):
-        return pl.BlockSpec(memory_space=pltpu.HBM)
+        return pl.BlockSpec(memory_space=pl.ANY)
 
     def partial(self, role, place, cols, feats, tiles, after=()):
         def body(place, cols, feats, tiles, out, buffer, sems):
@@ -158,7 +159,7 @@
         return self.call(
             body, (place, cols), (1,),
             [self.full(self.slices, self.owned), self.tiles_spec()], (feats, tiles),
-            self.slots_spec(), self.slots(), scratch=self.fetched(1), after=after, vmem=TILE_VMEM_BYTES,
+            self.slots_spec(), self.slots(), scratch=self.fetched(1), after=after,
         )
 
     def local(self, place, cols, rows, feats, tiles):
@@ -181,7 +182,7 @@
         return self.call(
             body, (place, cols, rows), (1,),
             [self.full(self.slices, self.owned), self.tiles_spec()], (feats, tiles),
-            self.full(*shape), jax.ShapeDtypeStruct(shape, F32), scratch=self.fetched(4), vmem=TILE_VMEM_BYTES,
+            self.full(*shape), jax.ShapeDtypeStruct(shape, F32), scratch=self.fetched(4),
         )
 
     def own_rows(self, place, tables):
@@ -225,16 +226,25 @@
             self.dense_spec(), self.dense(),
         )
 
-    def turned(self, feats, cotangent):
-        def body(feats, cotangent, feats_out, cotangent_out):
-            feats_out[...] = feats[...]
+    def loaded(self, feats, tiles, cotangent):
+        def body(feats, tiles, cotangent, feats_out, tiles_out, cotangent_out, sems):
+            copies = [
+                pltpu.make_async_copy(feats, feats_out, sems.at[0]),
+                pltpu.make_async_copy(tiles, tiles_out, sems.at[1]),
+            ]
+            for copy in copies:
+                copy.start()
             cotangent_out[...] = cotangent[...].T
+            for copy in copies:
+                copy.wait()
 
         rows, cols = cotangent.shape
-        whole, turned = self.full(*feats.shape), self.full(cols, rows)
-        return self.call(
-            body, (), (1,), [whole, self.full(rows, cols)], (feats, cotangent), [whole, turned],
-            [jax.ShapeDtypeStruct(feats.shape, F32), jax.ShapeDtypeStruct((cols, rows), F32)],
+        anywhere = pl.BlockSpec(memory_space=pl.ANY)
+        return self.call(
+            body, (), (1,), [anywhere, anywhere, self.full(rows, cols)], (feats, tiles, cotangent),
+            [anywhere, anywhere, self.full(cols, rows)],
+            [pltpu.VMEM(feats.shape, F32), pltpu.VMEM(tiles.shape, F32), jax.ShapeDtypeStruct((cols, rows), F32)],
+            scratch=[pltpu.SemaphoreType.DMA((2,))],
         )
 
     def copied(self, table):
@@ -444,7 +454,8 @@
 
         def body(place, cols, rows, tiles, *rest):
             arrays, more = rest[: sum(counts)], rest[sum(counts) : sum(counts) + len(extra)]
-            out, held, buffer, sems = rest[sum(counts) + len(extra) :]
+            out, done, held, buffer, sems = rest[sum(counts) + len(extra) :]
+            done[...] = jnp.zeros_like(done)
             z, x = place[0], place[1]
             owners = [owner(role, z) * 2 + (1 - x if n == 1 else x) for (role, _), n in zip(jobs, counts)]
             copies = [self.fetch(tiles, buffer, sems, owned_by, i) for i, owned_by in enumerate(owners)]
@@ -478,11 +489,11 @@
         in_specs += [whole] if self_back is None else [self.dense_spec()] * CHUNKS
         args += extra
         return self.call(
-            body, (place, cols, rows), (1,), in_specs, args, whole,
-            jax.ShapeDtypeStruct((self.slices, self.owned), F32),
+            body, (place, cols, rows), (1,), in_specs, args, [whole, self.full(8, TB)],
+            [jax.ShapeDtypeStruct((self.slices, self.owned), F32), jax.ShapeDtypeStruct((8, TB), F32)],
             scratch=[self.held(), *self.fetched(len(jobs))],
-            aliases={3 + len(args) - 1: 0} if self_back is None else {}, vmem=TILE_VMEM_BYTES,
-        )
+            aliases={3 + len(args) - 1: 0} if self_back is None else {},
+        )[0]
 
 
 def pairs_z(steps):
@@ -510,57 +521,63 @@
 
 
 ORDER = [
+    ("load",),
     ("slots", FAR_OUTER),
     ("table_out",),
-    ("turn",),
     ("rows_in",),
     ("local",),
     ("slots", FAR_INNER),
     ("join", FAR_OUTER, 0),
     ("join", FAR_INNER, 0),
+    ("pass_on", FAR_OUTER, 0),
     ("slots", NEAR),
-    ("pass_on", FAR_OUTER, 0),
-    ("feats_on",),
     ("join", FAR_OUTER, 1),
     ("join", NEAR, 0),
-    ("pass_on", FAR_INNER, 0),
+    ("feats_on",),
     ("slots", SELF),
     ("pass_on", NEAR, 0),
-    ("self_part",),
+    ("pass_on", FAR_INNER, 0),
+    ("join", SELF, 1),
+    ("join", SELF, 0),
     ("pass_on", FAR_OUTER, 1),
-    ("join", SELF, 0),
+    ("join", NEAR, 1),
     ("join", FAR_INNER, 1),
     ("mean", 0),
     ("cotangents_on",),
-    ("join", SELF, 1),
-    ("join", NEAR, 1),
+    ("self_part",),
     ("pass_on", NEAR, 1),
     ("pass_on", FAR_INNER, 1),
     ("means_on", 0),
     ("activate", 0),
     ("mean", 1),
+    ("near_on", 0),
     ("inner_on", 0),
     ("means_on", 1),
-    ("near_on", 0),
     ("weight", 0),
     ("activate", 1),
+    ("outer_on", 0),
+    ("wait", "inner", 0, 1),
+    ("pick", SELF),
     ("weight", 1),
+    ("spread", SELF, None),
+    ("wait", "returned", SELF),
+    ("wait", "inner", 1, 0),
+    ("wait", "near", 1),
+    ("near_on", 1),
     ("weight_x",),
-    ("outer_on", 0),
-    ("pick", SELF),
     ("inner_on", 1),
+    ("pick", NEAR),
+    ("wait", "outer", 0, 1),
     ("weight_near",),
-    ("near_on", 1),
+    ("outer_on", 1),
+    ("spread", NEAR, SELF),
     ("weight_far",),
-    ("pick", NEAR),
-    ("spread", SELF, None),
-    ("spread", NEAR, SELF),
-    ("outer_on", 1),
     ("pick", FAR_INNER),
+    ("spread", FAR_INNER, NEAR),
     ("weight_halves",),
     ("pick", FAR_OUTER),
     ("weight_cores",),
-    ("spread", FAR_INNER, NEAR),
+    ("wait", "returned", FAR_INNER),
     ("spread", FAR_OUTER, FAR_INNER),
     ("weight_whole",),
     ("spread", None, FAR_OUTER),
@@ -573,10 +590,15 @@
         self.cols, self.table, self.inverse = send_col, recv_row, inverse
         self.w_self, self.w_neigh, self.bias, self.cotangent = w_self, w_neigh, bias, cotangent
         self.slots_in, self.joined, self.inward, self.returned = {}, {}, {}, {}
-        self.sent = []
         self.across, self.outward, self.means, self.mean_parts = {}, {}, {}, {}
         self.grads, self.own, self.near, self.inner, self.outer = {}, {}, {}, {}, {}
         self.self_back, self.activated, self.weights, self.total = {}, None, None, None
+
+    def wait(self, name, *key):
+        held = getattr(self, name)
+        for index in key:
+            held = held[index]
+        self.layer.pending.append(held)
 
     def slots(self, role):
         after = [self.slots_in[role - 1]] if role else []
@@ -593,9 +615,10 @@
     def local(self):
         self.sums = self.layer.local(self.place, self.cols, self.rows, self.feats, self.tiles)
 
-    def turn(self):
-        feats, cotangent = self.layer.turned(self.feats, self.cotangent)
-        self.feat_parts = [self.feats, feat_swap(feats, OTHER_Y), feat_swap(feats, OTHER_CORE)]
+    def load(self):
+        feats, self.tiles, cotangent = self.layer.loaded(self.feats, self.tiles, self.cotangent)
+        self.feats = feats
+        self.feat_parts = [feats, feat_swap(feats, OTHER_Y), feat_swap(feats, OTHER_CORE)]
         self.cotangents = [cotangent, feat_swap(cotangent, OTHER_Y), feat_swap(cotangent, OTHER_CORE)]
 
     def on(self, parts):
@@ -612,12 +635,12 @@
         self.self_parts = self.layer.self_part(self.place, self.feat_parts, self.w_self, self.bias)
 
     def join(self, role, k):
-        after = [] if role == SELF else self.sent[-2:-1]
+        early = 3 * k + role - 2
+        after = [] if role == SELF or early < 0 else [self.inward[early % 3, early // 3]]
         part = self.layer.joined(role, k, self.place, self.rows, self.sums, self.slots_in[role], after=after)
         self.joined[role, k] = part
         if role != SELF:
             self.inward[role, k] = node_swap(part, INWARD)
-            self.sent.append(self.inward[role, k])
 
     def pass_on(self, role, k):
         if role == NEAR:

time: 264 us -> 226 us (0.86)
  Pallas kernels: 95.8 us -> 57.1 us
  local copies, waits for them, and re-layouts: 21.3 us -> 6.57 us
  waiting for transfers between devices: 81.4 us -> 90.9 us
  starting transfers between devices: 60.7 us -> 69.3 us
    pallas_call x54, Pallas kernels: 95.8 us -> 57.1 us  [call(): pl.pallas_call(ordered, grid_spec=pltpu.PrefetchScalarGridSpec(num_scalar...]
    ppermute x37, waiting for transfers between devices: 66 us -> 82.2 us  [node_swap(): return lax.ppermute(value, 'node', pairs)]
    unnamed x114 -> x21, local copies, waits for them, and re-layouts: 21.3 us -> 6.57 us
    ppermute x37, starting transfers between devices: 52.5 us -> 60.8 us  [node_swap(): return lax.ppermute(value, 'node', pairs)]
    ppermute x14, waiting for transfers between devices: 15.5 us -> 8.78 us  [feat_swap(): return lax.ppermute(value, 'feat', pairs)]
  transfers between devices with their start and end apart: 51 -> 51, of which waited for: 17 -> 25; matrix products, arithmetic and copies ran while one was open for 2% -> 0% of each run, Pallas kernels for 33% -> 22%
where the time goes in v4:
time: 226 us; the launch traced here: 225 us
  waiting for transfers between devices  90.9 us (40%)
  starting transfers between devices  69.3 us (31%)
  Pallas kernels  57.1 us (25%)
  local copies, waits for them, and re-layouts  6.57 us (3%)
    ppermute x37, waiting for transfers between devices, node_swap(): return lax.ppermute(value, 'node', pairs)  82.2 us
    ppermute x37, starting transfers between devices, node_swap(): return lax.ppermute(value, 'node', pairs)  60.8 us
    pallas_call x54, Pallas kernels, call(): pl.pallas_call(ordered, grid_spec=pltpu.PrefetchScalarGridSpec(num_scalar...  57.1 us
    ppermute x14, waiting for transfers between devices, feat_swap(): return lax.ppermute(value, 'feat', pairs)  8.78 us
    ppermute x14, starting transfers between devices, feat_swap(): return lax.ppermute(value, 'feat', pairs)  8.53 us
    unnamed x21, local copies, waits for them, and re-layouts  6.57 us
  transfers between devices with their start and end apart: 51, of which 25 were waited for; matrix products, arithmetic and copies ran while one was open for 0% of the time, Pallas kernels for 22%

profile of v4, /device:TPU:0, one launch (start us, length us, event | category | flops | bytes accessed | tf_op | source)
XLA Modules:
  0.0 225.5 jit_solution(2950654043993278236)
XLA Ops:
  0.7 3.4 %copy-done = f32[8,16,128,128]{3,2,1,0:T(8,128)S(1)} copy-done((f32[8,16,128,128]{3,2,1,0:T(8,128)S(1)}, f32[8,16,128,128]{3,2,1,0:T(8,128)}, u32[]{:S(2)}) %copy-start) | copy-done | bytes 8388632
  8.7 3.0 %collective-permute-start.3 = (f32[16,64,128]{2,1,0:T(8,128)S(1)}, f32[16,64,128]{2,1,0:T(8,128)S(1)}, u32[]{:S(2)}, u32[]{:S(2)}) collective-permute-start(f32[16,64,128]{2,1,0:T(8,128)S(1)} %shard_map.129.refs_1_), channel_id=1, source_target_pairs={{0,1},{1,0},{2,3},{3,2},{4,5},{5,4},{6,7},{7,6},{8,9},{9,8},{10,11... | collective-permute-start | bytes 1572872 | tf_op jit(solution)/shard_map/ppermute | solution.py:516
  13.3 2.6 %collective-permute-start.1 = (s32[8,16]{1,0:T(8,128)S(1)}, s32[8,16]{1,0:T(8,128)S(1)}, u32[]{:S(2)}, u32[]{:S(2)}) collective-permute-start(s32[8,16]{1,0:T(8,128)S(1)} %shard_map.130.refs_5_), channel_id=1, source_target_pairs={{0,4},{1,5},{2,6},{3,7},{4,0},{5,1},{6,2},{7,3},{8,12},{9,13},{10,... | collective-permute-start | bytes 1544 | tf_op jit(solution)/shard_map/ppermute | solution.py:516
  16.1 1.7 collective-permute-done.1.refs_3_
  17.8 3.5 %collective-permute-done.2.refs_4_ = s32[8,16]{1,0:T(8,128)S(1)} collective-permute-done((s32[8,16]{1,0:T(8,128)S(1)}, s32[8,16]{1,0:T(8,128)S(1)}, u32[]{:S(2)}, u32[]{:S(2)}) %collective-permute-start.2) | collective-permute-done | bytes 544 | tf_op jit(solution)/shard_map/ppermute | solution.py:516
  21.9 3.1 %shard_map.132.refs_5_.refs_2_ = f32[4,32,64,128]{3,2,1,0:T(8,128)S(1)} custom-call(s32[4]{0:T(128)S(1)} %pad_add_fusion.refs_0_, s32[8,16]{1,0:T(8,128)S(1)} %copy-done.5, s32[8,16]{1,0:T(8,128)S(1)} %shard_map.131.refs_2_.refs_5_.refs_1_, f32[64,4096]{1,0:T(8,128)S(1)} %get-tuple-element.31.refs_2_.refs_3_.refs_1_, ...), custom_call_target="tpu_custom_call" | custom-call | flops 1 | bytes 1 | tf_op jit(solution)/shard_map/pallas_call | solution.py:107
  27.6 3.4 %collective-permute-start.5 = (f32[16,64,128]{2,1,0:T(8,128)S(1)}, f32[16,64,128]{2,1,0:T(8,128)S(1)}, u32[]{:S(2)}, u32[]{:S(2)}) collective-permute-start(f32[16,64,128]{2,1,0:T(8,128)S(1)} %shard_map.134.refs_4_.refs_0_), channel_id=1, source_target_pairs={{0,2},{1,3},{6,4},{7,5},{8,10},{9,11},{14,12},{15,13},{16,18},{17,... | collective-permute-start | bytes 1572872 | tf_op jit(solution)/shard_map/ppermute | solution.py:516
  30.9 1.6 collective-permute-start.7
  32.5 5.5 %collective-permute-done.4.refs_3_.refs_4_ = f32[16,64,128]{2,1,0:T(8,128)S(1)} collective-permute-done((f32[16,64,128]{2,1,0:T(8,128)S(1)}, f32[16,64,128]{2,1,0:T(8,128)S(1)}, u32[]{:S(2)}, u32[]{:S(2)}) %collective-permute-start.4) | collective-permute-done | bytes 524320 | tf_op jit(solution)/shard_map/ppermute | solution.py:516
  38.8 3.4 %collective-permute-start.8 = (f32[16,64,128]{2,1,0:T(8,128)S(1)}, f32[16,64,128]{2,1,0:T(8,128)S(1)}, u32[]{:S(2)}, u32[]{:S(2)}) collective-permute-start(f32[16,64,128]{2,1,0:T(8,128)S(1)} %shard_map.135.refs_2_.refs_0_), channel_id=1, source_target_pairs={{0,2},{1,3},{6,4},{7,5},{8,10},{9,11},{14,12},{15,13},{16,18},{17,... | collective-permute-start | bytes 1572872 | tf_op jit(solution)/shard_map/ppermute | solution.py:516
  43.5 1.6 collective-permute-start.6
  45.7 6.4 %collective-permute-done.8.refs_4_.refs_1_ = f32[16,64,128]{2,1,0:T(8,128)S(1)} collective-permute-done((f32[16,64,128]{2,1,0:T(8,128)S(1)}, f32[16,64,128]{2,1,0:T(8,128)S(1)}, u32[]{:S(2)}, u32[]{:S(2)}) %collective-permute-start.8) | collective-permute-done | bytes 524320 | tf_op jit(solution)/shard_map/ppermute | solution.py:516
  52.9 2.2 collective-permute-done.6.refs_3_.refs_4_
  58.6 2.1 collective-permute-start.11
  62.1 1.6 collective-permute-start.18
  63.7 4.1 %collective-permute-done.9.refs_3_ = f32[16,64,128]{2,1,0:T(8,128)S(1)} collective-permute-done((f32[16,64,128]{2,1,0:T(8,128)S(1)}, f32[16,64,128]{2,1,0:T(8,128)S(1)}, u32[]{:S(2)}, u32[]{:S(2)}) %collective-permute-start.9) | collective-permute-done | bytes 524320 | tf_op jit(solution)/shard_map/ppermute | solution.py:516
  68.0 5.1 %collective-permute-done.11.refs_1_.refs_4_ = f32[16,64,128]{2,1,0:T(8,128)S(1)} collective-permute-done((f32[16,64,128]{2,1,0:T(8,128)S(1)}, f32[16,64,128]{2,1,0:T(8,128)S(1)}, u32[]{:S(2)}, u32[]{:S(2)}) %collective-permute-start.11) | collective-permute-done | bytes 524320 | tf_op jit(solution)/shard_map/ppermute | solution.py:516
  73.8 6.1 %collective-permute-done.13.refs_4_.refs_1_ = f32[16,64,128]{2,1,0:T(8,128)S(1)} collective-permute-done((f32[16,64,128]{2,1,0:T(8,128)S(1)}, f32[16,64,128]{2,1,0:T(8,128)S(1)}, u32[]{:S(2)}, u32[]{:S(2)}) %collective-permute-start.13) | collective-permute-done | bytes 524320 | tf_op jit(solution)/shard_map/ppermute | solution.py:516
  82.9 8.4 %collective-permute-done.20.refs_3_ = f32[16,64,128]{2,1,0:T(8,128)S(1)} collective-permute-done((f32[16,64,128]{2,1,0:T(8,128)S(1)}, f32[16,64,128]{2,1,0:T(8,128)S(1)}, u32[]{:S(2)}, u32[]{:S(2)}) %collective-permute-start.20) | collective-permute-done | bytes 524320 | tf_op jit(solution)/shard_map/ppermute | solution.py:516
  93.8 4.3 %collective-permute-start.14 = (f32[16,64,128]{2,1,0:T(8,128)S(1)}, f32[16,64,128]{2,1,0:T(8,128)S(1)}, u32[]{:S(2)}, u32[]{:S(2)}) collective-permute-start(f32[16,64,128]{2,1,0:T(8,128)S(1)} %shard_map.148.refs_5_.refs_0_), channel_id=1, source_target_pairs={{0,2},{1,3},{6,4},{7,5},{8,10},{9,11},{14,12},{15,13},{16,18},{17,... | collective-permute-start | bytes 1572872 | tf_op jit(solution)/shard_map/ppermute | solution.py:516
  98.1 1.6 collective-permute-start.23
  100.2 4.9 %shard_map.151.refs_2_.refs_6_ = f32[2,256,2048]{2,1,0:T(8,128)S(1)} custom-call(s32[4]{0:T(128)S(1)} %pad_add_fusion.refs_0_, f32[64,4096]{1,0:T(8,128)S(1)} %get-tuple-element.31.refs_2_.refs_3_.refs_1_, f32[64,4096]{1,0:T(8,128)S(1)} %shard_map.140.refs_5_.refs_2_, f32[64,4096]{1,0:T(8,128)S(1)} %collective-permute-done.16.refs_3_, ...), custom_call_target="tpu_custom_call" | custom-call | flops 1 | bytes 1 | tf_op jit(solution)/shard_map/pallas_call | solution.py:107
  105.4 2.3 %collective-permute-done.23.refs_0_ = f32[16,64,128]{2,1,0:T(8,128)S(1)} collective-permute-done((f32[16,64,128]{2,1,0:T(8,128)S(1)}, f32[16,64,128]{2,1,0:T(8,128)S(1)}, u32[]{:S(2)}, u32[]{:S(2)}) %collective-permute-start.23) | collective-permute-done | bytes 524320 | tf_op jit(solution)/shard_map/ppermute | solution.py:520
  107.7 2.7 %collective-permute-start.12 = (f32[16,64,128]{2,1,0:T(8,128)S(1)}, f32[16,64,128]{2,1,0:T(8,128)S(1)}, u32[]{:S(2)}, u32[]{:S(2)}) collective-permute-start(f32[16,64,128]{2,1,0:T(8,128)S(1)} %shard_map.147.refs_5_.refs_0_), channel_id=1, source_target_pairs={{0,2},{1,3},{6,4},{7,5},{8,10},{9,11},{14,12},{15,13},{16,18},{17,... | collective-permute-start | bytes 1572872 | tf_op jit(solution)/shard_map/ppermute | solution.py:516
  112.5 4.0 %shard_map.155 = (f32[1024,256]{1,0:T(8,128)}, f32[256,2048]{1,0:T(8,128)S(1)}, f32[16,64,128]{2,1,0:T(8,128)S(1)}) custom-call(s32[4]{0:T(128)S(1)} %pad_add_fusion.refs_0_, f32[16,64,128]{2,1,0:T(8,128)S(1)} %shard_map.149.refs_1_.refs_3_, f32[16,64,128]{2,1,0:T(8,128)S(1)} %shard_map.154.refs_2_.refs_12_, ...), custom_call_target="tpu_custom_call" | custom-call | flops 1 | bytes 1 | tf_op jit(solution)/shard_map/pallas_call | solution.py:107
  116.6 2.7 %collective-permute-start.30 = (f32[16,64,128]{2,1,0:T(8,128)S(1)}, f32[16,64,128]{2,1,0:T(8,128)S(1)}, u32[]{:S(2)}, u32[]{:S(2)}) collective-permute-start(f32[16,64,128]{2,1,0:T(8,128)S(1)} %get-tuple-element.34.refs_5_.refs_2_.refs_4_), channel_id=1, source_target_pairs={{0,2},{1,3},{2,0},{3,1},{4,6},{5,7},{6,4},{7,5},{8,10},{9,11},{10,... | collective-permute-start | bytes 1572872 | tf_op jit(solution)/shard_map/ppermute | solution.py:516
  120.1 2.6 %collective-permute-done.12.refs_1_ = f32[16,64,128]{2,1,0:T(8,128)S(1)} collective-permute-done((f32[16,64,128]{2,1,0:T(8,128)S(1)}, f32[16,64,128]{2,1,0:T(8,128)S(1)}, u32[]{:S(2)}, u32[]{:S(2)}) %collective-permute-start.12) | collective-permute-done | bytes 524320 | tf_op jit(solution)/shard_map/ppermute | solution.py:516
  122.7 5.2 %collective-permute-done.22.refs_3_ = f32[16,64,128]{2,1,0:T(8,128)S(1)} collective-permute-done((f32[16,64,128]{2,1,0:T(8,128)S(1)}, f32[16,64,128]{2,1,0:T(8,128)S(1)}, u32[]{:S(2)}, u32[]{:S(2)}) %collective-permute-start.22) | collective-permute-done | bytes 524320 | tf_op jit(solution)/shard_map/ppermute | solution.py:516
  128.1 1.6 collective-permute-start.28
  129.6 8.2 %collective-permute-done.30.refs_0_ = f32[16,64,128]{2,1,0:T(8,128)S(1)} collective-permute-done((f32[16,64,128]{2,1,0:T(8,128)S(1)}, f32[16,64,128]{2,1,0:T(8,128)S(1)}, u32[]{:S(2)}, u32[]{:S(2)}) %collective-permute-start.30) | collective-permute-done | bytes 524320 | tf_op jit(solution)/shard_map/ppermute | solution.py:516
  137.9 1.7 collective-permute-done.28.refs_0_
  141.6 2.1 shard_map.160
  143.6 4.0 %shard_map.161 = (f32[1024,256]{1,0:T(8,128)}, f32[256,2048]{1,0:T(8,128)S(1)}, f32[16,64,128]{2,1,0:T(8,128)S(1)}) custom-call(s32[4]{0:T(128)S(1)} %pad_add_fusion.refs_0_, f32[16,64,128]{2,1,0:T(8,128)S(1)} %shard_map.156.refs_1_.refs_3_, f32[16,64,128]{2,1,0:T(8,128)S(1)} %shard_map.159.refs_5_.refs_2_, ...), custom_call_target="tpu_custom_call", output_to_operand_aliasing={{0}: (12, {})} | custom-call | flops 1 | bytes 1 | tf_op jit(solution)/shard_map/pallas_call | solution.py:107
  147.7 2.7 %collective-permute-start.34 = (f32[16,64,128]{2,1,0:T(8,128)S(1)}, f32[16,64,128]{2,1,0:T(8,128)S(1)}, u32[]{:S(2)}, u32[]{:S(2)}) collective-permute-start(f32[16,64,128]{2,1,0:T(8,128)S(1)} %get-tuple-element.39.refs_1_.refs_3_.refs_5_), channel_id=1, source_target_pairs={{0,2},{1,3},{2,0},{3,1},{4,6},{5,7},{6,4},{7,5},{8,10},{9,11},{10,... | collective-permute-start | bytes 1572872 | tf_op jit(solution)/shard_map/ppermute | solution.py:516
  150.4 6.5 %collective-permute-done.35.refs_4_.refs_6_ = f32[16,64,128]{2,1,0:T(8,128)S(1)} collective-permute-done((f32[16,64,128]{2,1,0:T(8,128)S(1)}, f32[16,64,128]{2,1,0:T(8,128)S(1)}, u32[]{:S(2)}, u32[]{:S(2)}) %collective-permute-start.35) | collective-permute-done | bytes 524320 | tf_op jit(solution)/shard_map/ppermute | solution.py:516
  161.2 2.1 shard_map.164
  163.3 2.3 %shard_map.165 = (f32[64,4096]{1,0:T(8,128)}, f32[8,128]{1,0:T(8,128)S(1)}) custom-call(s32[4]{0:T(128)S(1)} %pad_add_fusion.refs_0_, s32[8,16]{1,0:T(8,128)S(1)} %copy-done.5, s32[8,16]{1,0:T(8,128)S(1)} %shard_map.131.refs_2_.refs_5_.refs_1_, f32[8,16,128,128]{3,2,1,0:T(8,128)S(1)} %get-tuple-element.32.refs_3_.refs_4_, ...), custom_call_target="tpu_custom_call" | custom-call | flops 1 | bytes 1 | tf_op jit(solution)/shard_map/pallas_call | solution.py:107
  165.6 2.5 %collective-permute-done.34.refs_3_ = f32[16,64,128]{2,1,0:T(8,128)S(1)} collective-permute-done((f32[16,64,128]{2,1,0:T(8,128)S(1)}, f32[16,64,128]{2,1,0:T(8,128)S(1)}, u32[]{:S(2)}, u32[]{:S(2)}) %collective-permute-start.34) | collective-permute-done | bytes 524320 | tf_op jit(solution)/shard_map/ppermute | solution.py:516
  168.2 2.8 %collective-permute-done.36.refs_1_.refs_6_ = f32[16,64,128]{2,1,0:T(8,128)S(1)} collective-permute-done((f32[16,64,128]{2,1,0:T(8,128)S(1)}, f32[16,64,128]{2,1,0:T(8,128)S(1)}, u32[]{:S(2)}, u32[]{:S(2)}) %collective-permute-start.36) | collective-permute-done | bytes 524320 | tf_op jit(solution)/shard_map/ppermute | solution.py:516
  173.2 2.9 %collective-permute-done.39.refs_1_ = f32[72,256]{1,0:T(8,128)S(1)} collective-permute-done((f32[72,256]{1,0:T(8,128)S(1)}, f32[72,256]{1,0:T(8,128)S(1)}, u32[]{:S(2)}, u32[]{:S(2)}) %collective-permute-start.39) | collective-permute-done | bytes 73760 | tf_op jit(solution)/shard_map/ppermute | solution.py:516
  176.0 5.5 %collective-permute-start.40 = (f32[72,256]{1,0:T(8,128)S(1)}, f32[72,256]{1,0:T(8,128)S(1)}, u32[]{:S(2)}, u32[]{:S(2)}) collective-permute-start(f32[72,256]{1,0:T(8,128)S(1)} %shard_map.167.refs_1_.refs_0_), channel_id=1, source_target_pairs={{0,2},{1,3},{2,0},{3,1},{4,6},{5,7},{6,4},{7,5},{8,10},{9,11},{10,... | collective-permute-start | bytes 221192 | tf_op jit(solution)/shard_map/ppermute | solution.py:516
  187.3 4.1 %shard_map.172 = (f32[64,4096]{1,0:T(8,128)}, f32[8,128]{1,0:T(8,128)S(1)}) custom-call(s32[4]{0:T(128)S(1)} %pad_add_fusion.refs_0_, s32[8,16]{1,0:T(8,128)S(1)} %copy-done.5, s32[8,16]{1,0:T(8,128)S(1)} %shard_map.131.refs_2_.refs_5_.refs_1_, f32[8,16,128,128]{3,2,1,0:T(8,128)S(1)} %get-tuple-element.32.refs_3_.refs_4_, ...), custom_call_target="tpu_custom_call", output_to_operand_aliasing={{0}: (7, {})} | custom-call | flops 1 | bytes 1 | tf_op jit(solution)/shard_map/pallas_call | solution.py:107
  193.5 5.7 %collective-permute-done.45.refs_5_.refs_7_ = f32[16,64,128]{2,1,0:T(8,128)S(1)} collective-permute-done((f32[16,64,128]{2,1,0:T(8,128)S(1)}, f32[16,64,128]{2,1,0:T(8,128)S(1)}, u32[]{:S(2)}, u32[]{:S(2)}) %collective-permute-start.45) | collective-permute-done | bytes 524320 | tf_op jit(solution)/shard_map/ppermute | solution.py:516
  201.3 4.1 %shard_map.175 = (f32[64,4096]{1,0:T(8,128)}, f32[8,128]{1,0:T(8,128)S(1)}) custom-call(s32[4]{0:T(128)S(1)} %pad_add_fusion.refs_0_, s32[8,16]{1,0:T(8,128)S(1)} %copy-done.5, s32[8,16]{1,0:T(8,128)S(1)} %shard_map.131.refs_2_.refs_5_.refs_1_, f32[8,16,128,128]{3,2,1,0:T(8,128)S(1)} %get-tuple-element.32.refs_3_.refs_4_, ...), custom_call_target="tpu_custom_call", output_to_operand_aliasing={{0}: (9, {})} | custom-call | flops 1 | bytes 1 | tf_op jit(solution)/shard_map/pallas_call | solution.py:107
  210.7 1.6 collective-permute-start.50
  212.3 4.1 %shard_map.179 = (f32[64,4096]{1,0:T(8,128)}, f32[8,128]{1,0:T(8,128)S(1)}) custom-call(s32[4]{0:T(128)S(1)} %pad_add_fusion.refs_0_, s32[8,16]{1,0:T(8,128)S(1)} %copy-done.5, s32[8,16]{1,0:T(8,128)S(1)} %shard_map.131.refs_2_.refs_5_.refs_1_, f32[8,16,128,128]{3,2,1,0:T(8,128)S(1)} %get-tuple-element.32.refs_3_.refs_4_, ...), custom_call_target="tpu_custom_call", output_to_operand_aliasing={{0}: (9, {})} | custom-call | flops 1 | bytes 1 | tf_op jit(solution)/shard_map/pallas_call | solution.py:107
  216.3 3.5 %collective-permute-done.50.refs_2_ = f32[2,144,256]{2,1,0:T(8,128)S(1)} collective-permute-done((f32[2,144,256]{2,1,0:T(8,128)S(1)}, f32[2,144,256]{2,1,0:T(8,128)S(1)}, u32[]{:S(2)}, u32[]{:S(2)}) %collective-permute-start.50) | collective-permute-done | bytes 294944 | tf_op jit(solution)/shard_map/ppermute | solution.py:520
  221.9 3.5 %shard_map.181 = (f32[64,4096]{1,0:T(8,128)}, f32[8,128]{1,0:T(8,128)}) custom-call(s32[4]{0:T(128)S(1)} %pad_add_fusion.refs_0_, s32[8,16]{1,0:T(8,128)S(1)} %copy-done.5, s32[8,16]{1,0:T(8,128)S(1)} %shard_map.131.refs_2_.refs_5_.refs_1_, f32[8,16,128,128]{3,2,1,0:T(8,128)S(1)} %get-tuple-element.32.refs_3_.refs_4_, ...), custom_call_target="tpu_custom_call", output_to_operand_aliasing={{0}: (5, {})} | custom-call | flops 1 | bytes 1 | tf_op jit(solution)/shard_map/pallas_call | solution.py:107
  (131 shorter events, 53.8 us)
Async XLA Ops:
  8.7 16.3 %collective-permute-start.3 = (f32[16,64,128]{2,1,0:T(8,128)S(1)}, f32[16,64,128]{2,1,0:T(8,128)S(1)}, u32[]{:S(2)}, u32[]{:S(2)}) collective-permute-start(f32[16,64,128]{2,1,0:T(8,128)S(1)} %shard_map.129.refs_1_), channel_id=1, source_target_pairs={{0,1},{1,0},{2,3},{3,2},{4,5},{5,4},{6,7},{7,6},{8,9},{9,8},{10,11... | collective-permute-start | bytes 1572872 | tf_op jit(solution)/shard_map/ppermute | solution.py:516
  13.3 4.5 %collective-permute-start.1 = (s32[8,16]{1,0:T(8,128)S(1)}, s32[8,16]{1,0:T(8,128)S(1)}, u32[]{:S(2)}, u32[]{:S(2)}) collective-permute-start(s32[8,16]{1,0:T(8,128)S(1)} %shard_map.130.refs_5_), channel_id=1, source_target_pairs={{0,4},{1,5},{2,6},{3,7},{4,0},{5,1},{6,2},{7,3},{8,12},{9,13},{10,... | collective-permute-start | bytes 1544 | tf_op jit(solution)/shard_map/ppermute | solution.py:516
  15.9 5.4 %collective-permute-start.2 = (s32[8,16]{1,0:T(8,128)S(1)}, s32[8,16]{1,0:T(8,128)S(1)}, u32[]{:S(2)}, u32[]{:S(2)}) collective-permute-start(s32[8,16]{1,0:T(8,128)S(1)} %shard_map.130.refs_5_), channel_id=1, source_target_pairs={{0,6},{1,7},{2,4},{3,5},{4,2},{5,3},{6,0},{7,1},{8,14},{9,15},{10,... | collective-permute-start | bytes 1544 | tf_op jit(solution)/shard_map/ppermute | solution.py:516
  26.1 11.8 %collective-permute-start.4 = (f32[16,64,128]{2,1,0:T(8,128)S(1)}, f32[16,64,128]{2,1,0:T(8,128)S(1)}, u32[]{:S(2)}, u32[]{:S(2)}) collective-permute-start(f32[16,64,128]{2,1,0:T(8,128)S(1)} %shard_map.133.refs_4_), channel_id=1, source_target_pairs={{0,1},{1,0},{2,3},{3,2},{4,5},{5,4},{6,7},{7,6},{8,9},{9,8},{10,11... | collective-permute-start | bytes 1572872 | tf_op jit(solution)/shard_map/ppermute | solution.py:516
  27.6 14.7 %collective-permute-start.5 = (f32[16,64,128]{2,1,0:T(8,128)S(1)}, f32[16,64,128]{2,1,0:T(8,128)S(1)}, u32[]{:S(2)}, u32[]{:S(2)}) collective-permute-start(f32[16,64,128]{2,1,0:T(8,128)S(1)} %shard_map.134.refs_4_.refs_0_), channel_id=1, source_target_pairs={{0,2},{1,3},{6,4},{7,5},{8,10},{9,11},{14,12},{15,13},{16,18},{17,... | collective-permute-start | bytes 1572872 | tf_op jit(solution)/shard_map/ppermute | solution.py:516
  30.9 25.0 %collective-permute-start.7 = (f32[64,4096]{1,0:T(8,128)S(1)}, f32[64,4096]{1,0:T(8,128)S(1)}, u32[]{:S(2)}, u32[]{:S(2)}) collective-permute-start(f32[64,4096]{1,0:T(8,128)S(1)} %get-tuple-element.31.refs_2_.refs_3_.refs_1_), channel_id=1, source_target_pairs={{0,16},{8,24},{16,0},{24,8},{1,17},{9,25},{17,1},{25,9},{2,18},{10... | collective-permute-start | bytes 3145736 | tf_op jit(solution)/shard_map/ppermute | solution.py:520
  38.8 13.4 %collective-permute-start.8 = (f32[16,64,128]{2,1,0:T(8,128)S(1)}, f32[16,64,128]{2,1,0:T(8,128)S(1)}, u32[]{:S(2)}, u32[]{:S(2)}) collective-permute-start(f32[16,64,128]{2,1,0:T(8,128)S(1)} %shard_map.135.refs_2_.refs_0_), channel_id=1, source_target_pairs={{0,2},{1,3},{6,4},{7,5},{8,10},{9,11},{14,12},{15,13},{16,18},{17,... | collective-permute-start | bytes 1572872 | tf_op jit(solution)/shard_map/ppermute | solution.py:516
  43.5 11.7 %collective-permute-start.6 = (f32[16,64,128]{2,1,0:T(8,128)S(1)}, f32[16,64,128]{2,1,0:T(8,128)S(1)}, u32[]{:S(2)}, u32[]{:S(2)}) collective-permute-start(f32[16,64,128]{2,1,0:T(8,128)S(1)} %shard_map.137.refs_5_), channel_id=1, source_target_pairs={{0,1},{1,0},{2,3},{3,2},{4,5},{5,4},{6,7},{7,6},{8,9},{9,8},{10,11... | collective-permute-start | bytes 1572872 | tf_op jit(solution)/shard_map/ppermute | solution.py:516
  45.0 18.6 %collective-permute-start.10 = (f32[16,64,128]{2,1,0:T(8,128)S(1)}, f32[16,64,128]{2,1,0:T(8,128)S(1)}, u32[]{:S(2)}, u32[]{:S(2)}) collective-permute-start(f32[16,64,128]{2,1,0:T(8,128)S(1)} %shard_map.136.refs_5_), channel_id=1, source_target_pairs={{2,4},{3,5},{4,2},{5,3},{10,12},{11,13},{12,10},{13,11},{18,20},{1... | collective-permute-start | bytes 1572872 | tf_op jit(solution)/shard_map/ppermute | solution.py:516
  57.1 10.7 %collective-permute-start.9 = (f32[16,64,128]{2,1,0:T(8,128)S(1)}, f32[16,64,128]{2,1,0:T(8,128)S(1)}, u32[]{:S(2)}, u32[]{:S(2)}) collective-permute-start(f32[16,64,128]{2,1,0:T(8,128)S(1)} %shard_map.141.refs_2_), channel_id=1, source_target_pairs={{0,1},{1,0},{2,3},{3,2},{4,5},{5,4},{6,7},{7,6},{8,9},{9,8},{10,11... | collective-permute-start | bytes 1572872 | tf_op jit(solution)/shard_map/ppermute | solution.py:516
  58.6 14.4 %collective-permute-start.11 = (f32[16,64,128]{2,1,0:T(8,128)S(1)}, f32[16,64,128]{2,1,0:T(8,128)S(1)}, u32[]{:S(2)}, u32[]{:S(2)}) collective-permute-start(f32[16,64,128]{2,1,0:T(8,128)S(1)} %shard_map.138.refs_5_.refs_0_), channel_id=1, source_target_pairs={{0,2},{1,3},{6,4},{7,5},{8,10},{9,11},{14,12},{15,13},{16,18},{17,... | collective-permute-start | bytes 1572872 | tf_op jit(solution)/shard_map/ppermute | solution.py:516
  60.8 19.1 %collective-permute-start.13 = (f32[16,64,128]{2,1,0:T(8,128)S(1)}, f32[16,64,128]{2,1,0:T(8,128)S(1)}, u32[]{:S(2)}, u32[]{:S(2)}) collective-permute-start(f32[16,64,128]{2,1,0:T(8,128)S(1)} %shard_map.139.refs_1_.refs_0_), channel_id=1, source_target_pairs={{0,2},{1,3},{6,4},{7,5},{8,10},{9,11},{14,12},{15,13},{16,18},{17,... | collective-permute-start | bytes 1572872 | tf_op jit(solution)/shard_map/ppermute | solution.py:516
  62.1 31.7 %collective-permute-start.18 = (f32[256,1024]{1,0:T(8,128)S(1)}, f32[256,1024]{1,0:T(8,128)S(1)}, u32[]{:S(2)}, u32[]{:S(2)}) collective-permute-start(f32[256,1024]{1,0:T(8,128)S(1)} %get-tuple-element.33.refs_4_.refs_7_), channel_id=1, source_target_pairs={{0,16},{8,24},{16,0},{24,8},{1,17},{9,25},{17,1},{25,9},{2,18},{10... | collective-permute-start | bytes 3145736 | tf_op jit(solution)/shard_map/ppermute | solution.py:520
  63.7 34.4 %collective-permute-start.16 = (f32[64,4096]{1,0:T(8,128)S(1)}, f32[64,4096]{1,0:T(8,128)S(1)}, u32[]{:S(2)}, u32[]{:S(2)}) collective-permute-start(f32[64,4096]{1,0:T(8,128)S(1)} %get-tuple-element.31.refs_2_.refs_3_.refs_1_), channel_id=1, source_target_pairs={{0,8},{8,0},{16,24},{24,16},{1,9},{9,1},{17,25},{25,17},{2,10},{10... | collective-permute-start | bytes 3145736 | tf_op jit(solution)/shard_map/ppermute | solution.py:520
  67.8 31.9 %collective-permute-start.17 = (f32[64,4096]{1,0:T(8,128)S(1)}, f32[64,4096]{1,0:T(8,128)S(1)}, u32[]{:S(2)}, u32[]{:S(2)}) collective-permute-start(f32[64,4096]{1,0:T(8,128)S(1)} %shard_map.140.refs_5_.refs_2_), channel_id=1, source_target_pairs={{0,8},{8,0},{16,24},{24,16},{1,9},{9,1},{17,25},{25,17},{2,10},{10... | collective-permute-start | bytes 3145736 | tf_op jit(solution)/shard_map/ppermute | solution.py:520
  73.1 9.7 %collective-permute-start.19 = (f32[16,64,128]{2,1,0:T(8,128)S(1)}, f32[16,64,128]{2,1,0:T(8,128)S(1)}, u32[]{:S(2)}, u32[]{:S(2)}) collective-permute-start(f32[16,64,128]{2,1,0:T(8,128)S(1)} %shard_map.143.refs_4_), channel_id=1, source_target_pairs={{2,4},{3,5},{4,2},{5,3},{10,12},{11,13},{12,10},{13,11},{18,20},{1... | collective-permute-start | bytes 1572872 | tf_op jit(solution)/shard_map/ppermute | solution.py:516
  79.8 11.5 %collective-permute-start.20 = (f32[16,64,128]{2,1,0:T(8,128)S(1)}, f32[16,64,128]{2,1,0:T(8,128)S(1)}, u32[]{:S(2)}, u32[]{:S(2)}) collective-permute-start(f32[16,64,128]{2,1,0:T(8,128)S(1)} %shard_map.142.refs_2_), channel_id=1, source_target_pairs={{2,0},{3,1},{4,6},{5,7},{10,8},{11,9},{12,14},{13,15},{18,16},{19,... | collective-permute-start | bytes 1572872 | tf_op jit(solution)/shard_map/ppermute | solution.py:516
  82.8 27.6 %collective-permute-start.26 = (f32[256,1024]{1,0:T(8,128)S(1)}, f32[256,1024]{1,0:T(8,128)S(1)}, u32[]{:S(2)}, u32[]{:S(2)}) collective-permute-start(f32[256,1024]{1,0:T(8,128)S(1)} %get-tuple-element.33.refs_4_.refs_7_), channel_id=1, source_target_pairs={{0,8},{8,0},{16,24},{24,16},{1,9},{9,1},{17,25},{25,17},{2,10},{10... | collective-permute-start | bytes 3145736 | tf_op jit(solution)/shard_map/ppermute | solution.py:520
  91.3 8.4 %collective-permute-start.15 = (f32[16,64,128]{2,1,0:T(8,128)S(1)}, f32[16,64,128]{2,1,0:T(8,128)S(1)}, u32[]{:S(2)}, u32[]{:S(2)}) collective-permute-start(f32[16,64,128]{2,1,0:T(8,128)S(1)} %shard_map.146.refs_5_), channel_id=1, source_target_pairs={{2,4},{3,5},{4,2},{5,3},{10,12},{11,13},{12,10},{13,11},{18,20},{1... | collective-permute-start | bytes 1572872 | tf_op jit(solution)/shard_map/ppermute | solution.py:516
  93.8 11.6 %collective-permute-start.14 = (f32[16,64,128]{2,1,0:T(8,128)S(1)}, f32[16,64,128]{2,1,0:T(8,128)S(1)}, u32[]{:S(2)}, u32[]{:S(2)}) collective-permute-start(f32[16,64,128]{2,1,0:T(8,128)S(1)} %shard_map.148.refs_5_.refs_0_), channel_id=1, source_target_pairs={{0,2},{1,3},{6,4},{7,5},{8,10},{9,11},{14,12},{15,13},{16,18},{17,... | collective-permute-start | bytes 1572872 | tf_op jit(solution)/shard_map/ppermute | solution.py:516
  98.1 9.6 %collective-permute-start.23 = (f32[16,64,128]{2,1,0:T(8,128)S(1)}, f32[16,64,128]{2,1,0:T(8,128)S(1)}, u32[]{:S(2)}, u32[]{:S(2)}) collective-permute-start(f32[16,64,128]{2,1,0:T(8,128)S(1)} %shard_map.149.refs_1_.refs_3_), channel_id=1, source_target_pairs={{0,16},{8,24},{16,0},{24,8},{1,17},{9,25},{17,1},{25,9},{2,18},{10... | collective-permute-start | bytes 1572872 | tf_op jit(solution)/shard_map/ppermute | solution.py:520
  99.7 12.8 %collective-permute-start.27 = (f32[256,1024]{1,0:T(8,128)S(1)}, f32[256,1024]{1,0:T(8,128)S(1)}, u32[]{:S(2)}, u32[]{:S(2)}) collective-permute-start(f32[256,1024]{1,0:T(8,128)S(1)} %shard_map.150.refs_7_.refs_8_), channel_id=1, source_target_pairs={{0,8},{8,0},{16,24},{24,16},{1,9},{9,1},{17,25},{25,17},{2,10},{10... | collective-permute-start | bytes 3145736 | tf_op jit(solution)/shard_map/ppermute | solution.py:520
  99.7 11.5 %collective-permute-start.24 = (f32[16,64,128]{2,1,0:T(8,128)S(1)}, f32[16,64,128]{2,1,0:T(8,128)S(1)}, u32[]{:S(2)}, u32[]{:S(2)}) collective-permute-start(f32[16,64,128]{2,1,0:T(8,128)S(1)} %shard_map.149.refs_1_.refs_3_), channel_id=1, source_target_pairs={{0,8},{8,0},{16,24},{24,16},{1,9},{9,1},{17,25},{25,17},{2,10},{10... | collective-permute-start | bytes 1572872 | tf_op jit(solution)/shard_map/ppermute | solution.py:520
  107.7 4.8 %collective-permute-start.25 = (f32[16,64,128]{2,1,0:T(8,128)S(1)}, f32[16,64,128]{2,1,0:T(8,128)S(1)}, u32[]{:S(2)}, u32[]{:S(2)}) collective-permute-start(f32[16,64,128]{2,1,0:T(8,128)S(1)} %shard_map.154.refs_2_.refs_12_), channel_id=1, source_target_pairs={{0,8},{8,0},{16,24},{24,16},{1,9},{9,1},{17,25},{25,17},{2,10},{10... | collective-permute-start | bytes 1572872 | tf_op jit(solution)/shard_map/ppermute | solution.py:520
  107.7 15.0 %collective-permute-start.12 = (f32[16,64,128]{2,1,0:T(8,128)S(1)}, f32[16,64,128]{2,1,0:T(8,128)S(1)}, u32[]{:S(2)}, u32[]{:S(2)}) collective-permute-start(f32[16,64,128]{2,1,0:T(8,128)S(1)} %shard_map.147.refs_5_.refs_0_), channel_id=1, source_target_pairs={{0,2},{1,3},{6,4},{7,5},{8,10},{9,11},{14,12},{15,13},{16,18},{17,... | collective-permute-start | bytes 1572872 | tf_op jit(solution)/shard_map/ppermute | solution.py:516
  110.5 12.2 %collective-permute-start.21 = (f32[16,64,128]{2,1,0:T(8,128)S(1)}, f32[16,64,128]{2,1,0:T(8,128)S(1)}, u32[]{:S(2)}, u32[]{:S(2)}) collective-permute-start(f32[16,64,128]{2,1,0:T(8,128)S(1)} %shard_map.153.refs_1_), channel_id=1, source_target_pairs={{2,4},{3,5},{4,2},{5,3},{10,12},{11,13},{12,10},{13,11},{18,20},{1... | collective-permute-start | bytes 1572872 | tf_op jit(solution)/shard_map/ppermute | solution.py:516
  111.2 16.7 %collective-permute-start.22 = (f32[16,64,128]{2,1,0:T(8,128)S(1)}, f32[16,64,128]{2,1,0:T(8,128)S(1)}, u32[]{:S(2)}, u32[]{:S(2)}) collective-permute-start(f32[16,64,128]{2,1,0:T(8,128)S(1)} %shard_map.152.refs_2_), channel_id=1, source_target_pairs={{2,0},{3,1},{4,6},{5,7},{10,8},{11,9},{12,14},{13,15},{18,16},{19,... | collective-permute-start | bytes 1572872 | tf_op jit(solution)/shard_map/ppermute | solution.py:516
  116.6 21.3 %collective-permute-start.30 = (f32[16,64,128]{2,1,0:T(8,128)S(1)}, f32[16,64,128]{2,1,0:T(8,128)S(1)}, u32[]{:S(2)}, u32[]{:S(2)}) collective-permute-start(f32[16,64,128]{2,1,0:T(8,128)S(1)} %get-tuple-element.34.refs_5_.refs_2_.refs_4_), channel_id=1, source_target_pairs={{0,2},{1,3},{2,0},{3,1},{4,6},{5,7},{6,4},{7,5},{8,10},{9,11},{10,... | collective-permute-start | bytes 1572872 | tf_op jit(solution)/shard_map/ppermute | solution.py:516
  119.2 18.7 %collective-permute-start.29 = (f32[16,64,128]{2,1,0:T(8,128)S(1)}, f32[16,64,128]{2,1,0:T(8,128)S(1)}, u32[]{:S(2)}, u32[]{:S(2)}) collective-permute-start(f32[16,64,128]{2,1,0:T(8,128)S(1)} %get-tuple-element.34.refs_5_.refs_2_.refs_4_), channel_id=1, source_target_pairs={{2,4},{3,5},{4,2},{5,3},{10,12},{11,13},{12,10},{13,11},{18,20},{1... | collective-permute-start | bytes 1572872 | tf_op jit(solution)/shard_map/ppermute | solution.py:516
  128.1 11.5 %collective-permute-start.28 = (f32[16,64,128]{2,1,0:T(8,128)S(1)}, f32[16,64,128]{2,1,0:T(8,128)S(1)}, u32[]{:S(2)}, u32[]{:S(2)}) collective-permute-start(f32[16,64,128]{2,1,0:T(8,128)S(1)} %shard_map.156.refs_1_.refs_3_), channel_id=1, source_target_pairs={{0,16},{8,24},{16,0},{24,8},{1,17},{9,25},{17,1},{25,9},{2,18},{10... | collective-permute-start | bytes 1572872 | tf_op jit(solution)/shard_map/ppermute | solution.py:520
  129.6 14.0 %collective-permute-start.31 = (f32[16,64,128]{2,1,0:T(8,128)S(1)}, f32[16,64,128]{2,1,0:T(8,128)S(1)}, u32[]{:S(2)}, u32[]{:S(2)}) collective-permute-start(f32[16,64,128]{2,1,0:T(8,128)S(1)} %shard_map.156.refs_1_.refs_3_), channel_id=1, source_target_pairs={{0,8},{8,0},{16,24},{24,16},{1,9},{9,1},{17,25},{25,17},{2,10},{10... | collective-permute-start | bytes 1572872 | tf_op jit(solution)/shard_map/ppermute | solution.py:520
  139.6 10.8 %collective-permute-start.33 = (f32[16,64,128]{2,1,0:T(8,128)S(1)}, f32[16,64,128]{2,1,0:T(8,128)S(1)}, u32[]{:S(2)}, u32[]{:S(2)}) collective-permute-start(f32[16,64,128]{2,1,0:T(8,128)S(1)} %shard_map.157.refs_1_.refs_2_.refs_4_), channel_id=1, source_target_pairs={{2,4},{3,5},{4,2},{5,3},{10,12},{11,13},{12,10},{13,11},{18,20},{1... | collective-permute-start | bytes 1572872 | tf_op jit(solution)/shard_map/ppermute | solution.py:516
  140.3 16.6 %collective-permute-start.35 = (f32[16,64,128]{2,1,0:T(8,128)S(1)}, f32[16,64,128]{2,1,0:T(8,128)S(1)}, u32[]{:S(2)}, u32[]{:S(2)}) collective-permute-start(f32[16,64,128]{2,1,0:T(8,128)S(1)} %shard_map.158.refs_1_.refs_2_.refs_4_), channel_id=1, source_target_pairs={{2,0},{3,1},{4,6},{5,7},{10,8},{11,9},{12,14},{13,15},{18,16},{19,... | collective-permute-start | bytes 1572872 | tf_op jit(solution)/shard_map/ppermute | solution.py:516
  147.7 20.4 %collective-permute-start.34 = (f32[16,64,128]{2,1,0:T(8,128)S(1)}, f32[16,64,128]{2,1,0:T(8,128)S(1)}, u32[]{:S(2)}, u32[]{:S(2)}) collective-permute-start(f32[16,64,128]{2,1,0:T(8,128)S(1)} %get-tuple-element.39.refs_1_.refs_3_.refs_5_), channel_id=1, source_target_pairs={{0,2},{1,3},{2,0},{3,1},{4,6},{5,7},{6,4},{7,5},{8,10},{9,11},{10,... | collective-permute-start | bytes 1572872 | tf_op jit(solution)/shard_map/ppermute | solution.py:516
  157.7 13.2 %collective-permute-start.36 = (f32[16,64,128]{2,1,0:T(8,128)S(1)}, f32[16,64,128]{2,1,0:T(8,128)S(1)}, u32[]{:S(2)}, u32[]{:S(2)}) collective-permute-start(f32[16,64,128]{2,1,0:T(8,128)S(1)} %shard_map.163.refs_6_), channel_id=1, source_target_pairs={{0,1},{1,0},{2,3},{3,2},{4,5},{5,4},{6,7},{7,6},{8,9},{9,8},{10,11... | collective-permute-start | bytes 1572872 | tf_op jit(solution)/shard_map/ppermute | solution.py:516
  159.2 11.7 %collective-permute-start.37 = (f32[16,64,128]{2,1,0:T(8,128)S(1)}, f32[16,64,128]{2,1,0:T(8,128)S(1)}, u32[]{:S(2)}, u32[]{:S(2)}) collective-permute-start(f32[16,64,128]{2,1,0:T(8,128)S(1)} %get-tuple-element.39.refs_1_.refs_3_.refs_5_), channel_id=1, source_target_pairs={{2,4},{3,5},{4,2},{5,3},{10,12},{11,13},{12,10},{13,11},{18,20},{1... | collective-permute-start | bytes 1572872 | tf_op jit(solution)/shard_map/ppermute | solution.py:516
  159.9 24.3 %collective-permute-start.41 = (f32[16,64,128]{2,1,0:T(8,128)S(1)}, f32[16,64,128]{2,1,0:T(8,128)S(1)}, u32[]{:S(2)}, u32[]{:S(2)}) collective-permute-start(f32[16,64,128]{2,1,0:T(8,128)S(1)} %shard_map.162.refs_5_.refs_2_.refs_4_), channel_id=1, source_target_pairs={{2,0},{3,1},{4,6},{5,7},{10,8},{11,9},{12,14},{13,15},{18,16},{19,... | collective-permute-start | bytes 1572872 | tf_op jit(solution)/shard_map/ppermute | solution.py:516
  170.9 13.7 %collective-permute-start.38 = (f32[16,64,128]{2,1,0:T(8,128)S(1)}, f32[16,64,128]{2,1,0:T(8,128)S(1)}, u32[]{:S(2)}, u32[]{:S(2)}) collective-permute-start(f32[16,64,128]{2,1,0:T(8,128)S(1)} %shard_map.166.refs_2_.refs_3_.refs_5_), channel_id=1, source_target_pairs={{2,4},{3,5},{4,2},{5,3},{10,12},{11,13},{12,10},{13,11},{18,20},{1... | collective-permute-start | bytes 1572872 | tf_op jit(solution)/shard_map/ppermute | solution.py:516
  171.6 4.4 %collective-permute-start.39 = (f32[72,256]{1,0:T(8,128)S(1)}, f32[72,256]{1,0:T(8,128)S(1)}, u32[]{:S(2)}, u32[]{:S(2)}) collective-permute-start(f32[72,256]{1,0:T(8,128)S(1)} %get-tuple-element.45), channel_id=1, source_target_pairs={{0,1},{1,0},{2,3},{3,2},{4,5},{5,4},{6,7},{7,6},{8,9},{9,8},{10,11... | collective-permute-start | bytes 221192 | tf_op jit(solution)/shard_map/ppermute | solution.py:516
  176.0 8.6 %collective-permute-start.40 = (f32[72,256]{1,0:T(8,128)S(1)}, f32[72,256]{1,0:T(8,128)S(1)}, u32[]{:S(2)}, u32[]{:S(2)}) collective-permute-start(f32[72,256]{1,0:T(8,128)S(1)} %shard_map.167.refs_1_.refs_0_), channel_id=1, source_target_pairs={{0,2},{1,3},{2,0},{3,1},{4,6},{5,7},{6,4},{7,5},{8,10},{9,11},{10,... | collective-permute-start | bytes 221192 | tf_op jit(solution)/shard_map/ppermute | solution.py:516
  181.5 17.7 %collective-permute-start.45 = (f32[16,64,128]{2,1,0:T(8,128)S(1)}, f32[16,64,128]{2,1,0:T(8,128)S(1)}, u32[]{:S(2)}, u32[]{:S(2)}) collective-permute-start(f32[16,64,128]{2,1,0:T(8,128)S(1)} %shard_map.168.refs_4_.refs_3_.refs_5_), channel_id=1, source_target_pairs={{2,0},{3,1},{4,6},{5,7},{10,8},{11,9},{12,14},{13,15},{18,16},{19,... | collective-permute-start | bytes 1572872 | tf_op jit(solution)/shard_map/ppermute | solution.py:516
  183.6 17.7 %collective-permute-start.46 = (f32[16,64,128]{2,1,0:T(8,128)S(1)}, f32[16,64,128]{2,1,0:T(8,128)S(1)}, u32[]{:S(2)}, u32[]{:S(2)}) collective-permute-start(f32[16,64,128]{2,1,0:T(8,128)S(1)} %shard_map.169.refs_3_), channel_id=1, source_target_pairs={{0,1},{1,0},{2,3},{3,2},{4,5},{5,4},{6,7},{7,6},{8,9},{9,8},{10,11... | collective-permute-start | bytes 1572872 | tf_op jit(solution)/shard_map/ppermute | solution.py:516
  184.6 22.7 %collective-permute-start.42 = (f32[16,64,128]{2,1,0:T(8,128)S(1)}, f32[16,64,128]{2,1,0:T(8,128)S(1)}, u32[]{:S(2)}, u32[]{:S(2)}) collective-permute-start(f32[16,64,128]{2,1,0:T(8,128)S(1)} %shard_map.171.refs_8_.refs_3_.refs_5_), channel_id=1, source_target_pairs={{2,0},{3,1},{4,6},{5,7},{10,8},{11,9},{12,14},{13,15},{18,16},{19,... | collective-permute-start | bytes 1572872 | tf_op jit(solution)/shard_map/ppermute | solution.py:516
  185.9 6.3 %collective-permute-start.43 = (f32[72,256]{1,0:T(8,128)S(1)}, f32[72,256]{1,0:T(8,128)S(1)}, u32[]{:S(2)}, u32[]{:S(2)}) collective-permute-start(f32[72,256]{1,0:T(8,128)S(1)} %shard_map.170.refs_1_.refs_0_), channel_id=1, source_target_pairs={{0,6},{1,7},{2,4},{3,5},{4,2},{5,3},{6,0},{7,1},{8,14},{9,15},{10,... | collective-permute-start | bytes 221192 | tf_op jit(solution)/shard_map/ppermute | solution.py:516
  192.3 13.1 %collective-permute-start.44 = (f32[72,256]{1,0:T(8,128)S(1)}, f32[72,256]{1,0:T(8,128)S(1)}, u32[]{:S(2)}, u32[]{:S(2)}) collective-permute-start(f32[72,256]{1,0:T(8,128)S(1)} %shard_map.173.refs_6_.refs_1_), channel_id=1, source_target_pairs={{0,1},{1,0},{2,3},{3,2},{4,5},{5,4},{6,7},{7,6},{8,9},{9,8},{10,11... | collective-permute-start | bytes 221192 | tf_op jit(solution)/shard_map/ppermute | solution.py:516
  200.1 12.2 %collective-permute-start.48 = (f32[16,64,128]{2,1,0:T(8,128)S(1)}, f32[16,64,128]{2,1,0:T(8,128)S(1)}, u32[]{:S(2)}, u32[]{:S(2)}) collective-permute-start(f32[16,64,128]{2,1,0:T(8,128)S(1)} %shard_map.174.refs_10_), channel_id=1, source_target_pairs={{0,1},{1,0},{2,3},{3,2},{4,5},{5,4},{6,7},{7,6},{8,9},{9,8},{10,11... | collective-permute-start | bytes 1572872 | tf_op jit(solution)/shard_map/ppermute | solution.py:516
  208.1 13.0 %collective-permute-start.47 = (f32[16,64,128]{2,1,0:T(8,128)S(1)}, f32[16,64,128]{2,1,0:T(8,128)S(1)}, u32[]{:S(2)}, u32[]{:S(2)}) collective-permute-start(f32[16,64,128]{2,1,0:T(8,128)S(1)} %shard_map.177.refs_3_), channel_id=1, source_target_pairs={{0,1},{1,0},{2,3},{3,2},{4,5},{5,4},{6,7},{7,6},{8,9},{9,8},{10,11... | collective-permute-start | bytes 1572872 | tf_op jit(solution)/shard_map/ppermute | solution.py:516
  210.7 9.1 %collective-permute-start.50 = (f32[2,144,256]{2,1,0:T(8,128)S(1)}, f32[2,144,256]{2,1,0:T(8,128)S(1)}, u32[]{:S(2)}, u32[]{:S(2)}) collective-permute-start(f32[2,144,256]{2,1,0:T(8,128)S(1)} %shard_map.178.refs_11_.refs_1_), channel_id=1, source_target_pairs={{0,16},{8,24},{16,0},{24,8},{1,17},{9,25},{17,1},{25,9},{2,18},{10... | collective-permute-start | bytes 884744 | tf_op jit(solution)/shard_map/ppermute | solution.py:520
  (13 other events, 52.2 us)

commit v5 on v4

--- a/solution.py
+++ b/solution.py
@@ -11,6 +11,7 @@
 HIGH = lax.Precision.HIGH
 CHUNKS = 2
 VMEM_BYTES = 28 * 2**20
+FIRST_VMEM_BYTES = 57 * 2**20
 
 FAR_OUTER, FAR_INNER, NEAR, SELF = range(4)
 
@@ -96,7 +97,7 @@
     def dense(self):
         return jax.ShapeDtypeStruct((self.per_chunk, self.slices, TB), F32)
 
-    def call(self, body, scalars, grid, in_specs, args, out_specs, out_shape, scratch=(), aliases=None, after=()):
+    def call(self, body, scalars, grid, in_specs, args, out_specs, out_shape, scratch=(), aliases=None, after=(), vmem=VMEM_BYTES):
         given = len(scalars) + len(args)
         waits = list(after) + self.pending + ([] if self.token is None else [self.token])
         self.pending = []
@@ -115,20 +116,20 @@
             ),
             out_shape=out_shape,
             input_output_aliases=aliases or {},
-            compiler_params=pltpu.CompilerParams(vmem_limit_bytes=VMEM_BYTES),
+            compiler_params=pltpu.CompilerParams(vmem_limit_bytes=vmem),
             cost_estimate=pl.CostEstimate(flops=1, bytes_accessed=1, transcendentals=0),
         )(*scalars, *args, *waits)
         self.token = jax.tree.leaves(out)[-1]
         return out
 
-    def relay(self, value):
+    def relay(self, value, after=()):
         def body(value, out):
             pass
 
         anywhere = pl.BlockSpec(memory_space=pl.ANY)
         return self.call(
             body, (), (1,), [anywhere], (value,), anywhere, jax.ShapeDtypeStruct(value.shape, value.dtype),
-            aliases={0: 0},
+            aliases={0: 0}, after=after,
         )
 
     def added(self, a, b):
@@ -147,82 +148,119 @@
     def tiles_spec(self):
         return pl.BlockSpec(memory_space=pl.ANY)
 
-    def partial(self, role, place, cols, feats, tiles, after=()):
-        def body(place, cols, feats, tiles, out, buffer, sems):
+    def first_slots(self, role, place, cols, feats, tiles):
+        groups = 4
+        per_group = self.cap // groups
+
+        def body(place, cols, feats, tiles, out, held, buffer, sems):
             owned_by = owner(role, place[0]) * 2 + 1 - place[1]
+            copies = [pltpu.make_async_copy(feats, held, sems.at[groups])]
+            for g in range(groups):
+                some = pl.ds(g * per_group, per_group)
+                copies.append(pltpu.make_async_copy(tiles.at[owned_by, some], buffer.at[some], sems.at[g]))
+            for copy in copies:
+                copy.start()
+            for g in range(groups):
+                if g == 0:
+                    copies[0].wait()
+                copies[1 + g].wait()
+                for c in range(g * per_group, (g + 1) * per_group):
+                    out[c] = times_tile_t(held[:, lanes(cols[owned_by, c])], buffer[c])
+
+        return self.call(
+            body, (place, cols), (1,), [self.tiles_spec()] * 2, (feats, tiles), self.slots_spec(), self.slots(),
+            scratch=[
+                pltpu.VMEM((self.slices, self.owned), F32),
+                pltpu.VMEM((self.cap, TB, TB), F32),
+                pltpu.SemaphoreType.DMA((groups + 1,)),
+            ],
+            vmem=FIRST_VMEM_BYTES,
+        )
+
+    def later_slots(self, roles, place, cols, feats, tiles):
+        def body(place, cols, feats, tiles, *rest):
+            outs, (buffer, sems) = rest[: len(roles)], rest[len(roles) :]
+            owners = [owner(role, place[0]) * 2 + 1 - place[1] for role in roles]
+            copies = [self.fetch(tiles, buffer, sems, owned_by, i) for i, owned_by in enumerate(owners)]
+            for copy in copies:
+                copy.start()
+            for i, owned_by in enumerate(owners):
+                copies[i].wait()
+                for c in range(self.cap):
+                    outs[i][c] = times_tile_t(feats[:, lanes(cols[owned_by, c])], buffer[i, c])
+
+        return self.call(
+            body, (place, cols), (1,), [self.full(self.slices, self.owned), self.tiles_spec()], (feats, tiles),
+            [self.slots_spec()] * len(roles), [self.slots()] * len(roles), scratch=self.fetched(len(roles)),
+        )
+
+    def dense_sums(self, role, place, cols, rows, feats, tiles, slots):
+        def body(place, cols, rows, feats, tiles, slots, *rest):
+            outs, (buffer, sems) = rest[:CHUNKS], rest[CHUNKS:]
+            z, x = place[0], place[1]
+            owned_by = owner(role, z) * 2 + x
             copy = self.fetch(tiles, buffer, sems, owned_by, 0)
             copy.start()
+            for out in outs:
+                out[...] = jnp.zeros_like(out)
+
+            def add(row, value):
+                chunk, spot = self.spot(row)
+                for k, out in enumerate(outs):
+                    out[spot] += jnp.where((row >= 0) & (chunk == k), value, 0.0)
+
+            for c in range(self.cap):
+                add(rows[self.row_index(role, z, 1 - x), c], slots[c])
             copy.wait()
             for c in range(self.cap):
-                out[c] = times_tile_t(feats[:, lanes(cols[owned_by, c])], buffer[0, c])
-
-        return self.call(
-            body, (place, cols), (1,),
-            [self.full(self.slices, self.owned), self.tiles_spec()], (feats, tiles),
-            self.slots_spec(), self.slots(), scratch=self.fetched(1), after=after,
-        )
-
-    def local(self, place, cols, rows, feats, tiles):
-        def body(place, cols, rows, feats, tiles, out, buffer, sems):
-            z, x = place[0], place[1]
-            copies = [self.fetch(tiles, buffer, sems, owner(role, z) * 2 + x, role) for role in range(4)]
-            for copy in copies:
-                copy.start()
-            for role in range(4):
-                out[role] = jnp.zeros(out.shape[1:], F32)
-                copies[role].wait()
-                owned_by, row_of = owner(role, z) * 2 + x, self.row_index(role, z, x)
-                for c in range(self.cap):
-                    row = rows[row_of, c]
-                    chunk, spot = self.spot(row)
-                    value = times_tile_t(feats[:, lanes(cols[owned_by, c])], buffer[role, c])
-                    out[role, chunk * self.per_chunk + spot] += jnp.where(row >= 0, value, 0.0)
-
-        shape = (4, self.blocks, self.slices, TB)
+                value = times_tile_t(feats[:, lanes(cols[owned_by, c])], buffer[0, c])
+                add(rows[self.row_index(role, z, x), c], value)
+
         return self.call(
             body, (place, cols, rows), (1,),
-            [self.full(self.slices, self.owned), self.tiles_spec()], (feats, tiles),
-            self.full(*shape), jax.ShapeDtypeStruct(shape, F32), scratch=self.fetched(4),
-        )
-
-    def own_rows(self, place, tables):
-        def body(place, *refs):
-            for distance, table in enumerate(refs[:4]):
-                refs[4][2 * distance : 2 * distance + 2, :] = table[pl.ds(2 * place[0], 2), :]
-
-        spec = self.full(*tables[0].shape)
-        return self.call(
-            body, (place,), (1,), [spec] * 4, tables, spec, jax.ShapeDtypeStruct(tables[0].shape, jnp.int32)
+            [self.full(self.slices, self.owned), self.tiles_spec(), self.slots_spec()], (feats, tiles, slots),
+            [self.dense_spec()] * CHUNKS, [self.dense()] * CHUNKS, scratch=self.fetched(1),
+        )
+
+    def stacked_tables(self, first, second):
+        def body(first, second, out):
+            out[: first.shape[0], :] = first[...]
+            out[first.shape[0] :, :] = second[...]
+
+        shape = (2 * first.shape[0], first.shape[1])
+        return self.call(
+            body, (), (1,), [self.full(*first.shape)] * 2, (first, second), self.full(*shape),
+            jax.ShapeDtypeStruct(shape, first.dtype),
+        )
+
+    def own_rows(self, place, pair, other_pair):
+        half = pair.shape[0] // 2
+
+        def body(place, pair, other, out):
+            for distance in range(4):
+                table = (pair, other)[distance // 2]
+                start = half * (distance % 2) + 2 * place[0]
+                out[2 * distance : 2 * distance + 2, :] = table[pl.ds(start, 2), :]
+
+        shape = (half, pair.shape[1])
+        return self.call(
+            body, (place,), (1,), [self.full(*pair.shape)] * 2, (pair, other_pair), self.full(*shape),
+            jax.ShapeDtypeStruct(shape, pair.dtype),
         )
 
     def row_index(self, role, z, sender_x):
         return (owner(role, z) ^ z) * 2 + sender_x
 
-    def joined(self, role, k, place, rows, sums, slots, after=()):
-        def body(place, rows, sums, slots, out):
-            out[...] = sums[0]
-            row_of = self.row_index(role, place[0], 1 - place[1])
-            for c in range(self.cap):
-                row = rows[row_of, c]
-                chunk, spot = self.spot(row)
-                out[spot] += jnp.where((row >= 0) & (chunk == k), slots[c], 0.0)
-
-        return self.call(
-            body, (place, rows), (1,),
-            [pl.BlockSpec((1, self.per_chunk, self.slices, TB), lambda *_: (role, k, 0, 0)), self.slots_spec()],
-            (sums, slots), self.dense_spec(), self.dense(), after=after,
-        )
-
     def means(self, k, pieces, inverse):
-        def body(own, near, inner, outer, inverse, out):
+        def body(own, near, inner, inverse, out):
             for part in range(self.parts):
                 for j in range(self.per_piece):
                     spot, block = part * self.per_piece + j, self.block(k, part, j)
-                    total = own[spot] + near[spot] + inner[spot] + outer[spot]
+                    total = own[spot] + near[spot] + inner[spot]
                     out[spot] = total * inverse[block : block + 1, :]
 
         return self.call(
-            body, (), (1,), [self.dense_spec()] * 4 + [self.full(self.blocks, TB)], (*pieces, inverse),
+            body, (), (1,), [self.dense_spec()] * 3 + [self.full(self.blocks, TB)], (*pieces, inverse),
             self.dense_spec(), self.dense(),
         )
 
@@ -329,13 +367,11 @@
         )
 
     def weight_grad(self, k, place, w_self, feats, means, grad, before):
-        last = k == CHUNKS - 1
-        rows_all = 2 * self.slices + 16
-        shapes = [(rows_all // 2, self.width)] * 2 if last else [(rows_all, self.width)]
+        shape = (2 * self.slices + 16, self.width)
 
         def body(place, w_self, feats, means, grad, *rest):
-            total = rest[0][...] if before is not None else jnp.zeros((rows_all, self.width), F32)
-            self_out, outs = rest[before is not None], rest[1 + (before is not None) :]
+            self_out, weights_out = rest[-2:]
+            total = rest[0][...] if before is not None else jnp.zeros(shape, F32)
             for part in range(self.parts):
                 first = part * self.per_piece
                 at = slice(part * self.piece, (part + 1) * self.piece)
@@ -354,35 +390,15 @@
                 )
                 rows_high, rows_low = split(rows)
                 total += (dot_nt(rows_high, high) + dot_nt(rows_low, high)) + dot_nt(rows_high, low)
-            if last:
-                x0 = place[1] == 0
-                lower, upper = total[: rows_all // 2], total[rows_all // 2 :]
-                outs[0][...] = jnp.where(x0, upper, lower)
-                outs[1][...] = jnp.where(x0, lower, upper)
-            else:
-                outs[0][...] = total
+            weights_out[...] = total
 
         weight_rows = pl.BlockSpec((self.slices, self.width), lambda i, place, *_: (2 * place[2] + place[3], 0))
         args = [w_self, feats, means, grad] + ([] if before is None else [before])
         return self.call(
             body, (place,), (1,),
             [weight_rows, self.full(self.slices, self.owned), self.dense_spec(), self.full(self.width, self.span)]
-            + [self.full(rows_all, self.width)] * (before is not None),
-            args, [self.dense_spec()] + [self.full(*shape) for shape in shapes],
-            [self.dense()] + [jax.ShapeDtypeStruct(shape, F32) for shape in shapes],
-        )
-
-    def both_halves(self, place, mine, other):
-        half = mine.shape[0]
-
-        def body(place, mine, other, out):
-            out[pl.ds(pl.multiple_of(place[1] * half, 8), half), :] = mine[...]
-            out[pl.ds(pl.multiple_of((1 - place[1]) * half, 8), half), :] = other[...]
-
-        shape = (2 * half, self.width)
-        return self.call(
-            body, (place,), (1,), [self.full(*mine.shape)] * 2, (mine, other), self.full(*shape),
-            jax.ShapeDtypeStruct(shape, F32),
+            + [self.full(*shape)] * (before is not None),
+            args, [self.dense_spec(), self.full(*shape)], [self.dense(), jax.ShapeDtypeStruct(shape, F32)],
         )
 
     def both_cores(self, place, mine, other):
@@ -521,62 +537,57 @@
 
 
 ORDER = [
+    ("slots_first",),
+    ("table_out",),
     ("load",),
-    ("slots", FAR_OUTER),
-    ("table_out",),
+    ("tables_out",),
+    ("slots_later",),
     ("rows_in",),
-    ("local",),
+    ("dense", FAR_OUTER),
     ("slots", FAR_INNER),
-    ("join", FAR_OUTER, 0),
-    ("join", FAR_INNER, 0),
+    ("send_in", FAR_OUTER, 1),
     ("pass_on", FAR_OUTER, 0),
+    ("dense", FAR_INNER),
     ("slots", NEAR),
-    ("join", FAR_OUTER, 1),
-    ("join", NEAR, 0),
+    ("send_in", FAR_INNER, 1),
+    ("pass_on", FAR_OUTER, 1),
+    ("slots", SELF),
+    ("dense", NEAR),
+    ("pass_on", FAR_INNER, 0),
     ("feats_on",),
-    ("slots", SELF),
     ("pass_on", NEAR, 0),
-    ("pass_on", FAR_INNER, 0),
-    ("join", SELF, 1),
-    ("join", SELF, 0),
-    ("pass_on", FAR_OUTER, 1),
-    ("join", NEAR, 1),
-    ("join", FAR_INNER, 1),
+    ("pass_on", NEAR, 1),
+    ("pass_on", FAR_INNER, 1),
+    ("dense", SELF),
     ("mean", 0),
     ("cotangents_on",),
     ("self_part",),
-    ("pass_on", NEAR, 1),
-    ("pass_on", FAR_INNER, 1),
     ("means_on", 0),
+    ("mean", 1),
     ("activate", 0),
-    ("mean", 1),
-    ("near_on", 0),
-    ("inner_on", 0),
     ("means_on", 1),
     ("weight", 0),
     ("activate", 1),
+    ("weight", 1),
+    ("near_on", 0),
+    ("inner_on", 0),
+    ("weight_sum", along_z(1)),
+    ("near_on", 1),
+    ("pick", SELF),
+    ("wait", "inner", 0, 1),
+    ("inner_on", 1),
+    ("spread", SELF, None),
+    ("pick", NEAR),
+    ("weight_sum", along_z(3)),
     ("outer_on", 0),
-    ("wait", "inner", 0, 1),
-    ("pick", SELF),
-    ("weight", 1),
-    ("spread", SELF, None),
-    ("wait", "returned", SELF),
-    ("wait", "inner", 1, 0),
-    ("wait", "near", 1),
-    ("near_on", 1),
-    ("weight_x",),
-    ("inner_on", 1),
-    ("pick", NEAR),
+    ("spread", NEAR, SELF),
+    ("pick", FAR_INNER),
+    ("weight_sum", None),
+    ("outer_on", 1),
     ("wait", "outer", 0, 1),
-    ("weight_near",),
-    ("outer_on", 1),
-    ("spread", NEAR, SELF),
-    ("weight_far",),
-    ("pick", FAR_INNER),
+    ("weight_cores",),
     ("spread", FAR_INNER, NEAR),
-    ("weight_halves",),
     ("pick", FAR_OUTER),
-    ("weight_cores",),
     ("wait", "returned", FAR_INNER),
     ("spread", FAR_OUTER, FAR_INNER),
     ("weight_whole",),
@@ -590,7 +601,7 @@
         self.cols, self.table, self.inverse = send_col, recv_row, inverse
         self.w_self, self.w_neigh, self.bias, self.cotangent = w_self, w_neigh, bias, cotangent
         self.slots_in, self.joined, self.inward, self.returned = {}, {}, {}, {}
-        self.across, self.outward, self.means, self.mean_parts = {}, {}, {}, {}
+        self.across, self.nearby, self.means, self.mean_parts = {}, {}, {}, {}
         self.grads, self.own, self.near, self.inner, self.outer = {}, {}, {}, {}, {}
         self.self_back, self.activated, self.weights, self.total = {}, None, None, None
 
@@ -600,20 +611,27 @@
             held = held[index]
         self.layer.pending.append(held)
 
+    def slots_first(self):
+        part = self.layer.first_slots(FAR_OUTER, self.place, self.cols, self.feats, self.tiles)
+        self.slots_in[FAR_OUTER] = node_swap(part, OTHER_X)
+
+    def slots_later(self):
+        self.parts = self.layer.later_slots((FAR_INNER, NEAR, SELF), self.place, self.cols, self.feats, self.tiles)
+
     def slots(self, role):
-        after = [self.slots_in[role - 1]] if role else []
-        part = self.layer.partial(role, self.place, self.cols, self.feats, self.tiles, after=after)
+        part = self.layer.relay(self.parts[role - 1], after=[self.slots_in[role - 1]])
         self.slots_in[role] = node_swap(part, OTHER_X)
 
     def table_out(self):
-        table = self.layer.copied(self.table)
-        self.tables = [self.table] + [node_swap(table, along_z(distance)) for distance in (1, 2, 3)]
+        self.table = self.layer.copied(self.table)
+        self.table_in = node_swap(self.table, along_z(1))
+
+    def tables_out(self):
+        self.tables = self.layer.stacked_tables(self.table, self.table_in)
+        self.tables_in = node_swap(self.tables, along_z(2))
 
     def rows_in(self):
-        self.rows = self.layer.own_rows(self.place, self.tables)
-
-    def local(self):
-        self.sums = self.layer.local(self.place, self.cols, self.rows, self.feats, self.tiles)
+        self.rows = self.layer.own_rows(self.place, self.tables, self.tables_in)
 
     def load(self):
         feats, self.tiles, cotangent = self.layer.loaded(self.feats, self.tiles, self.cotangent)
@@ -634,24 +652,29 @@
     def self_part(self):
         self.self_parts = self.layer.self_part(self.place, self.feat_parts, self.w_self, self.bias)
 
-    def join(self, role, k):
-        early = 3 * k + role - 2
-        after = [] if role == SELF or early < 0 else [self.inward[early % 3, early // 3]]
-        part = self.layer.joined(role, k, self.place, self.rows, self.sums, self.slots_in[role], after=after)
-        self.joined[role, k] = part
-        if role != SELF:
-            self.inward[role, k] = node_swap(part, INWARD)
+    def dense(self, role):
+        sums = self.layer.dense_sums(
+            role, self.place, self.cols, self.rows, self.feats, self.tiles, self.slots_in[role]
+        )
+        for k in range(CHUNKS):
+            self.joined[role, k] = sums[k]
+        if role in (FAR_OUTER, FAR_INNER):
+            self.inward[role, 0] = node_swap(sums[0], INWARD)
+
+    def send_in(self, role, k):
+        self.joined[role, k] = self.layer.relay(self.joined[role, k])
+        self.inward[role, k] = node_swap(self.joined[role, k], INWARD)
 
     def pass_on(self, role, k):
         if role == NEAR:
             part = self.layer.added(self.joined[NEAR, k], self.across[FAR_OUTER, k])
-            self.outward[k] = node_swap(part, OUTWARD)
+            self.nearby[k] = node_swap(part, along_z(1))
         else:
             part = self.layer.added(self.joined[role, k], self.inward[role, k])
             self.across[role, k] = node_swap(part, ACROSS)
 
     def mean(self, k):
-        pieces = (self.joined[SELF, k], self.inward[NEAR, k], self.across[FAR_INNER, k], self.outward[k])
+        pieces = (self.joined[SELF, k], self.nearby[k], self.across[FAR_INNER, k])
         means = self.layer.means(k, pieces, self.inverse)
         self.means[k] = means
         self.mean_parts[k] = [means, feat_swap(means, OTHER_Y), feat_swap(means, OTHER_CORE)]
@@ -680,31 +703,20 @@
         self.outer[k].append(node_swap(self.outer[k][0], OUTWARD))
 
     def weight(self, k):
-        back, *weights = self.layer.weight_grad(
+        back, weights = self.layer.weight_grad(
             k, self.place, self.w_self, self.feats, self.means[k], self.grads[k], self.weights
         )
         self.self_back[k] = back
+        self.weights = weights
         if k == CHUNKS - 1:
-            send, self.weights = weights
-            self.weights_in = node_swap(send, OTHER_X)
+            self.weights_in = node_swap(weights, OTHER_X)
+
+    def weight_sum(self, pairs):
+        self.weights = self.layer.added(self.weights, self.weights_in)
+        if pairs is None:
+            self.weights_in = feat_swap(self.weights, OTHER_CORE)
         else:
-            self.weights = weights[0]
-
-    def weight_x(self):
-        self.weights = self.layer.added(self.weights, self.weights_in)
-        self.weights_in = node_swap(self.weights, along_z(1))
-
-    def weight_near(self):
-        self.weights = self.layer.added(self.weights, self.weights_in)
-        self.weights_in = node_swap(self.weights, along_z(3))
-
-    def weight_far(self):
-        self.weights = self.layer.added(self.weights, self.weights_in)
-        self.weights_in = node_swap(self.weights, OTHER_X)
-
-    def weight_halves(self):
-        self.weights = self.layer.both_halves(self.place, self.weights, self.weights_in)
-        self.weights_in = feat_swap(self.weights, OTHER_CORE)
+            self.weights_in = node_swap(self.weights, pairs)
 
     def weight_cores(self):
         self.weights = self.layer.both_cores(self.place, self.weights, self.weights_in)

time: 226 us -> 220 us (0.973)
  waiting for transfers between devices: 90.9 us -> 87 us
  Pallas kernels: 57.1 us -> 54.4 us
    ppermute x37 -> x33, waiting for transfers between devices: 82.2 us -> 72.6 us  [node_swap(): return lax.ppermute(value, 'node', pairs)]
    ppermute x14, waiting for transfers between devices: 8.78 us -> 14.4 us  [feat_swap(): return lax.ppermute(value, 'feat', pairs)]
    ppermute x37 -> x33, starting transfers between devices: 60.8 us -> 63.6 us  [node_swap(): return lax.ppermute(value, 'node', pairs)]
    pallas_call x54 -> x52, Pallas kernels: 57.1 us -> 54.4 us  [call(): pl.pallas_call(ordered, grid_spec=pltpu.PrefetchScalarGridSpec(num_scalar...]
    unnamed x21 -> x24, local copies, waits for them, and re-layouts: 6.57 us -> 5.18 us
  transfers between devices with their start and end apart: 51 -> 47, of which waited for: 25 -> 19; matrix products, arithmetic and copies ran while one was open for 0% -> 0% of each run, Pallas kernels for 22% -> 21%
where the time goes in v5:
time: 220 us; the launch traced here: 219 us
  waiting for transfers between devices  87 us (40%)
  starting transfers between devices  70.4 us (32%)
  Pallas kernels  54.4 us (25%)
  local copies, waits for them, and re-layouts  5.18 us (2%)
    ppermute x33, waiting for transfers between devices, node_swap(): return lax.ppermute(value, 'node', pairs)  72.6 us
    ppermute x33, starting transfers between devices, node_swap(): return lax.ppermute(value, 'node', pairs)  63.6 us
    pallas_call x52, Pallas kernels, call(): pl.pallas_call(ordered, grid_spec=pltpu.PrefetchScalarGridSpec(num_scalar...  54.4 us
    ppermute x14, waiting for transfers between devices, feat_swap(): return lax.ppermute(value, 'feat', pairs)  14.4 us
    ppermute x14, starting transfers between devices, feat_swap(): return lax.ppermute(value, 'feat', pairs)  6.78 us
    unnamed x24, local copies, waits for them, and re-layouts  5.18 us
  transfers between devices with their start and end apart: 47, of which 19 were waited for; matrix products, arithmetic and copies ran while one was open for 0% of the time, Pallas kernels for 21%

profile of v5, /device:TPU:0, one launch (start us, length us, event | category | flops | bytes accessed | tf_op | source)
XLA Modules:
  0.0 219.1 jit_solution(15729680388085656694)
XLA Ops:
  1.3 3.9 %shard_map.128.refs_1_ = f32[16,64,128]{2,1,0:T(8,128)} custom-call(s32[4]{0:T(128)} %pad_add_fusion.refs_0_, s32[8,16]{1,0:T(8,128)} %refs_1_.27, f32[64,4096]{1,0:T(8,128)} %refs_0_.3, f32[8,16,128,128]{3,2,1,0:T(8,128)} %refs_1_.15), custom_call_target="tpu_custom_call" | custom-call | flops 1 | bytes 1 | tf_op jit(solution)/shard_map/pallas_call | solution.py:108
  5.2 3.0 %collective-permute-start.2 = (f32[16,64,128]{2,1,0:T(8,128)}, f32[16,64,128]{2,1,0:T(8,128)S(1)}, u32[]{:S(2)}, u32[]{:S(2)}) collective-permute-start(f32[16,64,128]{2,1,0:T(8,128)} %shard_map.128.refs_1_), channel_id=1, source_target_pairs={{0,1},{1,0},{2,3},{3,2},{4,5},{5,4},{6,7},{7,6},{8,9},{9,8},{10,11... | collective-permute-start | bytes 1572872 | tf_op jit(solution)/shard_map/ppermute | solution.py:532
  9.3 1.6 collective-permute-start
  10.8 3.4 %copy-done = f32[8,16,128,128]{3,2,1,0:T(8,128)S(1)} copy-done((f32[8,16,128,128]{3,2,1,0:T(8,128)S(1)}, f32[8,16,128,128]{3,2,1,0:T(8,128)}, u32[]{:S(2)}) %copy-start) | copy-done | bytes 8388632
  15.2 2.7 %collective-permute-start.1 = (s32[16,16]{1,0:T(8,128)S(1)}, s32[16,16]{1,0:T(8,128)S(1)}, u32[]{:S(2)}, u32[]{:S(2)}) collective-permute-start(s32[16,16]{1,0:T(8,128)S(1)} %shard_map.131.refs_4_.refs_1_), channel_id=1, source_target_pairs={{0,4},{1,5},{2,6},{3,7},{4,0},{5,1},{6,2},{7,3},{8,12},{9,13},{10,... | collective-permute-start | bytes 3080 | tf_op jit(solution)/shard_map/ppermute | solution.py:532
  17.9 2.2 %shard_map.132 = (f32[16,64,128]{2,1,0:T(8,128)S(1)}, f32[16,64,128]{2,1,0:T(8,128)S(1)}, f32[16,64,128]{2,1,0:T(8,128)S(1)}) custom-call(s32[4]{0:T(128)S(1)} %copy-done.7, s32[8,16]{1,0:T(8,128)S(1)} %copy-done.6, f32[64,4096]{1,0:T(8,128)S(1)} %get-tuple-element.42.refs_2_.refs_3_.refs_1_, f32[8,16,128,128]{3,2,1,0:T(8,128)S(1)} %get-tuple-element.43.refs_3_.refs_4_, ...), custom_call_target="tpu_custom_call" | custom-call | flops 1 | bytes 1 | tf_op jit(solution)/shard_map/pallas_call | solution.py:108
  22.2 3.4 %collective-permute-start.4 = (f32[16,64,128]{2,1,0:T(8,128)S(1)}, f32[16,64,128]{2,1,0:T(8,128)S(1)}, u32[]{:S(2)}, u32[]{:S(2)}) collective-permute-start(f32[16,64,128]{2,1,0:T(8,128)S(1)} %get-tuple-element.48.refs_0_), channel_id=1, source_target_pairs={{0,2},{1,3},{6,4},{7,5},{8,10},{9,11},{14,12},{15,13},{16,18},{17,... | collective-permute-start | bytes 1572872 | tf_op jit(solution)/shard_map/ppermute | solution.py:532
  25.5 1.6 collective-permute-start.3
  27.1 1.5 collective-permute-start.11
  30.0 7.9 %collective-permute-done.4.refs_1_ = f32[16,64,128]{2,1,0:T(8,128)S(1)} collective-permute-done((f32[16,64,128]{2,1,0:T(8,128)S(1)}, f32[16,64,128]{2,1,0:T(8,128)S(1)}, u32[]{:S(2)}, u32[]{:S(2)}) %collective-permute-start.4) | collective-permute-done | bytes 524320 | tf_op jit(solution)/shard_map/ppermute | solution.py:532
  39.6 1.6 collective-permute-start.5
  41.2 4.2 %collective-permute-start.12 = (f32[16,64,128]{2,1,0:T(8,128)S(1)}, f32[16,64,128]{2,1,0:T(8,128)S(1)}, u32[]{:S(2)}, u32[]{:S(2)}) collective-permute-start(f32[16,64,128]{2,1,0:T(8,128)S(1)} %get-tuple-element.52.refs_0_), channel_id=1, source_target_pairs={{0,2},{1,3},{6,4},{7,5},{8,10},{9,11},{14,12},{15,13},{16,18},{17,... | collective-permute-start | bytes 1572872 | tf_op jit(solution)/shard_map/ppermute | solution.py:532
  46.1 3.0 %collective-permute-done.6.refs_1_ = f32[16,64,128]{2,1,0:T(8,128)S(1)} collective-permute-done((f32[16,64,128]{2,1,0:T(8,128)S(1)}, f32[16,64,128]{2,1,0:T(8,128)S(1)}, u32[]{:S(2)}, u32[]{:S(2)}) %collective-permute-start.6) | collective-permute-done | bytes 524320 | tf_op jit(solution)/shard_map/ppermute | solution.py:532
  51.2 5.8 %collective-permute-start.8 = (f32[16,64,128]{2,1,0:T(8,128)S(1)}, f32[16,64,128]{2,1,0:T(8,128)S(1)}, u32[]{:S(2)}, u32[]{:S(2)}) collective-permute-start(f32[16,64,128]{2,1,0:T(8,128)S(1)} %shard_map.140.refs_2_.refs_0_), channel_id=1, source_target_pairs={{0,2},{1,3},{6,4},{7,5},{8,10},{9,11},{14,12},{15,13},{16,18},{17,... | collective-permute-start | bytes 1572872 | tf_op jit(solution)/shard_map/ppermute | solution.py:532
  57.1 3.2 %collective-permute-done.12.refs_1_ = f32[16,64,128]{2,1,0:T(8,128)S(1)} collective-permute-done((f32[16,64,128]{2,1,0:T(8,128)S(1)}, f32[16,64,128]{2,1,0:T(8,128)S(1)}, u32[]{:S(2)}, u32[]{:S(2)}) %collective-permute-start.12) | collective-permute-done | bytes 524320 | tf_op jit(solution)/shard_map/ppermute | solution.py:532
  60.3 1.5 collective-permute-start.7
  63.4 1.6 collective-permute-start.20
  65.5 4.0 %collective-permute-done.8.refs_1_ = f32[16,64,128]{2,1,0:T(8,128)S(1)} collective-permute-done((f32[16,64,128]{2,1,0:T(8,128)S(1)}, f32[16,64,128]{2,1,0:T(8,128)S(1)}, u32[]{:S(2)}, u32[]{:S(2)}) %collective-permute-start.8) | collective-permute-done | bytes 524320 | tf_op jit(solution)/shard_map/ppermute | solution.py:532
  69.5 2.5 %collective-permute-start.15 = (f32[16,64,128]{2,1,0:T(8,128)S(1)}, f32[16,64,128]{2,1,0:T(8,128)S(1)}, u32[]{:S(2)}, u32[]{:S(2)}) collective-permute-start(f32[16,64,128]{2,1,0:T(8,128)S(1)} %shard_map.146.refs_2_), channel_id=1, source_target_pairs={{0,2},{1,3},{2,0},{3,1},{4,6},{5,7},{6,4},{7,5},{8,10},{9,11},{10,... | collective-permute-start | bytes 1572872 | tf_op jit(solution)/shard_map/ppermute | solution.py:532
  74.3 7.8 %collective-permute-done.15.refs_1_ = f32[16,64,128]{2,1,0:T(8,128)S(1)} collective-permute-done((f32[16,64,128]{2,1,0:T(8,128)S(1)}, f32[16,64,128]{2,1,0:T(8,128)S(1)}, u32[]{:S(2)}, u32[]{:S(2)}) %collective-permute-start.15) | collective-permute-done | bytes 524320 | tf_op jit(solution)/shard_map/ppermute | solution.py:532
  84.2 1.5 collective-permute-start.17
  85.7 5.3 %collective-permute-start.13 = (f32[16,64,128]{2,1,0:T(8,128)S(1)}, f32[16,64,128]{2,1,0:T(8,128)S(1)}, u32[]{:S(2)}, u32[]{:S(2)}) collective-permute-start(f32[16,64,128]{2,1,0:T(8,128)S(1)} %shard_map.147.refs_2_), channel_id=1, source_target_pairs={{0,2},{1,3},{2,0},{3,1},{4,6},{5,7},{6,4},{7,5},{8,10},{9,11},{10,... | collective-permute-start | bytes 1572872 | tf_op jit(solution)/shard_map/ppermute | solution.py:532
  91.0 4.9 %shard_map.152.refs_1_.refs_6_ = f32[2,256,2048]{2,1,0:T(8,128)S(1)} custom-call(s32[4]{0:T(128)S(1)} %copy-done.7, f32[64,4096]{1,0:T(8,128)S(1)} %get-tuple-element.42.refs_2_.refs_3_.refs_1_, f32[64,4096]{1,0:T(8,128)S(1)} %shard_map.145.refs_2_, f32[64,4096]{1,0:T(8,128)S(1)} %collective-permute-done.18.refs_3_, ...), custom_call_target="tpu_custom_call" | custom-call | flops 1 | bytes 1 | tf_op jit(solution)/shard_map/pallas_call | solution.py:108
  97.8 5.7 %collective-permute-done.13.refs_1_ = f32[16,64,128]{2,1,0:T(8,128)S(1)} collective-permute-done((f32[16,64,128]{2,1,0:T(8,128)S(1)}, f32[16,64,128]{2,1,0:T(8,128)S(1)}, u32[]{:S(2)}, u32[]{:S(2)}) %collective-permute-start.13) | collective-permute-done | bytes 524320 | tf_op jit(solution)/shard_map/ppermute | solution.py:532
  104.3 4.1 %shard_map.155 = (f32[1024,256]{1,0:T(8,128)}, f32[256,2048]{1,0:T(8,128)S(1)}, f32[16,64,128]{2,1,0:T(8,128)S(1)}) custom-call(s32[4]{0:T(128)S(1)} %copy-done.7, f32[16,64,128]{2,1,0:T(8,128)S(1)} %shard_map.150.refs_1_.refs_3_, f32[16,64,128]{2,1,0:T(8,128)S(1)} %shard_map.153.refs_4_.refs_2_, f32[16,64,128]{2,1,0:T(8,128)S(1)} %collective-permute-done.22.refs_3_, ...), custom_call_target="tpu_custom_call" | custom-call | flops 1 | bytes 1 | tf_op jit(solution)/shard_map/pallas_call | solution.py:108
  108.3 9.1 %collective-permute-done.21.refs_0_ = f32[16,64,128]{2,1,0:T(8,128)S(1)} collective-permute-done((f32[16,64,128]{2,1,0:T(8,128)S(1)}, f32[16,64,128]{2,1,0:T(8,128)S(1)}, u32[]{:S(2)}, u32[]{:S(2)}) %collective-permute-start.21) | collective-permute-done | bytes 524320 | tf_op jit(solution)/shard_map/ppermute | solution.py:536
  117.4 1.5 collective-permute-start.28
  119.8 2.1 shard_map.157
  121.9 4.1 %shard_map.158 = (f32[1024,256]{1,0:T(8,128)}, f32[256,2048]{1,0:T(8,128)S(1)}, f32[16,64,128]{2,1,0:T(8,128)S(1)}) custom-call(s32[4]{0:T(128)S(1)} %copy-done.7, f32[16,64,128]{2,1,0:T(8,128)S(1)} %shard_map.154.refs_12_.refs_1_.refs_3_, f32[16,64,128]{2,1,0:T(8,128)S(1)} %shard_map.156.refs_5_.refs_2_, ...), custom_call_target="tpu_custom_call", output_to_operand_aliasing={{0}: (12, {})} | custom-call | flops 1 | bytes 1 | tf_op jit(solution)/shard_map/pallas_call | solution.py:108
  126.7 5.0 %collective-permute-start.33 = (f32[16,64,128]{2,1,0:T(8,128)S(1)}, f32[16,64,128]{2,1,0:T(8,128)S(1)}, u32[]{:S(2)}, u32[]{:S(2)}) collective-permute-start(f32[16,64,128]{2,1,0:T(8,128)S(1)} %get-tuple-element.61.refs_6_.refs_3_.refs_5_), channel_id=1, source_target_pairs={{0,2},{1,3},{2,0},{3,1},{4,6},{5,7},{6,4},{7,5},{8,10},{9,11},{10,... | collective-permute-start | bytes 1572872 | tf_op jit(solution)/shard_map/ppermute | solution.py:532
  131.7 2.1 shard_map.159
  135.1 1.6 collective-permute-start.30
  137.3 3.0 %collective-permute-done.30.refs_1_ = f32[144,256]{1,0:T(8,128)S(1)} collective-permute-done((f32[144,256]{1,0:T(8,128)S(1)}, f32[144,256]{1,0:T(8,128)S(1)}, u32[]{:S(2)}, u32[]{:S(2)}) %collective-permute-start.30) | collective-permute-done | bytes 147488 | tf_op jit(solution)/shard_map/ppermute | solution.py:532
  140.3 4.1 %collective-permute-done.33.refs_0_ = f32[16,64,128]{2,1,0:T(8,128)S(1)} collective-permute-done((f32[16,64,128]{2,1,0:T(8,128)S(1)}, f32[16,64,128]{2,1,0:T(8,128)S(1)}, u32[]{:S(2)}, u32[]{:S(2)}) %collective-permute-start.33) | collective-permute-done | bytes 524320 | tf_op jit(solution)/shard_map/ppermute | solution.py:532
  145.2 1.6 collective-permute-start.39
  146.8 7.9 %collective-permute-done.35.refs_1_.refs_4_.refs_6_ = f32[16,64,128]{2,1,0:T(8,128)S(1)} collective-permute-done((f32[16,64,128]{2,1,0:T(8,128)S(1)}, f32[16,64,128]{2,1,0:T(8,128)S(1)}, u32[]{:S(2)}, u32[]{:S(2)}) %collective-permute-start.35) | collective-permute-done | bytes 524320 | tf_op jit(solution)/shard_map/ppermute | solution.py:532
  156.7 4.4 %collective-permute-start.32 = (f32[144,256]{1,0:T(8,128)S(1)}, f32[144,256]{1,0:T(8,128)S(1)}, u32[]{:S(2)}, u32[]{:S(2)}) collective-permute-start(f32[144,256]{1,0:T(8,128)S(1)} %shard_map.162.refs_1_.refs_0_), channel_id=1, source_target_pairs={{0,2},{1,3},{2,0},{3,1},{4,6},{5,7},{6,4},{7,5},{8,10},{9,11},{10,... | collective-permute-start | bytes 442376 | tf_op jit(solution)/shard_map/ppermute | solution.py:532
  161.1 2.3 %shard_map.166 = (f32[64,4096]{1,0:T(8,128)}, f32[8,128]{1,0:T(8,128)S(1)}) custom-call(s32[4]{0:T(128)S(1)} %copy-done.7, s32[8,16]{1,0:T(8,128)S(1)} %copy-done.6, s32[8,16]{1,0:T(8,128)S(1)} %shard_map.133.refs_2_.refs_6_.refs_1_, f32[8,16,128,128]{3,2,1,0:T(8,128)S(1)} %get-tuple-element.43.refs_3_.refs_4_, ...), custom_call_target="tpu_custom_call" | custom-call | flops 1 | bytes 1 | tf_op jit(solution)/shard_map/pallas_call | solution.py:108
  164.2 8.5 %collective-permute-done.32.refs_1_ = f32[144,256]{1,0:T(8,128)S(1)} collective-permute-done((f32[144,256]{1,0:T(8,128)S(1)}, f32[144,256]{1,0:T(8,128)S(1)}, u32[]{:S(2)}, u32[]{:S(2)}) %collective-permute-start.32) | collective-permute-done | bytes 147488 | tf_op jit(solution)/shard_map/ppermute | solution.py:532
  174.1 1.5 collective-permute-start.42
  176.9 4.1 %shard_map.170 = (f32[64,4096]{1,0:T(8,128)}, f32[8,128]{1,0:T(8,128)S(1)}) custom-call(s32[4]{0:T(128)S(1)} %copy-done.7, s32[8,16]{1,0:T(8,128)S(1)} %copy-done.6, s32[8,16]{1,0:T(8,128)S(1)} %shard_map.133.refs_2_.refs_6_.refs_1_, f32[8,16,128,128]{3,2,1,0:T(8,128)S(1)} %get-tuple-element.43.refs_3_.refs_4_, ...), custom_call_target="tpu_custom_call", output_to_operand_aliasing={{0}: (7, {})} | custom-call | flops 1 | bytes 1 | tf_op jit(solution)/shard_map/pallas_call | solution.py:108
  183.8 8.5 %collective-permute-done.40.refs_3_.refs_4_.refs_6_ = f32[16,64,128]{2,1,0:T(8,128)S(1)} collective-permute-done((f32[16,64,128]{2,1,0:T(8,128)S(1)}, f32[16,64,128]{2,1,0:T(8,128)S(1)}, u32[]{:S(2)}, u32[]{:S(2)}) %collective-permute-start.40) | collective-permute-done | bytes 524320 | tf_op jit(solution)/shard_map/ppermute | solution.py:532
  192.9 4.1 %shard_map.175 = (f32[64,4096]{1,0:T(8,128)}, f32[8,128]{1,0:T(8,128)S(1)}) custom-call(s32[4]{0:T(128)S(1)} %copy-done.7, s32[8,16]{1,0:T(8,128)S(1)} %copy-done.6, s32[8,16]{1,0:T(8,128)S(1)} %shard_map.133.refs_2_.refs_6_.refs_1_, f32[8,16,128,128]{3,2,1,0:T(8,128)S(1)} %get-tuple-element.43.refs_3_.refs_4_, ...), custom_call_target="tpu_custom_call", output_to_operand_aliasing={{0}: (9, {})} | custom-call | flops 1 | bytes 1 | tf_op jit(solution)/shard_map/pallas_call | solution.py:108
  197.0 4.7 %collective-permute-done.41.refs_5_.refs_7_ = f32[16,64,128]{2,1,0:T(8,128)S(1)} collective-permute-done((f32[16,64,128]{2,1,0:T(8,128)S(1)}, f32[16,64,128]{2,1,0:T(8,128)S(1)}, u32[]{:S(2)}, u32[]{:S(2)}) %collective-permute-start.41) | collective-permute-done | bytes 524320 | tf_op jit(solution)/shard_map/ppermute | solution.py:532
  203.9 4.1 %shard_map.177 = (f32[64,4096]{1,0:T(8,128)}, f32[8,128]{1,0:T(8,128)S(1)}) custom-call(s32[4]{0:T(128)S(1)} %copy-done.7, s32[8,16]{1,0:T(8,128)S(1)} %copy-done.6, s32[8,16]{1,0:T(8,128)S(1)} %shard_map.133.refs_2_.refs_6_.refs_1_, f32[8,16,128,128]{3,2,1,0:T(8,128)S(1)} %get-tuple-element.43.refs_3_.refs_4_, ...), custom_call_target="tpu_custom_call", output_to_operand_aliasing={{0}: (9, {})} | custom-call | flops 1 | bytes 1 | tf_op jit(solution)/shard_map/pallas_call | solution.py:108
  208.0 2.6 %collective-permute-done.46.refs_2_ = f32[2,144,256]{2,1,0:T(8,128)S(1)} collective-permute-done((f32[2,144,256]{2,1,0:T(8,128)S(1)}, f32[2,144,256]{2,1,0:T(8,128)S(1)}, u32[]{:S(2)}, u32[]{:S(2)}) %collective-permute-start.46) | collective-permute-done | bytes 294944 | tf_op jit(solution)/shard_map/ppermute | solution.py:536
  212.0 2.7 %collective-permute-done.44.refs_4_ = f32[16,64,128]{2,1,0:T(8,128)S(1)} collective-permute-done((f32[16,64,128]{2,1,0:T(8,128)S(1)}, f32[16,64,128]{2,1,0:T(8,128)S(1)}, u32[]{:S(2)}, u32[]{:S(2)}) %collective-permute-start.44) | collective-permute-done | bytes 524320 | tf_op jit(solution)/shard_map/ppermute | solution.py:532
  215.4 3.5 %shard_map.179 = (f32[64,4096]{1,0:T(8,128)}, f32[8,128]{1,0:T(8,128)}) custom-call(s32[4]{0:T(128)S(1)} %copy-done.7, s32[8,16]{1,0:T(8,128)S(1)} %copy-done.6, s32[8,16]{1,0:T(8,128)S(1)} %shard_map.133.refs_2_.refs_6_.refs_1_, f32[8,16,128,128]{3,2,1,0:T(8,128)S(1)} %get-tuple-element.43.refs_3_.refs_4_, ...), custom_call_target="tpu_custom_call", output_to_operand_aliasing={{0}: (5, {})} | custom-call | flops 1 | bytes 1 | tf_op jit(solution)/shard_map/pallas_call | solution.py:108
  (124 shorter events, 37.0 us)
Async XLA Ops:
  5.2 15.5 %collective-permute-start.2 = (f32[16,64,128]{2,1,0:T(8,128)}, f32[16,64,128]{2,1,0:T(8,128)S(1)}, u32[]{:S(2)}, u32[]{:S(2)}) collective-permute-start(f32[16,64,128]{2,1,0:T(8,128)} %shard_map.128.refs_1_), channel_id=1, source_target_pairs={{0,1},{1,0},{2,3},{3,2},{4,5},{5,4},{6,7},{7,6},{8,9},{9,8},{10,11... | collective-permute-start | bytes 1572872 | tf_op jit(solution)/shard_map/ppermute | solution.py:532
  9.3 6.0 %collective-permute-start = (s32[8,16]{1,0:T(8,128)S(1)}, s32[8,16]{1,0:T(8,128)S(1)}, u32[]{:S(2)}, u32[]{:S(2)}) collective-permute-start(s32[8,16]{1,0:T(8,128)S(1)} %shard_map.129.refs_3_.refs_0_), channel_id=1, source_target_pairs={{0,2},{1,3},{2,0},{3,1},{4,6},{5,7},{6,4},{7,5},{8,10},{9,11},{10,... | collective-permute-start | bytes 1544 | tf_op jit(solution)/shard_map/ppermute | solution.py:532
  15.2 4.9 %collective-permute-start.1 = (s32[16,16]{1,0:T(8,128)S(1)}, s32[16,16]{1,0:T(8,128)S(1)}, u32[]{:S(2)}, u32[]{:S(2)}) collective-permute-start(s32[16,16]{1,0:T(8,128)S(1)} %shard_map.131.refs_4_.refs_1_), channel_id=1, source_target_pairs={{0,4},{1,5},{2,6},{3,7},{4,0},{5,1},{6,2},{7,3},{8,12},{9,13},{10,... | collective-permute-start | bytes 3080 | tf_op jit(solution)/shard_map/ppermute | solution.py:532
  22.2 15.7 %collective-permute-start.4 = (f32[16,64,128]{2,1,0:T(8,128)S(1)}, f32[16,64,128]{2,1,0:T(8,128)S(1)}, u32[]{:S(2)}, u32[]{:S(2)}) collective-permute-start(f32[16,64,128]{2,1,0:T(8,128)S(1)} %get-tuple-element.48.refs_0_), channel_id=1, source_target_pairs={{0,2},{1,3},{6,4},{7,5},{8,10},{9,11},{14,12},{15,13},{16,18},{17,... | collective-permute-start | bytes 1572872 | tf_op jit(solution)/shard_map/ppermute | solution.py:532
  25.5 12.6 %collective-permute-start.3 = (f32[16,64,128]{2,1,0:T(8,128)S(1)}, f32[16,64,128]{2,1,0:T(8,128)S(1)}, u32[]{:S(2)}, u32[]{:S(2)}) collective-permute-start(f32[16,64,128]{2,1,0:T(8,128)S(1)} %shard_map.135.refs_1_), channel_id=1, source_target_pairs={{0,1},{1,0},{2,3},{3,2},{4,5},{5,4},{6,7},{7,6},{8,9},{9,8},{10,11... | collective-permute-start | bytes 1572872 | tf_op jit(solution)/shard_map/ppermute | solution.py:532
  27.1 36.3 %collective-permute-start.11 = (f32[64,4096]{1,0:T(8,128)S(1)}, f32[64,4096]{1,0:T(8,128)S(1)}, u32[]{:S(2)}, u32[]{:S(2)}) collective-permute-start(f32[64,4096]{1,0:T(8,128)S(1)} %get-tuple-element.42.refs_2_.refs_3_.refs_1_), channel_id=1, source_target_pairs={{0,16},{8,24},{16,0},{24,8},{1,17},{9,25},{17,1},{25,9},{2,18},{10... | collective-permute-start | bytes 3145736 | tf_op jit(solution)/shard_map/ppermute | solution.py:536
  28.6 20.5 %collective-permute-start.6 = (f32[16,64,128]{2,1,0:T(8,128)S(1)}, f32[16,64,128]{2,1,0:T(8,128)S(1)}, u32[]{:S(2)}, u32[]{:S(2)}) collective-permute-start(f32[16,64,128]{2,1,0:T(8,128)S(1)} %shard_map.136.refs_2_.refs_0_), channel_id=1, source_target_pairs={{0,2},{1,3},{6,4},{7,5},{8,10},{9,11},{14,12},{15,13},{16,18},{17,... | collective-permute-start | bytes 1572872 | tf_op jit(solution)/shard_map/ppermute | solution.py:532
  39.6 11.7 %collective-permute-start.5 = (f32[16,64,128]{2,1,0:T(8,128)S(1)}, f32[16,64,128]{2,1,0:T(8,128)S(1)}, u32[]{:S(2)}, u32[]{:S(2)}) collective-permute-start(f32[16,64,128]{2,1,0:T(8,128)S(1)} %shard_map.139.refs_1_), channel_id=1, source_target_pairs={{0,1},{1,0},{2,3},{3,2},{4,5},{5,4},{6,7},{7,6},{8,9},{9,8},{10,11... | collective-permute-start | bytes 1572872 | tf_op jit(solution)/shard_map/ppermute | solution.py:532
  41.2 19.2 %collective-permute-start.12 = (f32[16,64,128]{2,1,0:T(8,128)S(1)}, f32[16,64,128]{2,1,0:T(8,128)S(1)}, u32[]{:S(2)}, u32[]{:S(2)}) collective-permute-start(f32[16,64,128]{2,1,0:T(8,128)S(1)} %get-tuple-element.52.refs_0_), channel_id=1, source_target_pairs={{0,2},{1,3},{6,4},{7,5},{8,10},{9,11},{14,12},{15,13},{16,18},{17,... | collective-permute-start | bytes 1572872 | tf_op jit(solution)/shard_map/ppermute | solution.py:532
  45.4 19.6 %collective-permute-start.10 = (f32[16,64,128]{2,1,0:T(8,128)S(1)}, f32[16,64,128]{2,1,0:T(8,128)S(1)}, u32[]{:S(2)}, u32[]{:S(2)}) collective-permute-start(f32[16,64,128]{2,1,0:T(8,128)S(1)} %shard_map.137.refs_6_), channel_id=1, source_target_pairs={{2,4},{3,5},{4,2},{5,3},{10,12},{11,13},{12,10},{13,11},{18,20},{1... | collective-permute-start | bytes 1572872 | tf_op jit(solution)/shard_map/ppermute | solution.py:532
  49.2 15.8 %collective-permute-start.9 = (f32[16,64,128]{2,1,0:T(8,128)S(1)}, f32[16,64,128]{2,1,0:T(8,128)S(1)}, u32[]{:S(2)}, u32[]{:S(2)}) collective-permute-start(f32[16,64,128]{2,1,0:T(8,128)S(1)} %shard_map.141.refs_2_), channel_id=1, source_target_pairs={{2,4},{3,5},{4,2},{5,3},{10,12},{11,13},{12,10},{13,11},{18,20},{1... | collective-permute-start | bytes 1572872 | tf_op jit(solution)/shard_map/ppermute | solution.py:532
  51.2 18.3 %collective-permute-start.8 = (f32[16,64,128]{2,1,0:T(8,128)S(1)}, f32[16,64,128]{2,1,0:T(8,128)S(1)}, u32[]{:S(2)}, u32[]{:S(2)}) collective-permute-start(f32[16,64,128]{2,1,0:T(8,128)S(1)} %shard_map.140.refs_2_.refs_0_), channel_id=1, source_target_pairs={{0,2},{1,3},{6,4},{7,5},{8,10},{9,11},{14,12},{15,13},{16,18},{17,... | collective-permute-start | bytes 1572872 | tf_op jit(solution)/shard_map/ppermute | solution.py:532
  60.3 11.6 %collective-permute-start.7 = (f32[16,64,128]{2,1,0:T(8,128)S(1)}, f32[16,64,128]{2,1,0:T(8,128)S(1)}, u32[]{:S(2)}, u32[]{:S(2)}) collective-permute-start(f32[16,64,128]{2,1,0:T(8,128)S(1)} %shard_map.142.refs_6_), channel_id=1, source_target_pairs={{0,1},{1,0},{2,3},{3,2},{4,5},{5,4},{6,7},{7,6},{8,9},{9,8},{10,11... | collective-permute-start | bytes 1572872 | tf_op jit(solution)/shard_map/ppermute | solution.py:532
  63.4 20.8 %collective-permute-start.20 = (f32[256,1024]{1,0:T(8,128)S(1)}, f32[256,1024]{1,0:T(8,128)S(1)}, u32[]{:S(2)}, u32[]{:S(2)}) collective-permute-start(f32[256,1024]{1,0:T(8,128)S(1)} %get-tuple-element.41.refs_2_.refs_7_), channel_id=1, source_target_pairs={{0,16},{8,24},{16,0},{24,8},{1,17},{9,25},{17,1},{25,9},{2,18},{10... | collective-permute-start | bytes 3145736 | tf_op jit(solution)/shard_map/ppermute | solution.py:536
  65.0 20.8 %collective-permute-start.18 = (f32[64,4096]{1,0:T(8,128)S(1)}, f32[64,4096]{1,0:T(8,128)S(1)}, u32[]{:S(2)}, u32[]{:S(2)}) collective-permute-start(f32[64,4096]{1,0:T(8,128)S(1)} %get-tuple-element.42.refs_2_.refs_3_.refs_1_), channel_id=1, source_target_pairs={{0,8},{8,0},{16,24},{24,16},{1,9},{9,1},{17,25},{25,17},{2,10},{10... | collective-permute-start | bytes 3145736 | tf_op jit(solution)/shard_map/ppermute | solution.py:536
  65.0 20.8 %collective-permute-start.19 = (f32[64,4096]{1,0:T(8,128)S(1)}, f32[64,4096]{1,0:T(8,128)S(1)}, u32[]{:S(2)}, u32[]{:S(2)}) collective-permute-start(f32[64,4096]{1,0:T(8,128)S(1)} %shard_map.145.refs_2_), channel_id=1, source_target_pairs={{0,8},{8,0},{16,24},{24,16},{1,9},{9,1},{17,25},{25,17},{2,10},{10... | collective-permute-start | bytes 3145736 | tf_op jit(solution)/shard_map/ppermute | solution.py:536
  69.5 12.6 %collective-permute-start.15 = (f32[16,64,128]{2,1,0:T(8,128)S(1)}, f32[16,64,128]{2,1,0:T(8,128)S(1)}, u32[]{:S(2)}, u32[]{:S(2)}) collective-permute-start(f32[16,64,128]{2,1,0:T(8,128)S(1)} %shard_map.146.refs_2_), channel_id=1, source_target_pairs={{0,2},{1,3},{2,0},{3,1},{4,6},{5,7},{6,4},{7,5},{8,10},{9,11},{10,... | collective-permute-start | bytes 1572872 | tf_op jit(solution)/shard_map/ppermute | solution.py:532
  72.0 10.1 %collective-permute-start.16 = (f32[16,64,128]{2,1,0:T(8,128)S(1)}, f32[16,64,128]{2,1,0:T(8,128)S(1)}, u32[]{:S(2)}, u32[]{:S(2)}) collective-permute-start(f32[16,64,128]{2,1,0:T(8,128)S(1)} %shard_map.144.refs_1_), channel_id=1, source_target_pairs={{2,4},{3,5},{4,2},{5,3},{10,12},{11,13},{12,10},{13,11},{18,20},{1... | collective-permute-start | bytes 1572872 | tf_op jit(solution)/shard_map/ppermute | solution.py:532
  74.3 16.7 %copy-start.2 = (f32[256,256]{1,0:T(8,128)S(1)}, f32[256,256]{1,0:T(8,128)}, u32[]{:S(2)}) copy-start(f32[256,256]{1,0:T(8,128)} %refs_1_.22) | copy-start | bytes 786436
  82.1 22.1 %collective-permute-start.24 = (f32[256,1024]{1,0:T(8,128)S(1)}, f32[256,1024]{1,0:T(8,128)S(1)}, u32[]{:S(2)}, u32[]{:S(2)}) collective-permute-start(f32[256,1024]{1,0:T(8,128)S(1)} %get-tuple-element.41.refs_2_.refs_7_), channel_id=1, source_target_pairs={{0,8},{8,0},{16,24},{24,16},{1,9},{9,1},{17,25},{25,17},{2,10},{10... | collective-permute-start | bytes 3145736 | tf_op jit(solution)/shard_map/ppermute | solution.py:536
  82.1 15.2 %collective-permute-start.14 = (f32[16,64,128]{2,1,0:T(8,128)S(1)}, f32[16,64,128]{2,1,0:T(8,128)S(1)}, u32[]{:S(2)}, u32[]{:S(2)}) collective-permute-start(f32[16,64,128]{2,1,0:T(8,128)S(1)} %shard_map.148.refs_6_), channel_id=1, source_target_pairs={{2,4},{3,5},{4,2},{5,3},{10,12},{11,13},{12,10},{13,11},{18,20},{1... | collective-permute-start | bytes 1572872 | tf_op jit(solution)/shard_map/ppermute | solution.py:532
  84.2 13.1 %collective-permute-start.17 = (f32[16,64,128]{2,1,0:T(8,128)S(1)}, f32[16,64,128]{2,1,0:T(8,128)S(1)}, u32[]{:S(2)}, u32[]{:S(2)}) collective-permute-start(f32[16,64,128]{2,1,0:T(8,128)S(1)} %shard_map.150.refs_1_.refs_3_), channel_id=1, source_target_pairs={{0,16},{8,24},{16,0},{24,8},{1,17},{9,25},{17,1},{25,9},{2,18},{10... | collective-permute-start | bytes 1572872 | tf_op jit(solution)/shard_map/ppermute | solution.py:536
  85.7 18.5 %collective-permute-start.25 = (f32[256,1024]{1,0:T(8,128)S(1)}, f32[256,1024]{1,0:T(8,128)S(1)}, u32[]{:S(2)}, u32[]{:S(2)}) collective-permute-start(f32[256,1024]{1,0:T(8,128)S(1)} %shard_map.151.refs_7_.refs_8_), channel_id=1, source_target_pairs={{0,8},{8,0},{16,24},{24,16},{1,9},{9,1},{17,25},{25,17},{2,10},{10... | collective-permute-start | bytes 3145736 | tf_op jit(solution)/shard_map/ppermute | solution.py:536
  85.7 17.8 %collective-permute-start.13 = (f32[16,64,128]{2,1,0:T(8,128)S(1)}, f32[16,64,128]{2,1,0:T(8,128)S(1)}, u32[]{:S(2)}, u32[]{:S(2)}) collective-permute-start(f32[16,64,128]{2,1,0:T(8,128)S(1)} %shard_map.147.refs_2_), channel_id=1, source_target_pairs={{0,2},{1,3},{2,0},{3,1},{4,6},{5,7},{6,4},{7,5},{8,10},{9,11},{10,... | collective-permute-start | bytes 1572872 | tf_op jit(solution)/shard_map/ppermute | solution.py:532
  97.3 6.9 %collective-permute-start.22 = (f32[16,64,128]{2,1,0:T(8,128)S(1)}, f32[16,64,128]{2,1,0:T(8,128)S(1)}, u32[]{:S(2)}, u32[]{:S(2)}) collective-permute-start(f32[16,64,128]{2,1,0:T(8,128)S(1)} %shard_map.150.refs_1_.refs_3_), channel_id=1, source_target_pairs={{0,8},{8,0},{16,24},{24,16},{1,9},{9,1},{17,25},{25,17},{2,10},{10... | collective-permute-start | bytes 1572872 | tf_op jit(solution)/shard_map/ppermute | solution.py:536
  97.3 6.9 %collective-permute-start.23 = (f32[16,64,128]{2,1,0:T(8,128)S(1)}, f32[16,64,128]{2,1,0:T(8,128)S(1)}, u32[]{:S(2)}, u32[]{:S(2)}) collective-permute-start(f32[16,64,128]{2,1,0:T(8,128)S(1)} %shard_map.153.refs_4_.refs_2_), channel_id=1, source_target_pairs={{0,8},{8,0},{16,24},{24,16},{1,9},{9,1},{17,25},{25,17},{2,10},{10... | collective-permute-start | bytes 1572872 | tf_op jit(solution)/shard_map/ppermute | solution.py:536
  103.7 13.8 %collective-permute-start.21 = (f32[16,64,128]{2,1,0:T(8,128)S(1)}, f32[16,64,128]{2,1,0:T(8,128)S(1)}, u32[]{:S(2)}, u32[]{:S(2)}) collective-permute-start(f32[16,64,128]{2,1,0:T(8,128)S(1)} %shard_map.154.refs_12_.refs_1_.refs_3_), channel_id=1, source_target_pairs={{0,16},{8,24},{16,0},{24,8},{1,17},{9,25},{17,1},{25,9},{2,18},{10... | collective-permute-start | bytes 1572872 | tf_op jit(solution)/shard_map/ppermute | solution.py:536
  104.2 17.6 %collective-permute-start.26 = (f32[16,64,128]{2,1,0:T(8,128)S(1)}, f32[16,64,128]{2,1,0:T(8,128)S(1)}, u32[]{:S(2)}, u32[]{:S(2)}) collective-permute-start(f32[16,64,128]{2,1,0:T(8,128)S(1)} %shard_map.154.refs_12_.refs_1_.refs_3_), channel_id=1, source_target_pairs={{0,8},{8,0},{16,24},{24,16},{1,9},{9,1},{17,25},{25,17},{2,10},{10... | collective-permute-start | bytes 1572872 | tf_op jit(solution)/shard_map/ppermute | solution.py:536
  117.4 4.5 %collective-permute-start.27 = (f32[16,64,128]{2,1,0:T(8,128)S(1)}, f32[16,64,128]{2,1,0:T(8,128)S(1)}, u32[]{:S(2)}, u32[]{:S(2)}) collective-permute-start(f32[16,64,128]{2,1,0:T(8,128)S(1)} %shard_map.156.refs_5_.refs_2_), channel_id=1, source_target_pairs={{0,8},{8,0},{16,24},{24,16},{1,9},{9,1},{17,25},{25,17},{2,10},{10... | collective-permute-start | bytes 1572872 | tf_op jit(solution)/shard_map/ppermute | solution.py:536
  117.4 16.3 %collective-permute-start.28 = (f32[16,64,128]{2,1,0:T(8,128)S(1)}, f32[16,64,128]{2,1,0:T(8,128)S(1)}, u32[]{:S(2)}, u32[]{:S(2)}) collective-permute-start(f32[16,64,128]{2,1,0:T(8,128)S(1)} %get-tuple-element.55.refs_1_.refs_2_.refs_4_), channel_id=1, source_target_pairs={{0,2},{1,3},{2,0},{3,1},{4,6},{5,7},{6,4},{7,5},{8,10},{9,11},{10,... | collective-permute-start | bytes 1572872 | tf_op jit(solution)/shard_map/ppermute | solution.py:532
  119.0 14.8 %collective-permute-start.31 = (f32[16,64,128]{2,1,0:T(8,128)S(1)}, f32[16,64,128]{2,1,0:T(8,128)S(1)}, u32[]{:S(2)}, u32[]{:S(2)}) collective-permute-start(f32[16,64,128]{2,1,0:T(8,128)S(1)} %get-tuple-element.55.refs_1_.refs_2_.refs_4_), channel_id=1, source_target_pairs={{2,4},{3,5},{4,2},{5,3},{10,12},{11,13},{12,10},{13,11},{18,20},{1... | collective-permute-start | bytes 1572872 | tf_op jit(solution)/shard_map/ppermute | solution.py:532
  126.0 20.9 %collective-permute-start.34 = (f32[16,64,128]{2,1,0:T(8,128)S(1)}, f32[16,64,128]{2,1,0:T(8,128)S(1)}, u32[]{:S(2)}, u32[]{:S(2)}) collective-permute-start(f32[16,64,128]{2,1,0:T(8,128)S(1)} %get-tuple-element.61.refs_6_.refs_3_.refs_5_), channel_id=1, source_target_pairs={{2,4},{3,5},{4,2},{5,3},{10,12},{11,13},{12,10},{13,11},{18,20},{1... | collective-permute-start | bytes 1572872 | tf_op jit(solution)/shard_map/ppermute | solution.py:532
  126.7 17.8 %collective-permute-start.33 = (f32[16,64,128]{2,1,0:T(8,128)S(1)}, f32[16,64,128]{2,1,0:T(8,128)S(1)}, u32[]{:S(2)}, u32[]{:S(2)}) collective-permute-start(f32[16,64,128]{2,1,0:T(8,128)S(1)} %get-tuple-element.61.refs_6_.refs_3_.refs_5_), channel_id=1, source_target_pairs={{0,2},{1,3},{2,0},{3,1},{4,6},{5,7},{6,4},{7,5},{8,10},{9,11},{10,... | collective-permute-start | bytes 1572872 | tf_op jit(solution)/shard_map/ppermute | solution.py:532
  133.8 20.9 %collective-permute-start.35 = (f32[16,64,128]{2,1,0:T(8,128)S(1)}, f32[16,64,128]{2,1,0:T(8,128)S(1)}, u32[]{:S(2)}, u32[]{:S(2)}) collective-permute-start(f32[16,64,128]{2,1,0:T(8,128)S(1)} %shard_map.161.refs_2_.refs_4_), channel_id=1, source_target_pairs={{2,0},{3,1},{4,6},{5,7},{10,8},{11,9},{12,14},{13,15},{18,16},{19,... | collective-permute-start | bytes 1572872 | tf_op jit(solution)/shard_map/ppermute | solution.py:532
  135.1 5.2 %collective-permute-start.30 = (f32[144,256]{1,0:T(8,128)S(1)}, f32[144,256]{1,0:T(8,128)S(1)}, u32[]{:S(2)}, u32[]{:S(2)}) collective-permute-start(f32[144,256]{1,0:T(8,128)S(1)} %get-tuple-element.62.refs_1_.refs_0_), channel_id=1, source_target_pairs={{0,1},{1,0},{2,3},{3,2},{4,5},{5,4},{6,7},{7,6},{8,9},{9,8},{10,11... | collective-permute-start | bytes 442376 | tf_op jit(solution)/shard_map/ppermute | solution.py:532
  136.6 37.4 %collective-permute-start.29 = (f32[16,64,128]{2,1,0:T(8,128)S(1)}, f32[16,64,128]{2,1,0:T(8,128)S(1)}, u32[]{:S(2)}, u32[]{:S(2)}) collective-permute-start(f32[16,64,128]{2,1,0:T(8,128)S(1)} %shard_map.160.refs_1_.refs_2_.refs_4_), channel_id=1, source_target_pairs={{2,4},{3,5},{4,2},{5,3},{10,12},{11,13},{12,10},{13,11},{18,20},{1... | collective-permute-start | bytes 1572872 | tf_op jit(solution)/shard_map/ppermute | solution.py:532
  145.2 30.4 %collective-permute-start.39 = (f32[16,64,128]{2,1,0:T(8,128)S(1)}, f32[16,64,128]{2,1,0:T(8,128)S(1)}, u32[]{:S(2)}, u32[]{:S(2)}) collective-permute-start(f32[16,64,128]{2,1,0:T(8,128)S(1)} %shard_map.164.refs_2_), channel_id=1, source_target_pairs={{0,1},{1,0},{2,3},{3,2},{4,5},{5,4},{6,7},{7,6},{8,9},{9,8},{10,11... | collective-permute-start | bytes 1572872 | tf_op jit(solution)/shard_map/ppermute | solution.py:532
  154.7 26.3 %collective-permute-start.38 = (f32[16,64,128]{2,1,0:T(8,128)S(1)}, f32[16,64,128]{2,1,0:T(8,128)S(1)}, u32[]{:S(2)}, u32[]{:S(2)}) collective-permute-start(f32[16,64,128]{2,1,0:T(8,128)S(1)} %shard_map.165.refs_8_.refs_3_.refs_5_), channel_id=1, source_target_pairs={{2,0},{3,1},{4,6},{5,7},{10,8},{11,9},{12,14},{13,15},{18,16},{19,... | collective-permute-start | bytes 1572872 | tf_op jit(solution)/shard_map/ppermute | solution.py:532
  156.0 25.9 %collective-permute-start.36 = (f32[16,64,128]{2,1,0:T(8,128)S(1)}, f32[16,64,128]{2,1,0:T(8,128)S(1)}, u32[]{:S(2)}, u32[]{:S(2)}) collective-permute-start(f32[16,64,128]{2,1,0:T(8,128)S(1)} %shard_map.163.refs_4_.refs_3_.refs_5_), channel_id=1, source_target_pairs={{2,4},{3,5},{4,2},{5,3},{10,12},{11,13},{12,10},{13,11},{18,20},{1... | collective-permute-start | bytes 1572872 | tf_op jit(solution)/shard_map/ppermute | solution.py:532
  156.7 16.0 %collective-permute-start.32 = (f32[144,256]{1,0:T(8,128)S(1)}, f32[144,256]{1,0:T(8,128)S(1)}, u32[]{:S(2)}, u32[]{:S(2)}) collective-permute-start(f32[144,256]{1,0:T(8,128)S(1)} %shard_map.162.refs_1_.refs_0_), channel_id=1, source_target_pairs={{0,2},{1,3},{2,0},{3,1},{4,6},{5,7},{6,4},{7,5},{8,10},{9,11},{10,... | collective-permute-start | bytes 442376 | tf_op jit(solution)/shard_map/ppermute | solution.py:532
  172.7 9.1 %collective-permute-start.37 = (f32[144,256]{1,0:T(8,128)S(1)}, f32[144,256]{1,0:T(8,128)S(1)}, u32[]{:S(2)}, u32[]{:S(2)}) collective-permute-start(f32[144,256]{1,0:T(8,128)S(1)} %shard_map.168.refs_1_.refs_0_), channel_id=1, source_target_pairs={{0,6},{1,7},{2,4},{3,5},{4,2},{5,3},{6,0},{7,1},{8,14},{9,15},{10,... | collective-permute-start | bytes 442376 | tf_op jit(solution)/shard_map/ppermute | solution.py:532
  174.1 18.8 %collective-permute-start.42 = (f32[16,64,128]{2,1,0:T(8,128)S(1)}, f32[16,64,128]{2,1,0:T(8,128)S(1)}, u32[]{:S(2)}, u32[]{:S(2)}) collective-permute-start(f32[16,64,128]{2,1,0:T(8,128)S(1)} %shard_map.167.refs_2_), channel_id=1, source_target_pairs={{0,1},{1,0},{2,3},{3,2},{4,5},{5,4},{6,7},{7,6},{8,9},{9,8},{10,11... | collective-permute-start | bytes 1572872 | tf_op jit(solution)/shard_map/ppermute | solution.py:532
  175.6 16.7 %collective-permute-start.40 = (f32[16,64,128]{2,1,0:T(8,128)S(1)}, f32[16,64,128]{2,1,0:T(8,128)S(1)}, u32[]{:S(2)}, u32[]{:S(2)}) collective-permute-start(f32[16,64,128]{2,1,0:T(8,128)S(1)} %shard_map.169.refs_8_.refs_2_.refs_4_), channel_id=1, source_target_pairs={{2,0},{3,1},{4,6},{5,7},{10,8},{11,9},{12,14},{13,15},{18,16},{19,... | collective-permute-start | bytes 1572872 | tf_op jit(solution)/shard_map/ppermute | solution.py:532
  181.9 19.9 %collective-permute-start.41 = (f32[16,64,128]{2,1,0:T(8,128)S(1)}, f32[16,64,128]{2,1,0:T(8,128)S(1)}, u32[]{:S(2)}, u32[]{:S(2)}) collective-permute-start(f32[16,64,128]{2,1,0:T(8,128)S(1)} %shard_map.173.refs_4_.refs_3_.refs_5_), channel_id=1, source_target_pairs={{2,0},{3,1},{4,6},{5,7},{10,8},{11,9},{12,14},{13,15},{18,16},{19,... | collective-permute-start | bytes 1572872 | tf_op jit(solution)/shard_map/ppermute | solution.py:532
  183.2 9.2 %collective-permute-start.43 = (f32[144,256]{1,0:T(8,128)S(1)}, f32[144,256]{1,0:T(8,128)S(1)}, u32[]{:S(2)}, u32[]{:S(2)}) collective-permute-start(f32[144,256]{1,0:T(8,128)S(1)} %shard_map.172.refs_1_), channel_id=1, source_target_pairs={{0,8},{8,0},{16,24},{24,16},{1,9},{9,1},{17,25},{25,17},{2,10},{10... | collective-permute-start | bytes 442376 | tf_op jit(solution)/shard_map/ppermute | solution.py:536
  183.3 20.7 %collective-permute-start.45 = (f32[16,64,128]{2,1,0:T(8,128)S(1)}, f32[16,64,128]{2,1,0:T(8,128)S(1)}, u32[]{:S(2)}, u32[]{:S(2)}) collective-permute-start(f32[16,64,128]{2,1,0:T(8,128)S(1)} %shard_map.171.refs_2_), channel_id=1, source_target_pairs={{0,1},{1,0},{2,3},{3,2},{4,5},{5,4},{6,7},{7,6},{8,9},{9,8},{10,11... | collective-permute-start | bytes 1572872 | tf_op jit(solution)/shard_map/ppermute | solution.py:532
  202.6 12.2 %collective-permute-start.44 = (f32[16,64,128]{2,1,0:T(8,128)S(1)}, f32[16,64,128]{2,1,0:T(8,128)S(1)}, u32[]{:S(2)}, u32[]{:S(2)}) collective-permute-start(f32[16,64,128]{2,1,0:T(8,128)S(1)} %shard_map.176.refs_11_), channel_id=1, source_target_pairs={{0,1},{1,0},{2,3},{3,2},{4,5},{5,4},{6,7},{7,6},{8,9},{9,8},{10,11... | collective-permute-start | bytes 1572872 | tf_op jit(solution)/shard_map/ppermute | solution.py:532
  203.5 7.2 %collective-permute-start.46 = (f32[2,144,256]{2,1,0:T(8,128)S(1)}, f32[2,144,256]{2,1,0:T(8,128)S(1)}, u32[]{:S(2)}, u32[]{:S(2)}) collective-permute-start(f32[2,144,256]{2,1,0:T(8,128)S(1)} %shard_map.174.refs_10_.refs_1_), channel_id=1, source_target_pairs={{0,16},{8,24},{16,0},{24,8},{1,17},{9,25},{17,1},{25,9},{2,18},{10... | collective-permute-start | bytes 884744 | tf_op jit(solution)/shard_map/ppermute | solution.py:536
  (11 other events, 73.1 us)

commit v6 on v5

--- a/solution.py
+++ b/solution.py
@@ -24,6 +24,10 @@
     if role == NEAR:
         return z + 1 - 2 * (z % 2)
     return z
+
+
+def inner_place(place):
+    return (place[0] == 1) | (place[0] == 2)
 
 
 def split(value):
@@ -139,6 +143,12 @@
         spec = self.full(*a.shape)
         return self.call(body, (), (1,), [spec] * 2, (a, b), spec, jax.ShapeDtypeStruct(a.shape, F32))
 
+    def added_across(self, place, a, across):
+        def body(place, a, across, out):
+            out[...] = a[...] + jnp.where(inner_place(place), across[...], 0.0)
+
+        return self.call(body, (place,), (1,), [self.dense_spec()] * 2, (a, across), self.dense_spec(), self.dense())
+
     def fetched(self, count):
         return [pltpu.VMEM((count, self.cap, TB, TB), F32), pltpu.SemaphoreType.DMA((count,))]
 
@@ -152,7 +162,8 @@
         groups = 4
         per_group = self.cap // groups
 
-        def body(place, cols, feats, tiles, out, held, buffer, sems):
+        def body(place, cols, feats, tiles, out, done, held, buffer, sems):
+            done[...] = jnp.zeros_like(done)
             owned_by = owner(role, place[0]) * 2 + 1 - place[1]
             copies = [pltpu.make_async_copy(feats, held, sems.at[groups])]
             for g in range(groups):
@@ -168,14 +179,15 @@
                     out[c] = times_tile_t(held[:, lanes(cols[owned_by, c])], buffer[c])
 
         return self.call(
-            body, (place, cols), (1,), [self.tiles_spec()] * 2, (feats, tiles), self.slots_spec(), self.slots(),
+            body, (place, cols), (1,), [self.tiles_spec()] * 2, (feats, tiles), [self.slots_spec(), self.full(8, TB)],
+            [self.slots(), jax.ShapeDtypeStruct((8, TB), F32)],
             scratch=[
                 pltpu.VMEM((self.slices, self.owned), F32),
                 pltpu.VMEM((self.cap, TB, TB), F32),
                 pltpu.SemaphoreType.DMA((groups + 1,)),
             ],
             vmem=FIRST_VMEM_BYTES,
-        )
+        )[0]
 
     def later_slots(self, roles, place, cols, feats, tiles):
         def body(place, cols, feats, tiles, *rest):
@@ -251,16 +263,16 @@
     def row_index(self, role, z, sender_x):
         return (owner(role, z) ^ z) * 2 + sender_x
 
-    def means(self, k, pieces, inverse):
-        def body(own, near, inner, inverse, out):
+    def means(self, k, place, pieces, inverse):
+        def body(place, own, near, across, inverse, out):
             for part in range(self.parts):
                 for j in range(self.per_piece):
                     spot, block = part * self.per_piece + j, self.block(k, part, j)
-                    total = own[spot] + near[spot] + inner[spot]
+                    total = own[spot] + near[spot] + jnp.where(inner_place(place), across[spot], 0.0)
                     out[spot] = total * inverse[block : block + 1, :]
 
         return self.call(
-            body, (), (1,), [self.dense_spec()] * 3 + [self.full(self.blocks, TB)], (*pieces, inverse),
+            body, (place,), (1,), [self.dense_spec()] * 3 + [self.full(self.blocks, TB)], (*pieces, inverse),
             self.dense_spec(), self.dense(),
         )
 
@@ -429,18 +441,18 @@
         )
 
     def gather(self, place, sources, held):
-        outer = (place[0] == 0) | (place[0] == 3)
+        inner = inner_place(place)
         for k in range(CHUNKS):
             spots = slice(k * self.per_chunk, (k + 1) * self.per_chunk)
             if len(sources) == CHUNKS:
                 held[spots] = sources[k][...]
             else:
 
-                @pl.when(outer)
+                @pl.when(jnp.logical_not(inner))
                 def _():
                     held[spots] = sources[CHUNKS + k][...]
 
-                @pl.when(jnp.logical_not(outer))
+                @pl.when(inner)
                 def _():
                     held[spots] = sources[k][...]
 
@@ -516,9 +528,7 @@
     return [(2 * a + x, 2 * b + x) for a, b in steps for x in range(2)]
 
 
-INWARD = pairs_z([(0, 1), (3, 2)])
-ACROSS = pairs_z([(1, 2), (2, 1)])
-OUTWARD = pairs_z([(1, 0), (2, 3)])
+ACROSS = pairs_z([(1, 2), (2, 1), (0, 0), (3, 3)])
 OTHER_X = [(n, n ^ 1) for n in range(8)]
 OTHER_CORE = [(f, f ^ 1) for f in range(4)]
 OTHER_Y = [(f, f ^ 2) for f in range(4)]
@@ -539,8 +549,8 @@
 ORDER = [
     ("slots_first",),
     ("table_out",),
+    ("tables_out",),
     ("load",),
-    ("tables_out",),
     ("slots_later",),
     ("rows_in",),
     ("dense", FAR_OUTER),
@@ -548,47 +558,49 @@
     ("send_in", FAR_OUTER, 1),
     ("pass_on", FAR_OUTER, 0),
     ("dense", FAR_INNER),
+    ("send_in", FAR_INNER, 1),
     ("slots", NEAR),
-    ("send_in", FAR_INNER, 1),
     ("pass_on", FAR_OUTER, 1),
-    ("slots", SELF),
     ("dense", NEAR),
     ("pass_on", FAR_INNER, 0),
-    ("feats_on",),
+    ("slots", SELF),
     ("pass_on", NEAR, 0),
     ("pass_on", NEAR, 1),
     ("pass_on", FAR_INNER, 1),
+    ("feats_on",),
     ("dense", SELF),
     ("mean", 0),
     ("cotangents_on",),
+    ("mean", 1),
+    ("means_on", 0),
     ("self_part",),
-    ("means_on", 0),
-    ("mean", 1),
+    ("means_on", 1),
     ("activate", 0),
-    ("means_on", 1),
+    ("activate", 1),
     ("weight", 0),
-    ("activate", 1),
+    ("inner_on", 0),
     ("weight", 1),
+    ("pick", SELF),
     ("near_on", 0),
-    ("inner_on", 0),
+    ("inner_on", 1),
+    ("near_on", 1),
     ("weight_sum", along_z(1)),
-    ("near_on", 1),
-    ("pick", SELF),
     ("wait", "inner", 0, 1),
-    ("inner_on", 1),
+    ("wait", "outer", 0, 0),
+    ("pick", NEAR),
+    ("outer_on", 0),
+    ("weight_sum", along_z(3)),
+    ("pick", FAR_INNER),
+    ("wait", "returned", SELF),
+    ("outer_on", 1),
     ("spread", SELF, None),
-    ("pick", NEAR),
-    ("weight_sum", along_z(3)),
-    ("outer_on", 0),
     ("spread", NEAR, SELF),
-    ("pick", FAR_INNER),
+    ("wait", "outer", 0, 1),
+    ("spread", FAR_INNER, NEAR),
     ("weight_sum", None),
-    ("outer_on", 1),
-    ("wait", "outer", 0, 1),
+    ("wait", "returned", FAR_INNER),
+    ("pick", FAR_OUTER),
     ("weight_cores",),
-    ("spread", FAR_INNER, NEAR),
-    ("pick", FAR_OUTER),
-    ("wait", "returned", FAR_INNER),
     ("spread", FAR_OUTER, FAR_INNER),
     ("weight_whole",),
     ("spread", None, FAR_OUTER),
@@ -659,15 +671,15 @@
         for k in range(CHUNKS):
             self.joined[role, k] = sums[k]
         if role in (FAR_OUTER, FAR_INNER):
-            self.inward[role, 0] = node_swap(sums[0], INWARD)
+            self.inward[role, 0] = node_swap(sums[0], along_z(1))
 
     def send_in(self, role, k):
         self.joined[role, k] = self.layer.relay(self.joined[role, k])
-        self.inward[role, k] = node_swap(self.joined[role, k], INWARD)
+        self.inward[role, k] = node_swap(self.joined[role, k], along_z(1))
 
     def pass_on(self, role, k):
         if role == NEAR:
-            part = self.layer.added(self.joined[NEAR, k], self.across[FAR_OUTER, k])
+            part = self.layer.added_across(self.place, self.joined[NEAR, k], self.across[FAR_OUTER, k])
             self.nearby[k] = node_swap(part, along_z(1))
         else:
             part = self.layer.added(self.joined[role, k], self.inward[role, k])
@@ -675,7 +687,7 @@
 
     def mean(self, k):
         pieces = (self.joined[SELF, k], self.nearby[k], self.across[FAR_INNER, k])
-        means = self.layer.means(k, pieces, self.inverse)
+        means = self.layer.means(k, self.place, pieces, self.inverse)
         self.means[k] = means
         self.mean_parts[k] = [means, feat_swap(means, OTHER_Y), feat_swap(means, OTHER_CORE)]
 
@@ -696,11 +708,11 @@
 
     def inner_on(self, k):
         self.inner[k][0] = self.layer.relay(self.inner[k][0])
-        self.inner[k].append(node_swap(self.inner[k][0], OUTWARD))
+        self.inner[k].append(node_swap(self.inner[k][0], along_z(1)))
 
     def outer_on(self, k):
         self.outer[k][0] = self.layer.relay(self.outer[k][0])
-        self.outer[k].append(node_swap(self.outer[k][0], OUTWARD))
+        self.outer[k].append(node_swap(self.outer[k][0], along_z(1)))
 
     def weight(self, k):
         back, weights = self.layer.weight_grad(

time: 220 us -> 225 us (1.023)
  waiting for transfers between devices: 87 us -> 95.4 us
  starting transfers between devices: 70.4 us -> 65.7 us
    ppermute x33, waiting for transfers between devices: 72.6 us -> 82.1 us  [node_swap(): return lax.ppermute(value, 'node', pairs)]
    ppermute x33, starting transfers between devices: 63.6 us -> 56.6 us  [node_swap(): return lax.ppermute(value, 'node', pairs)]
    ppermute x14, starting transfers between devices: 6.78 us -> 9.08 us  [feat_swap(): return lax.ppermute(value, 'feat', pairs)]
    unnamed x24 -> x25, local copies, waits for them, and re-layouts: 5.18 us -> 4.83 us
  transfers between devices with their start and end apart: 47 -> 47, of which waited for: 19 -> 16; matrix products, arithmetic and copies ran while one was open for 0% -> 0% of each run, Pallas kernels for 21% -> 20%
where the time goes in v6:
time: 225 us; the launch traced here: 224 us
  waiting for transfers between devices  95.4 us (42%)
  starting transfers between devices  65.7 us (29%)
  Pallas kernels  56.6 us (25%)
  local copies, waits for them, and re-layouts  4.83 us (2%)
    ppermute x33, waiting for transfers between devices, node_swap(): return lax.ppermute(value, 'node', pairs)  82.1 us
    ppermute x33, starting transfers between devices, node_swap(): return lax.ppermute(value, 'node', pairs)  56.6 us
    pallas_call x52, Pallas kernels, call(): pl.pallas_call(ordered, grid_spec=pltpu.PrefetchScalarGridSpec(num_scalar...  56.6 us
    ppermute x14, waiting for transfers between devices, feat_swap(): return lax.ppermute(value, 'feat', pairs)  13.4 us
    ppermute x14, starting transfers between devices, feat_swap(): return lax.ppermute(value, 'feat', pairs)  9.08 us
    unnamed x25, local copies, waits for them, and re-layouts  4.83 us
  transfers between devices with their start and end apart: 47, of which 16 were waited for; matrix products, arithmetic and copies ran while one was open for 0% of the time, Pallas kernels for 20%

profile of v6, /device:TPU:0, one launch (start us, length us, event | category | flops | bytes accessed | tf_op | source)
XLA Modules:
  0.0 224.5 jit_solution(5522841512304315486)
XLA Ops:
  1.3 3.9 %shard_map.128 = (f32[16,64,128]{2,1,0:T(8,128)}, f32[8,128]{1,0:T(8,128)}) custom-call(s32[4]{0:T(128)} %pad_add_fusion.refs_0_, s32[8,16]{1,0:T(8,128)} %refs_1_.27, f32[64,4096]{1,0:T(8,128)} %refs_0_.3, f32[8,16,128,128]{3,2,1,0:T(8,128)} %refs_1_.15), custom_call_target="tpu_custom_call" | custom-call | flops 1 | bytes 1 | tf_op jit(solution)/shard_map/pallas_call | solution.py:112
  5.2 3.0 %collective-permute-start.2 = (f32[16,64,128]{2,1,0:T(8,128)}, f32[16,64,128]{2,1,0:T(8,128)S(1)}, u32[]{:S(2)}, u32[]{:S(2)}) collective-permute-start(f32[16,64,128]{2,1,0:T(8,128)} %get-tuple-element.50), channel_id=1, source_target_pairs={{0,1},{1,0},{2,3},{3,2},{4,5},{5,4},{6,7},{7,6},{8,9},{9,8},{10,11... | collective-permute-start | bytes 1572872 | tf_op jit(solution)/shard_map/ppermute | solution.py:542
  8.9 1.6 collective-permute-start
  10.5 2.0 collective-permute-done.refs_1_
  12.5 2.6 %collective-permute-start.1 = (s32[16,16]{1,0:T(8,128)S(1)}, s32[16,16]{1,0:T(8,128)S(1)}, u32[]{:S(2)}, u32[]{:S(2)}) collective-permute-start(s32[16,16]{1,0:T(8,128)S(1)} %shard_map.130.refs_3_.refs_1_), channel_id=1, source_target_pairs={{0,4},{1,5},{2,6},{3,7},{4,0},{5,1},{6,2},{7,3},{8,12},{9,13},{10,... | collective-permute-start | bytes 3080 | tf_op jit(solution)/shard_map/ppermute | solution.py:542
  15.1 3.4 %copy-done = f32[8,16,128,128]{3,2,1,0:T(8,128)S(1)} copy-done((f32[8,16,128,128]{3,2,1,0:T(8,128)S(1)}, f32[8,16,128,128]{3,2,1,0:T(8,128)}, u32[]{:S(2)}) %copy-start) | copy-done | bytes 8388632
  19.5 2.2 shard_map.132
  23.7 1.6 collective-permute-start.4
  25.9 10.1 %collective-permute-done.4.refs_1_ = f32[16,64,128]{2,1,0:T(8,128)S(1)} collective-permute-done((f32[16,64,128]{2,1,0:T(8,128)S(1)}, f32[16,64,128]{2,1,0:T(8,128)S(1)}, u32[]{:S(2)}, u32[]{:S(2)}) %collective-permute-start.4) | collective-permute-done | bytes 524320 | tf_op jit(solution)/shard_map/ppermute | solution.py:542
  39.7 1.6 collective-permute-start.6
  41.3 1.5 collective-permute-start.9
  43.5 10.3 %collective-permute-done.7.refs_1_ = f32[16,64,128]{2,1,0:T(8,128)S(1)} collective-permute-done((f32[16,64,128]{2,1,0:T(8,128)S(1)}, f32[16,64,128]{2,1,0:T(8,128)S(1)}, u32[]{:S(2)}, u32[]{:S(2)}) %collective-permute-start.7) | collective-permute-done | bytes 524320 | tf_op jit(solution)/shard_map/ppermute | solution.py:542
  54.6 3.3 %collective-permute-start.10 = (f32[16,64,128]{2,1,0:T(8,128)S(1)}, f32[16,64,128]{2,1,0:T(8,128)S(1)}, u32[]{:S(2)}, u32[]{:S(2)}) collective-permute-start(f32[16,64,128]{2,1,0:T(8,128)S(1)} %shard_map.139.refs_2_.refs_0_), channel_id=1, source_target_pairs={{0,2},{1,3},{2,0},{3,1},{4,6},{5,7},{6,4},{7,5},{8,10},{9,11},{10,... | collective-permute-start | bytes 1572872 | tf_op jit(solution)/shard_map/ppermute | solution.py:542
  57.8 7.2 %collective-permute-done.6.refs_1_ = f32[16,64,128]{2,1,0:T(8,128)S(1)} collective-permute-done((f32[16,64,128]{2,1,0:T(8,128)S(1)}, f32[16,64,128]{2,1,0:T(8,128)S(1)}, u32[]{:S(2)}, u32[]{:S(2)}) %collective-permute-start.6) | collective-permute-done | bytes 524320 | tf_op jit(solution)/shard_map/ppermute | solution.py:542
  65.0 1.5 collective-permute-start.15
  69.6 6.7 %collective-permute-done.10.refs_1_ = f32[16,64,128]{2,1,0:T(8,128)S(1)} collective-permute-done((f32[16,64,128]{2,1,0:T(8,128)S(1)}, f32[16,64,128]{2,1,0:T(8,128)S(1)}, u32[]{:S(2)}, u32[]{:S(2)}) %collective-permute-start.10) | collective-permute-done | bytes 524320 | tf_op jit(solution)/shard_map/ppermute | solution.py:542
  78.4 5.3 %collective-permute-done.16.refs_2_ = f32[16,64,128]{2,1,0:T(8,128)S(1)} collective-permute-done((f32[16,64,128]{2,1,0:T(8,128)S(1)}, f32[16,64,128]{2,1,0:T(8,128)S(1)}, u32[]{:S(2)}, u32[]{:S(2)}) %collective-permute-start.16) | collective-permute-done | bytes 524320 | tf_op jit(solution)/shard_map/ppermute | solution.py:542
  86.7 1.6 collective-permute-start.21
  88.3 9.7 %collective-permute-done.13.refs_2_ = f32[16,64,128]{2,1,0:T(8,128)S(1)} collective-permute-done((f32[16,64,128]{2,1,0:T(8,128)S(1)}, f32[16,64,128]{2,1,0:T(8,128)S(1)}, u32[]{:S(2)}, u32[]{:S(2)}) %collective-permute-start.13) | collective-permute-done | bytes 524320 | tf_op jit(solution)/shard_map/ppermute | solution.py:542
  98.7 2.2 collective-permute-done.21.refs_0_
  100.9 1.5 collective-permute-start.18
  103.0 4.9 %shard_map.154.refs_1_.refs_6_ = f32[2,256,2048]{2,1,0:T(8,128)S(1)} custom-call(s32[4]{0:T(128)S(1)} %copy-done.6, f32[64,4096]{1,0:T(8,128)S(1)} %get-tuple-element.44.refs_2_.refs_3_.refs_1_, f32[64,4096]{1,0:T(8,128)S(1)} %shard_map.148.refs_6_.refs_2_, f32[64,4096]{1,0:T(8,128)S(1)} %collective-permute-done.19.refs_3_, ...), custom_call_target="tpu_custom_call" | custom-call | flops 1 | bytes 1 | tf_op jit(solution)/shard_map/pallas_call | solution.py:112
  107.9 6.3 %collective-permute-done.18.refs_0_ = f32[16,64,128]{2,1,0:T(8,128)S(1)} collective-permute-done((f32[16,64,128]{2,1,0:T(8,128)S(1)}, f32[16,64,128]{2,1,0:T(8,128)S(1)}, u32[]{:S(2)}, u32[]{:S(2)}) %collective-permute-start.18) | collective-permute-done | bytes 524320 | tf_op jit(solution)/shard_map/ppermute | solution.py:546
  114.7 4.1 %shard_map.156 = (f32[1024,256]{1,0:T(8,128)}, f32[256,2048]{1,0:T(8,128)S(1)}, f32[16,64,128]{2,1,0:T(8,128)S(1)}) custom-call(s32[4]{0:T(128)S(1)} %copy-done.6, f32[16,64,128]{2,1,0:T(8,128)S(1)} %shard_map.150.refs_1_.refs_3_, f32[16,64,128]{2,1,0:T(8,128)S(1)} %shard_map.153.refs_7_.refs_2_, f32[16,64,128]{2,1,0:T(8,128)S(1)} %collective-permute-done.26.refs_3_, ...), custom_call_target="tpu_custom_call" | custom-call | flops 1 | bytes 1 | tf_op jit(solution)/shard_map/pallas_call | solution.py:112
  119.7 10.4 %collective-permute-start.28 = (f32[16,64,128]{2,1,0:T(8,128)S(1)}, f32[16,64,128]{2,1,0:T(8,128)S(1)}, u32[]{:S(2)}, u32[]{:S(2)}) collective-permute-start(f32[16,64,128]{2,1,0:T(8,128)S(1)} %get-tuple-element.60.refs_13_.refs_2_.refs_4_), channel_id=1, source_target_pairs={{0,2},{1,3},{2,0},{3,1},{4,6},{5,7},{6,4},{7,5},{8,10},{9,11},{10,... | collective-permute-start | bytes 1572872 | tf_op jit(solution)/shard_map/ppermute | solution.py:542
  130.0 4.1 %shard_map.157 = (f32[1024,256]{1,0:T(8,128)}, f32[256,2048]{1,0:T(8,128)S(1)}, f32[16,64,128]{2,1,0:T(8,128)S(1)}) custom-call(s32[4]{0:T(128)S(1)} %copy-done.6, f32[16,64,128]{2,1,0:T(8,128)S(1)} %shard_map.152.refs_1_.refs_3_, f32[16,64,128]{2,1,0:T(8,128)S(1)} %shard_map.155.refs_12_.refs_2_, ...), custom_call_target="tpu_custom_call", output_to_operand_aliasing={{0}: (12, {})} | custom-call | flops 1 | bytes 1 | tf_op jit(solution)/shard_map/pallas_call | solution.py:112
  134.8 1.6 collective-permute-start.31
  136.4 2.0 shard_map.158
  138.4 4.3 %collective-permute-start.33 = (f32[16,64,128]{2,1,0:T(8,128)S(1)}, f32[16,64,128]{2,1,0:T(8,128)S(1)}, u32[]{:S(2)}, u32[]{:S(2)}) collective-permute-start(f32[16,64,128]{2,1,0:T(8,128)S(1)} %shard_map.159.refs_6_.refs_2_.refs_4_), channel_id=1, source_target_pairs={{0,2},{1,3},{2,0},{3,1},{4,6},{5,7},{6,4},{7,5},{8,10},{9,11},{10,... | collective-permute-start | bytes 1572872 | tf_op jit(solution)/shard_map/ppermute | solution.py:542
  142.8 2.1 shard_map.160
  144.8 1.5 collective-permute-start.34
  147.9 6.1 %collective-permute-start.37 = (f32[16,64,128]{2,1,0:T(8,128)S(1)}, f32[16,64,128]{2,1,0:T(8,128)S(1)}, u32[]{:S(2)}, u32[]{:S(2)}) collective-permute-start(f32[16,64,128]{2,1,0:T(8,128)S(1)} %shard_map.163.refs_1_.refs_3_.refs_5_), channel_id=1, source_target_pairs={{0,2},{1,3},{2,0},{3,1},{4,6},{5,7},{6,4},{7,5},{8,10},{9,11},{10,... | collective-permute-start | bytes 1572872 | tf_op jit(solution)/shard_map/ppermute | solution.py:542
  154.0 1.5 collective-permute-start.36
  156.2 9.0 %collective-permute-done.33.refs_4_.refs_6_ = f32[16,64,128]{2,1,0:T(8,128)S(1)} collective-permute-done((f32[16,64,128]{2,1,0:T(8,128)S(1)}, f32[16,64,128]{2,1,0:T(8,128)S(1)}, u32[]{:S(2)}, u32[]{:S(2)}) %collective-permute-start.33) | collective-permute-done | bytes 524320 | tf_op jit(solution)/shard_map/ppermute | solution.py:542
  165.2 2.1 collective-permute-start.38
  168.2 11.4 %collective-permute-done.38.refs_1_ = f32[144,256]{1,0:T(8,128)S(1)} collective-permute-done((f32[144,256]{1,0:T(8,128)S(1)}, f32[144,256]{1,0:T(8,128)S(1)}, u32[]{:S(2)}, u32[]{:S(2)}) %collective-permute-start.38) | collective-permute-done | bytes 147488 | tf_op jit(solution)/shard_map/ppermute | solution.py:542
  179.6 1.5 collective-permute-start.43
  182.0 2.1 collective-permute-start.40
  185.9 2.3 %shard_map.171 = (f32[64,4096]{1,0:T(8,128)}, f32[8,128]{1,0:T(8,128)S(1)}) custom-call(s32[4]{0:T(128)S(1)} %copy-done.6, s32[8,16]{1,0:T(8,128)S(1)} %copy-done.5, s32[8,16]{1,0:T(8,128)S(1)} %shard_map.133.refs_2_.refs_6_.refs_1_, f32[8,16,128,128]{3,2,1,0:T(8,128)S(1)} %get-tuple-element.45.refs_3_.refs_4_, ...), custom_call_target="tpu_custom_call" | custom-call | flops 1 | bytes 1 | tf_op jit(solution)/shard_map/pallas_call | solution.py:112
  188.2 4.1 %shard_map.172 = (f32[64,4096]{1,0:T(8,128)}, f32[8,128]{1,0:T(8,128)S(1)}) custom-call(s32[4]{0:T(128)S(1)} %copy-done.6, s32[8,16]{1,0:T(8,128)S(1)} %copy-done.5, s32[8,16]{1,0:T(8,128)S(1)} %shard_map.133.refs_2_.refs_6_.refs_1_, f32[8,16,128,128]{3,2,1,0:T(8,128)S(1)} %get-tuple-element.45.refs_3_.refs_4_, ...), custom_call_target="tpu_custom_call", output_to_operand_aliasing={{0}: (7, {})} | custom-call | flops 1 | bytes 1 | tf_op jit(solution)/shard_map/pallas_call | solution.py:112
  192.3 2.2 collective-permute-done.43.refs_8_
  194.5 4.0 %shard_map.173 = (f32[64,4096]{1,0:T(8,128)}, f32[8,128]{1,0:T(8,128)S(1)}) custom-call(s32[4]{0:T(128)S(1)} %copy-done.6, s32[8,16]{1,0:T(8,128)S(1)} %copy-done.5, s32[8,16]{1,0:T(8,128)S(1)} %shard_map.133.refs_2_.refs_6_.refs_1_, f32[8,16,128,128]{3,2,1,0:T(8,128)S(1)} %get-tuple-element.45.refs_3_.refs_4_, ...), custom_call_target="tpu_custom_call", output_to_operand_aliasing={{0}: (9, {})} | custom-call | flops 1 | bytes 1 | tf_op jit(solution)/shard_map/pallas_call | solution.py:112
  198.6 6.8 %collective-permute-done.42.refs_1_ = f32[144,256]{1,0:T(8,128)S(1)} collective-permute-done((f32[144,256]{1,0:T(8,128)S(1)}, f32[144,256]{1,0:T(8,128)S(1)}, u32[]{:S(2)}, u32[]{:S(2)}) %collective-permute-start.42) | collective-permute-done | bytes 147488 | tf_op jit(solution)/shard_map/ppermute | solution.py:542
  206.2 1.5 collective-permute-start.44
  209.7 1.6 collective-permute-start.46
  211.3 4.1 %shard_map.177 = (f32[64,4096]{1,0:T(8,128)}, f32[8,128]{1,0:T(8,128)S(1)}) custom-call(s32[4]{0:T(128)S(1)} %copy-done.6, s32[8,16]{1,0:T(8,128)S(1)} %copy-done.5, s32[8,16]{1,0:T(8,128)S(1)} %shard_map.133.refs_2_.refs_6_.refs_1_, f32[8,16,128,128]{3,2,1,0:T(8,128)S(1)} %get-tuple-element.45.refs_3_.refs_4_, ...), custom_call_target="tpu_custom_call", output_to_operand_aliasing={{0}: (9, {})} | custom-call | flops 1 | bytes 1 | tf_op jit(solution)/shard_map/pallas_call | solution.py:112
  215.4 3.4 %collective-permute-done.46.refs_2_ = f32[2,144,256]{2,1,0:T(8,128)S(1)} collective-permute-done((f32[2,144,256]{2,1,0:T(8,128)S(1)}, f32[2,144,256]{2,1,0:T(8,128)S(1)}, u32[]{:S(2)}, u32[]{:S(2)}) %collective-permute-start.46) | collective-permute-done | bytes 294944 | tf_op jit(solution)/shard_map/ppermute | solution.py:546
  220.8 3.5 %shard_map.179 = (f32[64,4096]{1,0:T(8,128)}, f32[8,128]{1,0:T(8,128)}) custom-call(s32[4]{0:T(128)S(1)} %copy-done.6, s32[8,16]{1,0:T(8,128)S(1)} %copy-done.5, s32[8,16]{1,0:T(8,128)S(1)} %shard_map.133.refs_2_.refs_6_.refs_1_, f32[8,16,128,128]{3,2,1,0:T(8,128)S(1)} %get-tuple-element.45.refs_3_.refs_4_, ...), custom_call_target="tpu_custom_call", output_to_operand_aliasing={{0}: (5, {})} | custom-call | flops 1 | bytes 1 | tf_op jit(solution)/shard_map/pallas_call | solution.py:112
  (125 shorter events, 31.7 us)
Async XLA Ops:
  5.2 17.1 %collective-permute-start.2 = (f32[16,64,128]{2,1,0:T(8,128)}, f32[16,64,128]{2,1,0:T(8,128)S(1)}, u32[]{:S(2)}, u32[]{:S(2)}) collective-permute-start(f32[16,64,128]{2,1,0:T(8,128)} %get-tuple-element.50), channel_id=1, source_target_pairs={{0,1},{1,0},{2,3},{3,2},{4,5},{5,4},{6,7},{7,6},{8,9},{9,8},{10,11... | collective-permute-start | bytes 1572872 | tf_op jit(solution)/shard_map/ppermute | solution.py:542
  8.9 3.6 %collective-permute-start = (s32[8,16]{1,0:T(8,128)S(1)}, s32[8,16]{1,0:T(8,128)S(1)}, u32[]{:S(2)}, u32[]{:S(2)}) collective-permute-start(s32[8,16]{1,0:T(8,128)S(1)} %shard_map.129.refs_0_.refs_2_), channel_id=1, source_target_pairs={{0,2},{1,3},{2,0},{3,1},{4,6},{5,7},{6,4},{7,5},{8,10},{9,11},{10,... | collective-permute-start | bytes 1544 | tf_op jit(solution)/shard_map/ppermute | solution.py:542
  12.5 9.2 %collective-permute-start.1 = (s32[16,16]{1,0:T(8,128)S(1)}, s32[16,16]{1,0:T(8,128)S(1)}, u32[]{:S(2)}, u32[]{:S(2)}) collective-permute-start(s32[16,16]{1,0:T(8,128)S(1)} %shard_map.130.refs_3_.refs_1_), channel_id=1, source_target_pairs={{0,4},{1,5},{2,6},{3,7},{4,0},{5,1},{6,2},{7,3},{8,12},{9,13},{10,... | collective-permute-start | bytes 3080 | tf_op jit(solution)/shard_map/ppermute | solution.py:542
  23.7 12.3 %collective-permute-start.4 = (f32[16,64,128]{2,1,0:T(8,128)S(1)}, f32[16,64,128]{2,1,0:T(8,128)S(1)}, u32[]{:S(2)}, u32[]{:S(2)}) collective-permute-start(f32[16,64,128]{2,1,0:T(8,128)S(1)} %get-tuple-element.52.refs_0_), channel_id=1, source_target_pairs={{0,2},{1,3},{2,0},{3,1},{4,6},{5,7},{6,4},{7,5},{8,10},{9,11},{10,... | collective-permute-start | bytes 1572872 | tf_op jit(solution)/shard_map/ppermute | solution.py:542
  25.4 12.0 %collective-permute-start.3 = (f32[16,64,128]{2,1,0:T(8,128)S(1)}, f32[16,64,128]{2,1,0:T(8,128)S(1)}, u32[]{:S(2)}, u32[]{:S(2)}) collective-permute-start(f32[16,64,128]{2,1,0:T(8,128)S(1)} %shard_map.135.refs_1_), channel_id=1, source_target_pairs={{0,1},{1,0},{2,3},{3,2},{4,5},{5,4},{6,7},{7,6},{8,9},{9,8},{10,11... | collective-permute-start | bytes 1572872 | tf_op jit(solution)/shard_map/ppermute | solution.py:542
  38.9 14.9 %collective-permute-start.7 = (f32[16,64,128]{2,1,0:T(8,128)S(1)}, f32[16,64,128]{2,1,0:T(8,128)S(1)}, u32[]{:S(2)}, u32[]{:S(2)}) collective-permute-start(f32[16,64,128]{2,1,0:T(8,128)S(1)} %shard_map.136.refs_2_.refs_0_), channel_id=1, source_target_pairs={{0,2},{1,3},{2,0},{3,1},{4,6},{5,7},{6,4},{7,5},{8,10},{9,11},{10,... | collective-permute-start | bytes 1572872 | tf_op jit(solution)/shard_map/ppermute | solution.py:542
  39.4 15.2 %collective-permute-start.5 = (f32[16,64,128]{2,1,0:T(8,128)S(1)}, f32[16,64,128]{2,1,0:T(8,128)S(1)}, u32[]{:S(2)}, u32[]{:S(2)}) collective-permute-start(f32[16,64,128]{2,1,0:T(8,128)S(1)} %shard_map.140.refs_2_), channel_id=1, source_target_pairs={{0,1},{1,0},{2,3},{3,2},{4,5},{5,4},{6,7},{7,6},{8,9},{9,8},{10,11... | collective-permute-start | bytes 1572872 | tf_op jit(solution)/shard_map/ppermute | solution.py:542
  39.7 25.3 %collective-permute-start.6 = (f32[16,64,128]{2,1,0:T(8,128)S(1)}, f32[16,64,128]{2,1,0:T(8,128)S(1)}, u32[]{:S(2)}, u32[]{:S(2)}) collective-permute-start(f32[16,64,128]{2,1,0:T(8,128)S(1)} %get-tuple-element.54.refs_0_), channel_id=1, source_target_pairs={{0,2},{1,3},{2,0},{3,1},{4,6},{5,7},{6,4},{7,5},{8,10},{9,11},{10,... | collective-permute-start | bytes 1572872 | tf_op jit(solution)/shard_map/ppermute | solution.py:542
  41.3 36.4 %collective-permute-start.9 = (f32[64,4096]{1,0:T(8,128)S(1)}, f32[64,4096]{1,0:T(8,128)S(1)}, u32[]{:S(2)}, u32[]{:S(2)}) collective-permute-start(f32[64,4096]{1,0:T(8,128)S(1)} %get-tuple-element.44.refs_2_.refs_3_.refs_1_), channel_id=1, source_target_pairs={{0,16},{8,24},{16,0},{24,8},{1,17},{9,25},{17,1},{25,9},{2,18},{10... | collective-permute-start | bytes 3145736 | tf_op jit(solution)/shard_map/ppermute | solution.py:546
  42.8 25.3 %collective-permute-start.12 = (f32[16,64,128]{2,1,0:T(8,128)S(1)}, f32[16,64,128]{2,1,0:T(8,128)S(1)}, u32[]{:S(2)}, u32[]{:S(2)}) collective-permute-start(f32[16,64,128]{2,1,0:T(8,128)S(1)} %shard_map.137.refs_6_), channel_id=1, source_target_pairs={{2,4},{3,5},{4,2},{5,3},{0,0},{1,1},{6,6},{7,7},{10,12},{11,13},{1... | collective-permute-start | bytes 1572872 | tf_op jit(solution)/shard_map/ppermute | solution.py:542
  53.8 15.4 %collective-permute-start.11 = (f32[16,64,128]{2,1,0:T(8,128)S(1)}, f32[16,64,128]{2,1,0:T(8,128)S(1)}, u32[]{:S(2)}, u32[]{:S(2)}) collective-permute-start(f32[16,64,128]{2,1,0:T(8,128)S(1)} %shard_map.141.refs_6_), channel_id=1, source_target_pairs={{2,4},{3,5},{4,2},{5,3},{0,0},{1,1},{6,6},{7,7},{10,12},{11,13},{1... | collective-permute-start | bytes 1572872 | tf_op jit(solution)/shard_map/ppermute | solution.py:542
  54.6 21.7 %collective-permute-start.10 = (f32[16,64,128]{2,1,0:T(8,128)S(1)}, f32[16,64,128]{2,1,0:T(8,128)S(1)}, u32[]{:S(2)}, u32[]{:S(2)}) collective-permute-start(f32[16,64,128]{2,1,0:T(8,128)S(1)} %shard_map.139.refs_2_.refs_0_), channel_id=1, source_target_pairs={{0,2},{1,3},{2,0},{3,1},{4,6},{5,7},{6,4},{7,5},{8,10},{9,11},{10,... | collective-permute-start | bytes 1572872 | tf_op jit(solution)/shard_map/ppermute | solution.py:542
  65.0 21.7 %collective-permute-start.15 = (f32[256,1024]{1,0:T(8,128)S(1)}, f32[256,1024]{1,0:T(8,128)S(1)}, u32[]{:S(2)}, u32[]{:S(2)}) collective-permute-start(f32[256,1024]{1,0:T(8,128)S(1)} %get-tuple-element.46.refs_4_.refs_7_), channel_id=1, source_target_pairs={{0,16},{8,24},{16,0},{24,8},{1,17},{9,25},{17,1},{25,9},{2,18},{10... | collective-permute-start | bytes 3145736 | tf_op jit(solution)/shard_map/ppermute | solution.py:546
  68.1 16.4 %copy-start.11 = (s32[4096]{0:T(1024)S(1)}, s32[4096]{0:T(1024)}, u32[]{:S(2)}) copy-start(s32[4096]{0:T(1024)} %param.13) | copy-start | bytes 49156
  68.7 14.9 %collective-permute-start.16 = (f32[16,64,128]{2,1,0:T(8,128)S(1)}, f32[16,64,128]{2,1,0:T(8,128)S(1)}, u32[]{:S(2)}, u32[]{:S(2)}) collective-permute-start(f32[16,64,128]{2,1,0:T(8,128)S(1)} %shard_map.145.refs_3_), channel_id=1, source_target_pairs={{0,2},{1,3},{2,0},{3,1},{4,6},{5,7},{6,4},{7,5},{8,10},{9,11},{10,... | collective-permute-start | bytes 1572872 | tf_op jit(solution)/shard_map/ppermute | solution.py:542
  69.2 14.4 %collective-permute-start.8 = (f32[16,64,128]{2,1,0:T(8,128)S(1)}, f32[16,64,128]{2,1,0:T(8,128)S(1)}, u32[]{:S(2)}, u32[]{:S(2)}) collective-permute-start(f32[16,64,128]{2,1,0:T(8,128)S(1)} %shard_map.144.refs_3_), channel_id=1, source_target_pairs={{0,1},{1,0},{2,3},{3,2},{4,5},{5,4},{6,7},{7,6},{8,9},{9,8},{10,11... | collective-permute-start | bytes 1572872 | tf_op jit(solution)/shard_map/ppermute | solution.py:542
  76.3 8.1 %collective-permute-start.17 = (f32[16,64,128]{2,1,0:T(8,128)S(1)}, f32[16,64,128]{2,1,0:T(8,128)S(1)}, u32[]{:S(2)}, u32[]{:S(2)}) collective-permute-start(f32[16,64,128]{2,1,0:T(8,128)S(1)} %shard_map.143.refs_2_), channel_id=1, source_target_pairs={{2,4},{3,5},{4,2},{5,3},{0,0},{1,1},{6,6},{7,7},{10,12},{11,13},{1... | collective-permute-start | bytes 1572872 | tf_op jit(solution)/shard_map/ppermute | solution.py:542
  77.7 10.7 %collective-permute-start.14 = (f32[16,64,128]{2,1,0:T(8,128)S(1)}, f32[16,64,128]{2,1,0:T(8,128)S(1)}, u32[]{:S(2)}, u32[]{:S(2)}) collective-permute-start(f32[16,64,128]{2,1,0:T(8,128)S(1)} %shard_map.147.refs_1_), channel_id=1, source_target_pairs={{2,4},{3,5},{4,2},{5,3},{0,0},{1,1},{6,6},{7,7},{10,12},{11,13},{1... | collective-permute-start | bytes 1572872 | tf_op jit(solution)/shard_map/ppermute | solution.py:542
  83.7 18.8 %collective-permute-start.19 = (f32[64,4096]{1,0:T(8,128)S(1)}, f32[64,4096]{1,0:T(8,128)S(1)}, u32[]{:S(2)}, u32[]{:S(2)}) collective-permute-start(f32[64,4096]{1,0:T(8,128)S(1)} %get-tuple-element.44.refs_2_.refs_3_.refs_1_), channel_id=1, source_target_pairs={{0,8},{8,0},{16,24},{24,16},{1,9},{9,1},{17,25},{25,17},{2,10},{10... | collective-permute-start | bytes 3145736 | tf_op jit(solution)/shard_map/ppermute | solution.py:546
  83.7 14.3 %collective-permute-start.13 = (f32[16,64,128]{2,1,0:T(8,128)S(1)}, f32[16,64,128]{2,1,0:T(8,128)S(1)}, u32[]{:S(2)}, u32[]{:S(2)}) collective-permute-start(f32[16,64,128]{2,1,0:T(8,128)S(1)} %shard_map.146.refs_2_), channel_id=1, source_target_pairs={{0,2},{1,3},{2,0},{3,1},{4,6},{5,7},{6,4},{7,5},{8,10},{9,11},{10,... | collective-permute-start | bytes 1572872 | tf_op jit(solution)/shard_map/ppermute | solution.py:542
  84.3 18.1 %collective-permute-start.20 = (f32[64,4096]{1,0:T(8,128)S(1)}, f32[64,4096]{1,0:T(8,128)S(1)}, u32[]{:S(2)}, u32[]{:S(2)}) collective-permute-start(f32[64,4096]{1,0:T(8,128)S(1)} %shard_map.148.refs_6_.refs_2_), channel_id=1, source_target_pairs={{0,8},{8,0},{16,24},{24,16},{1,9},{9,1},{17,25},{25,17},{2,10},{10... | collective-permute-start | bytes 3145736 | tf_op jit(solution)/shard_map/ppermute | solution.py:546
  86.7 14.2 %collective-permute-start.21 = (f32[16,64,128]{2,1,0:T(8,128)S(1)}, f32[16,64,128]{2,1,0:T(8,128)S(1)}, u32[]{:S(2)}, u32[]{:S(2)}) collective-permute-start(f32[16,64,128]{2,1,0:T(8,128)S(1)} %shard_map.150.refs_1_.refs_3_), channel_id=1, source_target_pairs={{0,16},{8,24},{16,0},{24,8},{1,17},{9,25},{17,1},{25,9},{2,18},{10... | collective-permute-start | bytes 1572872 | tf_op jit(solution)/shard_map/ppermute | solution.py:546
  88.3 25.9 %collective-permute-start.24 = (f32[256,1024]{1,0:T(8,128)S(1)}, f32[256,1024]{1,0:T(8,128)S(1)}, u32[]{:S(2)}, u32[]{:S(2)}) collective-permute-start(f32[256,1024]{1,0:T(8,128)S(1)} %get-tuple-element.46.refs_4_.refs_7_), channel_id=1, source_target_pairs={{0,8},{8,0},{16,24},{24,16},{1,9},{9,1},{17,25},{25,17},{2,10},{10... | collective-permute-start | bytes 3145736 | tf_op jit(solution)/shard_map/ppermute | solution.py:546
  98.0 16.7 %collective-permute-start.25 = (f32[256,1024]{1,0:T(8,128)S(1)}, f32[256,1024]{1,0:T(8,128)S(1)}, u32[]{:S(2)}, u32[]{:S(2)}) collective-permute-start(f32[256,1024]{1,0:T(8,128)S(1)} %shard_map.151.refs_5_.refs_8_), channel_id=1, source_target_pairs={{0,8},{8,0},{16,24},{24,16},{1,9},{9,1},{17,25},{25,17},{2,10},{10... | collective-permute-start | bytes 3145736 | tf_op jit(solution)/shard_map/ppermute | solution.py:546
  100.9 13.3 %collective-permute-start.18 = (f32[16,64,128]{2,1,0:T(8,128)S(1)}, f32[16,64,128]{2,1,0:T(8,128)S(1)}, u32[]{:S(2)}, u32[]{:S(2)}) collective-permute-start(f32[16,64,128]{2,1,0:T(8,128)S(1)} %shard_map.152.refs_1_.refs_3_), channel_id=1, source_target_pairs={{0,16},{8,24},{16,0},{24,8},{1,17},{9,25},{17,1},{25,9},{2,18},{10... | collective-permute-start | bytes 1572872 | tf_op jit(solution)/shard_map/ppermute | solution.py:546
  102.4 12.3 %collective-permute-start.26 = (f32[16,64,128]{2,1,0:T(8,128)S(1)}, f32[16,64,128]{2,1,0:T(8,128)S(1)}, u32[]{:S(2)}, u32[]{:S(2)}) collective-permute-start(f32[16,64,128]{2,1,0:T(8,128)S(1)} %shard_map.150.refs_1_.refs_3_), channel_id=1, source_target_pairs={{0,8},{8,0},{16,24},{24,16},{1,9},{9,1},{17,25},{25,17},{2,10},{10... | collective-permute-start | bytes 1572872 | tf_op jit(solution)/shard_map/ppermute | solution.py:546
  102.5 12.3 %collective-permute-start.27 = (f32[16,64,128]{2,1,0:T(8,128)S(1)}, f32[16,64,128]{2,1,0:T(8,128)S(1)}, u32[]{:S(2)}, u32[]{:S(2)}) collective-permute-start(f32[16,64,128]{2,1,0:T(8,128)S(1)} %shard_map.153.refs_7_.refs_2_), channel_id=1, source_target_pairs={{0,8},{8,0},{16,24},{24,16},{1,9},{9,1},{17,25},{25,17},{2,10},{10... | collective-permute-start | bytes 1572872 | tf_op jit(solution)/shard_map/ppermute | solution.py:546
  114.2 15.8 %collective-permute-start.22 = (f32[16,64,128]{2,1,0:T(8,128)S(1)}, f32[16,64,128]{2,1,0:T(8,128)S(1)}, u32[]{:S(2)}, u32[]{:S(2)}) collective-permute-start(f32[16,64,128]{2,1,0:T(8,128)S(1)} %shard_map.152.refs_1_.refs_3_), channel_id=1, source_target_pairs={{0,8},{8,0},{16,24},{24,16},{1,9},{9,1},{17,25},{25,17},{2,10},{10... | collective-permute-start | bytes 1572872 | tf_op jit(solution)/shard_map/ppermute | solution.py:546
  114.2 15.8 %collective-permute-start.23 = (f32[16,64,128]{2,1,0:T(8,128)S(1)}, f32[16,64,128]{2,1,0:T(8,128)S(1)}, u32[]{:S(2)}, u32[]{:S(2)}) collective-permute-start(f32[16,64,128]{2,1,0:T(8,128)S(1)} %shard_map.155.refs_12_.refs_2_), channel_id=1, source_target_pairs={{0,8},{8,0},{16,24},{24,16},{1,9},{9,1},{17,25},{25,17},{2,10},{10... | collective-permute-start | bytes 1572872 | tf_op jit(solution)/shard_map/ppermute | solution.py:546
  118.8 19.6 %collective-permute-start.29 = (f32[16,64,128]{2,1,0:T(8,128)S(1)}, f32[16,64,128]{2,1,0:T(8,128)S(1)}, u32[]{:S(2)}, u32[]{:S(2)}) collective-permute-start(f32[16,64,128]{2,1,0:T(8,128)S(1)} %get-tuple-element.60.refs_13_.refs_2_.refs_4_), channel_id=1, source_target_pairs={{2,4},{3,5},{4,2},{5,3},{0,0},{1,1},{6,6},{7,7},{10,12},{11,13},{1... | collective-permute-start | bytes 1572872 | tf_op jit(solution)/shard_map/ppermute | solution.py:542
  119.7 27.5 %collective-permute-start.28 = (f32[16,64,128]{2,1,0:T(8,128)S(1)}, f32[16,64,128]{2,1,0:T(8,128)S(1)}, u32[]{:S(2)}, u32[]{:S(2)}) collective-permute-start(f32[16,64,128]{2,1,0:T(8,128)S(1)} %get-tuple-element.60.refs_13_.refs_2_.refs_4_), channel_id=1, source_target_pairs={{0,2},{1,3},{2,0},{3,1},{4,6},{5,7},{6,4},{7,5},{8,10},{9,11},{10,... | collective-permute-start | bytes 1572872 | tf_op jit(solution)/shard_map/ppermute | solution.py:542
  134.1 13.8 %collective-permute-start.32 = (f32[16,64,128]{2,1,0:T(8,128)S(1)}, f32[16,64,128]{2,1,0:T(8,128)S(1)}, u32[]{:S(2)}, u32[]{:S(2)}) collective-permute-start(f32[16,64,128]{2,1,0:T(8,128)S(1)} %get-tuple-element.62.refs_5_.refs_3_), channel_id=1, source_target_pairs={{2,4},{3,5},{4,2},{5,3},{0,0},{1,1},{6,6},{7,7},{10,12},{11,13},{1... | collective-permute-start | bytes 1572872 | tf_op jit(solution)/shard_map/ppermute | solution.py:542
  134.8 19.2 %collective-permute-start.31 = (f32[16,64,128]{2,1,0:T(8,128)S(1)}, f32[16,64,128]{2,1,0:T(8,128)S(1)}, u32[]{:S(2)}, u32[]{:S(2)}) collective-permute-start(f32[16,64,128]{2,1,0:T(8,128)S(1)} %get-tuple-element.62.refs_5_.refs_3_), channel_id=1, source_target_pairs={{0,2},{1,3},{2,0},{3,1},{4,6},{5,7},{6,4},{7,5},{8,10},{9,11},{10,... | collective-permute-start | bytes 1572872 | tf_op jit(solution)/shard_map/ppermute | solution.py:542
  138.4 26.8 %collective-permute-start.33 = (f32[16,64,128]{2,1,0:T(8,128)S(1)}, f32[16,64,128]{2,1,0:T(8,128)S(1)}, u32[]{:S(2)}, u32[]{:S(2)}) collective-permute-start(f32[16,64,128]{2,1,0:T(8,128)S(1)} %shard_map.159.refs_6_.refs_2_.refs_4_), channel_id=1, source_target_pairs={{0,2},{1,3},{2,0},{3,1},{4,6},{5,7},{6,4},{7,5},{8,10},{9,11},{10,... | collective-permute-start | bytes 1572872 | tf_op jit(solution)/shard_map/ppermute | solution.py:542
  144.8 10.7 %collective-permute-start.34 = (f32[144,256]{1,0:T(8,128)S(1)}, f32[144,256]{1,0:T(8,128)S(1)}, u32[]{:S(2)}, u32[]{:S(2)}) collective-permute-start(f32[144,256]{1,0:T(8,128)S(1)} %get-tuple-element.66.refs_4_.refs_0_), channel_id=1, source_target_pairs={{0,1},{1,0},{2,3},{3,2},{4,5},{5,4},{6,7},{7,6},{8,9},{9,8},{10,11... | collective-permute-start | bytes 442376 | tf_op jit(solution)/shard_map/ppermute | solution.py:542
  147.2 20.1 %collective-permute-start.30 = (f32[16,64,128]{2,1,0:T(8,128)S(1)}, f32[16,64,128]{2,1,0:T(8,128)S(1)}, u32[]{:S(2)}, u32[]{:S(2)}) collective-permute-start(f32[16,64,128]{2,1,0:T(8,128)S(1)} %shard_map.162.refs_1_.refs_2_.refs_4_), channel_id=1, source_target_pairs={{2,4},{3,5},{4,2},{5,3},{0,0},{1,1},{6,6},{7,7},{10,12},{11,13},{1... | collective-permute-start | bytes 1572872 | tf_op jit(solution)/shard_map/ppermute | solution.py:542
  147.9 33.2 %collective-permute-start.37 = (f32[16,64,128]{2,1,0:T(8,128)S(1)}, f32[16,64,128]{2,1,0:T(8,128)S(1)}, u32[]{:S(2)}, u32[]{:S(2)}) collective-permute-start(f32[16,64,128]{2,1,0:T(8,128)S(1)} %shard_map.163.refs_1_.refs_3_.refs_5_), channel_id=1, source_target_pairs={{0,2},{1,3},{2,0},{3,1},{4,6},{5,7},{6,4},{7,5},{8,10},{9,11},{10,... | collective-permute-start | bytes 1572872 | tf_op jit(solution)/shard_map/ppermute | solution.py:542
  154.0 28.0 %collective-permute-start.36 = (f32[16,64,128]{2,1,0:T(8,128)S(1)}, f32[16,64,128]{2,1,0:T(8,128)S(1)}, u32[]{:S(2)}, u32[]{:S(2)}) collective-permute-start(f32[16,64,128]{2,1,0:T(8,128)S(1)} %shard_map.161.refs_1_), channel_id=1, source_target_pairs={{0,1},{1,0},{2,3},{3,2},{4,5},{5,4},{6,7},{7,6},{8,9},{9,8},{10,11... | collective-permute-start | bytes 1572872 | tf_op jit(solution)/shard_map/ppermute | solution.py:542
  155.5 26.5 %collective-permute-start.35 = (f32[16,64,128]{2,1,0:T(8,128)S(1)}, f32[16,64,128]{2,1,0:T(8,128)S(1)}, u32[]{:S(2)}, u32[]{:S(2)}) collective-permute-start(f32[16,64,128]{2,1,0:T(8,128)S(1)} %shard_map.164.refs_2_.refs_3_.refs_5_), channel_id=1, source_target_pairs={{2,4},{3,5},{4,2},{5,3},{0,0},{1,1},{6,6},{7,7},{10,12},{11,13},{1... | collective-permute-start | bytes 1572872 | tf_op jit(solution)/shard_map/ppermute | solution.py:542
  165.2 14.4 %collective-permute-start.38 = (f32[144,256]{1,0:T(8,128)S(1)}, f32[144,256]{1,0:T(8,128)S(1)}, u32[]{:S(2)}, u32[]{:S(2)}) collective-permute-start(f32[144,256]{1,0:T(8,128)S(1)} %shard_map.165.refs_6_.refs_0_), channel_id=1, source_target_pairs={{0,2},{1,3},{2,0},{3,1},{4,6},{5,7},{6,4},{7,5},{8,10},{9,11},{10,... | collective-permute-start | bytes 442376 | tf_op jit(solution)/shard_map/ppermute | solution.py:542
  168.1 24.1 %collective-permute-start.39 = (f32[16,64,128]{2,1,0:T(8,128)S(1)}, f32[16,64,128]{2,1,0:T(8,128)S(1)}, u32[]{:S(2)}, u32[]{:S(2)}) collective-permute-start(f32[16,64,128]{2,1,0:T(8,128)S(1)} %shard_map.167.refs_2_.refs_4_), channel_id=1, source_target_pairs={{0,2},{1,3},{2,0},{3,1},{4,6},{5,7},{6,4},{7,5},{8,10},{9,11},{10,... | collective-permute-start | bytes 1572872 | tf_op jit(solution)/shard_map/ppermute | solution.py:542
  179.6 14.9 %collective-permute-start.43 = (f32[16,64,128]{2,1,0:T(8,128)S(1)}, f32[16,64,128]{2,1,0:T(8,128)S(1)}, u32[]{:S(2)}, u32[]{:S(2)}) collective-permute-start(f32[16,64,128]{2,1,0:T(8,128)S(1)} %shard_map.166.refs_1_), channel_id=1, source_target_pairs={{0,1},{1,0},{2,3},{3,2},{4,5},{5,4},{6,7},{7,6},{8,9},{9,8},{10,11... | collective-permute-start | bytes 1572872 | tf_op jit(solution)/shard_map/ppermute | solution.py:542
  182.0 23.3 %collective-permute-start.40 = (f32[16,64,128]{2,1,0:T(8,128)S(1)}, f32[16,64,128]{2,1,0:T(8,128)S(1)}, u32[]{:S(2)}, u32[]{:S(2)}) collective-permute-start(f32[16,64,128]{2,1,0:T(8,128)S(1)} %shard_map.170.refs_8_.refs_3_.refs_5_), channel_id=1, source_target_pairs={{0,2},{1,3},{2,0},{3,1},{4,6},{5,7},{6,4},{7,5},{8,10},{9,11},{10,... | collective-permute-start | bytes 1572872 | tf_op jit(solution)/shard_map/ppermute | solution.py:542
  184.1 21.2 %collective-permute-start.41 = (f32[16,64,128]{2,1,0:T(8,128)S(1)}, f32[16,64,128]{2,1,0:T(8,128)S(1)}, u32[]{:S(2)}, u32[]{:S(2)}) collective-permute-start(f32[16,64,128]{2,1,0:T(8,128)S(1)} %shard_map.169.refs_2_), channel_id=1, source_target_pairs={{0,1},{1,0},{2,3},{3,2},{4,5},{5,4},{6,7},{7,6},{8,9},{9,8},{10,11... | collective-permute-start | bytes 1572872 | tf_op jit(solution)/shard_map/ppermute | solution.py:542
  184.7 20.6 %collective-permute-start.42 = (f32[144,256]{1,0:T(8,128)S(1)}, f32[144,256]{1,0:T(8,128)S(1)}, u32[]{:S(2)}, u32[]{:S(2)}) collective-permute-start(f32[144,256]{1,0:T(8,128)S(1)} %shard_map.168.refs_6_.refs_0_), channel_id=1, source_target_pairs={{0,6},{1,7},{2,4},{3,5},{4,2},{5,3},{6,0},{7,1},{8,14},{9,15},{10,... | collective-permute-start | bytes 442376 | tf_op jit(solution)/shard_map/ppermute | solution.py:542
  206.2 14.0 %collective-permute-start.44 = (f32[16,64,128]{2,1,0:T(8,128)S(1)}, f32[16,64,128]{2,1,0:T(8,128)S(1)}, u32[]{:S(2)}, u32[]{:S(2)}) collective-permute-start(f32[16,64,128]{2,1,0:T(8,128)S(1)} %shard_map.175.refs_3_), channel_id=1, source_target_pairs={{0,1},{1,0},{2,3},{3,2},{4,5},{5,4},{6,7},{7,6},{8,9},{9,8},{10,11... | collective-permute-start | bytes 1572872 | tf_op jit(solution)/shard_map/ppermute | solution.py:542
  207.7 1.4 collective-permute-start.45
  209.7 9.1 %collective-permute-start.46 = (f32[2,144,256]{2,1,0:T(8,128)S(1)}, f32[2,144,256]{2,1,0:T(8,128)S(1)}, u32[]{:S(2)}, u32[]{:S(2)}) collective-permute-start(f32[2,144,256]{2,1,0:T(8,128)S(1)} %shard_map.176.refs_10_.refs_1_), channel_id=1, source_target_pairs={{0,16},{8,24},{16,0},{24,8},{1,17},{9,25},{17,1},{25,9},{2,18},{10... | collective-permute-start | bytes 884744 | tf_op jit(solution)/shard_map/ppermute | solution.py:546
  (11 other events, 80.7 us)

commit v7 on v6

--- a/solution.py
+++ b/solution.py
@@ -476,7 +476,7 @@
             self.slots_spec(), self.slots(), scratch=[self.held()],
         )
 
-    def spread(self, place, cols, rows, tiles, jobs, total=None, self_back=None):
+    def spread(self, place, cols, rows, tiles, jobs, total=None, self_back=None, last=False):
         counts = [len(sources) for _, sources in jobs]
         extra = [total] if self_back is None else list(self_back)
 
@@ -509,7 +509,8 @@
                         value = sources[0][c]
                     out[:, lanes(cols[owners[i], c])] += times_tile(value, buffer[i, c])
 
-        whole = self.full(self.slices, self.owned)
+        shape = (self.slices, self.owned)
+        whole = self.full(*shape)
         in_specs, args = [self.tiles_spec()], [tiles]
         for _, sources in jobs:
             in_specs += [self.slots_spec() if len(sources) == 1 else self.dense_spec()] * len(sources)
@@ -518,9 +519,12 @@
         args += extra
         return self.call(
             body, (place, cols, rows), (1,), in_specs, args, [whole, self.full(8, TB)],
-            [jax.ShapeDtypeStruct((self.slices, self.owned), F32), jax.ShapeDtypeStruct((8, TB), F32)],
+            [
+                jax.ShapeDtypeStruct(shape, F32) if last else pltpu.VMEM(shape, F32),
+                jax.ShapeDtypeStruct((8, TB), F32),
+            ],
             scratch=[self.held(), *self.fetched(len(jobs))],
-            aliases={3 + len(args) - 1: 0} if self_back is None else {},
+            aliases={} if last or self_back is not None else {3 + len(args) - 1: 0},
         )[0]
 
 
@@ -529,6 +533,7 @@
 
 
 ACROSS = pairs_z([(1, 2), (2, 1), (0, 0), (3, 3)])
+OUTWARD = pairs_z([(1, 0), (2, 3)])
 OTHER_X = [(n, n ^ 1) for n in range(8)]
 OTHER_CORE = [(f, f ^ 1) for f in range(4)]
 OTHER_Y = [(f, f ^ 2) for f in range(4)]
@@ -549,55 +554,56 @@
 ORDER = [
     ("slots_first",),
     ("table_out",),
+    ("load",),
     ("tables_out",),
-    ("load",),
     ("slots_later",),
     ("rows_in",),
     ("dense", FAR_OUTER),
     ("slots", FAR_INNER),
     ("send_in", FAR_OUTER, 1),
     ("pass_on", FAR_OUTER, 0),
+    ("slots", NEAR),
     ("dense", FAR_INNER),
+    ("pass_on", FAR_OUTER, 1),
     ("send_in", FAR_INNER, 1),
-    ("slots", NEAR),
-    ("pass_on", FAR_OUTER, 1),
     ("dense", NEAR),
+    ("feats_on",),
     ("pass_on", FAR_INNER, 0),
+    ("pass_on", NEAR, 0),
     ("slots", SELF),
-    ("pass_on", NEAR, 0),
+    ("pass_on", FAR_INNER, 1),
     ("pass_on", NEAR, 1),
-    ("pass_on", FAR_INNER, 1),
-    ("feats_on",),
+    ("cotangents_on",),
     ("dense", SELF),
     ("mean", 0),
-    ("cotangents_on",),
+    ("wait", "nearby", 1),
     ("mean", 1),
     ("means_on", 0),
     ("self_part",),
     ("means_on", 1),
     ("activate", 0),
     ("activate", 1),
+    ("pick", SELF),
     ("weight", 0),
+    ("weight", 1),
     ("inner_on", 0),
-    ("weight", 1),
-    ("pick", SELF),
     ("near_on", 0),
     ("inner_on", 1),
+    ("weight_sum", along_z(1)),
     ("near_on", 1),
-    ("weight_sum", along_z(1)),
     ("wait", "inner", 0, 1),
-    ("wait", "outer", 0, 0),
+    ("outer_on", 0),
+    ("spread", SELF, None),
     ("pick", NEAR),
-    ("outer_on", 0),
+    ("spread", NEAR, SELF),
     ("weight_sum", along_z(3)),
+    ("outer_on", 1),
     ("pick", FAR_INNER),
-    ("wait", "returned", SELF),
-    ("outer_on", 1),
-    ("spread", SELF, None),
-    ("spread", NEAR, SELF),
+    ("wait", "returned", NEAR),
+    ("wait", "weights_in"),
     ("wait", "outer", 0, 1),
+    ("weight_sum", None),
     ("spread", FAR_INNER, NEAR),
-    ("weight_sum", None),
     ("wait", "returned", FAR_INNER),
     ("pick", FAR_OUTER),
     ("weight_cores",),
@@ -708,11 +714,11 @@
 
     def inner_on(self, k):
         self.inner[k][0] = self.layer.relay(self.inner[k][0])
-        self.inner[k].append(node_swap(self.inner[k][0], along_z(1)))
+        self.inner[k].append(node_swap(self.inner[k][0], OUTWARD))
 
     def outer_on(self, k):
         self.outer[k][0] = self.layer.relay(self.outer[k][0])
-        self.outer[k].append(node_swap(self.outer[k][0], along_z(1)))
+        self.outer[k].append(node_swap(self.outer[k][0], OUTWARD))
 
     def weight(self, k):
         back, weights = self.layer.weight_grad(
@@ -751,7 +757,9 @@
         jobs += [] if slots is None else [(slots, [self.returned[slots]])]
         first = self.total is None
         back = [self.self_back[k] for k in range(CHUNKS)] if first else None
-        self.total = self.layer.spread(self.place, self.cols, self.rows, self.tiles, jobs, self.total, back)
+        self.total = self.layer.spread(
+            self.place, self.cols, self.rows, self.tiles, jobs, self.total, back, last=local is None
+        )
 
 
 def chain_shards(node_feats, tiles, send_col, recv_row, degree, w_self, w_neigh, bias, cotangent):

time: 225 us -> 213 us (0.947)
  starting transfers between devices: 65.7 us -> 47.1 us
  waiting for transfers between devices: 95.4 us -> 110 us
  Pallas kernels: 56.6 us -> 48.2 us
    ppermute x33, starting transfers between devices: 56.6 us -> 41.2 us  [node_swap(): return lax.ppermute(value, 'node', pairs)]
    pallas_call x52, Pallas kernels: 56.6 us -> 48.2 us  [call(): pl.pallas_call(ordered, grid_spec=pltpu.PrefetchScalarGridSpec(num_scalar...]
    ppermute x14, waiting for transfers between devices: 13.4 us -> 21.3 us  [feat_swap(): return lax.ppermute(value, 'feat', pairs)]
    ppermute x33, waiting for transfers between devices: 82.1 us -> 88.9 us  [node_swap(): return lax.ppermute(value, 'node', pairs)]
    ppermute x14, starting transfers between devices: 9.08 us -> 5.96 us  [feat_swap(): return lax.ppermute(value, 'feat', pairs)]
    unnamed x25 -> x24, local copies, waits for them, and re-layouts: 4.83 us -> 4.79 us
  transfers between devices with their start and end apart: 47 -> 47, of which waited for: 16 -> 18; matrix products, arithmetic and copies ran while one was open for 0% -> 0% of each run, Pallas kernels for 20% -> 19%
where the time goes in v7:
time: 213 us; the launch traced here: 212 us
  waiting for transfers between devices  110 us (52%)
  Pallas kernels  48.2 us (23%)
  starting transfers between devices  47.1 us (22%)
  local copies, waits for them, and re-layouts  4.79 us (2%)
    ppermute x33, waiting for transfers between devices, node_swap(): return lax.ppermute(value, 'node', pairs)  88.9 us
    pallas_call x52, Pallas kernels, call(): pl.pallas_call(ordered, grid_spec=pltpu.PrefetchScalarGridSpec(num_scalar...  48.2 us
    ppermute x33, starting transfers between devices, node_swap(): return lax.ppermute(value, 'node', pairs)  41.2 us
    ppermute x14, waiting for transfers between devices, feat_swap(): return lax.ppermute(value, 'feat', pairs)  21.3 us
    ppermute x14, starting transfers between devices, feat_swap(): return lax.ppermute(value, 'feat', pairs)  5.96 us
    unnamed x24, local copies, waits for them, and re-layouts  4.79 us
  transfers between devices with their start and end apart: 47, of which 18 were waited for; matrix products, arithmetic and copies ran while one was open for 0% of the time, Pallas kernels for 19%

profile of v7, /device:TPU:0, one launch (start us, length us, event | category | flops | bytes accessed | tf_op | source)
XLA Modules:
  0.0 212.3 jit_solution(8279388803994106988)
XLA Ops:
  1.3 3.9 %shard_map.128 = (f32[16,64,128]{2,1,0:T(8,128)}, f32[8,128]{1,0:T(8,128)}) custom-call(s32[4]{0:T(128)} %pad_add_fusion.refs_0_, s32[8,16]{1,0:T(8,128)} %refs_1_.27, f32[64,4096]{1,0:T(8,128)} %refs_0_.3, f32[8,16,128,128]{3,2,1,0:T(8,128)} %refs_1_.15), custom_call_target="tpu_custom_call" | custom-call | flops 1 | bytes 1 | tf_op jit(solution)/shard_map/pallas_call | solution.py:112
  5.2 3.0 %collective-permute-start.2 = (f32[16,64,128]{2,1,0:T(8,128)}, f32[16,64,128]{2,1,0:T(8,128)S(1)}, u32[]{:S(2)}, u32[]{:S(2)}) collective-permute-start(f32[16,64,128]{2,1,0:T(8,128)} %get-tuple-element.50), channel_id=1, source_target_pairs={{0,1},{1,0},{2,3},{3,2},{4,5},{5,4},{6,7},{7,6},{8,9},{9,8},{10,11... | collective-permute-start | bytes 1572872 | tf_op jit(solution)/shard_map/ppermute | solution.py:547
  8.9 1.6 collective-permute-start
  10.5 3.4 %copy-done = f32[8,16,128,128]{3,2,1,0:T(8,128)S(1)} copy-done((f32[8,16,128,128]{3,2,1,0:T(8,128)S(1)}, f32[8,16,128,128]{3,2,1,0:T(8,128)}, u32[]{:S(2)}) %copy-start) | copy-done | bytes 8388632
  14.9 2.7 %collective-permute-start.1 = (s32[16,16]{1,0:T(8,128)S(1)}, s32[16,16]{1,0:T(8,128)S(1)}, u32[]{:S(2)}, u32[]{:S(2)}) collective-permute-start(s32[16,16]{1,0:T(8,128)S(1)} %shard_map.131.refs_4_.refs_1_), channel_id=1, source_target_pairs={{0,4},{1,5},{2,6},{3,7},{4,0},{5,1},{6,2},{7,3},{8,12},{9,13},{10,... | collective-permute-start | bytes 3080 | tf_op jit(solution)/shard_map/ppermute | solution.py:547
  17.5 1.5 collective-permute-start.9
  19.0 2.2 %shard_map.132 = (f32[16,64,128]{2,1,0:T(8,128)S(1)}, f32[16,64,128]{2,1,0:T(8,128)S(1)}, f32[16,64,128]{2,1,0:T(8,128)S(1)}) custom-call(s32[4]{0:T(128)S(1)} %copy-done.6, s32[8,16]{1,0:T(8,128)S(1)} %copy-done.5, f32[64,4096]{1,0:T(8,128)S(1)} %get-tuple-element.45.refs_2_.refs_3_.refs_1_, f32[8,16,128,128]{3,2,1,0:T(8,128)S(1)} %get-tuple-element.46.refs_3_.refs_4_, ...), custom_call_target="tpu_custom_call" | custom-call | flops 1 | bytes 1 | tf_op jit(solution)/shard_map/pallas_call | solution.py:112
  21.8 1.5 shard_map.134
  23.8 1.4 collective-permute-start.3
  25.9 12.3 %collective-permute-done.4.refs_1_ = f32[16,64,128]{2,1,0:T(8,128)S(1)} collective-permute-done((f32[16,64,128]{2,1,0:T(8,128)S(1)}, f32[16,64,128]{2,1,0:T(8,128)S(1)}, u32[]{:S(2)}, u32[]{:S(2)}) %collective-permute-start.4) | collective-permute-done | bytes 524320 | tf_op jit(solution)/shard_map/ppermute | solution.py:547
  38.9 1.5 shard_map.139
  40.4 1.3 collective-permute-start.8
  42.4 7.1 %collective-permute-done.6.refs_1_ = f32[16,64,128]{2,1,0:T(8,128)S(1)} collective-permute-done((f32[16,64,128]{2,1,0:T(8,128)S(1)}, f32[16,64,128]{2,1,0:T(8,128)S(1)}, u32[]{:S(2)}, u32[]{:S(2)}) %collective-permute-start.6) | collective-permute-done | bytes 524320 | tf_op jit(solution)/shard_map/ppermute | solution.py:547
  50.1 1.4 collective-permute-start.13
  52.2 1.5 shard_map.142
  53.6 7.1 %collective-permute-done.8.refs_1_ = f32[16,64,128]{2,1,0:T(8,128)S(1)} collective-permute-done((f32[16,64,128]{2,1,0:T(8,128)S(1)}, f32[16,64,128]{2,1,0:T(8,128)S(1)}, u32[]{:S(2)}, u32[]{:S(2)}) %collective-permute-start.8) | collective-permute-done | bytes 524320 | tf_op jit(solution)/shard_map/ppermute | solution.py:547
  63.3 8.6 %collective-permute-done.13.refs_1_ = f32[16,64,128]{2,1,0:T(8,128)S(1)} collective-permute-done((f32[16,64,128]{2,1,0:T(8,128)S(1)}, f32[16,64,128]{2,1,0:T(8,128)S(1)}, u32[]{:S(2)}, u32[]{:S(2)}) %collective-permute-start.13) | collective-permute-done | bytes 524320 | tf_op jit(solution)/shard_map/ppermute | solution.py:547
  73.3 3.2 %collective-permute-start.14 = (f32[16,64,128]{2,1,0:T(8,128)S(1)}, f32[16,64,128]{2,1,0:T(8,128)S(1)}, u32[]{:S(2)}, u32[]{:S(2)}) collective-permute-start(f32[16,64,128]{2,1,0:T(8,128)S(1)} %shard_map.148.refs_1_), channel_id=1, source_target_pairs={{0,2},{1,3},{2,0},{3,1},{4,6},{5,7},{6,4},{7,5},{8,10},{9,11},{10,... | collective-permute-start | bytes 1572872 | tf_op jit(solution)/shard_map/ppermute | solution.py:547
  77.3 5.9 %collective-permute-done.16.refs_2_ = f32[16,64,128]{2,1,0:T(8,128)S(1)} collective-permute-done((f32[16,64,128]{2,1,0:T(8,128)S(1)}, f32[16,64,128]{2,1,0:T(8,128)S(1)}, u32[]{:S(2)}, u32[]{:S(2)}) %collective-permute-start.16) | collective-permute-done | bytes 524320 | tf_op jit(solution)/shard_map/ppermute | solution.py:547
  83.2 1.5 shard_map.150
  85.9 6.2 %collective-permute-done.14.refs_2_.refs_5_ = f32[16,64,128]{2,1,0:T(8,128)S(1)} collective-permute-done((f32[16,64,128]{2,1,0:T(8,128)S(1)}, f32[16,64,128]{2,1,0:T(8,128)S(1)}, u32[]{:S(2)}, u32[]{:S(2)}) %collective-permute-start.14) | collective-permute-done | bytes 524320 | tf_op jit(solution)/shard_map/ppermute | solution.py:547
  93.3 6.5 %collective-permute-done.21.refs_0_ = f32[16,64,128]{2,1,0:T(8,128)S(1)} collective-permute-done((f32[16,64,128]{2,1,0:T(8,128)S(1)}, f32[16,64,128]{2,1,0:T(8,128)S(1)}, u32[]{:S(2)}, u32[]{:S(2)}) %collective-permute-start.21) | collective-permute-done | bytes 524320 | tf_op jit(solution)/shard_map/ppermute | solution.py:551
  100.8 4.9 %shard_map.154.refs_1_.refs_6_ = f32[2,256,2048]{2,1,0:T(8,128)S(1)} custom-call(s32[4]{0:T(128)S(1)} %copy-done.6, f32[64,4096]{1,0:T(8,128)S(1)} %get-tuple-element.45.refs_2_.refs_3_.refs_1_, f32[64,4096]{1,0:T(8,128)S(1)} %shard_map.143.refs_2_, f32[64,4096]{1,0:T(8,128)S(1)} %collective-permute-done.19.refs_3_, ...), custom_call_target="tpu_custom_call" | custom-call | flops 1 | bytes 1 | tf_op jit(solution)/shard_map/pallas_call | solution.py:112
  105.7 7.6 %collective-permute-done.18.refs_0_ = f32[16,64,128]{2,1,0:T(8,128)S(1)} collective-permute-done((f32[16,64,128]{2,1,0:T(8,128)S(1)}, f32[16,64,128]{2,1,0:T(8,128)S(1)}, u32[]{:S(2)}, u32[]{:S(2)}) %collective-permute-start.18) | collective-permute-done | bytes 524320 | tf_op jit(solution)/shard_map/ppermute | solution.py:551
  113.8 4.1 %shard_map.156 = (f32[1024,256]{1,0:T(8,128)}, f32[256,2048]{1,0:T(8,128)S(1)}, f32[16,64,128]{2,1,0:T(8,128)S(1)}) custom-call(s32[4]{0:T(128)S(1)} %copy-done.6, f32[16,64,128]{2,1,0:T(8,128)S(1)} %shard_map.151.refs_6_.refs_1_.refs_3_, f32[16,64,128]{2,1,0:T(8,128)S(1)} %shard_map.153.refs_7_.refs_2_, f32[16,64,128]{2,1,0:T(8,128)S(1)} %collective-permute-done.26.refs_3_, ...), custom_call_target="tpu_custom_call" | custom-call | flops 1 | bytes 1 | tf_op jit(solution)/shard_map/pallas_call | solution.py:112
  119.7 4.0 %shard_map.157 = (f32[1024,256]{1,0:T(8,128)}, f32[256,2048]{1,0:T(8,128)S(1)}, f32[16,64,128]{2,1,0:T(8,128)S(1)}) custom-call(s32[4]{0:T(128)S(1)} %copy-done.6, f32[16,64,128]{2,1,0:T(8,128)S(1)} %shard_map.152.refs_1_.refs_3_, f32[16,64,128]{2,1,0:T(8,128)S(1)} %shard_map.155.refs_12_.refs_2_, ...), custom_call_target="tpu_custom_call", output_to_operand_aliasing={{0}: (12, {})} | custom-call | flops 1 | bytes 1 | tf_op jit(solution)/shard_map/pallas_call | solution.py:112
  124.4 3.9 %collective-permute-start.32 = (f32[16,64,128]{2,1,0:T(8,128)S(1)}, f32[16,64,128]{2,1,0:T(8,128)S(1)}, u32[]{:S(2)}, u32[]{:S(2)}) collective-permute-start(f32[16,64,128]{2,1,0:T(8,128)S(1)} %get-tuple-element.64.refs_3_.refs_4_.refs_5_), channel_id=1, source_target_pairs={{0,2},{1,3},{2,0},{3,1},{4,6},{5,7},{6,4},{7,5},{8,10},{9,11},{10,... | collective-permute-start | bytes 1572872 | tf_op jit(solution)/shard_map/ppermute | solution.py:547
  129.1 2.1 shard_map.159
  131.2 2.1 shard_map.160
  133.2 1.6 collective-permute-start.33
  138.5 6.3 %collective-permute-done.32.refs_0_ = f32[16,64,128]{2,1,0:T(8,128)S(1)} collective-permute-done((f32[16,64,128]{2,1,0:T(8,128)S(1)}, f32[16,64,128]{2,1,0:T(8,128)S(1)}, u32[]{:S(2)}, u32[]{:S(2)}) %collective-permute-start.32) | collective-permute-done | bytes 524320 | tf_op jit(solution)/shard_map/ppermute | solution.py:547
  145.5 1.3 collective-permute-start.40
  146.8 9.2 %collective-permute-done.31.refs_1_.refs_4_.refs_6_ = f32[16,64,128]{2,1,0:T(8,128)S(1)} collective-permute-done((f32[16,64,128]{2,1,0:T(8,128)S(1)}, f32[16,64,128]{2,1,0:T(8,128)S(1)}, u32[]{:S(2)}, u32[]{:S(2)}) %collective-permute-start.31) | collective-permute-done | bytes 524320 | tf_op jit(solution)/shard_map/ppermute | solution.py:547
  156.1 1.3 collective-permute-start.38
  157.4 1.3 shard_map.167
  160.1 1.9 shard_map.169
  162.1 8.4 %collective-permute-done.36.refs_1_ = f32[144,256]{1,0:T(8,128)S(1)} collective-permute-done((f32[144,256]{1,0:T(8,128)S(1)}, f32[144,256]{1,0:T(8,128)S(1)}, u32[]{:S(2)}, u32[]{:S(2)}) %collective-permute-start.36) | collective-permute-done | bytes 147488 | tf_op jit(solution)/shard_map/ppermute | solution.py:547
  173.2 3.4 %collective-permute-start.43 = (f32[144,256]{1,0:T(8,128)S(1)}, f32[144,256]{1,0:T(8,128)S(1)}, u32[]{:S(2)}, u32[]{:S(2)}) collective-permute-start(f32[144,256]{1,0:T(8,128)S(1)} %shard_map.170.refs_1_.refs_0_), channel_id=1, source_target_pairs={{0,6},{1,7},{2,4},{3,5},{4,2},{5,3},{6,0},{7,1},{8,14},{9,15},{10,... | collective-permute-start | bytes 442376 | tf_op jit(solution)/shard_map/ppermute | solution.py:547
  176.6 3.8 %collective-permute-done.43.refs_1_.refs_3_ = f32[144,256]{1,0:T(8,128)S(1)} collective-permute-done((f32[144,256]{1,0:T(8,128)S(1)}, f32[144,256]{1,0:T(8,128)S(1)}, u32[]{:S(2)}, u32[]{:S(2)}) %collective-permute-start.43) | collective-permute-done | bytes 147488 | tf_op jit(solution)/shard_map/ppermute | solution.py:547
  180.4 4.4 %collective-permute-done.38.refs_4_.refs_6_ = f32[16,64,128]{2,1,0:T(8,128)S(1)} collective-permute-done((f32[16,64,128]{2,1,0:T(8,128)S(1)}, f32[16,64,128]{2,1,0:T(8,128)S(1)}, u32[]{:S(2)}, u32[]{:S(2)}) %collective-permute-start.38) | collective-permute-done | bytes 524320 | tf_op jit(solution)/shard_map/ppermute | solution.py:547
  184.9 2.0 shard_map.174
  186.9 8.3 %collective-permute-done.39.refs_5_.refs_7_ = f32[16,64,128]{2,1,0:T(8,128)S(1)} collective-permute-done((f32[16,64,128]{2,1,0:T(8,128)S(1)}, f32[16,64,128]{2,1,0:T(8,128)S(1)}, u32[]{:S(2)}, u32[]{:S(2)}) %collective-permute-start.39) | collective-permute-done | bytes 524320 | tf_op jit(solution)/shard_map/ppermute | solution.py:547
  196.7 1.4 collective-permute-done.45.refs_2_
  198.6 1.3 collective-permute-start.46
  199.9 2.0 shard_map.177
  201.9 5.8 %collective-permute-done.46.refs_2_ = f32[2,144,256]{2,1,0:T(8,128)S(1)} collective-permute-done((f32[2,144,256]{2,1,0:T(8,128)S(1)}, f32[2,144,256]{2,1,0:T(8,128)S(1)}, u32[]{:S(2)}, u32[]{:S(2)}) %collective-permute-start.46) | collective-permute-done | bytes 294944 | tf_op jit(solution)/shard_map/ppermute | solution.py:551
  207.7 1.4 shard_map.178
  209.9 2.2 %shard_map.179 = (f32[64,4096]{1,0:T(8,128)}, f32[8,128]{1,0:T(8,128)}) custom-call(s32[4]{0:T(128)S(1)} %copy-done.6, s32[8,16]{1,0:T(8,128)S(1)} %copy-done.5, s32[8,16]{1,0:T(8,128)S(1)} %shard_map.133.refs_2_.refs_6_.refs_1_, f32[8,16,128,128]{3,2,1,0:T(8,128)S(1)} %get-tuple-element.46.refs_3_.refs_4_, ...), custom_call_target="tpu_custom_call" | custom-call | flops 1 | bytes 1 | tf_op jit(solution)/shard_map/pallas_call | solution.py:112
  (124 shorter events, 29.9 us)
Async XLA Ops:
  5.2 16.6 %collective-permute-start.2 = (f32[16,64,128]{2,1,0:T(8,128)}, f32[16,64,128]{2,1,0:T(8,128)S(1)}, u32[]{:S(2)}, u32[]{:S(2)}) collective-permute-start(f32[16,64,128]{2,1,0:T(8,128)} %get-tuple-element.50), channel_id=1, source_target_pairs={{0,1},{1,0},{2,3},{3,2},{4,5},{5,4},{6,7},{7,6},{8,9},{9,8},{10,11... | collective-permute-start | bytes 1572872 | tf_op jit(solution)/shard_map/ppermute | solution.py:547
  8.9 6.0 %collective-permute-start = (s32[8,16]{1,0:T(8,128)S(1)}, s32[8,16]{1,0:T(8,128)S(1)}, u32[]{:S(2)}, u32[]{:S(2)}) collective-permute-start(s32[8,16]{1,0:T(8,128)S(1)} %shard_map.129.refs_3_.refs_0_), channel_id=1, source_target_pairs={{0,2},{1,3},{2,0},{3,1},{4,6},{5,7},{6,4},{7,5},{8,10},{9,11},{10,... | collective-permute-start | bytes 1544 | tf_op jit(solution)/shard_map/ppermute | solution.py:547
  14.9 6.4 %collective-permute-start.1 = (s32[16,16]{1,0:T(8,128)S(1)}, s32[16,16]{1,0:T(8,128)S(1)}, u32[]{:S(2)}, u32[]{:S(2)}) collective-permute-start(s32[16,16]{1,0:T(8,128)S(1)} %shard_map.131.refs_4_.refs_1_), channel_id=1, source_target_pairs={{0,4},{1,5},{2,6},{3,7},{4,0},{5,1},{6,2},{7,3},{8,12},{9,13},{10,... | collective-permute-start | bytes 3080 | tf_op jit(solution)/shard_map/ppermute | solution.py:547
  17.5 32.5 %collective-permute-start.9 = (f32[64,4096]{1,0:T(8,128)S(1)}, f32[64,4096]{1,0:T(8,128)S(1)}, u32[]{:S(2)}, u32[]{:S(2)}) collective-permute-start(f32[64,4096]{1,0:T(8,128)S(1)} %get-tuple-element.45.refs_2_.refs_3_.refs_1_), channel_id=1, source_target_pairs={{0,16},{8,24},{16,0},{24,8},{1,17},{9,25},{17,1},{25,9},{2,18},{10... | collective-permute-start | bytes 3145736 | tf_op jit(solution)/shard_map/ppermute | solution.py:551
  23.3 14.9 %collective-permute-start.4 = (f32[16,64,128]{2,1,0:T(8,128)S(1)}, f32[16,64,128]{2,1,0:T(8,128)S(1)}, u32[]{:S(2)}, u32[]{:S(2)}) collective-permute-start(f32[16,64,128]{2,1,0:T(8,128)S(1)} %get-tuple-element.52.refs_0_), channel_id=1, source_target_pairs={{0,2},{1,3},{2,0},{3,1},{4,6},{5,7},{6,4},{7,5},{8,10},{9,11},{10,... | collective-permute-start | bytes 1572872 | tf_op jit(solution)/shard_map/ppermute | solution.py:547
  23.8 14.5 %collective-permute-start.3 = (f32[16,64,128]{2,1,0:T(8,128)S(1)}, f32[16,64,128]{2,1,0:T(8,128)S(1)}, u32[]{:S(2)}, u32[]{:S(2)}) collective-permute-start(f32[16,64,128]{2,1,0:T(8,128)S(1)} %shard_map.135.refs_1_), channel_id=1, source_target_pairs={{0,1},{1,0},{2,3},{3,2},{4,5},{5,4},{6,7},{7,6},{8,9},{9,8},{10,11... | collective-permute-start | bytes 1572872 | tf_op jit(solution)/shard_map/ppermute | solution.py:547
  25.2 24.3 %collective-permute-start.6 = (f32[16,64,128]{2,1,0:T(8,128)S(1)}, f32[16,64,128]{2,1,0:T(8,128)S(1)}, u32[]{:S(2)}, u32[]{:S(2)}) collective-permute-start(f32[16,64,128]{2,1,0:T(8,128)S(1)} %shard_map.136.refs_2_.refs_0_), channel_id=1, source_target_pairs={{0,2},{1,3},{2,0},{3,1},{4,6},{5,7},{6,4},{7,5},{8,10},{9,11},{10,... | collective-permute-start | bytes 1572872 | tf_op jit(solution)/shard_map/ppermute | solution.py:547
  38.3 13.2 %collective-permute-start.5 = (f32[16,64,128]{2,1,0:T(8,128)S(1)}, f32[16,64,128]{2,1,0:T(8,128)S(1)}, u32[]{:S(2)}, u32[]{:S(2)}) collective-permute-start(f32[16,64,128]{2,1,0:T(8,128)S(1)} %shard_map.138.refs_6_), channel_id=1, source_target_pairs={{0,1},{1,0},{2,3},{3,2},{4,5},{5,4},{6,7},{7,6},{8,9},{9,8},{10,11... | collective-permute-start | bytes 1572872 | tf_op jit(solution)/shard_map/ppermute | solution.py:547
  40.4 20.3 %collective-permute-start.8 = (f32[16,64,128]{2,1,0:T(8,128)S(1)}, f32[16,64,128]{2,1,0:T(8,128)S(1)}, u32[]{:S(2)}, u32[]{:S(2)}) collective-permute-start(f32[16,64,128]{2,1,0:T(8,128)S(1)} %get-tuple-element.55.refs_0_), channel_id=1, source_target_pairs={{0,2},{1,3},{2,0},{3,1},{4,6},{5,7},{6,4},{7,5},{8,10},{9,11},{10,... | collective-permute-start | bytes 1572872 | tf_op jit(solution)/shard_map/ppermute | solution.py:547
  41.7 19.1 %collective-permute-start.7 = (f32[16,64,128]{2,1,0:T(8,128)S(1)}, f32[16,64,128]{2,1,0:T(8,128)S(1)}, u32[]{:S(2)}, u32[]{:S(2)}) collective-permute-start(f32[16,64,128]{2,1,0:T(8,128)S(1)} %shard_map.137.refs_2_), channel_id=1, source_target_pairs={{2,4},{3,5},{4,2},{5,3},{0,0},{1,1},{6,6},{7,7},{10,12},{11,13},{1... | collective-permute-start | bytes 1572872 | tf_op jit(solution)/shard_map/ppermute | solution.py:547
  49.5 27.1 %collective-permute-start.11 = (f32[256,1024]{1,0:T(8,128)S(1)}, f32[256,1024]{1,0:T(8,128)S(1)}, u32[]{:S(2)}, u32[]{:S(2)}) collective-permute-start(f32[256,1024]{1,0:T(8,128)S(1)} %get-tuple-element.44.refs_2_.refs_7_), channel_id=1, source_target_pairs={{0,16},{8,24},{16,0},{24,8},{1,17},{9,25},{17,1},{25,9},{2,18},{10... | collective-permute-start | bytes 3145736 | tf_op jit(solution)/shard_map/ppermute | solution.py:551
  50.1 21.9 %collective-permute-start.13 = (f32[16,64,128]{2,1,0:T(8,128)S(1)}, f32[16,64,128]{2,1,0:T(8,128)S(1)}, u32[]{:S(2)}, u32[]{:S(2)}) collective-permute-start(f32[16,64,128]{2,1,0:T(8,128)S(1)} %shard_map.141.refs_6_.refs_0_), channel_id=1, source_target_pairs={{0,2},{1,3},{2,0},{3,1},{4,6},{5,7},{6,4},{7,5},{8,10},{9,11},{10,... | collective-permute-start | bytes 1572872 | tf_op jit(solution)/shard_map/ppermute | solution.py:547
  51.5 21.2 %collective-permute-start.12 = (f32[16,64,128]{2,1,0:T(8,128)S(1)}, f32[16,64,128]{2,1,0:T(8,128)S(1)}, u32[]{:S(2)}, u32[]{:S(2)}) collective-permute-start(f32[16,64,128]{2,1,0:T(8,128)S(1)} %shard_map.140.refs_1_), channel_id=1, source_target_pairs={{2,4},{3,5},{4,2},{5,3},{0,0},{1,1},{6,6},{7,7},{10,12},{11,13},{1... | collective-permute-start | bytes 1572872 | tf_op jit(solution)/shard_map/ppermute | solution.py:547
  61.4 21.8 %copy-start.11 = (s32[4096]{0:T(1024)S(1)}, s32[4096]{0:T(1024)}, u32[]{:S(2)}) copy-start(s32[4096]{0:T(1024)} %param.13) | copy-start | bytes 49156
  61.4 15.1 %collective-permute-start.10 = (f32[16,64,128]{2,1,0:T(8,128)S(1)}, f32[16,64,128]{2,1,0:T(8,128)S(1)}, u32[]{:S(2)}, u32[]{:S(2)}) collective-permute-start(f32[16,64,128]{2,1,0:T(8,128)S(1)} %shard_map.146.refs_2_), channel_id=1, source_target_pairs={{0,1},{1,0},{2,3},{3,2},{4,5},{5,4},{6,7},{7,6},{8,9},{9,8},{10,11... | collective-permute-start | bytes 1572872 | tf_op jit(solution)/shard_map/ppermute | solution.py:547
  62.0 21.1 %collective-permute-start.16 = (f32[16,64,128]{2,1,0:T(8,128)S(1)}, f32[16,64,128]{2,1,0:T(8,128)S(1)}, u32[]{:S(2)}, u32[]{:S(2)}) collective-permute-start(f32[16,64,128]{2,1,0:T(8,128)S(1)} %shard_map.145.refs_2_), channel_id=1, source_target_pairs={{0,2},{1,3},{2,0},{3,1},{4,6},{5,7},{6,4},{7,5},{8,10},{9,11},{10,... | collective-permute-start | bytes 1572872 | tf_op jit(solution)/shard_map/ppermute | solution.py:547
  71.9 12.7 %collective-permute-start.17 = (f32[16,64,128]{2,1,0:T(8,128)S(1)}, f32[16,64,128]{2,1,0:T(8,128)S(1)}, u32[]{:S(2)}, u32[]{:S(2)}) collective-permute-start(f32[16,64,128]{2,1,0:T(8,128)S(1)} %shard_map.144.refs_3_), channel_id=1, source_target_pairs={{2,4},{3,5},{4,2},{5,3},{0,0},{1,1},{6,6},{7,7},{10,12},{11,13},{1... | collective-permute-start | bytes 1572872 | tf_op jit(solution)/shard_map/ppermute | solution.py:547
  73.3 18.8 %collective-permute-start.14 = (f32[16,64,128]{2,1,0:T(8,128)S(1)}, f32[16,64,128]{2,1,0:T(8,128)S(1)}, u32[]{:S(2)}, u32[]{:S(2)}) collective-permute-start(f32[16,64,128]{2,1,0:T(8,128)S(1)} %shard_map.148.refs_1_), channel_id=1, source_target_pairs={{0,2},{1,3},{2,0},{3,1},{4,6},{5,7},{6,4},{7,5},{8,10},{9,11},{10,... | collective-permute-start | bytes 1572872 | tf_op jit(solution)/shard_map/ppermute | solution.py:547
  76.5 23.7 %collective-permute-start.19 = (f32[64,4096]{1,0:T(8,128)S(1)}, f32[64,4096]{1,0:T(8,128)S(1)}, u32[]{:S(2)}, u32[]{:S(2)}) collective-permute-start(f32[64,4096]{1,0:T(8,128)S(1)} %get-tuple-element.45.refs_2_.refs_3_.refs_1_), channel_id=1, source_target_pairs={{0,8},{8,0},{16,24},{24,16},{1,9},{9,1},{17,25},{25,17},{2,10},{10... | collective-permute-start | bytes 3145736 | tf_op jit(solution)/shard_map/ppermute | solution.py:551
  76.6 15.6 %collective-permute-start.15 = (f32[16,64,128]{2,1,0:T(8,128)S(1)}, f32[16,64,128]{2,1,0:T(8,128)S(1)}, u32[]{:S(2)}, u32[]{:S(2)}) collective-permute-start(f32[16,64,128]{2,1,0:T(8,128)S(1)} %shard_map.147.refs_3_), channel_id=1, source_target_pairs={{2,4},{3,5},{4,2},{5,3},{0,0},{1,1},{6,6},{7,7},{10,12},{11,13},{1... | collective-permute-start | bytes 1572872 | tf_op jit(solution)/shard_map/ppermute | solution.py:547
  83.2 17.1 %collective-permute-start.20 = (f32[64,4096]{1,0:T(8,128)S(1)}, f32[64,4096]{1,0:T(8,128)S(1)}, u32[]{:S(2)}, u32[]{:S(2)}) collective-permute-start(f32[64,4096]{1,0:T(8,128)S(1)} %shard_map.143.refs_2_), channel_id=1, source_target_pairs={{0,8},{8,0},{16,24},{24,16},{1,9},{9,1},{17,25},{25,17},{2,10},{10... | collective-permute-start | bytes 3145736 | tf_op jit(solution)/shard_map/ppermute | solution.py:551
  85.3 14.4 %collective-permute-start.21 = (f32[16,64,128]{2,1,0:T(8,128)S(1)}, f32[16,64,128]{2,1,0:T(8,128)S(1)}, u32[]{:S(2)}, u32[]{:S(2)}) collective-permute-start(f32[16,64,128]{2,1,0:T(8,128)S(1)} %shard_map.151.refs_6_.refs_1_.refs_3_), channel_id=1, source_target_pairs={{0,16},{8,24},{16,0},{24,8},{1,17},{9,25},{17,1},{25,9},{2,18},{10... | collective-permute-start | bytes 1572872 | tf_op jit(solution)/shard_map/ppermute | solution.py:551
  92.1 21.2 %collective-permute-start.24 = (f32[256,1024]{1,0:T(8,128)S(1)}, f32[256,1024]{1,0:T(8,128)S(1)}, u32[]{:S(2)}, u32[]{:S(2)}) collective-permute-start(f32[256,1024]{1,0:T(8,128)S(1)} %get-tuple-element.44.refs_2_.refs_7_), channel_id=1, source_target_pairs={{0,8},{8,0},{16,24},{24,16},{1,9},{9,1},{17,25},{25,17},{2,10},{10... | collective-permute-start | bytes 3145736 | tf_op jit(solution)/shard_map/ppermute | solution.py:551
  92.1 21.7 %collective-permute-start.25 = (f32[256,1024]{1,0:T(8,128)S(1)}, f32[256,1024]{1,0:T(8,128)S(1)}, u32[]{:S(2)}, u32[]{:S(2)}) collective-permute-start(f32[256,1024]{1,0:T(8,128)S(1)} %shard_map.149.refs_6_.refs_8_), channel_id=1, source_target_pairs={{0,8},{8,0},{16,24},{24,16},{1,9},{9,1},{17,25},{25,17},{2,10},{10... | collective-permute-start | bytes 3145736 | tf_op jit(solution)/shard_map/ppermute | solution.py:551
  99.7 13.6 %collective-permute-start.18 = (f32[16,64,128]{2,1,0:T(8,128)S(1)}, f32[16,64,128]{2,1,0:T(8,128)S(1)}, u32[]{:S(2)}, u32[]{:S(2)}) collective-permute-start(f32[16,64,128]{2,1,0:T(8,128)S(1)} %shard_map.152.refs_1_.refs_3_), channel_id=1, source_target_pairs={{0,16},{8,24},{16,0},{24,8},{1,17},{9,25},{17,1},{25,9},{2,18},{10... | collective-permute-start | bytes 1572872 | tf_op jit(solution)/shard_map/ppermute | solution.py:551
  100.3 13.6 %collective-permute-start.26 = (f32[16,64,128]{2,1,0:T(8,128)S(1)}, f32[16,64,128]{2,1,0:T(8,128)S(1)}, u32[]{:S(2)}, u32[]{:S(2)}) collective-permute-start(f32[16,64,128]{2,1,0:T(8,128)S(1)} %shard_map.151.refs_6_.refs_1_.refs_3_), channel_id=1, source_target_pairs={{0,8},{8,0},{16,24},{24,16},{1,9},{9,1},{17,25},{25,17},{2,10},{10... | collective-permute-start | bytes 1572872 | tf_op jit(solution)/shard_map/ppermute | solution.py:551
  100.3 13.6 %collective-permute-start.27 = (f32[16,64,128]{2,1,0:T(8,128)S(1)}, f32[16,64,128]{2,1,0:T(8,128)S(1)}, u32[]{:S(2)}, u32[]{:S(2)}) collective-permute-start(f32[16,64,128]{2,1,0:T(8,128)S(1)} %shard_map.153.refs_7_.refs_2_), channel_id=1, source_target_pairs={{0,8},{8,0},{16,24},{24,16},{1,9},{9,1},{17,25},{25,17},{2,10},{10... | collective-permute-start | bytes 1572872 | tf_op jit(solution)/shard_map/ppermute | solution.py:551
  113.3 6.4 %collective-permute-start.22 = (f32[16,64,128]{2,1,0:T(8,128)S(1)}, f32[16,64,128]{2,1,0:T(8,128)S(1)}, u32[]{:S(2)}, u32[]{:S(2)}) collective-permute-start(f32[16,64,128]{2,1,0:T(8,128)S(1)} %shard_map.152.refs_1_.refs_3_), channel_id=1, source_target_pairs={{0,8},{8,0},{16,24},{24,16},{1,9},{9,1},{17,25},{25,17},{2,10},{10... | collective-permute-start | bytes 1572872 | tf_op jit(solution)/shard_map/ppermute | solution.py:551
  113.3 6.4 %collective-permute-start.23 = (f32[16,64,128]{2,1,0:T(8,128)S(1)}, f32[16,64,128]{2,1,0:T(8,128)S(1)}, u32[]{:S(2)}, u32[]{:S(2)}) collective-permute-start(f32[16,64,128]{2,1,0:T(8,128)S(1)} %shard_map.155.refs_12_.refs_2_), channel_id=1, source_target_pairs={{0,8},{8,0},{16,24},{24,16},{1,9},{9,1},{17,25},{25,17},{2,10},{10... | collective-permute-start | bytes 1572872 | tf_op jit(solution)/shard_map/ppermute | solution.py:551
  117.9 16.9 %collective-permute-start.29 = (f32[16,64,128]{2,1,0:T(8,128)S(1)}, f32[16,64,128]{2,1,0:T(8,128)S(1)}, u32[]{:S(2)}, u32[]{:S(2)}) collective-permute-start(f32[16,64,128]{2,1,0:T(8,128)S(1)} %get-tuple-element.60.refs_13_.refs_2_.refs_4_), channel_id=1, source_target_pairs={{2,4},{3,5},{4,2},{5,3},{0,0},{1,1},{6,6},{7,7},{10,12},{11,13},{1... | collective-permute-start | bytes 1572872 | tf_op jit(solution)/shard_map/ppermute | solution.py:547
  118.8 17.3 %collective-permute-start.28 = (f32[16,64,128]{2,1,0:T(8,128)S(1)}, f32[16,64,128]{2,1,0:T(8,128)S(1)}, u32[]{:S(2)}, u32[]{:S(2)}) collective-permute-start(f32[16,64,128]{2,1,0:T(8,128)S(1)} %get-tuple-element.60.refs_13_.refs_2_.refs_4_), channel_id=1, source_target_pairs={{0,2},{1,3},{2,0},{3,1},{4,6},{5,7},{6,4},{7,5},{8,10},{9,11},{10,... | collective-permute-start | bytes 1572872 | tf_op jit(solution)/shard_map/ppermute | solution.py:547
  123.7 13.1 %collective-permute-start.34 = (f32[16,64,128]{2,1,0:T(8,128)S(1)}, f32[16,64,128]{2,1,0:T(8,128)S(1)}, u32[]{:S(2)}, u32[]{:S(2)}) collective-permute-start(f32[16,64,128]{2,1,0:T(8,128)S(1)} %get-tuple-element.64.refs_3_.refs_4_.refs_5_), channel_id=1, source_target_pairs={{2,4},{3,5},{4,2},{5,3},{0,0},{1,1},{6,6},{7,7},{10,12},{11,13},{1... | collective-permute-start | bytes 1572872 | tf_op jit(solution)/shard_map/ppermute | solution.py:547
  124.4 20.4 %collective-permute-start.32 = (f32[16,64,128]{2,1,0:T(8,128)S(1)}, f32[16,64,128]{2,1,0:T(8,128)S(1)}, u32[]{:S(2)}, u32[]{:S(2)}) collective-permute-start(f32[16,64,128]{2,1,0:T(8,128)S(1)} %get-tuple-element.64.refs_3_.refs_4_.refs_5_), channel_id=1, source_target_pairs={{0,2},{1,3},{2,0},{3,1},{4,6},{5,7},{6,4},{7,5},{8,10},{9,11},{10,... | collective-permute-start | bytes 1572872 | tf_op jit(solution)/shard_map/ppermute | solution.py:547
  133.2 5.3 %collective-permute-start.33 = (f32[144,256]{1,0:T(8,128)S(1)}, f32[144,256]{1,0:T(8,128)S(1)}, u32[]{:S(2)}, u32[]{:S(2)}) collective-permute-start(f32[144,256]{1,0:T(8,128)S(1)} %get-tuple-element.66.refs_1_.refs_0_), channel_id=1, source_target_pairs={{0,1},{1,0},{2,3},{3,2},{4,5},{5,4},{6,7},{7,6},{8,9},{9,8},{10,11... | collective-permute-start | bytes 442376 | tf_op jit(solution)/shard_map/ppermute | solution.py:547
  134.8 21.3 %collective-permute-start.31 = (f32[16,64,128]{2,1,0:T(8,128)S(1)}, f32[16,64,128]{2,1,0:T(8,128)S(1)}, u32[]{:S(2)}, u32[]{:S(2)}) collective-permute-start(f32[16,64,128]{2,1,0:T(8,128)S(1)} %shard_map.161.refs_1_.refs_2_.refs_4_), channel_id=1, source_target_pairs={{2,0},{3,1},{4,6},{5,7},{10,8},{11,9},{12,14},{13,15},{18,16},{19,... | collective-permute-start | bytes 1572872 | tf_op jit(solution)/shard_map/ppermute | solution.py:547
  136.1 20.0 %collective-permute-start.30 = (f32[16,64,128]{2,1,0:T(8,128)S(1)}, f32[16,64,128]{2,1,0:T(8,128)S(1)}, u32[]{:S(2)}, u32[]{:S(2)}) collective-permute-start(f32[16,64,128]{2,1,0:T(8,128)S(1)} %shard_map.162.refs_1_.refs_2_.refs_4_), channel_id=1, source_target_pairs={{2,4},{3,5},{4,2},{5,3},{0,0},{1,1},{6,6},{7,7},{10,12},{11,13},{1... | collective-permute-start | bytes 1572872 | tf_op jit(solution)/shard_map/ppermute | solution.py:547
  136.8 22.7 %collective-permute-start.37 = (f32[16,64,128]{2,1,0:T(8,128)S(1)}, f32[16,64,128]{2,1,0:T(8,128)S(1)}, u32[]{:S(2)}, u32[]{:S(2)}) collective-permute-start(f32[16,64,128]{2,1,0:T(8,128)S(1)} %shard_map.158.refs_5_), channel_id=1, source_target_pairs={{0,1},{1,0},{2,3},{3,2},{4,5},{5,4},{6,7},{7,6},{8,9},{9,8},{10,11... | collective-permute-start | bytes 1572872 | tf_op jit(solution)/shard_map/ppermute | solution.py:547
  144.8 25.7 %collective-permute-start.35 = (f32[16,64,128]{2,1,0:T(8,128)S(1)}, f32[16,64,128]{2,1,0:T(8,128)S(1)}, u32[]{:S(2)}, u32[]{:S(2)}) collective-permute-start(f32[16,64,128]{2,1,0:T(8,128)S(1)} %shard_map.165.refs_2_.refs_3_.refs_5_), channel_id=1, source_target_pairs={{2,4},{3,5},{4,2},{5,3},{0,0},{1,1},{6,6},{7,7},{10,12},{11,13},{1... | collective-permute-start | bytes 1572872 | tf_op jit(solution)/shard_map/ppermute | solution.py:547
  145.5 25.0 %collective-permute-start.40 = (f32[16,64,128]{2,1,0:T(8,128)S(1)}, f32[16,64,128]{2,1,0:T(8,128)S(1)}, u32[]{:S(2)}, u32[]{:S(2)}) collective-permute-start(f32[16,64,128]{2,1,0:T(8,128)S(1)} %shard_map.163.refs_2_.refs_3_.refs_5_), channel_id=1, source_target_pairs={{2,0},{3,1},{4,6},{5,7},{10,8},{11,9},{12,14},{13,15},{18,16},{19,... | collective-permute-start | bytes 1572872 | tf_op jit(solution)/shard_map/ppermute | solution.py:547
  156.1 14.4 %collective-permute-start.36 = (f32[144,256]{1,0:T(8,128)S(1)}, f32[144,256]{1,0:T(8,128)S(1)}, u32[]{:S(2)}, u32[]{:S(2)}) collective-permute-start(f32[144,256]{1,0:T(8,128)S(1)} %shard_map.164.refs_1_.refs_0_), channel_id=1, source_target_pairs={{0,2},{1,3},{2,0},{3,1},{4,6},{5,7},{6,4},{7,5},{8,10},{9,11},{10,... | collective-permute-start | bytes 442376 | tf_op jit(solution)/shard_map/ppermute | solution.py:547
  156.1 28.8 %collective-permute-start.38 = (f32[16,64,128]{2,1,0:T(8,128)S(1)}, f32[16,64,128]{2,1,0:T(8,128)S(1)}, u32[]{:S(2)}, u32[]{:S(2)}) collective-permute-start(f32[16,64,128]{2,1,0:T(8,128)S(1)} %shard_map.166.refs_8_.refs_2_.refs_4_), channel_id=1, source_target_pairs={{2,0},{3,1},{4,6},{5,7},{10,8},{11,9},{12,14},{13,15},{18,16},{19,... | collective-permute-start | bytes 1572872 | tf_op jit(solution)/shard_map/ppermute | solution.py:547
  159.5 20.9 %collective-permute-start.42 = (f32[16,64,128]{2,1,0:T(8,128)S(1)}, f32[16,64,128]{2,1,0:T(8,128)S(1)}, u32[]{:S(2)}, u32[]{:S(2)}) collective-permute-start(f32[16,64,128]{2,1,0:T(8,128)S(1)} %shard_map.168.refs_8_), channel_id=1, source_target_pairs={{0,1},{1,0},{2,3},{3,2},{4,5},{5,4},{6,7},{7,6},{8,9},{9,8},{10,11... | collective-permute-start | bytes 1572872 | tf_op jit(solution)/shard_map/ppermute | solution.py:547
  171.4 15.5 %collective-permute-start.41 = (f32[16,64,128]{2,1,0:T(8,128)S(1)}, f32[16,64,128]{2,1,0:T(8,128)S(1)}, u32[]{:S(2)}, u32[]{:S(2)}) collective-permute-start(f32[16,64,128]{2,1,0:T(8,128)S(1)} %shard_map.172.refs_5_), channel_id=1, source_target_pairs={{0,1},{1,0},{2,3},{3,2},{4,5},{5,4},{6,7},{7,6},{8,9},{9,8},{10,11... | collective-permute-start | bytes 1572872 | tf_op jit(solution)/shard_map/ppermute | solution.py:547
  172.0 23.3 %collective-permute-start.39 = (f32[16,64,128]{2,1,0:T(8,128)S(1)}, f32[16,64,128]{2,1,0:T(8,128)S(1)}, u32[]{:S(2)}, u32[]{:S(2)}) collective-permute-start(f32[16,64,128]{2,1,0:T(8,128)S(1)} %shard_map.171.refs_6_.refs_3_.refs_5_), channel_id=1, source_target_pairs={{2,0},{3,1},{4,6},{5,7},{10,8},{11,9},{12,14},{13,15},{18,16},{19,... | collective-permute-start | bytes 1572872 | tf_op jit(solution)/shard_map/ppermute | solution.py:547
  173.2 7.2 %collective-permute-start.43 = (f32[144,256]{1,0:T(8,128)S(1)}, f32[144,256]{1,0:T(8,128)S(1)}, u32[]{:S(2)}, u32[]{:S(2)}) collective-permute-start(f32[144,256]{1,0:T(8,128)S(1)} %shard_map.170.refs_1_.refs_0_), channel_id=1, source_target_pairs={{0,6},{1,7},{2,4},{3,5},{4,2},{5,3},{6,0},{7,1},{8,14},{9,15},{10,... | collective-permute-start | bytes 442376 | tf_op jit(solution)/shard_map/ppermute | solution.py:547
  196.1 13.1 %collective-permute-start.44 = (f32[16,64,128]{2,1,0:T(8,128)S(1)}, f32[16,64,128]{2,1,0:T(8,128)S(1)}, u32[]{:S(2)}, u32[]{:S(2)}) collective-permute-start(f32[16,64,128]{2,1,0:T(8,128)S(1)} %shard_map.175.refs_3_), channel_id=1, source_target_pairs={{0,1},{1,0},{2,3},{3,2},{4,5},{5,4},{6,7},{7,6},{8,9},{9,8},{10,11... | collective-permute-start | bytes 1572872 | tf_op jit(solution)/shard_map/ppermute | solution.py:547
  196.7 1.4 collective-permute-start.45
  198.6 9.1 %collective-permute-start.46 = (f32[2,144,256]{2,1,0:T(8,128)S(1)}, f32[2,144,256]{2,1,0:T(8,128)S(1)}, u32[]{:S(2)}, u32[]{:S(2)}) collective-permute-start(f32[2,144,256]{2,1,0:T(8,128)S(1)} %shard_map.176.refs_10_.refs_1_), channel_id=1, source_target_pairs={{0,16},{8,24},{16,0},{24,8},{1,17},{9,25},{17,1},{25,9},{2,18},{10... | collective-permute-start | bytes 884744 | tf_op jit(solution)/shard_map/ppermute | solution.py:551
  (11 other events, 80.8 us)

commit v8 on v7

--- a/solution.py
+++ b/solution.py
@@ -555,59 +555,63 @@
     ("slots_first",),
     ("table_out",),
     ("load",),
+    ("slots_later",),
     ("tables_out",),
-    ("slots_later",),
     ("rows_in",),
     ("dense", FAR_OUTER),
     ("slots", FAR_INNER),
     ("send_in", FAR_OUTER, 1),
     ("pass_on", FAR_OUTER, 0),
+    ("dense", FAR_INNER),
     ("slots", NEAR),
-    ("dense", FAR_INNER),
     ("pass_on", FAR_OUTER, 1),
     ("send_in", FAR_INNER, 1),
     ("dense", NEAR),
     ("feats_on",),
+    ("slots", SELF),
+    ("pass_on", NEAR, 0),
     ("pass_on", FAR_INNER, 0),
-    ("pass_on", NEAR, 0),
-    ("slots", SELF),
-    ("pass_on", FAR_INNER, 1),
     ("pass_on", NEAR, 1),
     ("cotangents_on",),
+    ("pass_on", FAR_INNER, 1),
     ("dense", SELF),
     ("mean", 0),
-    ("wait", "nearby", 1),
     ("mean", 1),
     ("means_on", 0),
     ("self_part",),
     ("means_on", 1),
     ("activate", 0),
     ("activate", 1),
+    ("inner_on", 0),
+    ("weight", 0),
+    ("near_on", 0),
+    ("weight", 1),
     ("pick", SELF),
-    ("weight", 0),
-    ("weight", 1),
-    ("inner_on", 0),
-    ("near_on", 0),
+    ("wait", "inner", 1, 0),
+    ("wait", "near", 1),
     ("inner_on", 1),
+    ("near_on", 1),
+    ("pick", NEAR),
     ("weight_sum", along_z(1)),
-    ("near_on", 1),
     ("wait", "inner", 0, 1),
     ("outer_on", 0),
+    ("wait", "inner", 1, 1),
     ("spread", SELF, None),
-    ("pick", NEAR),
+    ("wait", "returned", SELF),
+    ("wait", "outer", 1, 0),
+    ("weight_sum", along_z(3)),
+    ("pick", FAR_INNER),
+    ("outer_on", 1),
     ("spread", NEAR, SELF),
-    ("weight_sum", along_z(3)),
-    ("outer_on", 1),
-    ("pick", FAR_INNER),
     ("wait", "returned", NEAR),
-    ("wait", "weights_in"),
     ("wait", "outer", 0, 1),
     ("weight_sum", None),
     ("spread", FAR_INNER, NEAR),
     ("wait", "returned", FAR_INNER),
+    ("weight_cores",),
     ("pick", FAR_OUTER),
-    ("weight_cores",),
     ("spread", FAR_OUTER, FAR_INNER),
+    ("wait", "weights_in"),
     ("weight_whole",),
     ("spread", None, FAR_OUTER),
 ]

time: 213 us -> 208 us (0.977)
  waiting for transfers between devices: 110 us -> 97.4 us
  starting transfers between devices: 47.1 us -> 55.1 us
    ppermute x14, waiting for transfers between devices: 21.3 us -> 13.3 us  [feat_swap(): return lax.ppermute(value, 'feat', pairs)]
    ppermute x33, starting transfers between devices: 41.2 us -> 46.4 us  [node_swap(): return lax.ppermute(value, 'node', pairs)]
    ppermute x33, waiting for transfers between devices: 88.9 us -> 84.1 us  [node_swap(): return lax.ppermute(value, 'node', pairs)]
    ppermute x14, starting transfers between devices: 5.96 us -> 8.72 us  [feat_swap(): return lax.ppermute(value, 'feat', pairs)]
    unnamed x24 -> x25, local copies, waits for them, and re-layouts: 4.79 us -> 4.83 us
  transfers between devices with their start and end apart: 47 -> 47, of which waited for: 18 -> 19; matrix products, arithmetic and copies ran while one was open for 0% -> 0% of each run, Pallas kernels for 19% -> 20%
where the time goes in v8:
time: 208 us
  waiting for transfers between devices  97.4 us (47%)
  starting transfers between devices  55.1 us (26%)
  Pallas kernels  48.2 us (23%)
  local copies, waits for them, and re-layouts  4.83 us (2%)
    ppermute x33, waiting for transfers between devices, node_swap(): return lax.ppermute(value, 'node', pairs)  84.1 us
    pallas_call x52, Pallas kernels, call(): pl.pallas_call(ordered, grid_spec=pltpu.PrefetchScalarGridSpec(num_scalar...  48.2 us
    ppermute x33, starting transfers between devices, node_swap(): return lax.ppermute(value, 'node', pairs)  46.4 us
    ppermute x14, waiting for transfers between devices, feat_swap(): return lax.ppermute(value, 'feat', pairs)  13.3 us
    ppermute x14, starting transfers between devices, feat_swap(): return lax.ppermute(value, 'feat', pairs)  8.72 us
    unnamed x25, local copies, waits for them, and re-layouts  4.83 us
  transfers between devices with their start and end apart: 47, of which 19 were waited for; matrix products, arithmetic and copies ran while one was open for 0% of the time, Pallas kernels for 20%

profile of v8, /device:TPU:0, one launch (start us, length us, event | category | flops | bytes accessed | tf_op | source)
XLA Modules:
  0.0 207.6 jit_solution(15486528066629118761)
XLA Ops:
  1.3 3.9 %shard_map.128 = (f32[16,64,128]{2,1,0:T(8,128)}, f32[8,128]{1,0:T(8,128)}) custom-call(s32[4]{0:T(128)} %pad_add_fusion.refs_0_, s32[8,16]{1,0:T(8,128)} %refs_1_.27, f32[64,4096]{1,0:T(8,128)} %refs_0_.3, f32[8,16,128,128]{3,2,1,0:T(8,128)} %refs_1_.15), custom_call_target="tpu_custom_call" | custom-call | flops 1 | bytes 1 | tf_op jit(solution)/shard_map/pallas_call | solution.py:112
  5.2 3.0 %collective-permute-start.2 = (f32[16,64,128]{2,1,0:T(8,128)}, f32[16,64,128]{2,1,0:T(8,128)S(1)}, u32[]{:S(2)}, u32[]{:S(2)}) collective-permute-start(f32[16,64,128]{2,1,0:T(8,128)} %get-tuple-element.50), channel_id=1, source_target_pairs={{0,1},{1,0},{2,3},{3,2},{4,5},{5,4},{6,7},{7,6},{8,9},{9,8},{10,11... | collective-permute-start | bytes 1572872 | tf_op jit(solution)/shard_map/ppermute | solution.py:547
  8.9 1.6 collective-permute-start
  10.5 3.4 %copy-done = f32[8,16,128,128]{3,2,1,0:T(8,128)S(1)} copy-done((f32[8,16,128,128]{3,2,1,0:T(8,128)S(1)}, f32[8,16,128,128]{3,2,1,0:T(8,128)}, u32[]{:S(2)}) %copy-start) | copy-done | bytes 8388632
  14.9 2.2 %shard_map.131 = (f32[16,64,128]{2,1,0:T(8,128)S(1)}, f32[16,64,128]{2,1,0:T(8,128)S(1)}, f32[16,64,128]{2,1,0:T(8,128)S(1)}) custom-call(s32[4]{0:T(128)S(1)} %copy-done.6, s32[8,16]{1,0:T(8,128)S(1)} %copy-done.5, f32[64,4096]{1,0:T(8,128)S(1)} %get-tuple-element.44.refs_2_.refs_3_.refs_1_, f32[8,16,128,128]{3,2,1,0:T(8,128)S(1)} %get-tuple-element.45.refs_3_.refs_4_, ...), custom_call_target="tpu_custom_call" | custom-call | flops 1 | bytes 1 | tf_op jit(solution)/shard_map/pallas_call | solution.py:112
  17.1 2.7 %collective-permute-start.1 = (s32[16,16]{1,0:T(8,128)S(1)}, s32[16,16]{1,0:T(8,128)S(1)}, u32[]{:S(2)}, u32[]{:S(2)}) collective-permute-start(s32[16,16]{1,0:T(8,128)S(1)} %shard_map.132.refs_1_.refs_3_), channel_id=1, source_target_pairs={{0,4},{1,5},{2,6},{3,7},{4,0},{5,1},{6,2},{7,3},{8,12},{9,13},{10,... | collective-permute-start | bytes 3080 | tf_op jit(solution)/shard_map/ppermute | solution.py:547
  19.8 1.5 collective-permute-start.6
  22.3 1.5 shard_map.134
  26.4 1.5 collective-permute-start.10
  27.9 10.8 %collective-permute-done.4.refs_1_ = f32[16,64,128]{2,1,0:T(8,128)S(1)} collective-permute-done((f32[16,64,128]{2,1,0:T(8,128)S(1)}, f32[16,64,128]{2,1,0:T(8,128)S(1)}, u32[]{:S(2)}, u32[]{:S(2)}) %collective-permute-start.4) | collective-permute-done | bytes 524320 | tf_op jit(solution)/shard_map/ppermute | solution.py:547
  38.7 1.5 shard_map.138
  41.5 5.6 %collective-permute-done.7.refs_1_ = f32[16,64,128]{2,1,0:T(8,128)S(1)} collective-permute-done((f32[16,64,128]{2,1,0:T(8,128)S(1)}, f32[16,64,128]{2,1,0:T(8,128)S(1)}, u32[]{:S(2)}, u32[]{:S(2)}) %collective-permute-start.7) | collective-permute-done | bytes 524320 | tf_op jit(solution)/shard_map/ppermute | solution.py:547
  49.5 3.5 %collective-permute-start.9 = (f32[16,64,128]{2,1,0:T(8,128)S(1)}, f32[16,64,128]{2,1,0:T(8,128)S(1)}, u32[]{:S(2)}, u32[]{:S(2)}) collective-permute-start(f32[16,64,128]{2,1,0:T(8,128)S(1)} %shard_map.141.refs_6_.refs_0_), channel_id=1, source_target_pairs={{0,2},{1,3},{2,0},{3,1},{4,6},{5,7},{6,4},{7,5},{8,10},{9,11},{10,... | collective-permute-start | bytes 1572872 | tf_op jit(solution)/shard_map/ppermute | solution.py:547
  52.9 1.5 shard_map.142
  55.0 7.0 %collective-permute-done.12.refs_1_ = f32[16,64,128]{2,1,0:T(8,128)S(1)} collective-permute-done((f32[16,64,128]{2,1,0:T(8,128)S(1)}, f32[16,64,128]{2,1,0:T(8,128)S(1)}, u32[]{:S(2)}, u32[]{:S(2)}) %collective-permute-start.12) | collective-permute-done | bytes 524320 | tf_op jit(solution)/shard_map/ppermute | solution.py:547
  63.4 4.5 %collective-permute-start.16 = (f32[16,64,128]{2,1,0:T(8,128)S(1)}, f32[16,64,128]{2,1,0:T(8,128)S(1)}, u32[]{:S(2)}, u32[]{:S(2)}) collective-permute-start(f32[16,64,128]{2,1,0:T(8,128)S(1)} %shard_map.145.refs_2_), channel_id=1, source_target_pairs={{0,2},{1,3},{2,0},{3,1},{4,6},{5,7},{6,4},{7,5},{8,10},{9,11},{10,... | collective-permute-start | bytes 1572872 | tf_op jit(solution)/shard_map/ppermute | solution.py:547
  68.6 4.7 %collective-permute-done.9.refs_1_ = f32[16,64,128]{2,1,0:T(8,128)S(1)} collective-permute-done((f32[16,64,128]{2,1,0:T(8,128)S(1)}, f32[16,64,128]{2,1,0:T(8,128)S(1)}, u32[]{:S(2)}, u32[]{:S(2)}) %collective-permute-start.9) | collective-permute-done | bytes 524320 | tf_op jit(solution)/shard_map/ppermute | solution.py:547
  74.1 5.9 %collective-permute-start.14 = (f32[16,64,128]{2,1,0:T(8,128)S(1)}, f32[16,64,128]{2,1,0:T(8,128)S(1)}, u32[]{:S(2)}, u32[]{:S(2)}) collective-permute-start(f32[16,64,128]{2,1,0:T(8,128)S(1)} %shard_map.147.refs_1_), channel_id=1, source_target_pairs={{0,2},{1,3},{2,0},{3,1},{4,6},{5,7},{6,4},{7,5},{8,10},{9,11},{10,... | collective-permute-start | bytes 1572872 | tf_op jit(solution)/shard_map/ppermute | solution.py:547
  80.0 1.5 shard_map.150
  83.9 8.1 %collective-permute-done.14.refs_2_ = f32[16,64,128]{2,1,0:T(8,128)S(1)} collective-permute-done((f32[16,64,128]{2,1,0:T(8,128)S(1)}, f32[16,64,128]{2,1,0:T(8,128)S(1)}, u32[]{:S(2)}, u32[]{:S(2)}) %collective-permute-start.14) | collective-permute-done | bytes 524320 | tf_op jit(solution)/shard_map/ppermute | solution.py:547
  92.7 3.8 %collective-permute-done.21.refs_0_ = f32[16,64,128]{2,1,0:T(8,128)S(1)} collective-permute-done((f32[16,64,128]{2,1,0:T(8,128)S(1)}, f32[16,64,128]{2,1,0:T(8,128)S(1)}, u32[]{:S(2)}, u32[]{:S(2)}) %collective-permute-start.21) | collective-permute-done | bytes 524320 | tf_op jit(solution)/shard_map/ppermute | solution.py:551
  96.5 1.5 collective-permute-start.18
  98.6 4.9 %shard_map.154.refs_1_.refs_6_ = f32[2,256,2048]{2,1,0:T(8,128)S(1)} custom-call(s32[4]{0:T(128)S(1)} %copy-done.6, f32[64,4096]{1,0:T(8,128)S(1)} %get-tuple-element.44.refs_2_.refs_3_.refs_1_, f32[64,4096]{1,0:T(8,128)S(1)} %shard_map.143.refs_2_, f32[64,4096]{1,0:T(8,128)S(1)} %collective-permute-done.19.refs_3_, ...), custom_call_target="tpu_custom_call" | custom-call | flops 1 | bytes 1 | tf_op jit(solution)/shard_map/pallas_call | solution.py:112
  103.5 6.3 %collective-permute-done.18.refs_0_ = f32[16,64,128]{2,1,0:T(8,128)S(1)} collective-permute-done((f32[16,64,128]{2,1,0:T(8,128)S(1)}, f32[16,64,128]{2,1,0:T(8,128)S(1)}, u32[]{:S(2)}, u32[]{:S(2)}) %collective-permute-start.18) | collective-permute-done | bytes 524320 | tf_op jit(solution)/shard_map/ppermute | solution.py:551
  110.3 4.0 %shard_map.156 = (f32[1024,256]{1,0:T(8,128)}, f32[256,2048]{1,0:T(8,128)S(1)}, f32[16,64,128]{2,1,0:T(8,128)S(1)}) custom-call(s32[4]{0:T(128)S(1)} %copy-done.6, f32[16,64,128]{2,1,0:T(8,128)S(1)} %shard_map.151.refs_5_.refs_1_.refs_3_, f32[16,64,128]{2,1,0:T(8,128)S(1)} %shard_map.153.refs_7_.refs_2_, f32[16,64,128]{2,1,0:T(8,128)S(1)} %collective-permute-done.26.refs_3_, ...), custom_call_target="tpu_custom_call" | custom-call | flops 1 | bytes 1 | tf_op jit(solution)/shard_map/pallas_call | solution.py:112
  115.3 1.6 collective-permute-start.28
  116.9 4.0 %shard_map.157 = (f32[1024,256]{1,0:T(8,128)}, f32[256,2048]{1,0:T(8,128)S(1)}, f32[16,64,128]{2,1,0:T(8,128)S(1)}) custom-call(s32[4]{0:T(128)S(1)} %copy-done.6, f32[16,64,128]{2,1,0:T(8,128)S(1)} %shard_map.152.refs_1_.refs_3_, f32[16,64,128]{2,1,0:T(8,128)S(1)} %shard_map.155.refs_12_.refs_2_, ...), custom_call_target="tpu_custom_call", output_to_operand_aliasing={{0}: (12, {})} | custom-call | flops 1 | bytes 1 | tf_op jit(solution)/shard_map/pallas_call | solution.py:112
  121.6 3.3 %collective-permute-start.33 = (f32[16,64,128]{2,1,0:T(8,128)S(1)}, f32[16,64,128]{2,1,0:T(8,128)S(1)}, u32[]{:S(2)}, u32[]{:S(2)}) collective-permute-start(f32[16,64,128]{2,1,0:T(8,128)S(1)} %get-tuple-element.63.refs_1_.refs_3_.refs_5_), channel_id=1, source_target_pairs={{0,2},{1,3},{2,0},{3,1},{4,6},{5,7},{6,4},{7,5},{8,10},{9,11},{10,... | collective-permute-start | bytes 1572872 | tf_op jit(solution)/shard_map/ppermute | solution.py:547
  124.9 1.3 collective-permute-start.31
  126.2 2.1 shard_map.159
  128.3 1.9 collective-permute-done.28.refs_0_
  130.1 2.1 shard_map.161
  134.4 6.9 %collective-permute-done.33.refs_2_.refs_0_ = f32[16,64,128]{2,1,0:T(8,128)S(1)} collective-permute-done((f32[16,64,128]{2,1,0:T(8,128)S(1)}, f32[16,64,128]{2,1,0:T(8,128)S(1)}, u32[]{:S(2)}, u32[]{:S(2)}) %collective-permute-start.33) | collective-permute-done | bytes 524320 | tf_op jit(solution)/shard_map/ppermute | solution.py:547
  144.9 7.7 %collective-permute-done.31.refs_1_.refs_4_.refs_6_ = f32[16,64,128]{2,1,0:T(8,128)S(1)} collective-permute-done((f32[16,64,128]{2,1,0:T(8,128)S(1)}, f32[16,64,128]{2,1,0:T(8,128)S(1)}, u32[]{:S(2)}, u32[]{:S(2)}) %collective-permute-start.31) | collective-permute-done | bytes 524320 | tf_op jit(solution)/shard_map/ppermute | solution.py:547
  153.2 10.6 %collective-permute-done.36.refs_8_.refs_5_.refs_7_ = f32[16,64,128]{2,1,0:T(8,128)S(1)} collective-permute-done((f32[16,64,128]{2,1,0:T(8,128)S(1)}, f32[16,64,128]{2,1,0:T(8,128)S(1)}, u32[]{:S(2)}, u32[]{:S(2)}) %collective-permute-start.36) | collective-permute-done | bytes 524320 | tf_op jit(solution)/shard_map/ppermute | solution.py:547
  165.1 1.3 shard_map.168
  169.3 1.9 collective-permute-start.41
  171.2 1.9 shard_map.172
  173.2 3.3 %collective-permute-done.41.refs_1_ = f32[144,256]{1,0:T(8,128)S(1)} collective-permute-done((f32[144,256]{1,0:T(8,128)S(1)}, f32[144,256]{1,0:T(8,128)S(1)}, u32[]{:S(2)}, u32[]{:S(2)}) %collective-permute-start.41) | collective-permute-done | bytes 147488 | tf_op jit(solution)/shard_map/ppermute | solution.py:547
  176.5 7.2 %collective-permute-done.39.refs_3_.refs_4_.refs_6_ = f32[16,64,128]{2,1,0:T(8,128)S(1)} collective-permute-done((f32[16,64,128]{2,1,0:T(8,128)S(1)}, f32[16,64,128]{2,1,0:T(8,128)S(1)}, u32[]{:S(2)}, u32[]{:S(2)}) %collective-permute-start.39) | collective-permute-done | bytes 524320 | tf_op jit(solution)/shard_map/ppermute | solution.py:547
  183.8 2.0 shard_map.174
  186.4 5.9 %collective-permute-done.40.refs_5_.refs_7_ = f32[16,64,128]{2,1,0:T(8,128)S(1)} collective-permute-done((f32[16,64,128]{2,1,0:T(8,128)S(1)}, f32[16,64,128]{2,1,0:T(8,128)S(1)}, u32[]{:S(2)}, u32[]{:S(2)}) %collective-permute-start.40) | collective-permute-done | bytes 524320 | tf_op jit(solution)/shard_map/ppermute | solution.py:547
  193.8 1.5 collective-permute-start.46
  195.3 2.0 shard_map.177
  197.4 3.2 %collective-permute-done.46.refs_2_.refs_3_ = f32[2,144,256]{2,1,0:T(8,128)S(1)} collective-permute-done((f32[2,144,256]{2,1,0:T(8,128)S(1)}, f32[2,144,256]{2,1,0:T(8,128)S(1)}, u32[]{:S(2)}, u32[]{:S(2)}) %collective-permute-start.46) | collective-permute-done | bytes 294944 | tf_op jit(solution)/shard_map/ppermute | solution.py:551
  200.5 1.4 shard_map.178
  201.9 2.6 %collective-permute-done.45.refs_4_ = f32[16,64,128]{2,1,0:T(8,128)S(1)} collective-permute-done((f32[16,64,128]{2,1,0:T(8,128)S(1)}, f32[16,64,128]{2,1,0:T(8,128)S(1)}, u32[]{:S(2)}, u32[]{:S(2)}) %collective-permute-start.45) | collective-permute-done | bytes 524320 | tf_op jit(solution)/shard_map/ppermute | solution.py:547
  205.2 2.2 %shard_map.179 = (f32[64,4096]{1,0:T(8,128)}, f32[8,128]{1,0:T(8,128)}) custom-call(s32[4]{0:T(128)S(1)} %copy-done.6, s32[8,16]{1,0:T(8,128)S(1)} %copy-done.5, s32[8,16]{1,0:T(8,128)S(1)} %shard_map.133.refs_2_.refs_6_.refs_1_, f32[8,16,128,128]{3,2,1,0:T(8,128)S(1)} %get-tuple-element.45.refs_3_.refs_4_, ...), custom_call_target="tpu_custom_call" | custom-call | flops 1 | bytes 1 | tf_op jit(solution)/shard_map/pallas_call | solution.py:112
  (125 shorter events, 32.0 us)
Async XLA Ops:
  5.2 17.1 %collective-permute-start.2 = (f32[16,64,128]{2,1,0:T(8,128)}, f32[16,64,128]{2,1,0:T(8,128)S(1)}, u32[]{:S(2)}, u32[]{:S(2)}) collective-permute-start(f32[16,64,128]{2,1,0:T(8,128)} %get-tuple-element.50), channel_id=1, source_target_pairs={{0,1},{1,0},{2,3},{3,2},{4,5},{5,4},{6,7},{7,6},{8,9},{9,8},{10,11... | collective-permute-start | bytes 1572872 | tf_op jit(solution)/shard_map/ppermute | solution.py:547
  8.9 8.2 %collective-permute-start = (s32[8,16]{1,0:T(8,128)S(1)}, s32[8,16]{1,0:T(8,128)S(1)}, u32[]{:S(2)}, u32[]{:S(2)}) collective-permute-start(s32[8,16]{1,0:T(8,128)S(1)} %shard_map.129.refs_3_.refs_0_), channel_id=1, source_target_pairs={{0,2},{1,3},{2,0},{3,1},{4,6},{5,7},{6,4},{7,5},{8,10},{9,11},{10,... | collective-permute-start | bytes 1544 | tf_op jit(solution)/shard_map/ppermute | solution.py:547
  17.1 4.6 %collective-permute-start.1 = (s32[16,16]{1,0:T(8,128)S(1)}, s32[16,16]{1,0:T(8,128)S(1)}, u32[]{:S(2)}, u32[]{:S(2)}) collective-permute-start(s32[16,16]{1,0:T(8,128)S(1)} %shard_map.132.refs_1_.refs_3_), channel_id=1, source_target_pairs={{0,4},{1,5},{2,6},{3,7},{4,0},{5,1},{6,2},{7,3},{8,12},{9,13},{10,... | collective-permute-start | bytes 3080 | tf_op jit(solution)/shard_map/ppermute | solution.py:547
  19.8 28.0 %collective-permute-start.6 = (f32[64,4096]{1,0:T(8,128)S(1)}, f32[64,4096]{1,0:T(8,128)S(1)}, u32[]{:S(2)}, u32[]{:S(2)}) collective-permute-start(f32[64,4096]{1,0:T(8,128)S(1)} %get-tuple-element.44.refs_2_.refs_3_.refs_1_), channel_id=1, source_target_pairs={{0,16},{8,24},{16,0},{24,8},{1,17},{9,25},{17,1},{25,9},{2,18},{10... | collective-permute-start | bytes 3145736 | tf_op jit(solution)/shard_map/ppermute | solution.py:551
  23.7 14.9 %collective-permute-start.4 = (f32[16,64,128]{2,1,0:T(8,128)S(1)}, f32[16,64,128]{2,1,0:T(8,128)S(1)}, u32[]{:S(2)}, u32[]{:S(2)}) collective-permute-start(f32[16,64,128]{2,1,0:T(8,128)S(1)} %get-tuple-element.52.refs_0_), channel_id=1, source_target_pairs={{0,2},{1,3},{2,0},{3,1},{4,6},{5,7},{6,4},{7,5},{8,10},{9,11},{10,... | collective-permute-start | bytes 1572872 | tf_op jit(solution)/shard_map/ppermute | solution.py:547
  24.2 14.5 %collective-permute-start.3 = (f32[16,64,128]{2,1,0:T(8,128)S(1)}, f32[16,64,128]{2,1,0:T(8,128)S(1)}, u32[]{:S(2)}, u32[]{:S(2)}) collective-permute-start(f32[16,64,128]{2,1,0:T(8,128)S(1)} %shard_map.135.refs_1_), channel_id=1, source_target_pairs={{0,1},{1,0},{2,3},{3,2},{4,5},{5,4},{6,7},{7,6},{8,9},{9,8},{10,11... | collective-permute-start | bytes 1572872 | tf_op jit(solution)/shard_map/ppermute | solution.py:547
  25.2 22.0 %collective-permute-start.7 = (f32[16,64,128]{2,1,0:T(8,128)S(1)}, f32[16,64,128]{2,1,0:T(8,128)S(1)}, u32[]{:S(2)}, u32[]{:S(2)}) collective-permute-start(f32[16,64,128]{2,1,0:T(8,128)S(1)} %shard_map.136.refs_2_.refs_0_), channel_id=1, source_target_pairs={{0,2},{1,3},{2,0},{3,1},{4,6},{5,7},{6,4},{7,5},{8,10},{9,11},{10,... | collective-permute-start | bytes 1572872 | tf_op jit(solution)/shard_map/ppermute | solution.py:547
  26.4 42.2 %collective-permute-start.10 = (f32[256,1024]{1,0:T(8,128)S(1)}, f32[256,1024]{1,0:T(8,128)S(1)}, u32[]{:S(2)}, u32[]{:S(2)}) collective-permute-start(f32[256,1024]{1,0:T(8,128)S(1)} %get-tuple-element.46.refs_4_.refs_7_), channel_id=1, source_target_pairs={{0,16},{8,24},{16,0},{24,8},{1,17},{9,25},{17,1},{25,9},{2,18},{10... | collective-permute-start | bytes 3145736 | tf_op jit(solution)/shard_map/ppermute | solution.py:551
  40.2 9.2 %collective-permute-start.5 = (f32[16,64,128]{2,1,0:T(8,128)S(1)}, f32[16,64,128]{2,1,0:T(8,128)S(1)}, u32[]{:S(2)}, u32[]{:S(2)}) collective-permute-start(f32[16,64,128]{2,1,0:T(8,128)S(1)} %shard_map.139.refs_2_), channel_id=1, source_target_pairs={{0,1},{1,0},{2,3},{3,2},{4,5},{5,4},{6,7},{7,6},{8,9},{9,8},{10,11... | collective-permute-start | bytes 1572872 | tf_op jit(solution)/shard_map/ppermute | solution.py:547
  40.8 13.6 %collective-permute-start.13 = (f32[16,64,128]{2,1,0:T(8,128)S(1)}, f32[16,64,128]{2,1,0:T(8,128)S(1)}, u32[]{:S(2)}, u32[]{:S(2)}) collective-permute-start(f32[16,64,128]{2,1,0:T(8,128)S(1)} %shard_map.137.refs_6_), channel_id=1, source_target_pairs={{2,4},{3,5},{4,2},{5,3},{0,0},{1,1},{6,6},{7,7},{10,12},{11,13},{1... | collective-permute-start | bytes 1572872 | tf_op jit(solution)/shard_map/ppermute | solution.py:547
  47.1 14.9 %collective-permute-start.12 = (f32[16,64,128]{2,1,0:T(8,128)S(1)}, f32[16,64,128]{2,1,0:T(8,128)S(1)}, u32[]{:S(2)}, u32[]{:S(2)}) collective-permute-start(f32[16,64,128]{2,1,0:T(8,128)S(1)} %get-tuple-element.55.refs_0_), channel_id=1, source_target_pairs={{0,2},{1,3},{2,0},{3,1},{4,6},{5,7},{6,4},{7,5},{8,10},{9,11},{10,... | collective-permute-start | bytes 1572872 | tf_op jit(solution)/shard_map/ppermute | solution.py:547
  47.8 15.6 %collective-permute-start.11 = (f32[16,64,128]{2,1,0:T(8,128)S(1)}, f32[16,64,128]{2,1,0:T(8,128)S(1)}, u32[]{:S(2)}, u32[]{:S(2)}) collective-permute-start(f32[16,64,128]{2,1,0:T(8,128)S(1)} %shard_map.140.refs_1_), channel_id=1, source_target_pairs={{2,4},{3,5},{4,2},{5,3},{0,0},{1,1},{6,6},{7,7},{10,12},{11,13},{1... | collective-permute-start | bytes 1572872 | tf_op jit(solution)/shard_map/ppermute | solution.py:547
  49.5 23.8 %collective-permute-start.9 = (f32[16,64,128]{2,1,0:T(8,128)S(1)}, f32[16,64,128]{2,1,0:T(8,128)S(1)}, u32[]{:S(2)}, u32[]{:S(2)}) collective-permute-start(f32[16,64,128]{2,1,0:T(8,128)S(1)} %shard_map.141.refs_6_.refs_0_), channel_id=1, source_target_pairs={{0,2},{1,3},{2,0},{3,1},{4,6},{5,7},{6,4},{7,5},{8,10},{9,11},{10,... | collective-permute-start | bytes 1572872 | tf_op jit(solution)/shard_map/ppermute | solution.py:547
  62.1 17.9 %copy-start.11 = (s32[4096]{0:T(1024)S(1)}, s32[4096]{0:T(1024)}, u32[]{:S(2)}) copy-start(s32[4096]{0:T(1024)} %param.13) | copy-start | bytes 49156
  62.1 12.0 %collective-permute-start.17 = (f32[16,64,128]{2,1,0:T(8,128)S(1)}, f32[16,64,128]{2,1,0:T(8,128)S(1)}, u32[]{:S(2)}, u32[]{:S(2)}) collective-permute-start(f32[16,64,128]{2,1,0:T(8,128)S(1)} %shard_map.146.refs_3_), channel_id=1, source_target_pairs={{2,4},{3,5},{4,2},{5,3},{0,0},{1,1},{6,6},{7,7},{10,12},{11,13},{1... | collective-permute-start | bytes 1572872 | tf_op jit(solution)/shard_map/ppermute | solution.py:547
  62.8 17.2 %collective-permute-start.8 = (f32[16,64,128]{2,1,0:T(8,128)S(1)}, f32[16,64,128]{2,1,0:T(8,128)S(1)}, u32[]{:S(2)}, u32[]{:S(2)}) collective-permute-start(f32[16,64,128]{2,1,0:T(8,128)S(1)} %shard_map.144.refs_3_), channel_id=1, source_target_pairs={{0,1},{1,0},{2,3},{3,2},{4,5},{5,4},{6,7},{7,6},{8,9},{9,8},{10,11... | collective-permute-start | bytes 1572872 | tf_op jit(solution)/shard_map/ppermute | solution.py:547
  63.4 18.5 %collective-permute-start.16 = (f32[16,64,128]{2,1,0:T(8,128)S(1)}, f32[16,64,128]{2,1,0:T(8,128)S(1)}, u32[]{:S(2)}, u32[]{:S(2)}) collective-permute-start(f32[16,64,128]{2,1,0:T(8,128)S(1)} %shard_map.145.refs_2_), channel_id=1, source_target_pairs={{0,2},{1,3},{2,0},{3,1},{4,6},{5,7},{6,4},{7,5},{8,10},{9,11},{10,... | collective-permute-start | bytes 1572872 | tf_op jit(solution)/shard_map/ppermute | solution.py:547
  73.3 10.4 %collective-permute-start.15 = (f32[16,64,128]{2,1,0:T(8,128)S(1)}, f32[16,64,128]{2,1,0:T(8,128)S(1)}, u32[]{:S(2)}, u32[]{:S(2)}) collective-permute-start(f32[16,64,128]{2,1,0:T(8,128)S(1)} %shard_map.149.refs_6_), channel_id=1, source_target_pairs={{2,4},{3,5},{4,2},{5,3},{0,0},{1,1},{6,6},{7,7},{10,12},{11,13},{1... | collective-permute-start | bytes 1572872 | tf_op jit(solution)/shard_map/ppermute | solution.py:547
  74.0 24.0 %collective-permute-start.19 = (f32[64,4096]{1,0:T(8,128)S(1)}, f32[64,4096]{1,0:T(8,128)S(1)}, u32[]{:S(2)}, u32[]{:S(2)}) collective-permute-start(f32[64,4096]{1,0:T(8,128)S(1)} %get-tuple-element.44.refs_2_.refs_3_.refs_1_), channel_id=1, source_target_pairs={{0,8},{8,0},{16,24},{24,16},{1,9},{9,1},{17,25},{25,17},{2,10},{10... | collective-permute-start | bytes 3145736 | tf_op jit(solution)/shard_map/ppermute | solution.py:551
  74.1 18.0 %collective-permute-start.14 = (f32[16,64,128]{2,1,0:T(8,128)S(1)}, f32[16,64,128]{2,1,0:T(8,128)S(1)}, u32[]{:S(2)}, u32[]{:S(2)}) collective-permute-start(f32[16,64,128]{2,1,0:T(8,128)S(1)} %shard_map.147.refs_1_), channel_id=1, source_target_pairs={{0,2},{1,3},{2,0},{3,1},{4,6},{5,7},{6,4},{7,5},{8,10},{9,11},{10,... | collective-permute-start | bytes 1572872 | tf_op jit(solution)/shard_map/ppermute | solution.py:547
  80.0 18.1 %collective-permute-start.20 = (f32[64,4096]{1,0:T(8,128)S(1)}, f32[64,4096]{1,0:T(8,128)S(1)}, u32[]{:S(2)}, u32[]{:S(2)}) collective-permute-start(f32[64,4096]{1,0:T(8,128)S(1)} %shard_map.143.refs_2_), channel_id=1, source_target_pairs={{0,8},{8,0},{16,24},{24,16},{1,9},{9,1},{17,25},{25,17},{2,10},{10... | collective-permute-start | bytes 3145736 | tf_op jit(solution)/shard_map/ppermute | solution.py:551
  82.5 14.0 %collective-permute-start.21 = (f32[16,64,128]{2,1,0:T(8,128)S(1)}, f32[16,64,128]{2,1,0:T(8,128)S(1)}, u32[]{:S(2)}, u32[]{:S(2)}) collective-permute-start(f32[16,64,128]{2,1,0:T(8,128)S(1)} %shard_map.151.refs_5_.refs_1_.refs_3_), channel_id=1, source_target_pairs={{0,16},{8,24},{16,0},{24,8},{1,17},{9,25},{17,1},{25,9},{2,18},{10... | collective-permute-start | bytes 1572872 | tf_op jit(solution)/shard_map/ppermute | solution.py:551
  83.8 26.0 %collective-permute-start.24 = (f32[256,1024]{1,0:T(8,128)S(1)}, f32[256,1024]{1,0:T(8,128)S(1)}, u32[]{:S(2)}, u32[]{:S(2)}) collective-permute-start(f32[256,1024]{1,0:T(8,128)S(1)} %get-tuple-element.46.refs_4_.refs_7_), channel_id=1, source_target_pairs={{0,8},{8,0},{16,24},{24,16},{1,9},{9,1},{17,25},{25,17},{2,10},{10... | collective-permute-start | bytes 3145736 | tf_op jit(solution)/shard_map/ppermute | solution.py:551
  92.1 18.2 %collective-permute-start.25 = (f32[256,1024]{1,0:T(8,128)S(1)}, f32[256,1024]{1,0:T(8,128)S(1)}, u32[]{:S(2)}, u32[]{:S(2)}) collective-permute-start(f32[256,1024]{1,0:T(8,128)S(1)} %shard_map.148.refs_2_.refs_8_), channel_id=1, source_target_pairs={{0,8},{8,0},{16,24},{24,16},{1,9},{9,1},{17,25},{25,17},{2,10},{10... | collective-permute-start | bytes 3145736 | tf_op jit(solution)/shard_map/ppermute | solution.py:551
  96.5 13.3 %collective-permute-start.18 = (f32[16,64,128]{2,1,0:T(8,128)S(1)}, f32[16,64,128]{2,1,0:T(8,128)S(1)}, u32[]{:S(2)}, u32[]{:S(2)}) collective-permute-start(f32[16,64,128]{2,1,0:T(8,128)S(1)} %shard_map.152.refs_1_.refs_3_), channel_id=1, source_target_pairs={{0,16},{8,24},{16,0},{24,8},{1,17},{9,25},{17,1},{25,9},{2,18},{10... | collective-permute-start | bytes 1572872 | tf_op jit(solution)/shard_map/ppermute | solution.py:551
  98.0 12.3 %collective-permute-start.26 = (f32[16,64,128]{2,1,0:T(8,128)S(1)}, f32[16,64,128]{2,1,0:T(8,128)S(1)}, u32[]{:S(2)}, u32[]{:S(2)}) collective-permute-start(f32[16,64,128]{2,1,0:T(8,128)S(1)} %shard_map.151.refs_5_.refs_1_.refs_3_), channel_id=1, source_target_pairs={{0,8},{8,0},{16,24},{24,16},{1,9},{9,1},{17,25},{25,17},{2,10},{10... | collective-permute-start | bytes 1572872 | tf_op jit(solution)/shard_map/ppermute | solution.py:551
  98.1 12.3 %collective-permute-start.27 = (f32[16,64,128]{2,1,0:T(8,128)S(1)}, f32[16,64,128]{2,1,0:T(8,128)S(1)}, u32[]{:S(2)}, u32[]{:S(2)}) collective-permute-start(f32[16,64,128]{2,1,0:T(8,128)S(1)} %shard_map.153.refs_7_.refs_2_), channel_id=1, source_target_pairs={{0,8},{8,0},{16,24},{24,16},{1,9},{9,1},{17,25},{25,17},{2,10},{10... | collective-permute-start | bytes 1572872 | tf_op jit(solution)/shard_map/ppermute | solution.py:551
  109.8 7.1 %collective-permute-start.22 = (f32[16,64,128]{2,1,0:T(8,128)S(1)}, f32[16,64,128]{2,1,0:T(8,128)S(1)}, u32[]{:S(2)}, u32[]{:S(2)}) collective-permute-start(f32[16,64,128]{2,1,0:T(8,128)S(1)} %shard_map.152.refs_1_.refs_3_), channel_id=1, source_target_pairs={{0,8},{8,0},{16,24},{24,16},{1,9},{9,1},{17,25},{25,17},{2,10},{10... | collective-permute-start | bytes 1572872 | tf_op jit(solution)/shard_map/ppermute | solution.py:551
  109.8 7.1 %collective-permute-start.23 = (f32[16,64,128]{2,1,0:T(8,128)S(1)}, f32[16,64,128]{2,1,0:T(8,128)S(1)}, u32[]{:S(2)}, u32[]{:S(2)}) collective-permute-start(f32[16,64,128]{2,1,0:T(8,128)S(1)} %shard_map.155.refs_12_.refs_2_), channel_id=1, source_target_pairs={{0,8},{8,0},{16,24},{24,16},{1,9},{9,1},{17,25},{25,17},{2,10},{10... | collective-permute-start | bytes 1572872 | tf_op jit(solution)/shard_map/ppermute | solution.py:551
  114.4 10.5 %collective-permute-start.29 = (f32[16,64,128]{2,1,0:T(8,128)S(1)}, f32[16,64,128]{2,1,0:T(8,128)S(1)}, u32[]{:S(2)}, u32[]{:S(2)}) collective-permute-start(f32[16,64,128]{2,1,0:T(8,128)S(1)} %get-tuple-element.60.refs_13_.refs_2_.refs_4_), channel_id=1, source_target_pairs={{2,4},{3,5},{4,2},{5,3},{0,0},{1,1},{6,6},{7,7},{10,12},{11,13},{1... | collective-permute-start | bytes 1572872 | tf_op jit(solution)/shard_map/ppermute | solution.py:547
  115.3 14.8 %collective-permute-start.28 = (f32[16,64,128]{2,1,0:T(8,128)S(1)}, f32[16,64,128]{2,1,0:T(8,128)S(1)}, u32[]{:S(2)}, u32[]{:S(2)}) collective-permute-start(f32[16,64,128]{2,1,0:T(8,128)S(1)} %get-tuple-element.60.refs_13_.refs_2_.refs_4_), channel_id=1, source_target_pairs={{0,2},{1,3},{2,0},{3,1},{4,6},{5,7},{6,4},{7,5},{8,10},{9,11},{10,... | collective-permute-start | bytes 1572872 | tf_op jit(solution)/shard_map/ppermute | solution.py:547
  120.9 13.4 %collective-permute-start.34 = (f32[16,64,128]{2,1,0:T(8,128)S(1)}, f32[16,64,128]{2,1,0:T(8,128)S(1)}, u32[]{:S(2)}, u32[]{:S(2)}) collective-permute-start(f32[16,64,128]{2,1,0:T(8,128)S(1)} %get-tuple-element.63.refs_1_.refs_3_.refs_5_), channel_id=1, source_target_pairs={{2,4},{3,5},{4,2},{5,3},{0,0},{1,1},{6,6},{7,7},{10,12},{11,13},{1... | collective-permute-start | bytes 1572872 | tf_op jit(solution)/shard_map/ppermute | solution.py:547
  121.6 19.7 %collective-permute-start.33 = (f32[16,64,128]{2,1,0:T(8,128)S(1)}, f32[16,64,128]{2,1,0:T(8,128)S(1)}, u32[]{:S(2)}, u32[]{:S(2)}) collective-permute-start(f32[16,64,128]{2,1,0:T(8,128)S(1)} %get-tuple-element.63.refs_1_.refs_3_.refs_5_), channel_id=1, source_target_pairs={{0,2},{1,3},{2,0},{3,1},{4,6},{5,7},{6,4},{7,5},{8,10},{9,11},{10,... | collective-permute-start | bytes 1572872 | tf_op jit(solution)/shard_map/ppermute | solution.py:547
  124.9 27.7 %collective-permute-start.31 = (f32[16,64,128]{2,1,0:T(8,128)S(1)}, f32[16,64,128]{2,1,0:T(8,128)S(1)}, u32[]{:S(2)}, u32[]{:S(2)}) collective-permute-start(f32[16,64,128]{2,1,0:T(8,128)S(1)} %shard_map.158.refs_5_.refs_2_.refs_4_), channel_id=1, source_target_pairs={{2,0},{3,1},{4,6},{5,7},{10,8},{11,9},{12,14},{13,15},{18,16},{19,... | collective-permute-start | bytes 1572872 | tf_op jit(solution)/shard_map/ppermute | solution.py:547
  132.2 11.2 %collective-permute-start.32 = (f32[144,256]{1,0:T(8,128)S(1)}, f32[144,256]{1,0:T(8,128)S(1)}, u32[]{:S(2)}, u32[]{:S(2)}) collective-permute-start(f32[144,256]{1,0:T(8,128)S(1)} %get-tuple-element.66.refs_4_.refs_0_), channel_id=1, source_target_pairs={{0,1},{1,0},{2,3},{3,2},{4,5},{5,4},{6,7},{7,6},{8,9},{9,8},{10,11... | collective-permute-start | bytes 442376 | tf_op jit(solution)/shard_map/ppermute | solution.py:547
  133.7 18.9 %collective-permute-start.30 = (f32[16,64,128]{2,1,0:T(8,128)S(1)}, f32[16,64,128]{2,1,0:T(8,128)S(1)}, u32[]{:S(2)}, u32[]{:S(2)}) collective-permute-start(f32[16,64,128]{2,1,0:T(8,128)S(1)} %shard_map.160.refs_6_.refs_2_.refs_4_), channel_id=1, source_target_pairs={{2,4},{3,5},{4,2},{5,3},{0,0},{1,1},{6,6},{7,7},{10,12},{11,13},{1... | collective-permute-start | bytes 1572872 | tf_op jit(solution)/shard_map/ppermute | solution.py:547
  141.3 22.5 %collective-permute-start.36 = (f32[16,64,128]{2,1,0:T(8,128)S(1)}, f32[16,64,128]{2,1,0:T(8,128)S(1)}, u32[]{:S(2)}, u32[]{:S(2)}) collective-permute-start(f32[16,64,128]{2,1,0:T(8,128)S(1)} %shard_map.163.refs_1_.refs_3_.refs_5_), channel_id=1, source_target_pairs={{2,0},{3,1},{4,6},{5,7},{10,8},{11,9},{12,14},{13,15},{18,16},{19,... | collective-permute-start | bytes 1572872 | tf_op jit(solution)/shard_map/ppermute | solution.py:547
  142.6 23.8 %collective-permute-start.35 = (f32[16,64,128]{2,1,0:T(8,128)S(1)}, f32[16,64,128]{2,1,0:T(8,128)S(1)}, u32[]{:S(2)}, u32[]{:S(2)}) collective-permute-start(f32[16,64,128]{2,1,0:T(8,128)S(1)} %shard_map.164.refs_3_.refs_4_.refs_5_), channel_id=1, source_target_pairs={{2,4},{3,5},{4,2},{5,3},{0,0},{1,1},{6,6},{7,7},{10,12},{11,13},{1... | collective-permute-start | bytes 1572872 | tf_op jit(solution)/shard_map/ppermute | solution.py:547
  143.4 23.1 %collective-permute-start.38 = (f32[16,64,128]{2,1,0:T(8,128)S(1)}, f32[16,64,128]{2,1,0:T(8,128)S(1)}, u32[]{:S(2)}, u32[]{:S(2)}) collective-permute-start(f32[16,64,128]{2,1,0:T(8,128)S(1)} %shard_map.162.refs_3_), channel_id=1, source_target_pairs={{0,1},{1,0},{2,3},{3,2},{4,5},{5,4},{6,7},{7,6},{8,9},{9,8},{10,11... | collective-permute-start | bytes 1572872 | tf_op jit(solution)/shard_map/ppermute | solution.py:547
  152.6 13.9 %collective-permute-start.37 = (f32[144,256]{1,0:T(8,128)S(1)}, f32[144,256]{1,0:T(8,128)S(1)}, u32[]{:S(2)}, u32[]{:S(2)}) collective-permute-start(f32[144,256]{1,0:T(8,128)S(1)} %shard_map.166.refs_2_.refs_0_), channel_id=1, source_target_pairs={{0,2},{1,3},{2,0},{3,1},{4,6},{5,7},{6,4},{7,5},{8,10},{9,11},{10,... | collective-permute-start | bytes 442376 | tf_op jit(solution)/shard_map/ppermute | solution.py:547
  152.6 20.6 %collective-permute-start.42 = (f32[16,64,128]{2,1,0:T(8,128)S(1)}, f32[16,64,128]{2,1,0:T(8,128)S(1)}, u32[]{:S(2)}, u32[]{:S(2)}) collective-permute-start(f32[16,64,128]{2,1,0:T(8,128)S(1)} %shard_map.165.refs_2_), channel_id=1, source_target_pairs={{0,1},{1,0},{2,3},{3,2},{4,5},{5,4},{6,7},{7,6},{8,9},{9,8},{10,11... | collective-permute-start | bytes 1572872 | tf_op jit(solution)/shard_map/ppermute | solution.py:547
  163.8 19.9 %collective-permute-start.39 = (f32[16,64,128]{2,1,0:T(8,128)S(1)}, f32[16,64,128]{2,1,0:T(8,128)S(1)}, u32[]{:S(2)}, u32[]{:S(2)}) collective-permute-start(f32[16,64,128]{2,1,0:T(8,128)S(1)} %shard_map.167.refs_9_.refs_2_.refs_4_), channel_id=1, source_target_pairs={{2,0},{3,1},{4,6},{5,7},{10,8},{11,9},{12,14},{13,15},{18,16},{19,... | collective-permute-start | bytes 1572872 | tf_op jit(solution)/shard_map/ppermute | solution.py:547
  167.3 18.5 %collective-permute-start.44 = (f32[16,64,128]{2,1,0:T(8,128)S(1)}, f32[16,64,128]{2,1,0:T(8,128)S(1)}, u32[]{:S(2)}, u32[]{:S(2)}) collective-permute-start(f32[16,64,128]{2,1,0:T(8,128)S(1)} %shard_map.170.refs_1_), channel_id=1, source_target_pairs={{0,1},{1,0},{2,3},{3,2},{4,5},{5,4},{6,7},{7,6},{8,9},{9,8},{10,11... | collective-permute-start | bytes 1572872 | tf_op jit(solution)/shard_map/ppermute | solution.py:547
  168.0 24.3 %collective-permute-start.40 = (f32[16,64,128]{2,1,0:T(8,128)S(1)}, f32[16,64,128]{2,1,0:T(8,128)S(1)}, u32[]{:S(2)}, u32[]{:S(2)}) collective-permute-start(f32[16,64,128]{2,1,0:T(8,128)S(1)} %shard_map.171.refs_8_.refs_3_.refs_5_), channel_id=1, source_target_pairs={{2,0},{3,1},{4,6},{5,7},{10,8},{11,9},{12,14},{13,15},{18,16},{19,... | collective-permute-start | bytes 1572872 | tf_op jit(solution)/shard_map/ppermute | solution.py:547
  169.3 7.2 %collective-permute-start.41 = (f32[144,256]{1,0:T(8,128)S(1)}, f32[144,256]{1,0:T(8,128)S(1)}, u32[]{:S(2)}, u32[]{:S(2)}) collective-permute-start(f32[144,256]{1,0:T(8,128)S(1)} %shard_map.169.refs_6_.refs_0_), channel_id=1, source_target_pairs={{0,6},{1,7},{2,4},{3,5},{4,2},{5,3},{6,0},{7,1},{8,14},{9,15},{10,... | collective-permute-start | bytes 442376 | tf_op jit(solution)/shard_map/ppermute | solution.py:547
  183.7 2.1 %collective-permute-start.43 = (f32[144,256]{1,0:T(8,128)S(1)}, f32[144,256]{1,0:T(8,128)S(1)}, u32[]{:S(2)}, u32[]{:S(2)}) collective-permute-start(f32[144,256]{1,0:T(8,128)S(1)} %shard_map.173.refs_10_.refs_1_), channel_id=1, source_target_pairs={{0,8},{8,0},{16,24},{24,16},{1,9},{9,1},{17,25},{25,17},{2,10},{10... | collective-permute-start | bytes 442376 | tf_op jit(solution)/shard_map/ppermute | solution.py:551
  193.1 11.3 %collective-permute-start.45 = (f32[16,64,128]{2,1,0:T(8,128)S(1)}, f32[16,64,128]{2,1,0:T(8,128)S(1)}, u32[]{:S(2)}, u32[]{:S(2)}) collective-permute-start(f32[16,64,128]{2,1,0:T(8,128)S(1)} %shard_map.176.refs_10_), channel_id=1, source_target_pairs={{0,1},{1,0},{2,3},{3,2},{4,5},{5,4},{6,7},{7,6},{8,9},{9,8},{10,11... | collective-permute-start | bytes 1572872 | tf_op jit(solution)/shard_map/ppermute | solution.py:547
  193.8 6.7 %collective-permute-start.46 = (f32[2,144,256]{2,1,0:T(8,128)S(1)}, f32[2,144,256]{2,1,0:T(8,128)S(1)}, u32[]{:S(2)}, u32[]{:S(2)}) collective-permute-start(f32[2,144,256]{2,1,0:T(8,128)S(1)} %shard_map.175.refs_6_.refs_1_), channel_id=1, source_target_pairs={{0,16},{8,24},{16,0},{24,8},{1,17},{9,25},{17,1},{25,9},{2,18},{10... | collective-permute-start | bytes 884744 | tf_op jit(solution)/shard_map/ppermute | solution.py:551
  (11 other events, 73.1 us)

commit v9 on v8

--- a/solution.py
+++ b/solution.py
@@ -555,24 +555,24 @@
     ("slots_first",),
     ("table_out",),
     ("load",),
+    ("tables_out",),
     ("slots_later",),
-    ("tables_out",),
     ("rows_in",),
     ("dense", FAR_OUTER),
     ("slots", FAR_INNER),
     ("send_in", FAR_OUTER, 1),
     ("pass_on", FAR_OUTER, 0),
+    ("slots", NEAR),
     ("dense", FAR_INNER),
-    ("slots", NEAR),
     ("pass_on", FAR_OUTER, 1),
     ("send_in", FAR_INNER, 1),
     ("dense", NEAR),
-    ("feats_on",),
+    ("pass_on", NEAR, 0),
     ("slots", SELF),
-    ("pass_on", NEAR, 0),
     ("pass_on", FAR_INNER, 0),
     ("pass_on", NEAR, 1),
     ("cotangents_on",),
+    ("feats_on",),
     ("pass_on", FAR_INNER, 1),
     ("dense", SELF),
     ("mean", 0),
@@ -582,13 +582,13 @@
     ("means_on", 1),
     ("activate", 0),
     ("activate", 1),
-    ("inner_on", 0),
     ("weight", 0),
     ("near_on", 0),
     ("weight", 1),
+    ("inner_on", 0),
     ("pick", SELF),
+    ("wait", "near", 1),
     ("wait", "inner", 1, 0),
-    ("wait", "near", 1),
     ("inner_on", 1),
     ("near_on", 1),
     ("pick", NEAR),
@@ -597,8 +597,8 @@
     ("outer_on", 0),
     ("wait", "inner", 1, 1),
     ("spread", SELF, None),
+    ("wait", "outer", 1, 0),
     ("wait", "returned", SELF),
-    ("wait", "outer", 1, 0),
     ("weight_sum", along_z(3)),
     ("pick", FAR_INNER),
     ("outer_on", 1),

time: 208 us -> 205 us (0.986)
  waiting for transfers between devices: 97.4 us -> 81.6 us
  starting transfers between devices: 55.1 us -> 67.6 us
    ppermute x33, waiting for transfers between devices: 84.1 us -> 68 us  [node_swap(): return lax.ppermute(value, 'node', pairs)]
    ppermute x33, starting transfers between devices: 46.4 us -> 59.3 us  [node_swap(): return lax.ppermute(value, 'node', pairs)]
  transfers between devices with their start and end apart: 47 -> 47, of which waited for: 19 -> 18; matrix products, arithmetic and copies ran while one was open for 0% -> 0% of each run, Pallas kernels for 20% -> 19%
where the time goes in v9:
time: 205 us; the launch traced here: 204 us
  waiting for transfers between devices  81.6 us (40%)
  starting transfers between devices  67.6 us (33%)
  Pallas kernels  48.2 us (24%)
  local copies, waits for them, and re-layouts  4.83 us (2%)
    ppermute x33, waiting for transfers between devices, node_swap(): return lax.ppermute(value, 'node', pairs)  68 us
    ppermute x33, starting transfers between devices, node_swap(): return lax.ppermute(value, 'node', pairs)  59.3 us
    pallas_call x52, Pallas kernels, call(): pl.pallas_call(ordered, grid_spec=pltpu.PrefetchScalarGridSpec(num_scalar...  48.2 us
    ppermute x14, waiting for transfers between devices, feat_swap(): return lax.ppermute(value, 'feat', pairs)  13.5 us
    ppermute x14, starting transfers between devices, feat_swap(): return lax.ppermute(value, 'feat', pairs)  8.27 us
    unnamed x25, local copies, waits for them, and re-layouts  4.83 us
  transfers between devices with their start and end apart: 47, of which 18 were waited for; matrix products, arithmetic and copies ran while one was open for 0% of the time, Pallas kernels for 19%

profile of v9, /device:TPU:0, one launch (start us, length us, event | category | flops | bytes accessed | tf_op | source)
XLA Modules:
  0.0 204.2 jit_solution(9301380223629883180)
XLA Ops:
  1.3 3.9 %shard_map.128 = (f32[16,64,128]{2,1,0:T(8,128)}, f32[8,128]{1,0:T(8,128)}) custom-call(s32[4]{0:T(128)} %pad_add_fusion.refs_0_, s32[8,16]{1,0:T(8,128)} %refs_1_.27, f32[64,4096]{1,0:T(8,128)} %refs_0_.3, f32[8,16,128,128]{3,2,1,0:T(8,128)} %refs_1_.15), custom_call_target="tpu_custom_call" | custom-call | flops 1 | bytes 1 | tf_op jit(solution)/shard_map/pallas_call | solution.py:112
  5.2 3.0 %collective-permute-start.2 = (f32[16,64,128]{2,1,0:T(8,128)}, f32[16,64,128]{2,1,0:T(8,128)S(1)}, u32[]{:S(2)}, u32[]{:S(2)}) collective-permute-start(f32[16,64,128]{2,1,0:T(8,128)} %get-tuple-element.50), channel_id=1, source_target_pairs={{0,1},{1,0},{2,3},{3,2},{4,5},{5,4},{6,7},{7,6},{8,9},{9,8},{10,11... | collective-permute-start | bytes 1572872 | tf_op jit(solution)/shard_map/ppermute | solution.py:547
  8.9 1.6 collective-permute-start
  10.5 3.4 %copy-done = f32[8,16,128,128]{3,2,1,0:T(8,128)S(1)} copy-done((f32[8,16,128,128]{3,2,1,0:T(8,128)S(1)}, f32[8,16,128,128]{3,2,1,0:T(8,128)}, u32[]{:S(2)}) %copy-start) | copy-done | bytes 8388632
  14.9 2.7 %collective-permute-start.1 = (s32[16,16]{1,0:T(8,128)S(1)}, s32[16,16]{1,0:T(8,128)S(1)}, u32[]{:S(2)}, u32[]{:S(2)}) collective-permute-start(s32[16,16]{1,0:T(8,128)S(1)} %shard_map.131.refs_4_.refs_1_), channel_id=1, source_target_pairs={{0,4},{1,5},{2,6},{3,7},{4,0},{5,1},{6,2},{7,3},{8,12},{9,13},{10,... | collective-permute-start | bytes 3080 | tf_op jit(solution)/shard_map/ppermute | solution.py:547
  17.5 2.2 %shard_map.132 = (f32[16,64,128]{2,1,0:T(8,128)S(1)}, f32[16,64,128]{2,1,0:T(8,128)S(1)}, f32[16,64,128]{2,1,0:T(8,128)S(1)}) custom-call(s32[4]{0:T(128)S(1)} %copy-done.6, s32[8,16]{1,0:T(8,128)S(1)} %copy-done.5, f32[64,4096]{1,0:T(8,128)S(1)} %get-tuple-element.45.refs_2_.refs_3_.refs_1_, f32[8,16,128,128]{3,2,1,0:T(8,128)S(1)} %get-tuple-element.46.refs_3_.refs_4_, ...), custom_call_target="tpu_custom_call" | custom-call | flops 1 | bytes 1 | tf_op jit(solution)/shard_map/pallas_call | solution.py:112
  20.3 1.5 shard_map.134
  21.8 1.9 collective-permute-start.4
  23.7 1.5 collective-permute-start.3
  25.6 1.5 collective-permute-start.11
  27.1 9.6 %collective-permute-done.4.refs_1_ = f32[16,64,128]{2,1,0:T(8,128)S(1)} collective-permute-done((f32[16,64,128]{2,1,0:T(8,128)S(1)}, f32[16,64,128]{2,1,0:T(8,128)S(1)}, u32[]{:S(2)}, u32[]{:S(2)}) %collective-permute-start.4) | collective-permute-done | bytes 524320 | tf_op jit(solution)/shard_map/ppermute | solution.py:547
  36.8 1.8 collective-permute-start.5
  38.6 1.5 collective-permute-start.10
  40.8 1.5 shard_map.139
  42.3 3.9 %collective-permute-done.6.refs_1_ = f32[16,64,128]{2,1,0:T(8,128)S(1)} collective-permute-done((f32[16,64,128]{2,1,0:T(8,128)S(1)}, f32[16,64,128]{2,1,0:T(8,128)S(1)}, u32[]{:S(2)}, u32[]{:S(2)}) %collective-permute-start.6) | collective-permute-done | bytes 524320 | tf_op jit(solution)/shard_map/ppermute | solution.py:547
  46.2 1.5 collective-permute-start.13
  48.5 7.1 %collective-permute-start.9 = (f32[16,64,128]{2,1,0:T(8,128)S(1)}, f32[16,64,128]{2,1,0:T(8,128)S(1)}, u32[]{:S(2)}, u32[]{:S(2)}) collective-permute-start(f32[16,64,128]{2,1,0:T(8,128)S(1)} %shard_map.141.refs_6_.refs_0_), channel_id=1, source_target_pairs={{0,2},{1,3},{2,0},{3,1},{4,6},{5,7},{6,4},{7,5},{8,10},{9,11},{10,... | collective-permute-start | bytes 1572872 | tf_op jit(solution)/shard_map/ppermute | solution.py:547
  55.6 1.5 shard_map.142
  57.7 3.4 %collective-permute-done.13.refs_1_ = f32[16,64,128]{2,1,0:T(8,128)S(1)} collective-permute-done((f32[16,64,128]{2,1,0:T(8,128)S(1)}, f32[16,64,128]{2,1,0:T(8,128)S(1)}, u32[]{:S(2)}, u32[]{:S(2)}) %collective-permute-start.13) | collective-permute-done | bytes 524320 | tf_op jit(solution)/shard_map/ppermute | solution.py:547
  61.8 1.5 collective-permute-start.8
  63.3 4.4 %collective-permute-start.16 = (f32[16,64,128]{2,1,0:T(8,128)S(1)}, f32[16,64,128]{2,1,0:T(8,128)S(1)}, u32[]{:S(2)}, u32[]{:S(2)}) collective-permute-start(f32[16,64,128]{2,1,0:T(8,128)S(1)} %shard_map.143.refs_2_), channel_id=1, source_target_pairs={{0,2},{1,3},{2,0},{3,1},{4,6},{5,7},{6,4},{7,5},{8,10},{9,11},{10,... | collective-permute-start | bytes 1572872 | tf_op jit(solution)/shard_map/ppermute | solution.py:547
  68.3 2.9 %collective-permute-done.10.refs_0_ = f32[64,4096]{1,0:T(8,128)S(1)} collective-permute-done((f32[64,4096]{1,0:T(8,128)S(1)}, f32[64,4096]{1,0:T(8,128)S(1)}, u32[]{:S(2)}, u32[]{:S(2)}) %collective-permute-start.10) | collective-permute-done | bytes 1048608 | tf_op jit(solution)/shard_map/ppermute | solution.py:551
  73.1 4.4 %collective-permute-start.14 = (f32[16,64,128]{2,1,0:T(8,128)S(1)}, f32[16,64,128]{2,1,0:T(8,128)S(1)}, u32[]{:S(2)}, u32[]{:S(2)}) collective-permute-start(f32[16,64,128]{2,1,0:T(8,128)S(1)} %shard_map.146.refs_1_), channel_id=1, source_target_pairs={{0,2},{1,3},{2,0},{3,1},{4,6},{5,7},{6,4},{7,5},{8,10},{9,11},{10,... | collective-permute-start | bytes 1572872 | tf_op jit(solution)/shard_map/ppermute | solution.py:547
  77.7 1.5 shard_map.150
  79.2 3.6 %collective-permute-done.16.refs_2_ = f32[16,64,128]{2,1,0:T(8,128)S(1)} collective-permute-done((f32[16,64,128]{2,1,0:T(8,128)S(1)}, f32[16,64,128]{2,1,0:T(8,128)S(1)}, u32[]{:S(2)}, u32[]{:S(2)}) %collective-permute-start.16) | collective-permute-done | bytes 524320 | tf_op jit(solution)/shard_map/ppermute | solution.py:547
  84.3 7.8 %collective-permute-done.14.refs_2_ = f32[16,64,128]{2,1,0:T(8,128)S(1)} collective-permute-done((f32[16,64,128]{2,1,0:T(8,128)S(1)}, f32[16,64,128]{2,1,0:T(8,128)S(1)}, u32[]{:S(2)}, u32[]{:S(2)}) %collective-permute-start.14) | collective-permute-done | bytes 524320 | tf_op jit(solution)/shard_map/ppermute | solution.py:547
  94.1 1.5 collective-permute-start.18
  96.1 4.9 %shard_map.154.refs_1_.refs_6_ = f32[2,256,2048]{2,1,0:T(8,128)S(1)} custom-call(s32[4]{0:T(128)S(1)} %copy-done.6, f32[64,4096]{1,0:T(8,128)S(1)} %get-tuple-element.45.refs_2_.refs_3_.refs_1_, f32[64,4096]{1,0:T(8,128)S(1)} %shard_map.148.refs_2_, f32[64,4096]{1,0:T(8,128)S(1)} %collective-permute-done.19.refs_3_, ...), custom_call_target="tpu_custom_call" | custom-call | flops 1 | bytes 1 | tf_op jit(solution)/shard_map/pallas_call | solution.py:112
  101.0 6.1 %collective-permute-done.18.refs_0_ = f32[16,64,128]{2,1,0:T(8,128)S(1)} collective-permute-done((f32[16,64,128]{2,1,0:T(8,128)S(1)}, f32[16,64,128]{2,1,0:T(8,128)S(1)}, u32[]{:S(2)}, u32[]{:S(2)}) %collective-permute-start.18) | collective-permute-done | bytes 524320 | tf_op jit(solution)/shard_map/ppermute | solution.py:551
  107.7 4.1 %shard_map.156 = (f32[1024,256]{1,0:T(8,128)}, f32[256,2048]{1,0:T(8,128)S(1)}, f32[16,64,128]{2,1,0:T(8,128)S(1)}) custom-call(s32[4]{0:T(128)S(1)} %copy-done.6, f32[16,64,128]{2,1,0:T(8,128)S(1)} %shard_map.151.refs_5_.refs_1_.refs_3_, f32[16,64,128]{2,1,0:T(8,128)S(1)} %shard_map.153.refs_7_.refs_2_, f32[16,64,128]{2,1,0:T(8,128)S(1)} %collective-permute-done.26.refs_3_, ...), custom_call_target="tpu_custom_call" | custom-call | flops 1 | bytes 1 | tf_op jit(solution)/shard_map/pallas_call | solution.py:112
  113.8 4.0 %shard_map.157 = (f32[1024,256]{1,0:T(8,128)}, f32[256,2048]{1,0:T(8,128)S(1)}, f32[16,64,128]{2,1,0:T(8,128)S(1)}) custom-call(s32[4]{0:T(128)S(1)} %copy-done.6, f32[16,64,128]{2,1,0:T(8,128)S(1)} %shard_map.152.refs_1_.refs_3_, f32[16,64,128]{2,1,0:T(8,128)S(1)} %shard_map.155.refs_12_.refs_2_, ...), custom_call_target="tpu_custom_call", output_to_operand_aliasing={{0}: (12, {})} | custom-call | flops 1 | bytes 1 | tf_op jit(solution)/shard_map/pallas_call | solution.py:112
  118.6 5.7 %collective-permute-start.33 = (f32[16,64,128]{2,1,0:T(8,128)S(1)}, f32[16,64,128]{2,1,0:T(8,128)S(1)}, u32[]{:S(2)}, u32[]{:S(2)}) collective-permute-start(f32[16,64,128]{2,1,0:T(8,128)S(1)} %get-tuple-element.63.refs_5_.refs_3_), channel_id=1, source_target_pairs={{0,2},{1,3},{2,0},{3,1},{4,6},{5,7},{6,4},{7,5},{8,10},{9,11},{10,... | collective-permute-start | bytes 1572872 | tf_op jit(solution)/shard_map/ppermute | solution.py:547
  124.2 2.1 %shard_map.158 = (f32[16,64,128]{2,1,0:T(8,128)S(1)}, f32[144,256]{1,0:T(8,128)S(1)}) custom-call(s32[4]{0:T(128)S(1)} %copy-done.6, f32[256,256]{1,0:T(8,128)S(1)} %copy-done.2, f32[64,4096]{1,0:T(8,128)S(1)} %get-tuple-element.45.refs_2_.refs_3_.refs_1_, f32[16,64,128]{2,1,0:T(8,128)S(1)} %shard_map.151.refs_5_.refs_1_.refs_3_, ...), custom_call_target="tpu_custom_call" | custom-call | flops 1 | bytes 1 | tf_op jit(solution)/shard_map/pallas_call | solution.py:112
  126.5 2.1 %shard_map.160 = (f32[16,64,128]{2,1,0:T(8,128)S(1)}, f32[144,256]{1,0:T(8,128)S(1)}) custom-call(s32[4]{0:T(128)S(1)} %copy-done.6, f32[256,256]{1,0:T(8,128)S(1)} %copy-done.2, f32[64,4096]{1,0:T(8,128)S(1)} %get-tuple-element.45.refs_2_.refs_3_.refs_1_, f32[16,64,128]{2,1,0:T(8,128)S(1)} %shard_map.152.refs_1_.refs_3_, ...), custom_call_target="tpu_custom_call" | custom-call | flops 1 | bytes 1 | tf_op jit(solution)/shard_map/pallas_call | solution.py:112
  132.8 5.0 %collective-permute-done.33.refs_1_.refs_0_ = f32[16,64,128]{2,1,0:T(8,128)S(1)} collective-permute-done((f32[16,64,128]{2,1,0:T(8,128)S(1)}, f32[16,64,128]{2,1,0:T(8,128)S(1)}, u32[]{:S(2)}, u32[]{:S(2)}) %collective-permute-start.33) | collective-permute-done | bytes 524320 | tf_op jit(solution)/shard_map/ppermute | solution.py:547
  141.5 7.5 %collective-permute-done.31.refs_1_.refs_4_.refs_6_ = f32[16,64,128]{2,1,0:T(8,128)S(1)} collective-permute-done((f32[16,64,128]{2,1,0:T(8,128)S(1)}, f32[16,64,128]{2,1,0:T(8,128)S(1)}, u32[]{:S(2)}, u32[]{:S(2)}) %collective-permute-start.31) | collective-permute-done | bytes 524320 | tf_op jit(solution)/shard_map/ppermute | solution.py:547
  150.4 9.9 %collective-permute-done.36.refs_8_.refs_5_.refs_7_ = f32[16,64,128]{2,1,0:T(8,128)S(1)} collective-permute-done((f32[16,64,128]{2,1,0:T(8,128)S(1)}, f32[16,64,128]{2,1,0:T(8,128)S(1)}, u32[]{:S(2)}, u32[]{:S(2)}) %collective-permute-start.36) | collective-permute-done | bytes 524320 | tf_op jit(solution)/shard_map/ppermute | solution.py:547
  165.9 4.0 %collective-permute-start.41 = (f32[144,256]{1,0:T(8,128)S(1)}, f32[144,256]{1,0:T(8,128)S(1)}, u32[]{:S(2)}, u32[]{:S(2)}) collective-permute-start(f32[144,256]{1,0:T(8,128)S(1)} %shard_map.169.refs_6_.refs_0_), channel_id=1, source_target_pairs={{0,6},{1,7},{2,4},{3,5},{4,2},{5,3},{6,0},{7,1},{8,14},{9,15},{10,... | collective-permute-start | bytes 442376 | tf_op jit(solution)/shard_map/ppermute | solution.py:547
  169.9 1.9 shard_map.172
  173.1 7.0 %collective-permute-done.39.refs_3_.refs_4_.refs_6_ = f32[16,64,128]{2,1,0:T(8,128)S(1)} collective-permute-done((f32[16,64,128]{2,1,0:T(8,128)S(1)}, f32[16,64,128]{2,1,0:T(8,128)S(1)}, u32[]{:S(2)}, u32[]{:S(2)}) %collective-permute-start.39) | collective-permute-done | bytes 524320 | tf_op jit(solution)/shard_map/ppermute | solution.py:547
  180.2 2.0 shard_map.174
  182.8 5.8 %collective-permute-done.40.refs_5_.refs_7_ = f32[16,64,128]{2,1,0:T(8,128)S(1)} collective-permute-done((f32[16,64,128]{2,1,0:T(8,128)S(1)}, f32[16,64,128]{2,1,0:T(8,128)S(1)}, u32[]{:S(2)}, u32[]{:S(2)}) %collective-permute-start.40) | collective-permute-done | bytes 524320 | tf_op jit(solution)/shard_map/ppermute | solution.py:547
  189.5 1.5 collective-permute-start.45
  191.0 1.6 collective-permute-start.46
  192.6 2.0 shard_map.177
  194.6 3.1 %collective-permute-done.46.refs_2_.refs_3_ = f32[2,144,256]{2,1,0:T(8,128)S(1)} collective-permute-done((f32[2,144,256]{2,1,0:T(8,128)S(1)}, f32[2,144,256]{2,1,0:T(8,128)S(1)}, u32[]{:S(2)}, u32[]{:S(2)}) %collective-permute-start.46) | collective-permute-done | bytes 294944 | tf_op jit(solution)/shard_map/ppermute | solution.py:551
  199.1 2.0 collective-permute-done.45.refs_4_
  201.8 2.2 %shard_map.179 = (f32[64,4096]{1,0:T(8,128)}, f32[8,128]{1,0:T(8,128)}) custom-call(s32[4]{0:T(128)S(1)} %copy-done.6, s32[8,16]{1,0:T(8,128)S(1)} %copy-done.5, s32[8,16]{1,0:T(8,128)S(1)} %shard_map.133.refs_2_.refs_6_.refs_1_, f32[8,16,128,128]{3,2,1,0:T(8,128)S(1)} %get-tuple-element.46.refs_3_.refs_4_, ...), custom_call_target="tpu_custom_call" | custom-call | flops 1 | bytes 1 | tf_op jit(solution)/shard_map/pallas_call | solution.py:112
  (125 shorter events, 36.0 us)
Async XLA Ops:
  5.2 15.1 %collective-permute-start.2 = (f32[16,64,128]{2,1,0:T(8,128)}, f32[16,64,128]{2,1,0:T(8,128)S(1)}, u32[]{:S(2)}, u32[]{:S(2)}) collective-permute-start(f32[16,64,128]{2,1,0:T(8,128)} %get-tuple-element.50), channel_id=1, source_target_pairs={{0,1},{1,0},{2,3},{3,2},{4,5},{5,4},{6,7},{7,6},{8,9},{9,8},{10,11... | collective-permute-start | bytes 1572872 | tf_op jit(solution)/shard_map/ppermute | solution.py:547
  8.9 6.0 %collective-permute-start = (s32[8,16]{1,0:T(8,128)S(1)}, s32[8,16]{1,0:T(8,128)S(1)}, u32[]{:S(2)}, u32[]{:S(2)}) collective-permute-start(s32[8,16]{1,0:T(8,128)S(1)} %shard_map.129.refs_3_.refs_0_), channel_id=1, source_target_pairs={{0,2},{1,3},{2,0},{3,1},{4,6},{5,7},{6,4},{7,5},{8,10},{9,11},{10,... | collective-permute-start | bytes 1544 | tf_op jit(solution)/shard_map/ppermute | solution.py:547
  14.9 4.9 %collective-permute-start.1 = (s32[16,16]{1,0:T(8,128)S(1)}, s32[16,16]{1,0:T(8,128)S(1)}, u32[]{:S(2)}, u32[]{:S(2)}) collective-permute-start(s32[16,16]{1,0:T(8,128)S(1)} %shard_map.131.refs_4_.refs_1_), channel_id=1, source_target_pairs={{0,4},{1,5},{2,6},{3,7},{4,0},{5,1},{6,2},{7,3},{8,12},{9,13},{10,... | collective-permute-start | bytes 3080 | tf_op jit(solution)/shard_map/ppermute | solution.py:547
  21.8 14.9 %collective-permute-start.4 = (f32[16,64,128]{2,1,0:T(8,128)S(1)}, f32[16,64,128]{2,1,0:T(8,128)S(1)}, u32[]{:S(2)}, u32[]{:S(2)}) collective-permute-start(f32[16,64,128]{2,1,0:T(8,128)S(1)} %get-tuple-element.52.refs_0_), channel_id=1, source_target_pairs={{0,2},{1,3},{2,0},{3,1},{4,6},{5,7},{6,4},{7,5},{8,10},{9,11},{10,... | collective-permute-start | bytes 1572872 | tf_op jit(solution)/shard_map/ppermute | solution.py:547
  23.7 13.1 %collective-permute-start.3 = (f32[16,64,128]{2,1,0:T(8,128)S(1)}, f32[16,64,128]{2,1,0:T(8,128)S(1)}, u32[]{:S(2)}, u32[]{:S(2)}) collective-permute-start(f32[16,64,128]{2,1,0:T(8,128)S(1)} %shard_map.135.refs_1_), channel_id=1, source_target_pairs={{0,1},{1,0},{2,3},{3,2},{4,5},{5,4},{6,7},{7,6},{8,9},{9,8},{10,11... | collective-permute-start | bytes 1572872 | tf_op jit(solution)/shard_map/ppermute | solution.py:547
  25.2 21.0 %collective-permute-start.6 = (f32[16,64,128]{2,1,0:T(8,128)S(1)}, f32[16,64,128]{2,1,0:T(8,128)S(1)}, u32[]{:S(2)}, u32[]{:S(2)}) collective-permute-start(f32[16,64,128]{2,1,0:T(8,128)S(1)} %shard_map.136.refs_2_.refs_0_), channel_id=1, source_target_pairs={{0,2},{1,3},{2,0},{3,1},{4,6},{5,7},{6,4},{7,5},{8,10},{9,11},{10,... | collective-permute-start | bytes 1572872 | tf_op jit(solution)/shard_map/ppermute | solution.py:547
  25.6 36.2 %collective-permute-start.11 = (f32[256,1024]{1,0:T(8,128)S(1)}, f32[256,1024]{1,0:T(8,128)S(1)}, u32[]{:S(2)}, u32[]{:S(2)}) collective-permute-start(f32[256,1024]{1,0:T(8,128)S(1)} %get-tuple-element.44.refs_2_.refs_7_), channel_id=1, source_target_pairs={{0,16},{8,24},{16,0},{24,8},{1,17},{9,25},{17,1},{25,9},{2,18},{10... | collective-permute-start | bytes 3145736 | tf_op jit(solution)/shard_map/ppermute | solution.py:551
  36.8 11.0 %collective-permute-start.5 = (f32[16,64,128]{2,1,0:T(8,128)S(1)}, f32[16,64,128]{2,1,0:T(8,128)S(1)}, u32[]{:S(2)}, u32[]{:S(2)}) collective-permute-start(f32[16,64,128]{2,1,0:T(8,128)S(1)} %shard_map.138.refs_6_), channel_id=1, source_target_pairs={{0,1},{1,0},{2,3},{3,2},{4,5},{5,4},{6,7},{7,6},{8,9},{9,8},{10,11... | collective-permute-start | bytes 1572872 | tf_op jit(solution)/shard_map/ppermute | solution.py:547
  38.6 32.7 %collective-permute-start.10 = (f32[64,4096]{1,0:T(8,128)S(1)}, f32[64,4096]{1,0:T(8,128)S(1)}, u32[]{:S(2)}, u32[]{:S(2)}) collective-permute-start(f32[64,4096]{1,0:T(8,128)S(1)} %get-tuple-element.45.refs_2_.refs_3_.refs_1_), channel_id=1, source_target_pairs={{0,16},{8,24},{16,0},{24,8},{1,17},{9,25},{17,1},{25,9},{2,18},{10... | collective-permute-start | bytes 3145736 | tf_op jit(solution)/shard_map/ppermute | solution.py:551
  40.1 8.4 %collective-permute-start.7 = (f32[16,64,128]{2,1,0:T(8,128)S(1)}, f32[16,64,128]{2,1,0:T(8,128)S(1)}, u32[]{:S(2)}, u32[]{:S(2)}) collective-permute-start(f32[16,64,128]{2,1,0:T(8,128)S(1)} %shard_map.137.refs_2_), channel_id=1, source_target_pairs={{2,4},{3,5},{4,2},{5,3},{0,0},{1,1},{6,6},{7,7},{10,12},{11,13},{1... | collective-permute-start | bytes 1572872 | tf_op jit(solution)/shard_map/ppermute | solution.py:547
  46.2 14.9 %collective-permute-start.13 = (f32[16,64,128]{2,1,0:T(8,128)S(1)}, f32[16,64,128]{2,1,0:T(8,128)S(1)}, u32[]{:S(2)}, u32[]{:S(2)}) collective-permute-start(f32[16,64,128]{2,1,0:T(8,128)S(1)} %get-tuple-element.56.refs_0_), channel_id=1, source_target_pairs={{0,2},{1,3},{2,0},{3,1},{4,6},{5,7},{6,4},{7,5},{8,10},{9,11},{10,... | collective-permute-start | bytes 1572872 | tf_op jit(solution)/shard_map/ppermute | solution.py:547
  47.8 15.5 %collective-permute-start.12 = (f32[16,64,128]{2,1,0:T(8,128)S(1)}, f32[16,64,128]{2,1,0:T(8,128)S(1)}, u32[]{:S(2)}, u32[]{:S(2)}) collective-permute-start(f32[16,64,128]{2,1,0:T(8,128)S(1)} %shard_map.140.refs_1_), channel_id=1, source_target_pairs={{2,4},{3,5},{4,2},{5,3},{0,0},{1,1},{6,6},{7,7},{10,12},{11,13},{1... | collective-permute-start | bytes 1572872 | tf_op jit(solution)/shard_map/ppermute | solution.py:547
  48.5 23.8 %collective-permute-start.9 = (f32[16,64,128]{2,1,0:T(8,128)S(1)}, f32[16,64,128]{2,1,0:T(8,128)S(1)}, u32[]{:S(2)}, u32[]{:S(2)}) collective-permute-start(f32[16,64,128]{2,1,0:T(8,128)S(1)} %shard_map.141.refs_6_.refs_0_), channel_id=1, source_target_pairs={{0,2},{1,3},{2,0},{3,1},{4,6},{5,7},{6,4},{7,5},{8,10},{9,11},{10,... | collective-permute-start | bytes 1572872 | tf_op jit(solution)/shard_map/ppermute | solution.py:547
  61.1 12.0 %collective-permute-start.17 = (f32[16,64,128]{2,1,0:T(8,128)S(1)}, f32[16,64,128]{2,1,0:T(8,128)S(1)}, u32[]{:S(2)}, u32[]{:S(2)}) collective-permute-start(f32[16,64,128]{2,1,0:T(8,128)S(1)} %shard_map.145.refs_3_), channel_id=1, source_target_pairs={{2,4},{3,5},{4,2},{5,3},{0,0},{1,1},{6,6},{7,7},{10,12},{11,13},{1... | collective-permute-start | bytes 1572872 | tf_op jit(solution)/shard_map/ppermute | solution.py:547
  61.8 15.7 %collective-permute-start.8 = (f32[16,64,128]{2,1,0:T(8,128)S(1)}, f32[16,64,128]{2,1,0:T(8,128)S(1)}, u32[]{:S(2)}, u32[]{:S(2)}) collective-permute-start(f32[16,64,128]{2,1,0:T(8,128)S(1)} %shard_map.144.refs_2_), channel_id=1, source_target_pairs={{0,1},{1,0},{2,3},{3,2},{4,5},{5,4},{6,7},{7,6},{8,9},{9,8},{10,11... | collective-permute-start | bytes 1572872 | tf_op jit(solution)/shard_map/ppermute | solution.py:547
  63.3 19.5 %collective-permute-start.16 = (f32[16,64,128]{2,1,0:T(8,128)S(1)}, f32[16,64,128]{2,1,0:T(8,128)S(1)}, u32[]{:S(2)}, u32[]{:S(2)}) collective-permute-start(f32[16,64,128]{2,1,0:T(8,128)S(1)} %shard_map.143.refs_2_), channel_id=1, source_target_pairs={{0,2},{1,3},{2,0},{3,1},{4,6},{5,7},{6,4},{7,5},{8,10},{9,11},{10,... | collective-permute-start | bytes 1572872 | tf_op jit(solution)/shard_map/ppermute | solution.py:547
  72.4 11.9 %collective-permute-start.15 = (f32[16,64,128]{2,1,0:T(8,128)S(1)}, f32[16,64,128]{2,1,0:T(8,128)S(1)}, u32[]{:S(2)}, u32[]{:S(2)}) collective-permute-start(f32[16,64,128]{2,1,0:T(8,128)S(1)} %shard_map.149.refs_6_), channel_id=1, source_target_pairs={{2,4},{3,5},{4,2},{5,3},{0,0},{1,1},{6,6},{7,7},{10,12},{11,13},{1... | collective-permute-start | bytes 1572872 | tf_op jit(solution)/shard_map/ppermute | solution.py:547
  73.1 22.6 %collective-permute-start.19 = (f32[64,4096]{1,0:T(8,128)S(1)}, f32[64,4096]{1,0:T(8,128)S(1)}, u32[]{:S(2)}, u32[]{:S(2)}) collective-permute-start(f32[64,4096]{1,0:T(8,128)S(1)} %get-tuple-element.45.refs_2_.refs_3_.refs_1_), channel_id=1, source_target_pairs={{0,8},{8,0},{16,24},{24,16},{1,9},{9,1},{17,25},{25,17},{2,10},{10... | collective-permute-start | bytes 3145736 | tf_op jit(solution)/shard_map/ppermute | solution.py:551
  73.1 18.9 %collective-permute-start.14 = (f32[16,64,128]{2,1,0:T(8,128)S(1)}, f32[16,64,128]{2,1,0:T(8,128)S(1)}, u32[]{:S(2)}, u32[]{:S(2)}) collective-permute-start(f32[16,64,128]{2,1,0:T(8,128)S(1)} %shard_map.146.refs_1_), channel_id=1, source_target_pairs={{0,2},{1,3},{2,0},{3,1},{4,6},{5,7},{6,4},{7,5},{8,10},{9,11},{10,... | collective-permute-start | bytes 1572872 | tf_op jit(solution)/shard_map/ppermute | solution.py:547
  77.5 18.1 %collective-permute-start.20 = (f32[64,4096]{1,0:T(8,128)S(1)}, f32[64,4096]{1,0:T(8,128)S(1)}, u32[]{:S(2)}, u32[]{:S(2)}) collective-permute-start(f32[64,4096]{1,0:T(8,128)S(1)} %shard_map.148.refs_2_), channel_id=1, source_target_pairs={{0,8},{8,0},{16,24},{24,16},{1,9},{9,1},{17,25},{25,17},{2,10},{10... | collective-permute-start | bytes 3145736 | tf_op jit(solution)/shard_map/ppermute | solution.py:551
  79.2 17.0 %copy-start.2 = (f32[256,256]{1,0:T(8,128)S(1)}, f32[256,256]{1,0:T(8,128)}, u32[]{:S(2)}) copy-start(f32[256,256]{1,0:T(8,128)} %refs_1_.22) | copy-start | bytes 786436
  83.4 10.6 %collective-permute-start.21 = (f32[16,64,128]{2,1,0:T(8,128)S(1)}, f32[16,64,128]{2,1,0:T(8,128)S(1)}, u32[]{:S(2)}, u32[]{:S(2)}) collective-permute-start(f32[16,64,128]{2,1,0:T(8,128)S(1)} %shard_map.151.refs_5_.refs_1_.refs_3_), channel_id=1, source_target_pairs={{0,16},{8,24},{16,0},{24,8},{1,17},{9,25},{17,1},{25,9},{2,18},{10... | collective-permute-start | bytes 1572872 | tf_op jit(solution)/shard_map/ppermute | solution.py:551
  84.3 22.9 %collective-permute-start.24 = (f32[256,1024]{1,0:T(8,128)S(1)}, f32[256,1024]{1,0:T(8,128)S(1)}, u32[]{:S(2)}, u32[]{:S(2)}) collective-permute-start(f32[256,1024]{1,0:T(8,128)S(1)} %get-tuple-element.44.refs_2_.refs_7_), channel_id=1, source_target_pairs={{0,8},{8,0},{16,24},{24,16},{1,9},{9,1},{17,25},{25,17},{2,10},{10... | collective-permute-start | bytes 3145736 | tf_op jit(solution)/shard_map/ppermute | solution.py:551
  92.1 15.6 %collective-permute-start.25 = (f32[256,1024]{1,0:T(8,128)S(1)}, f32[256,1024]{1,0:T(8,128)S(1)}, u32[]{:S(2)}, u32[]{:S(2)}) collective-permute-start(f32[256,1024]{1,0:T(8,128)S(1)} %shard_map.147.refs_1_.refs_8_), channel_id=1, source_target_pairs={{0,8},{8,0},{16,24},{24,16},{1,9},{9,1},{17,25},{25,17},{2,10},{10... | collective-permute-start | bytes 3145736 | tf_op jit(solution)/shard_map/ppermute | solution.py:551
  94.1 13.1 %collective-permute-start.18 = (f32[16,64,128]{2,1,0:T(8,128)S(1)}, f32[16,64,128]{2,1,0:T(8,128)S(1)}, u32[]{:S(2)}, u32[]{:S(2)}) collective-permute-start(f32[16,64,128]{2,1,0:T(8,128)S(1)} %shard_map.152.refs_1_.refs_3_), channel_id=1, source_target_pairs={{0,16},{8,24},{16,0},{24,8},{1,17},{9,25},{17,1},{25,9},{2,18},{10... | collective-permute-start | bytes 1572872 | tf_op jit(solution)/shard_map/ppermute | solution.py:551
  95.6 12.0 %collective-permute-start.26 = (f32[16,64,128]{2,1,0:T(8,128)S(1)}, f32[16,64,128]{2,1,0:T(8,128)S(1)}, u32[]{:S(2)}, u32[]{:S(2)}) collective-permute-start(f32[16,64,128]{2,1,0:T(8,128)S(1)} %shard_map.151.refs_5_.refs_1_.refs_3_), channel_id=1, source_target_pairs={{0,8},{8,0},{16,24},{24,16},{1,9},{9,1},{17,25},{25,17},{2,10},{10... | collective-permute-start | bytes 1572872 | tf_op jit(solution)/shard_map/ppermute | solution.py:551
  95.6 12.0 %collective-permute-start.27 = (f32[16,64,128]{2,1,0:T(8,128)S(1)}, f32[16,64,128]{2,1,0:T(8,128)S(1)}, u32[]{:S(2)}, u32[]{:S(2)}) collective-permute-start(f32[16,64,128]{2,1,0:T(8,128)S(1)} %shard_map.153.refs_7_.refs_2_), channel_id=1, source_target_pairs={{0,8},{8,0},{16,24},{24,16},{1,9},{9,1},{17,25},{25,17},{2,10},{10... | collective-permute-start | bytes 1572872 | tf_op jit(solution)/shard_map/ppermute | solution.py:551
  107.1 6.7 %collective-permute-start.22 = (f32[16,64,128]{2,1,0:T(8,128)S(1)}, f32[16,64,128]{2,1,0:T(8,128)S(1)}, u32[]{:S(2)}, u32[]{:S(2)}) collective-permute-start(f32[16,64,128]{2,1,0:T(8,128)S(1)} %shard_map.152.refs_1_.refs_3_), channel_id=1, source_target_pairs={{0,8},{8,0},{16,24},{24,16},{1,9},{9,1},{17,25},{25,17},{2,10},{10... | collective-permute-start | bytes 1572872 | tf_op jit(solution)/shard_map/ppermute | solution.py:551
  107.1 6.7 %collective-permute-start.23 = (f32[16,64,128]{2,1,0:T(8,128)S(1)}, f32[16,64,128]{2,1,0:T(8,128)S(1)}, u32[]{:S(2)}, u32[]{:S(2)}) collective-permute-start(f32[16,64,128]{2,1,0:T(8,128)S(1)} %shard_map.155.refs_12_.refs_2_), channel_id=1, source_target_pairs={{0,8},{8,0},{16,24},{24,16},{1,9},{9,1},{17,25},{25,17},{2,10},{10... | collective-permute-start | bytes 1572872 | tf_op jit(solution)/shard_map/ppermute | solution.py:551
  111.7 14.8 %collective-permute-start.28 = (f32[16,64,128]{2,1,0:T(8,128)S(1)}, f32[16,64,128]{2,1,0:T(8,128)S(1)}, u32[]{:S(2)}, u32[]{:S(2)}) collective-permute-start(f32[16,64,128]{2,1,0:T(8,128)S(1)} %get-tuple-element.60.refs_13_.refs_2_.refs_4_), channel_id=1, source_target_pairs={{0,2},{1,3},{2,0},{3,1},{4,6},{5,7},{6,4},{7,5},{8,10},{9,11},{10,... | collective-permute-start | bytes 1572872 | tf_op jit(solution)/shard_map/ppermute | solution.py:547
  112.9 15.6 %collective-permute-start.30 = (f32[16,64,128]{2,1,0:T(8,128)S(1)}, f32[16,64,128]{2,1,0:T(8,128)S(1)}, u32[]{:S(2)}, u32[]{:S(2)}) collective-permute-start(f32[16,64,128]{2,1,0:T(8,128)S(1)} %get-tuple-element.60.refs_13_.refs_2_.refs_4_), channel_id=1, source_target_pairs={{2,4},{3,5},{4,2},{5,3},{0,0},{1,1},{6,6},{7,7},{10,12},{11,13},{1... | collective-permute-start | bytes 1572872 | tf_op jit(solution)/shard_map/ppermute | solution.py:547
  117.9 14.8 %collective-permute-start.34 = (f32[16,64,128]{2,1,0:T(8,128)S(1)}, f32[16,64,128]{2,1,0:T(8,128)S(1)}, u32[]{:S(2)}, u32[]{:S(2)}) collective-permute-start(f32[16,64,128]{2,1,0:T(8,128)S(1)} %get-tuple-element.63.refs_5_.refs_3_), channel_id=1, source_target_pairs={{2,4},{3,5},{4,2},{5,3},{0,0},{1,1},{6,6},{7,7},{10,12},{11,13},{1... | collective-permute-start | bytes 1572872 | tf_op jit(solution)/shard_map/ppermute | solution.py:547
  118.6 19.2 %collective-permute-start.33 = (f32[16,64,128]{2,1,0:T(8,128)S(1)}, f32[16,64,128]{2,1,0:T(8,128)S(1)}, u32[]{:S(2)}, u32[]{:S(2)}) collective-permute-start(f32[16,64,128]{2,1,0:T(8,128)S(1)} %get-tuple-element.63.refs_5_.refs_3_), channel_id=1, source_target_pairs={{0,2},{1,3},{2,0},{3,1},{4,6},{5,7},{6,4},{7,5},{8,10},{9,11},{10,... | collective-permute-start | bytes 1572872 | tf_op jit(solution)/shard_map/ppermute | solution.py:547
  128.6 11.2 %collective-permute-start.32 = (f32[144,256]{1,0:T(8,128)S(1)}, f32[144,256]{1,0:T(8,128)S(1)}, u32[]{:S(2)}, u32[]{:S(2)}) collective-permute-start(f32[144,256]{1,0:T(8,128)S(1)} %get-tuple-element.66.refs_1_.refs_0_), channel_id=1, source_target_pairs={{0,1},{1,0},{2,3},{3,2},{4,5},{5,4},{6,7},{7,6},{8,9},{9,8},{10,11... | collective-permute-start | bytes 442376 | tf_op jit(solution)/shard_map/ppermute | solution.py:547
  130.7 18.3 %collective-permute-start.31 = (f32[16,64,128]{2,1,0:T(8,128)S(1)}, f32[16,64,128]{2,1,0:T(8,128)S(1)}, u32[]{:S(2)}, u32[]{:S(2)}) collective-permute-start(f32[16,64,128]{2,1,0:T(8,128)S(1)} %shard_map.161.refs_4_.refs_2_), channel_id=1, source_target_pairs={{2,0},{3,1},{4,6},{5,7},{10,8},{11,9},{12,14},{13,15},{18,16},{19,... | collective-permute-start | bytes 1572872 | tf_op jit(solution)/shard_map/ppermute | solution.py:547
  132.0 17.8 %collective-permute-start.29 = (f32[16,64,128]{2,1,0:T(8,128)S(1)}, f32[16,64,128]{2,1,0:T(8,128)S(1)}, u32[]{:S(2)}, u32[]{:S(2)}) collective-permute-start(f32[16,64,128]{2,1,0:T(8,128)S(1)} %shard_map.159.refs_6_.refs_2_.refs_4_), channel_id=1, source_target_pairs={{2,4},{3,5},{4,2},{5,3},{0,0},{1,1},{6,6},{7,7},{10,12},{11,13},{1... | collective-permute-start | bytes 1572872 | tf_op jit(solution)/shard_map/ppermute | solution.py:547
  137.7 22.5 %collective-permute-start.36 = (f32[16,64,128]{2,1,0:T(8,128)S(1)}, f32[16,64,128]{2,1,0:T(8,128)S(1)}, u32[]{:S(2)}, u32[]{:S(2)}) collective-permute-start(f32[16,64,128]{2,1,0:T(8,128)S(1)} %shard_map.163.refs_1_.refs_3_.refs_5_), channel_id=1, source_target_pairs={{2,0},{3,1},{4,6},{5,7},{10,8},{11,9},{12,14},{13,15},{18,16},{19,... | collective-permute-start | bytes 1572872 | tf_op jit(solution)/shard_map/ppermute | solution.py:547
  139.0 23.8 %collective-permute-start.35 = (f32[16,64,128]{2,1,0:T(8,128)S(1)}, f32[16,64,128]{2,1,0:T(8,128)S(1)}, u32[]{:S(2)}, u32[]{:S(2)}) collective-permute-start(f32[16,64,128]{2,1,0:T(8,128)S(1)} %shard_map.164.refs_3_.refs_4_.refs_5_), channel_id=1, source_target_pairs={{2,4},{3,5},{4,2},{5,3},{0,0},{1,1},{6,6},{7,7},{10,12},{11,13},{1... | collective-permute-start | bytes 1572872 | tf_op jit(solution)/shard_map/ppermute | solution.py:547
  139.8 23.1 %collective-permute-start.38 = (f32[16,64,128]{2,1,0:T(8,128)S(1)}, f32[16,64,128]{2,1,0:T(8,128)S(1)}, u32[]{:S(2)}, u32[]{:S(2)}) collective-permute-start(f32[16,64,128]{2,1,0:T(8,128)S(1)} %shard_map.162.refs_3_), channel_id=1, source_target_pairs={{0,1},{1,0},{2,3},{3,2},{4,5},{5,4},{6,7},{7,6},{8,9},{9,8},{10,11... | collective-permute-start | bytes 1572872 | tf_op jit(solution)/shard_map/ppermute | solution.py:547
  149.0 13.9 %collective-permute-start.37 = (f32[144,256]{1,0:T(8,128)S(1)}, f32[144,256]{1,0:T(8,128)S(1)}, u32[]{:S(2)}, u32[]{:S(2)}) collective-permute-start(f32[144,256]{1,0:T(8,128)S(1)} %shard_map.166.refs_2_.refs_0_), channel_id=1, source_target_pairs={{0,2},{1,3},{2,0},{3,1},{4,6},{5,7},{6,4},{7,5},{8,10},{9,11},{10,... | collective-permute-start | bytes 442376 | tf_op jit(solution)/shard_map/ppermute | solution.py:547
  149.8 22.0 %collective-permute-start.42 = (f32[16,64,128]{2,1,0:T(8,128)S(1)}, f32[16,64,128]{2,1,0:T(8,128)S(1)}, u32[]{:S(2)}, u32[]{:S(2)}) collective-permute-start(f32[16,64,128]{2,1,0:T(8,128)S(1)} %shard_map.165.refs_2_), channel_id=1, source_target_pairs={{0,1},{1,0},{2,3},{3,2},{4,5},{5,4},{6,7},{7,6},{8,9},{9,8},{10,11... | collective-permute-start | bytes 1572872 | tf_op jit(solution)/shard_map/ppermute | solution.py:547
  160.2 19.9 %collective-permute-start.39 = (f32[16,64,128]{2,1,0:T(8,128)S(1)}, f32[16,64,128]{2,1,0:T(8,128)S(1)}, u32[]{:S(2)}, u32[]{:S(2)}) collective-permute-start(f32[16,64,128]{2,1,0:T(8,128)S(1)} %shard_map.167.refs_9_.refs_2_.refs_4_), channel_id=1, source_target_pairs={{2,0},{3,1},{4,6},{5,7},{10,8},{11,9},{12,14},{13,15},{18,16},{19,... | collective-permute-start | bytes 1572872 | tf_op jit(solution)/shard_map/ppermute | solution.py:547
  163.8 18.5 %collective-permute-start.44 = (f32[16,64,128]{2,1,0:T(8,128)S(1)}, f32[16,64,128]{2,1,0:T(8,128)S(1)}, u32[]{:S(2)}, u32[]{:S(2)}) collective-permute-start(f32[16,64,128]{2,1,0:T(8,128)S(1)} %shard_map.170.refs_1_), channel_id=1, source_target_pairs={{0,1},{1,0},{2,3},{3,2},{4,5},{5,4},{6,7},{7,6},{8,9},{9,8},{10,11... | collective-permute-start | bytes 1572872 | tf_op jit(solution)/shard_map/ppermute | solution.py:547
  164.6 24.0 %collective-permute-start.40 = (f32[16,64,128]{2,1,0:T(8,128)S(1)}, f32[16,64,128]{2,1,0:T(8,128)S(1)}, u32[]{:S(2)}, u32[]{:S(2)}) collective-permute-start(f32[16,64,128]{2,1,0:T(8,128)S(1)} %shard_map.171.refs_8_.refs_3_.refs_5_), channel_id=1, source_target_pairs={{2,0},{3,1},{4,6},{5,7},{10,8},{11,9},{12,14},{13,15},{18,16},{19,... | collective-permute-start | bytes 1572872 | tf_op jit(solution)/shard_map/ppermute | solution.py:547
  165.9 7.2 %collective-permute-start.41 = (f32[144,256]{1,0:T(8,128)S(1)}, f32[144,256]{1,0:T(8,128)S(1)}, u32[]{:S(2)}, u32[]{:S(2)}) collective-permute-start(f32[144,256]{1,0:T(8,128)S(1)} %shard_map.169.refs_6_.refs_0_), channel_id=1, source_target_pairs={{0,6},{1,7},{2,4},{3,5},{4,2},{5,3},{6,0},{7,1},{8,14},{9,15},{10,... | collective-permute-start | bytes 442376 | tf_op jit(solution)/shard_map/ppermute | solution.py:547
  180.1 2.1 %collective-permute-start.43 = (f32[144,256]{1,0:T(8,128)S(1)}, f32[144,256]{1,0:T(8,128)S(1)}, u32[]{:S(2)}, u32[]{:S(2)}) collective-permute-start(f32[144,256]{1,0:T(8,128)S(1)} %shard_map.173.refs_10_.refs_1_), channel_id=1, source_target_pairs={{0,8},{8,0},{16,24},{24,16},{1,9},{9,1},{17,25},{25,17},{2,10},{10... | collective-permute-start | bytes 442376 | tf_op jit(solution)/shard_map/ppermute | solution.py:551
  189.5 11.6 %collective-permute-start.45 = (f32[16,64,128]{2,1,0:T(8,128)S(1)}, f32[16,64,128]{2,1,0:T(8,128)S(1)}, u32[]{:S(2)}, u32[]{:S(2)}) collective-permute-start(f32[16,64,128]{2,1,0:T(8,128)S(1)} %shard_map.176.refs_10_), channel_id=1, source_target_pairs={{0,1},{1,0},{2,3},{3,2},{4,5},{5,4},{6,7},{7,6},{8,9},{9,8},{10,11... | collective-permute-start | bytes 1572872 | tf_op jit(solution)/shard_map/ppermute | solution.py:547
  191.0 6.7 %collective-permute-start.46 = (f32[2,144,256]{2,1,0:T(8,128)S(1)}, f32[2,144,256]{2,1,0:T(8,128)S(1)}, u32[]{:S(2)}, u32[]{:S(2)}) collective-permute-start(f32[2,144,256]{2,1,0:T(8,128)S(1)} %shard_map.175.refs_6_.refs_1_), channel_id=1, source_target_pairs={{0,16},{8,24},{16,0},{24,8},{1,17},{9,25},{17,1},{25,9},{2,18},{10... | collective-permute-start | bytes 884744 | tf_op jit(solution)/shard_map/ppermute | solution.py:551
  (11 other events, 70.4 us)
